TPU v7x, 32 devices: a whole 2x2x4 slice. The times are simulated.
32 devices in a mesh: row: 4 (over y, x), col: 8 (over z, core).
Axes of the slice: x: 2, y: 2, z: 4, core: 2. Of those that a mesh axis runs over, the one named last changes fastest.
Arguments:
- embeddings: bfloat16 [8192, 1152], P(('col', 'row')), may hold values from -6 to 6
- seed_labels: bfloat16 [8192, 256], P(('col', 'row')), may hold values from 0 to 1
- pattern: int32 [64, 16], replicated, may hold values from 0 to 63, as said below
Outputs:
- propagated: float32 [8192, 256], P(('col', 'row'))
Inputs may be any that keep to these rules, and one draw needn't show every extreme that they name: `pattern`: each row names 16 different blocks, never its own block.
All inputs are finite; a program needn't handle non-finite values.
Results may differ from a plain program's by a relative error of at most 0.0012.
Values may be sent and summed in bfloat16 or wider, within the bound.
No kernel may reach another device: no remote copies, remote signals or barrier semaphores. Data moves between devices by JAX's collectives and lax.ppermute only.
A program may use at most 64 MiB of HBM per device.

v0:
```python
import jax
import jax.numpy as jnp
from jax import lax
from jax.sharding import PartitionSpec as P

BLOCK = 128
ITERS = 2


sharpness = 30.0
mixing = 0.8
epsilon = 1e-06


def normalize_rows(embeddings):
    values = embeddings.astype(jnp.float32)
    mean_square = jnp.mean(values * values, axis=1, keepdims=True)
    scaled = values * lax.rsqrt(mean_square + epsilon) * values.shape[1] ** (-0.5)
    return scaled.astype(jnp.bfloat16)


def on_device(embeddings, seed_labels, pattern):
    row_pos = lax.axis_index("row")
    col_pos = lax.axis_index("col")
    rows_count = lax.axis_size("row")
    cols_count = lax.axis_size("col")
    clip_dev = embeddings.shape[0]
    group_width = clip_dev * rows_count
    group_blocks = group_width // BLOCK
    unit_rows = normalize_rows(embeddings)
    col_units = lax.all_gather(unit_rows, "col", axis=0, tiled=True)
    row_units = lax.all_gather(unit_rows, "row", axis=0, tiled=True)
    spread = jnp.arange(cols_count * clip_dev, dtype=jnp.int32)
    col_blocks = (
        spread // clip_dev * group_width + row_pos * clip_dev + spread % clip_dev
    ) // BLOCK
    row_blocks = col_pos * group_blocks + jnp.arange(group_blocks, dtype=jnp.int32)
    own_seed = seed_labels.astype(jnp.float32)
    panel_rows = seed_labels
    labels = own_seed
    listed = jnp.any(pattern[col_blocks][:, None, :] == row_blocks[None, :, None], axis=2)
    listed = jnp.repeat(listed, BLOCK, axis=1)
    scores = jnp.einsum("id,jd->ij", col_units, row_units, preferred_element_type=jnp.float32)
    kernel = jnp.where(listed, jnp.exp(sharpness * scores), 0.0).astype(jnp.bfloat16)
    totals = jnp.sum(kernel.astype(jnp.float32), axis=1)
    for sweep_index in range(ITERS):
        partial_value = jnp.dot(
            kernel,
            lax.all_gather(panel_rows, "row", axis=0, tiled=True),
            preferred_element_type=jnp.float32,
        )
        numerators, denominators = (
            lax.psum_scatter(partial_value, "col", scatter_dimension=0, tiled=True),
            lax.psum_scatter(totals, "col", scatter_dimension=0, tiled=True),
        )
        labels = mixing * numerators / denominators[:, None] + (1.0 - mixing) * own_seed
        panel_rows = labels.astype(jnp.bfloat16)
    return labels


def solution(mesh):
    return jax.shard_map(
        on_device,
        mesh=mesh,
        in_specs=(P(("col", "row"), None), P(("col", "row"), None), P()),
        out_specs=P(("col", "row"), None),
        check_vma=False,
    )
```

profile of v0, /device:TPU:0, one launch (start us, length us, event | category | flops | bytes accessed | tf_op | source)
XLA Modules:
  0.0 213.7 jit_solution(8032496874631610690)
XLA Ops:
  6.5 1.3 fusion
  7.8 2.1 fusion.2
  10.0 0.7 all-gather.3.cloned.1.call-update
  10.7 0.8 copy.7
  11.5 0.1 compare_select_fusion
  11.6 5.5 %gather_fusion = s32[2048,16]{1,0:T(8,128)S(1)} fusion(s32[64,16]{1,0:T(8,128)S(1)} %copy.7, s32[2048]{0:T(1024)S(1)} %broadcast_clamp_fusion), kind=kCustom, calls=%fused_computation | custom fusion | bytes 270336 | tf_op jit(solution)/shard_map/gather | solution.py:41
  17.1 0.3 copy.8
  17.4 16.5 %all_gather.14 = bf16[1024,256]{1,0:T(8,128)(2,1)S(1)} all-gather(bf16[256,256]{1,0:T(8,128)(2,1)S(1)} %copy-done), channel_id=1, replica_groups=mesh['row'=4,'col'=8] {'row'}, dimensions={0}, use_global_device_ids=true | all-gather | bytes 655360 | tf_op jit(solution)/shard_map/all_gather | solution.py:49
  33.9 0.3 compare_reduce_fusion
  34.1 20.3 %all-gather.5.cloned.1.call-done = bf16[1024,1152]{1,0:T(8,128)(2,1)} async-done(((bf16[256,1152]{1,0:T(8,128)(2,1)}), bf16[1024,1152]{1,0:T(8,128)(2,1)}) %all-gather.5.cloned.1.call-update) | async-done | bytes 2359312 | tf_op jit(solution)/shard_map/all_gather | solution.py:32
  54.4 53.4 %all-gather.3.cloned.1.call-done = bf16[2048,1152]{1,0:T(8,128)(2,1)} async-done(((bf16[256,1152]{1,0:T(8,128)(2,1)}), bf16[2048,1152]{1,0:T(8,128)(2,1)}) %all-gather.3.cloned.1.call-update) | async-done | bytes 4718608 | tf_op jit(solution)/shard_map/all_gather | solution.py:31
  107.8 8.5 %convert_reduce_fusion = (f32[2048]{0:T(1024)S(1)}, bf16[2048,1024]{0,1:T(8,128)(2,1)S(1)}) fusion(bf16[2048,1152]{1,0:T(8,128)(2,1)} %all-gather.3.cloned.1.call-done, bf16[1024,1152]{1,0:T(8,128)(2,1)} %all-gather.5.cloned.1.call-done, pred[2048,8]{0,1:T(8,128)(4,1)S(1)} %compare_reduce_fusion), kind=kOutput, calls=%fused_computation.1 | convolution fusion | flops 4842321920 | bytes 11296768 | tf_op jit(solution)/shard_map/id,jd->ij/dot_general | solution.py:43
  116.3 1.9 copy-done.2
  118.2 2.6 %fusion.6 = f32[2048,256]{1,0:T(8,128)} fusion(bf16[2048,1024]{0,1:T(8,128)(2,1)S(1)} %get-tuple-element.6, bf16[1024,256]{1,0:T(8,128)(2,1)S(1)} %all_gather.14), kind=kOutput, calls=%fused_computation.28 | convolution fusion | flops 1073741824 | bytes 6815744 | tf_op jit(solution)/shard_map/dot_general | solution.py:47
  120.9 0.0 reduce-scatter.5.cloned.1.call-start
  120.9 0.6 dynamic-slice
  122.2 14.8 %all-reduce = f32[2048]{0:T(1024)S(1)} all-reduce(f32[2048]{0:T(1024)S(1)} %get-tuple-element.5), channel_id=3, replica_groups=mesh['row'=4,'col'=8] {'col'}, use_global_device_ids=true, to_apply=%region_4.5.clone | all-reduce | flops 2048 | bytes 16384
  136.9 0.1 dynamic-slice.1
  137.0 18.8 %reduce-scatter.3.cloned.1.call-done = f32[256,256]{1,0:T(8,128)} async-done(((f32[2048,256]{1,0:T(8,128)}), f32[256,256]{1,0:T(8,128)}) %reduce-scatter.3.cloned.1.call-update) | async-done | bytes 262160 | tf_op jit(solution)/shard_map/reduce_scatter | solution.py:53
  155.9 1.1 add_convert_fusion
  156.9 10.4 %all_gather.15 = bf16[1024,256]{1,0:T(8,128)(2,1)S(1)} all-gather(bf16[256,256]{1,0:T(8,128)(2,1)S(1)} %add_convert_fusion), channel_id=1, replica_groups=mesh['row'=4,'col'=8] {'row'}, dimensions={0}, use_global_device_ids=true | all-gather | bytes 655360 | tf_op jit(solution)/shard_map/all_gather | solution.py:49
  167.4 4.8 %fusion.7 = f32[2048,256]{1,0:T(8,128)} fusion(bf16[2048,1024]{0,1:T(8,128)(2,1)} %copy-done.2, bf16[1024,256]{1,0:T(8,128)(2,1)S(1)} %all_gather.15), kind=kOutput, calls=%fused_computation.29 | convolution fusion | flops 1073741824 | bytes 6815744 | tf_op jit(solution)/shard_map/dot_general | solution.py:47
  172.2 33.2 %reduce-scatter.5.cloned.1.call-done = f32[256,256]{1,0:T(8,128)} async-done(((f32[2048,256]{1,0:T(8,128)}), f32[256,256]{1,0:T(8,128)}) %reduce-scatter.5.cloned.1.call-update) | async-done | bytes 262160 | tf_op jit(solution)/shard_map/reduce_scatter | solution.py:53
  205.4 1.8 divide_add_fusion
  (14 shorter events, 0.2 us)
Async XLA Ops:
  6.5 47.9 %all-gather.5.cloned.1.call-start = ((), (), s32[]{:S(2)}) async-start(), calls=%async_computation.3 | async-start | bytes 2949120 | tf_op jit(solution)/shard_map/all_gather | solution.py:32
  9.9 97.9 %all-gather.3.cloned.1.call-start = ((), (), s32[]{:S(2)}) async-start(), calls=%async_computation.2 | async-start | bytes 5308416 | tf_op jit(solution)/shard_map/all_gather | solution.py:31
  10.7 145.2 %reduce-scatter.3.cloned.1.call-start = ((), (), s32[]{:S(2)}) async-start(), calls=%async_computation.4 | async-start | bytes 2359296 | tf_op jit(solution)/shard_map/reduce_scatter | solution.py:53
  11.6 5.8 %copy-start = (bf16[256,256]{1,0:T(8,128)(2,1)S(1)}, bf16[256,256]{1,0:T(8,128)(2,1)}, u32[]{:S(2)}) copy-start(bf16[256,256]{1,0:T(8,128)(2,1)} %param.4) | copy-start | bytes 393220
  116.3 1.9 copy-start.2
  118.2 2.7 %copy-start.1 = (u32[32]{0:T(128)S(1)}, u32[32]{0:T(128)}, u32[]{:S(2)}) copy-start(u32[32]{0:T(128)} %constant.75) | copy-start | bytes 388
  120.9 84.6 %reduce-scatter.5.cloned.1.call-start = ((), (), s32[]{:S(2)}) async-start(), calls=%async_computation.5 | async-start | bytes 2359296 | tf_op jit(solution)/shard_map/reduce_scatter | solution.py:53
Sparse Core Ops, SparseCore 0:
  10.0 44.3 all-gather.4
  56.0 51.6 all-gather.2
  121.0 34.8 reduce-scatter.2
  172.4 33.0 reduce-scatter.4
where the time goes:
time: 214 us
  waiting for transfers between devices  126 us (59%)
  blocking collectives  41.7 us (19%)
  matrix products  16 us (7%)
  between operations  13.9 us (6%)
  local copies, waits for them, and re-layouts  9.14 us (4%)
  other arithmetic  6.53 us (3%)
    all_gather x1, waiting for transfers between devices, on_device(): col_units = lax.all_gather(unit_rows, 'col', axis=0, tiled=True)  53.4 us
    reduce_scatter x2, waiting for transfers between devices, on_device(): lax.psum_scatter(partial_value, 'col', scatter_dimension=0, tiled=True)  52 us
    all_gather x2, blocking collectives, on_device(): lax.all_gather(panel_rows, 'row', axis=0, tiled=True)  26.9 us
    all_gather x1, waiting for transfers between devices, on_device(): row_units = lax.all_gather(unit_rows, 'row', axis=0, tiled=True)  20.3 us
    unnamed x1, blocking collectives  14.8 us
    dot_general x1, matrix products, on_device(): jnp.einsum('id,jd->ij', col_units, row_units, preferred_element_type=jnp....  8.49 us
    dot_general x2, matrix products, on_device(): jnp.dot(kernel, lax.all_gather(panel_rows, 'row', axis=0, tiled=True), pr...  7.48 us
    gather x2, local copies, waits for them, and re-layouts, on_device(): pattern[col_blocks][:, None, :] == row_blocks[None, :, None]  5.76 us
  transfers between devices with their start and end apart: 4, of which 4 were waited for; matrix products, arithmetic and copies ran while one was open for 4% of the time, Pallas kernels for 0%

commit v1 on v0

v1 whole, which is shorter than its diff:
```python
import functools
import math

import jax
import jax.numpy as jnp
from jax import lax
from jax.experimental import pallas as pl
from jax.experimental.pallas import tpu as pltpu
from jax.sharding import PartitionSpec as P

BLOCK = 128
ITERS = 2
AXES = ("row", "col")

sharpness = 30.0
mixing = 0.8
epsilon = 1e-06


def split_two(n):
    low = max(d for d in range(1, math.isqrt(n) + 1) if n % d == 0)
    return n // low, low


class Layout:
    def __init__(self, rows, cols):
        core = 2 if cols % 2 == 0 else 1
        ny, nx = split_two(rows)
        nzh, nzl = split_two(cols // core)
        self.sizes = dict(y=ny, x=nx, zh=nzh, zl=nzl, core=core)
        self.rows, self.cols = rows, cols

    def coords(self, row, col):
        s = self.sizes
        return dict(
            y=row // s["x"],
            x=row % s["x"],
            zh=col // (s["zl"] * s["core"]),
            zl=col // s["core"] % s["zl"],
            core=col % s["core"],
        )

    def moved(self, at, offset):
        return {k: (at[k] + offset.get(k, 0)) % self.sizes[k] for k in at}

    def row_col(self, at):
        s = self.sizes
        return at["y"] * s["x"] + at["x"], (at["zh"] * s["zl"] + at["zl"]) * s["core"] + at["core"]

    def fetch(self, value, **offset):
        if all(v % self.sizes[k] == 0 for k, v in offset.items()):
            return value
        pairs = []
        for row in range(self.rows):
            for col in range(self.cols):
                r, c = self.row_col(self.moved(self.coords(row, col), offset))
                pairs.append((r * self.cols + c, row * self.cols + col))
        return lax.ppermute(value, AXES, pairs)

    def device(self, offset):
        at = self.coords(lax.axis_index("row"), lax.axis_index("col"))
        row, col = self.row_col(self.moved(at, offset))
        return col * self.rows + row


def unit_kernel(emb_ref, out_ref):
    values = emb_ref[...].astype(jnp.float32)
    mean_square = jnp.mean(values * values, axis=1, keepdims=True)
    scaled = values * lax.rsqrt(mean_square + epsilon) * values.shape[1] ** (-0.5)
    out_ref[...] = scaled.astype(jnp.bfloat16)


def unit_rows(embeddings):
    return pl.pallas_call(
        unit_kernel,
        out_shape=jax.ShapeDtypeStruct(embeddings.shape, jnp.bfloat16),
    )(embeddings)


def store_numerators(kern, pcat, own_ref, other_refs, m, tile):
    rows = kern.shape[0]
    for t in range(rows // tile):
        part = jnp.dot(
            kern[pl.ds(t * tile, tile), :], pcat[...], preferred_element_type=jnp.float32
        )
        for q in range(tile // m):
            piece = t * (tile // m) + q
            value = part[q * m : (q + 1) * m]
            if piece == 0:
                own_ref[...] = value
            else:
                other_refs[piece - 1][...] = value.astype(jnp.bfloat16)


def gram_kernel(nt, ns, m, tile, flags, *refs):
    t_in, s_in, p_in = refs[:nt], refs[nt : nt + ns], refs[nt + ns : nt + 2 * ns]
    rest = refs[nt + 2 * ns :]
    kern_out, tot_out, own_ref = rest[:3]
    other_refs = rest[3 : 2 + nt]
    tcat, scat, pcat, kern, acc, sem_t, sem_s, sem_p, sem_k = rest[2 + nt :]
    copies_t = [
        pltpu.make_async_copy(t_in[i], tcat.at[pl.ds(i * m, m)], sem_t.at[i]) for i in range(nt)
    ]
    copies_s = [
        pltpu.make_async_copy(s_in[j], scat.at[pl.ds(j * m, m)], sem_s.at[j]) for j in range(ns)
    ]
    copies_p = [
        pltpu.make_async_copy(p_in[j], pcat.at[pl.ds(j * m, m)], sem_p.at[j]) for j in range(ns)
    ]
    for copy in copies_t + copies_s + copies_p:
        copy.start()
    rows = nt * m
    acc[...] = jnp.zeros_like(acc)
    for copy in copies_t:
        copy.wait()
    sub = min(m, BLOCK)
    for j in range(ns * m // tile):
        for i in range(tile // m):
            copies_s[j * (tile // m) + i].wait()

        def step(t, carry):
            at = pl.multiple_of(t * tile, tile)
            scores = lax.dot_general(
                tcat[pl.ds(at, tile), :],
                scat[pl.ds(j * tile, tile), :],
                (((1,), (1,)), ((), ())),
                preferred_element_type=jnp.float32,
            )
            value = jnp.exp(sharpness * scores).astype(jnp.bfloat16).astype(jnp.float32)
            for a in range(tile // sub):
                flag = flags[pl.ds(t * (tile // sub) + a, 1), pl.ds(j * tile, tile)]
                part = jnp.where(flag > 0, value[a * sub : (a + 1) * sub], 0.0)
                where = pl.ds(at + a * sub, sub)
                kern[where, pl.ds(j * tile, tile)] = part.astype(jnp.bfloat16)
                for b in range(tile // BLOCK):
                    acc[where, :] += part[:, b * BLOCK : (b + 1) * BLOCK]
            return carry

        lax.fori_loop(0, rows // tile, step, 0, unroll=rows // tile <= 4)
    copy_k = pltpu.make_async_copy(kern, kern_out, sem_k)
    copy_k.start()
    for k in range(rows // BLOCK):
        block = acc[pl.ds(k * BLOCK, BLOCK), :]
        tot_out[pl.ds(k, 1), :] = jnp.sum(block.T, axis=0, keepdims=True)
    for copy in copies_p:
        copy.wait()
    store_numerators(kern, pcat, own_ref, other_refs, m, tile)
    copy_k.wait()


def gram_call(flags, t_pieces, s_pieces, p_pieces):
    nt, ns = len(t_pieces), len(s_pieces)
    m, d = t_pieces[0].shape
    c = p_pieces[0].shape[1]
    rows, cols = nt * m, ns * m
    tile = max(m, 2 * BLOCK)
    any_spec = pl.BlockSpec(memory_space=pl.ANY)
    vmem = pl.BlockSpec(memory_space=pltpu.VMEM)
    return pl.pallas_call(
        functools.partial(gram_kernel, nt, ns, m, tile),
        out_shape=[
            jax.ShapeDtypeStruct((rows, cols), jnp.bfloat16),
            jax.ShapeDtypeStruct((rows // BLOCK, BLOCK), jnp.float32),
            jax.ShapeDtypeStruct((m, c), jnp.float32),
        ]
        + [jax.ShapeDtypeStruct((m, c), jnp.bfloat16)] * (nt - 1),
        in_specs=[vmem] + [any_spec] * (nt + 2 * ns),
        out_specs=[any_spec, vmem, vmem] + [vmem] * (nt - 1),
        scratch_shapes=[
            pltpu.VMEM((rows, d), jnp.bfloat16),
            pltpu.VMEM((cols, d), jnp.bfloat16),
            pltpu.VMEM((cols, c), jnp.bfloat16),
            pltpu.VMEM((rows, cols), jnp.bfloat16),
            pltpu.VMEM((rows, BLOCK), jnp.float32),
            pltpu.SemaphoreType.DMA((nt,)),
            pltpu.SemaphoreType.DMA((ns,)),
            pltpu.SemaphoreType.DMA((ns,)),
            pltpu.SemaphoreType.DMA,
        ],
        compiler_params=pltpu.CompilerParams(vmem_limit_bytes=56 * 2**20),
        cost_estimate=pl.CostEstimate(
            flops=2 * rows * cols * (d + c),
            bytes_accessed=2 * (rows + cols) * (d + c),
            transcendentals=rows * cols,
        ),
    )(flags, *t_pieces, *s_pieces, *p_pieces)


def spread_kernel(nt, ns, m, tile, kern_in, *refs):
    p_in, own_ref, other_refs = refs[:ns], refs[ns], refs[ns + 1 : ns + nt]
    pcat, kern, sem_p, sem_k = refs[ns + nt :]
    rows = nt * m
    copies_p = [
        pltpu.make_async_copy(p_in[j], pcat.at[pl.ds(j * m, m)], sem_p.at[j]) for j in range(ns)
    ]
    copy_k = pltpu.make_async_copy(kern_in, kern, sem_k)
    for copy in copies_p + [copy_k]:
        copy.start()
    for copy in copies_p + [copy_k]:
        copy.wait()
    store_numerators(kern, pcat, own_ref, other_refs, m, tile)


def spread_call(kern, p_pieces):
    ns = len(p_pieces)
    m, c = p_pieces[0].shape
    rows, cols = kern.shape
    nt = rows // m
    any_spec = pl.BlockSpec(memory_space=pl.ANY)
    vmem = pl.BlockSpec(memory_space=pltpu.VMEM)
    return pl.pallas_call(
        functools.partial(spread_kernel, nt, ns, m, max(m, 2 * BLOCK)),
        out_shape=[jax.ShapeDtypeStruct((m, c), jnp.float32)]
        + [jax.ShapeDtypeStruct((m, c), jnp.bfloat16)] * (nt - 1),
        in_specs=[any_spec] * (1 + ns),
        out_specs=[vmem] * nt,
        scratch_shapes=[
            pltpu.VMEM((cols, c), jnp.bfloat16),
            pltpu.VMEM((rows, cols), jnp.bfloat16),
            pltpu.SemaphoreType.DMA((ns,)),
            pltpu.SemaphoreType.DMA,
        ],
        compiler_params=pltpu.CompilerParams(vmem_limit_bytes=40 * 2**20),
        cost_estimate=pl.CostEstimate(
            flops=2 * rows * cols * c,
            bytes_accessed=2 * (rows * cols + cols * c),
            transcendentals=0,
        ),
    )(kern, *p_pieces)


def on_device(embeddings, seed_labels, pattern):
    layout = Layout(lax.axis_size("row"), lax.axis_size("col"))
    size = layout.sizes
    m = embeddings.shape[0]
    t_offsets = [dict(x=a, zl=b) for b in range(size["zl"]) for a in range(size["x"])]
    half_offsets = [dict(y=a, zh=b) for b in range(size["zh"]) for a in range(size["y"])]
    s_offsets = [dict(o, core=c) for o in half_offsets for c in range(size["core"])]

    sub = min(m, BLOCK)

    def blocks_of(offsets):
        starts = jnp.stack([layout.device(o) * m for o in offsets])
        rows = starts[:, None] + sub * jnp.arange(m // sub, dtype=starts.dtype)
        return rows.reshape(-1) // BLOCK

    t_blocks, s_blocks = blocks_of(t_offsets), blocks_of(s_offsets)
    flags = jnp.any(pattern[t_blocks][:, None, :] == s_blocks[None, :, None], axis=2)
    flags = jnp.repeat(flags.astype(jnp.int32), sub, axis=1)

    def gather(value, far, near):
        by_far = [layout.fetch(value, **{far: b}) for b in range(size[far])]
        return [layout.fetch(v, **{near: a}) for v in by_far for a in range(size[near])]

    def sources(value):
        return [
            layout.fetch(v, core=c) for v in gather(value, "zh", "y") for c in range(size["core"])
        ]

    units = unit_rows(embeddings)
    t_pieces = gather(units, "zl", "x")
    s_pieces = sources(units)
    own_seed = seed_labels.astype(jnp.float32)

    def collect(own, others):
        for value, o in zip(others, t_offsets[1:]):
            own = own + layout.fetch(value, **{k: -v for k, v in o.items()}).astype(jnp.float32)
        return own

    kern, tots, own, *others = gram_call(flags, t_pieces, s_pieces, sources(seed_labels))
    tots = tots.reshape(len(t_offsets), m)
    totals = collect(tots[0], [tots[i] for i in range(1, len(t_offsets))])[:, None]
    for sweep_index in range(ITERS):
        if sweep_index > 0:
            own, *others = spread_call(kern, sources(labels.astype(jnp.bfloat16)))
        labels = mixing * collect(own, others) / totals + (1.0 - mixing) * own_seed
    return labels


def solution(mesh):
    return jax.shard_map(
        on_device,
        mesh=mesh,
        in_specs=(P(("col", "row"), None), P(("col", "row"), None), P()),
        out_specs=P(("col", "row"), None),
        check_vma=False,
    )
```

time: 214 us -> 135 us (0.63)
  waiting for transfers between devices: 126 us -> 75.1 us
  blocking collectives: 41.7 us -> 0 us
  starting transfers between devices: 0.12 us -> 30.8 us
  Pallas kernels: 0 us -> 19.8 us
  matrix products: 16 us -> 0 us
  between operations: 13.9 us -> 0.23 us
  local copies, waits for them, and re-layouts: 9.14 us -> 5.43 us
  other arithmetic: 6.53 us -> 3.09 us
    ppermute x0 -> x33, waiting for transfers between devices: none -> 75.1 us  [fetch(): return lax.ppermute(value, AXES, pairs)]
    all_gather x2 -> x0, waiting for transfers between devices: 73.6 us -> none  [the longest x1 53.4 us: on_device(): col_units = lax.all_gather(unit_rows, 'col', axis=0, tiled=True)]
    reduce_scatter x2 -> x0, waiting for transfers between devices: 52 us -> none  [on_device(): lax.psum_scatter(partial_value, 'col', scatter_dimension=0, tiled=True)]
    ppermute x0 -> x33, starting transfers between devices: none -> 30.8 us  [fetch(): return lax.ppermute(value, AXES, pairs)]
    all_gather x2 -> x0, blocking collectives: 26.9 us -> none  [on_device(): lax.all_gather(panel_rows, 'row', axis=0, tiled=True)]
    pallas_call x0 -> x3, Pallas kernels: none -> 19.8 us  [the longest x1 14.7 us: gram_call(): pl.pallas_call(functools.partial(gram_kernel, nt, ns, m, tile), out_shape...]
    dot_general x3 -> x0, matrix products: 16 us -> none  [the longest x1 8.49 us: on_device(): jnp.einsum('id,jd->ij', col_units, row_units, preferred_element_type=jnp....]
    unnamed x1 -> x0, blocking collectives: 14.8 us -> none
  transfers between devices with their start and end apart: 4 -> 33, of which waited for: 4 -> 17; matrix products, arithmetic and copies ran while one was open for 4% -> 3% of each run, Pallas kernels for 0% -> 0%
where the time goes in v1:
time: 135 us; the launch traced here: 134 us
  waiting for transfers between devices  75.1 us (56%)
  starting transfers between devices  30.8 us (23%)
  Pallas kernels  19.8 us (15%)
  local copies, waits for them, and re-layouts  5.43 us (4%)
  other arithmetic  3.09 us (2%)
    ppermute x33, waiting for transfers between devices, fetch(): return lax.ppermute(value, AXES, pairs)  75.1 us
    ppermute x33, starting transfers between devices, fetch(): return lax.ppermute(value, AXES, pairs)  30.8 us
    pallas_call x1, Pallas kernels, gram_call(): pl.pallas_call(functools.partial(gram_kernel, nt, ns, m, tile), out_shape...  14.7 us
    unnamed x27, local copies, waits for them, and re-layouts  3.05 us
    pallas_call x1, Pallas kernels, spread_call(): pl.pallas_call(functools.partial(spread_kernel, nt, ns, m, max(m, 2 * BLO...  2.93 us
  transfers between devices with their start and end apart: 33, of which 17 were waited for; matrix products, arithmetic and copies ran while one was open for 3% of the time, Pallas kernels for 0%

profile of v1, /device:TPU:0, one launch (start us, length us, event | category | flops | bytes accessed | tf_op | source)
XLA Modules:
  0.0 134.4 jit_solution(4465792754066017483)
XLA Ops:
  0.0 2.1 %shard_map.37.refs_0_.refs_4_ = bf16[256,1152]{1,0:T(8,128)(2,1)} custom-call(bf16[256,1152]{1,0:T(8,128)(2,1)} %emb_ref.1), custom_call_target="tpu_custom_call" | custom-call | tf_op jit(solution)/shard_map/pallas_call | solution.py:74
  2.1 4.0 %collective-permute-start.6 = (bf16[256,1152]{1,0:T(8,128)(2,1)}, bf16[256,1152]{1,0:T(8,128)(2,1)S(1)}, u32[]{:S(2)}, u32[]{:S(2)}) collective-permute-start(bf16[256,1152]{1,0:T(8,128)(2,1)} %shard_map.37.refs_0_.refs_4_), channel_id=1, source_target_pairs={{4,0},{5,1},{6,2},{7,3},{0,4},{1,5},{2,6},{3,7},{12,8},{13,9},{14,... | collective-permute-start | bytes 1769480 | tf_op jit(solution)/shard_map/ppermute | solution.py:58
  6.2 1.8 %collective-permute-start.11 = (bf16[256,256]{1,0:T(8,128)(2,1)}, bf16[256,256]{1,0:T(8,128)(2,1)S(1)}, u32[]{:S(2)}, u32[]{:S(2)}) collective-permute-start(bf16[256,256]{1,0:T(8,128)(2,1)} %refs_12_.1), channel_id=1, source_target_pairs={{16,0},{17,1},{18,2},{19,3},{20,4},{21,5},{22,6},{23,7},{24,8},{25... | collective-permute-start | bytes 393224 | tf_op jit(solution)/shard_map/ppermute | solution.py:58
  8.3 29.6 %collective-permute-done.13.refs_16_ = bf16[256,256]{1,0:T(8,128)(2,1)S(1)} collective-permute-done((bf16[256,256]{1,0:T(8,128)(2,1)}, bf16[256,256]{1,0:T(8,128)(2,1)S(1)}, u32[]{:S(2)}, u32[]{:S(2)}) %collective-permute-start.13) | collective-permute-done | bytes 131104 | tf_op jit(solution)/shard_map/ppermute | solution.py:58
  38.0 1.6 %collective-permute-start.15 = (bf16[256,256]{1,0:T(8,128)(2,1)S(1)}, bf16[256,256]{1,0:T(8,128)(2,1)S(1)}, u32[]{:S(2)}, u32[]{:S(2)}) collective-permute-start(bf16[256,256]{1,0:T(8,128)(2,1)S(1)} %collective-permute-done.13.refs_16_), channel_id=1, source_target_pairs={{16,0},{17,1},{18,2},{19,3},{20,4},{21,5},{22,6},{23,7},{24,8},{25... | collective-permute-start | bytes 393224 | tf_op jit(solution)/shard_map/ppermute | solution.py:58
  40.7 2.2 %collective-permute-done.15.refs_18_ = bf16[256,256]{1,0:T(8,128)(2,1)S(1)} collective-permute-done((bf16[256,256]{1,0:T(8,128)(2,1)S(1)}, bf16[256,256]{1,0:T(8,128)(2,1)S(1)}, u32[]{:S(2)}, u32[]{:S(2)}) %collective-permute-start.15) | collective-permute-done | bytes 131104 | tf_op jit(solution)/shard_map/ppermute | solution.py:58
  42.9 1.6 %collective-permute-start.8 = (bf16[256,1152]{1,0:T(8,128)(2,1)S(1)}, bf16[256,1152]{1,0:T(8,128)(2,1)S(1)}, u32[]{:S(2)}, u32[]{:S(2)}) collective-permute-start(bf16[256,1152]{1,0:T(8,128)(2,1)S(1)} %collective-permute-done.6.refs_8_), channel_id=1, source_target_pairs={{16,0},{17,1},{18,2},{19,3},{20,4},{21,5},{22,6},{23,7},{24,8},{25... | collective-permute-start | bytes 1769480 | tf_op jit(solution)/shard_map/ppermute | solution.py:58
  47.5 1.5 %collective-permute-start = (bf16[256,1152]{1,0:T(8,128)(2,1)}, bf16[256,1152]{1,0:T(8,128)(2,1)}, u32[]{:S(2)}, u32[]{:S(2)}) collective-permute-start(bf16[256,1152]{1,0:T(8,128)(2,1)} %shard_map.37.refs_0_.refs_4_), channel_id=1, source_target_pairs={{8,0},{9,1},{10,2},{11,3},{12,4},{13,5},{14,6},{15,7},{0,8},{1,9},... | collective-permute-start | bytes 1769480 | tf_op jit(solution)/shard_map/ppermute | solution.py:58
  49.5 6.3 %collective-permute-done.1.refs_2_ = bf16[256,1152]{1,0:T(8,128)(2,1)S(1)} collective-permute-done((bf16[256,1152]{1,0:T(8,128)(2,1)}, bf16[256,1152]{1,0:T(8,128)(2,1)S(1)}, u32[]{:S(2)}, u32[]{:S(2)}) %collective-permute-start.1) | collective-permute-done | bytes 589856 | tf_op jit(solution)/shard_map/ppermute | solution.py:58
  55.8 1.5 %collective-permute-start.2 = (bf16[256,1152]{1,0:T(8,128)(2,1)S(1)}, bf16[256,1152]{1,0:T(8,128)(2,1)}, u32[]{:S(2)}, u32[]{:S(2)}) collective-permute-start(bf16[256,1152]{1,0:T(8,128)(2,1)S(1)} %collective-permute-done.1.refs_2_), channel_id=1, source_target_pairs={{8,0},{9,1},{10,2},{11,3},{12,4},{13,5},{14,6},{15,7},{0,8},{1,9},... | collective-permute-start | bytes 1769480 | tf_op jit(solution)/shard_map/ppermute | solution.py:58
  61.2 2.8 %collective-permute-done.refs_1_ = bf16[256,1152]{1,0:T(8,128)(2,1)} collective-permute-done((bf16[256,1152]{1,0:T(8,128)(2,1)}, bf16[256,1152]{1,0:T(8,128)(2,1)}, u32[]{:S(2)}, u32[]{:S(2)}) %collective-permute-start) | collective-permute-done | bytes 589856 | tf_op jit(solution)/shard_map/ppermute | solution.py:58
  64.0 11.9 %collective-permute-done.2.refs_3_ = bf16[256,1152]{1,0:T(8,128)(2,1)} collective-permute-done((bf16[256,1152]{1,0:T(8,128)(2,1)S(1)}, bf16[256,1152]{1,0:T(8,128)(2,1)}, u32[]{:S(2)}, u32[]{:S(2)}) %collective-permute-start.2) | collective-permute-done | bytes 589856 | tf_op jit(solution)/shard_map/ppermute | solution.py:58
  75.9 14.7 %shard_map.38 = (bf16[1024,2048]{1,0:T(8,128)(2,1)}, f32[8,128]{1,0:T(8,128)}, f32[256,256]{1,0:T(8,128)}, bf16[256,256]{1,0:T(8,128)(2,1)}, bf16[256,256]{1,0:T(8,128)(2,1)}, /*index=5*/bf16[256,256]{1,0:T(8,128)(2,1)}) custom-call(s32[8,2048]{1,0:T(8,128)} %broadcast_bitcast_fusion.flags, bf16[256,1152]{1,0:T(8,128)(2,1)} %shard_map.37.refs_0_.refs_4_, ...), custom_call_target="tpu_custom_call" | custom-call | flops 5905580032 | bytes 8650752 | tf_op jit(solution)/shard_map/pallas_call | solution.py:159
  94.9 1.5 %collective-permute-start.17 = (bf16[256,256]{1,0:T(8,128)(2,1)}, bf16[256,256]{1,0:T(8,128)(2,1)S(1)}, u32[]{:S(2)}, u32[]{:S(2)}) collective-permute-start(bf16[256,256]{1,0:T(8,128)(2,1)} %get-tuple-element.17), channel_id=1, source_target_pairs={{8,0},{9,1},{10,2},{11,3},{12,4},{13,5},{14,6},{15,7},{0,8},{1,9},... | collective-permute-start | bytes 393224 | tf_op jit(solution)/shard_map/ppermute | solution.py:58
  99.1 2.4 %collective-permute-done.17 = bf16[256,256]{1,0:T(8,128)(2,1)S(1)} collective-permute-done((bf16[256,256]{1,0:T(8,128)(2,1)}, bf16[256,256]{1,0:T(8,128)(2,1)S(1)}, u32[]{:S(2)}, u32[]{:S(2)}) %collective-permute-start.17) | collective-permute-done | bytes 131104 | tf_op jit(solution)/shard_map/ppermute | solution.py:58
  101.7 2.0 %collective-permute-done.19 = bf16[256,256]{1,0:T(8,128)(2,1)S(1)} collective-permute-done((bf16[256,256]{1,0:T(8,128)(2,1)}, bf16[256,256]{1,0:T(8,128)(2,1)S(1)}, u32[]{:S(2)}, u32[]{:S(2)}) %collective-permute-start.19) | collective-permute-done | bytes 131104 | tf_op jit(solution)/shard_map/ppermute | solution.py:58
  104.8 3.3 %collective-permute-start.26 = (bf16[256,256]{1,0:T(8,128)(2,1)S(1)}, bf16[256,256]{1,0:T(8,128)(2,1)S(1)}, u32[]{:S(2)}, u32[]{:S(2)}) collective-permute-start(bf16[256,256]{1,0:T(8,128)(2,1)S(1)} %add_convert_fusion.refs_0_), channel_id=1, source_target_pairs={{4,0},{5,1},{6,2},{7,3},{0,4},{1,5},{2,6},{3,7},{12,8},{13,9},{14,... | collective-permute-start | bytes 393224 | tf_op jit(solution)/shard_map/ppermute | solution.py:58
  109.3 3.2 %collective-permute-done.26.refs_4_ = bf16[256,256]{1,0:T(8,128)(2,1)S(1)} collective-permute-done((bf16[256,256]{1,0:T(8,128)(2,1)S(1)}, bf16[256,256]{1,0:T(8,128)(2,1)S(1)}, u32[]{:S(2)}, u32[]{:S(2)}) %collective-permute-start.26) | collective-permute-done | bytes 131104 | tf_op jit(solution)/shard_map/ppermute | solution.py:58
  114.2 3.3 %collective-permute-done.28.refs_6_ = bf16[256,256]{1,0:T(8,128)(2,1)S(1)} collective-permute-done((bf16[256,256]{1,0:T(8,128)(2,1)S(1)}, bf16[256,256]{1,0:T(8,128)(2,1)S(1)}, u32[]{:S(2)}, u32[]{:S(2)}) %collective-permute-start.28) | collective-permute-done | bytes 131104 | tf_op jit(solution)/shard_map/ppermute | solution.py:58
  118.8 2.2 %copy-done = bf16[1024,2048]{1,0:T(8,128)(2,1)S(1)} copy-done((bf16[1024,2048]{1,0:T(8,128)(2,1)S(1)}, bf16[1024,2048]{1,0:T(8,128)(2,1)}, u32[]{:S(2)}) %copy-start) | copy-done | bytes 4194328
  121.0 2.9 %shard_map.39 = (f32[256,256]{1,0:T(8,128)S(1)}, bf16[256,256]{1,0:T(8,128)(2,1)S(1)}, bf16[256,256]{1,0:T(8,128)(2,1)S(1)}, bf16[256,256]{1,0:T(8,128)(2,1)S(1)}) custom-call(bf16[1024,2048]{1,0:T(8,128)(2,1)S(1)} %copy-done, bf16[256,256]{1,0:T(8,128)(2,1)S(1)} %add_convert_fusion.refs_0_, bf16[256,256]{1,0:T(8,128)(2,1)S(1)} %collective-permute-done.23.refs_1_, ...), custom_call_target="tpu_custom_call" | custom-call | flops 1073741824 | bytes 5242880 | tf_op jit(solution)/shard_map/pallas_call | solution.py:211
  125.5 1.9 %collective-permute-start.32 = (bf16[256,256]{1,0:T(8,128)(2,1)S(1)}, bf16[256,256]{1,0:T(8,128)(2,1)S(1)}, u32[]{:S(2)}, u32[]{:S(2)}) collective-permute-start(bf16[256,256]{1,0:T(8,128)(2,1)S(1)} %get-tuple-element.24), channel_id=1, source_target_pairs={{10,0},{11,1},{8,2},{9,3},{14,4},{15,5},{12,6},{13,7},{2,8},{3,9},... | collective-permute-start | bytes 393224 | tf_op jit(solution)/shard_map/ppermute | solution.py:58
  127.5 2.1 %collective-permute-done.30 = bf16[256,256]{1,0:T(8,128)(2,1)S(1)} collective-permute-done((bf16[256,256]{1,0:T(8,128)(2,1)S(1)}, bf16[256,256]{1,0:T(8,128)(2,1)S(1)}, u32[]{:S(2)}, u32[]{:S(2)}) %collective-permute-start.30) | collective-permute-done | bytes 131104 | tf_op jit(solution)/shard_map/ppermute | solution.py:58
  130.9 2.6 %collective-permute-done.32 = bf16[256,256]{1,0:T(8,128)(2,1)S(1)} collective-permute-done((bf16[256,256]{1,0:T(8,128)(2,1)S(1)}, bf16[256,256]{1,0:T(8,128)(2,1)S(1)}, u32[]{:S(2)}, u32[]{:S(2)}) %collective-permute-start.32) | collective-permute-done | bytes 131104 | tf_op jit(solution)/shard_map/ppermute | solution.py:58
  (91 shorter events, 24.9 us)
Async XLA Ops:
  2.1 40.8 %collective-permute-start.6 = (bf16[256,1152]{1,0:T(8,128)(2,1)}, bf16[256,1152]{1,0:T(8,128)(2,1)S(1)}, u32[]{:S(2)}, u32[]{:S(2)}) collective-permute-start(bf16[256,1152]{1,0:T(8,128)(2,1)} %shard_map.37.refs_0_.refs_4_), channel_id=1, source_target_pairs={{4,0},{5,1},{6,2},{7,3},{0,4},{1,5},{2,6},{3,7},{12,8},{13,9},{14,... | collective-permute-start | bytes 1769480 | tf_op jit(solution)/shard_map/ppermute | solution.py:58
  6.2 31.8 %collective-permute-start.13 = (bf16[256,256]{1,0:T(8,128)(2,1)}, bf16[256,256]{1,0:T(8,128)(2,1)S(1)}, u32[]{:S(2)}, u32[]{:S(2)}) collective-permute-start(bf16[256,256]{1,0:T(8,128)(2,1)} %refs_12_.1), channel_id=1, source_target_pairs={{4,0},{5,1},{6,2},{7,3},{0,4},{1,5},{2,6},{3,7},{12,8},{13,9},{14,... | collective-permute-start | bytes 393224 | tf_op jit(solution)/shard_map/ppermute | solution.py:58
  6.2 33.6 %collective-permute-start.11 = (bf16[256,256]{1,0:T(8,128)(2,1)}, bf16[256,256]{1,0:T(8,128)(2,1)S(1)}, u32[]{:S(2)}, u32[]{:S(2)}) collective-permute-start(bf16[256,256]{1,0:T(8,128)(2,1)} %refs_12_.1), channel_id=1, source_target_pairs={{16,0},{17,1},{18,2},{19,3},{20,4},{21,5},{22,6},{23,7},{24,8},{25... | collective-permute-start | bytes 393224 | tf_op jit(solution)/shard_map/ppermute | solution.py:58
  8.0 31.8 %collective-permute-start.10 = (bf16[256,256]{1,0:T(8,128)(2,1)}, bf16[256,256]{1,0:T(8,128)(2,1)S(1)}, u32[]{:S(2)}, u32[]{:S(2)}) collective-permute-start(bf16[256,256]{1,0:T(8,128)(2,1)} %refs_12_.1), channel_id=1, source_target_pairs={{1,0},{0,1},{3,2},{2,3},{5,4},{4,5},{7,6},{6,7},{9,8},{8,9},{11,10... | collective-permute-start | bytes 393224 | tf_op jit(solution)/shard_map/ppermute | solution.py:58
  8.0 41.0 %collective-permute-start.4 = (bf16[256,1152]{1,0:T(8,128)(2,1)}, bf16[256,1152]{1,0:T(8,128)(2,1)S(1)}, u32[]{:S(2)}, u32[]{:S(2)}) collective-permute-start(bf16[256,1152]{1,0:T(8,128)(2,1)} %shard_map.37.refs_0_.refs_4_), channel_id=1, source_target_pairs={{16,0},{17,1},{18,2},{19,3},{20,4},{21,5},{22,6},{23,7},{24,8},{25... | collective-permute-start | bytes 1769480 | tf_op jit(solution)/shard_map/ppermute | solution.py:58
  38.0 5.0 %collective-permute-start.15 = (bf16[256,256]{1,0:T(8,128)(2,1)S(1)}, bf16[256,256]{1,0:T(8,128)(2,1)S(1)}, u32[]{:S(2)}, u32[]{:S(2)}) collective-permute-start(bf16[256,256]{1,0:T(8,128)(2,1)S(1)} %collective-permute-done.13.refs_16_), channel_id=1, source_target_pairs={{16,0},{17,1},{18,2},{19,3},{20,4},{21,5},{22,6},{23,7},{24,8},{25... | collective-permute-start | bytes 393224 | tf_op jit(solution)/shard_map/ppermute | solution.py:58
  39.8 9.2 %collective-permute-start.3 = (bf16[256,1152]{1,0:T(8,128)(2,1)}, bf16[256,1152]{1,0:T(8,128)(2,1)S(1)}, u32[]{:S(2)}, u32[]{:S(2)}) collective-permute-start(bf16[256,1152]{1,0:T(8,128)(2,1)} %shard_map.37.refs_0_.refs_4_), channel_id=1, source_target_pairs={{1,0},{0,1},{3,2},{2,3},{5,4},{4,5},{7,6},{6,7},{9,8},{8,9},{11,10... | collective-permute-start | bytes 1769480 | tf_op jit(solution)/shard_map/ppermute | solution.py:58
  39.9 15.9 %collective-permute-start.1 = (bf16[256,1152]{1,0:T(8,128)(2,1)}, bf16[256,1152]{1,0:T(8,128)(2,1)S(1)}, u32[]{:S(2)}, u32[]{:S(2)}) collective-permute-start(bf16[256,1152]{1,0:T(8,128)(2,1)} %shard_map.37.refs_0_.refs_4_), channel_id=1, source_target_pairs={{2,0},{3,1},{0,2},{1,3},{6,4},{7,5},{4,6},{5,7},{10,8},{11,9},{8,1... | collective-permute-start | bytes 1769480 | tf_op jit(solution)/shard_map/ppermute | solution.py:58
  42.9 15.7 %collective-permute-start.8 = (bf16[256,1152]{1,0:T(8,128)(2,1)S(1)}, bf16[256,1152]{1,0:T(8,128)(2,1)S(1)}, u32[]{:S(2)}, u32[]{:S(2)}) collective-permute-start(bf16[256,1152]{1,0:T(8,128)(2,1)S(1)} %collective-permute-done.6.refs_8_), channel_id=1, source_target_pairs={{16,0},{17,1},{18,2},{19,3},{20,4},{21,5},{22,6},{23,7},{24,8},{25... | collective-permute-start | bytes 1769480 | tf_op jit(solution)/shard_map/ppermute | solution.py:58
  47.5 16.5 %collective-permute-start = (bf16[256,1152]{1,0:T(8,128)(2,1)}, bf16[256,1152]{1,0:T(8,128)(2,1)}, u32[]{:S(2)}, u32[]{:S(2)}) collective-permute-start(bf16[256,1152]{1,0:T(8,128)(2,1)} %shard_map.37.refs_0_.refs_4_), channel_id=1, source_target_pairs={{8,0},{9,1},{10,2},{11,3},{12,4},{13,5},{14,6},{15,7},{0,8},{1,9},... | collective-permute-start | bytes 1769480 | tf_op jit(solution)/shard_map/ppermute | solution.py:58
  49.0 15.0 %collective-permute-start.7 = (bf16[256,1152]{1,0:T(8,128)(2,1)S(1)}, bf16[256,1152]{1,0:T(8,128)(2,1)}, u32[]{:S(2)}, u32[]{:S(2)}) collective-permute-start(bf16[256,1152]{1,0:T(8,128)(2,1)S(1)} %collective-permute-done.6.refs_8_), channel_id=1, source_target_pairs={{1,0},{0,1},{3,2},{2,3},{5,4},{4,5},{7,6},{6,7},{9,8},{8,9},{11,10... | collective-permute-start | bytes 1769480 | tf_op jit(solution)/shard_map/ppermute | solution.py:58
  49.0 15.0 %collective-permute-start.5 = (bf16[256,1152]{1,0:T(8,128)(2,1)S(1)}, bf16[256,1152]{1,0:T(8,128)(2,1)}, u32[]{:S(2)}, u32[]{:S(2)}) collective-permute-start(bf16[256,1152]{1,0:T(8,128)(2,1)S(1)} %collective-permute-done.4.refs_6_), channel_id=1, source_target_pairs={{1,0},{0,1},{3,2},{2,3},{5,4},{4,5},{7,6},{6,7},{9,8},{8,9},{11,10... | collective-permute-start | bytes 1769480 | tf_op jit(solution)/shard_map/ppermute | solution.py:58
  55.8 20.0 %collective-permute-start.2 = (bf16[256,1152]{1,0:T(8,128)(2,1)S(1)}, bf16[256,1152]{1,0:T(8,128)(2,1)}, u32[]{:S(2)}, u32[]{:S(2)}) collective-permute-start(bf16[256,1152]{1,0:T(8,128)(2,1)S(1)} %collective-permute-done.1.refs_2_), channel_id=1, source_target_pairs={{8,0},{9,1},{10,2},{11,3},{12,4},{13,5},{14,6},{15,7},{0,8},{1,9},... | collective-permute-start | bytes 1769480 | tf_op jit(solution)/shard_map/ppermute | solution.py:58
  58.7 17.2 %collective-permute-start.9 = (bf16[256,1152]{1,0:T(8,128)(2,1)S(1)}, bf16[256,1152]{1,0:T(8,128)(2,1)}, u32[]{:S(2)}, u32[]{:S(2)}) collective-permute-start(bf16[256,1152]{1,0:T(8,128)(2,1)S(1)} %collective-permute-done.8.refs_10_), channel_id=1, source_target_pairs={{1,0},{0,1},{3,2},{2,3},{5,4},{4,5},{7,6},{6,7},{9,8},{8,9},{11,10... | collective-permute-start | bytes 1769480 | tf_op jit(solution)/shard_map/ppermute | solution.py:58
  91.4 6.2 %collective-permute-start.20 = (f32[256]{0:T(256)S(1)}, f32[256]{0:T(256)S(1)}, u32[]{:S(2)}, u32[]{:S(2)}) collective-permute-start(f32[256]{0:T(256)S(1)} %get-tuple-element.25), channel_id=1, source_target_pairs={{8,0},{9,1},{10,2},{11,3},{12,4},{13,5},{14,6},{15,7},{0,8},{1,9},... | collective-permute-start | bytes 3080 | tf_op jit(solution)/shard_map/ppermute | solution.py:58
  92.9 5.5 %collective-permute-start.22 = (f32[256]{0:T(256)S(1)}, f32[256]{0:T(256)S(1)}, u32[]{:S(2)}, u32[]{:S(2)}) collective-permute-start(f32[256]{0:T(256)S(1)} %get-tuple-element.26), channel_id=1, source_target_pairs={{10,0},{11,1},{8,2},{9,3},{14,4},{15,5},{12,6},{13,7},{2,8},{3,9},... | collective-permute-start | bytes 3080 | tf_op jit(solution)/shard_map/ppermute | solution.py:58
  94.9 6.6 %collective-permute-start.17 = (bf16[256,256]{1,0:T(8,128)(2,1)}, bf16[256,256]{1,0:T(8,128)(2,1)S(1)}, u32[]{:S(2)}, u32[]{:S(2)}) collective-permute-start(bf16[256,256]{1,0:T(8,128)(2,1)} %get-tuple-element.17), channel_id=1, source_target_pairs={{8,0},{9,1},{10,2},{11,3},{12,4},{13,5},{14,6},{15,7},{0,8},{1,9},... | collective-permute-start | bytes 393224 | tf_op jit(solution)/shard_map/ppermute | solution.py:58
  96.4 5.3 %collective-permute-start.18 = (bf16[256,256]{1,0:T(8,128)(2,1)}, bf16[256,256]{1,0:T(8,128)(2,1)S(1)}, u32[]{:S(2)}, u32[]{:S(2)}) collective-permute-start(bf16[256,256]{1,0:T(8,128)(2,1)} %get-tuple-element.18), channel_id=1, source_target_pairs={{2,0},{3,1},{0,2},{1,3},{6,4},{7,5},{4,6},{5,7},{10,8},{11,9},{8,1... | collective-permute-start | bytes 393224 | tf_op jit(solution)/shard_map/ppermute | solution.py:58
  97.7 6.1 %collective-permute-start.19 = (bf16[256,256]{1,0:T(8,128)(2,1)}, bf16[256,256]{1,0:T(8,128)(2,1)S(1)}, u32[]{:S(2)}, u32[]{:S(2)}) collective-permute-start(bf16[256,256]{1,0:T(8,128)(2,1)} %get-tuple-element.19), channel_id=1, source_target_pairs={{10,0},{11,1},{8,2},{9,3},{14,4},{15,5},{12,6},{13,7},{2,8},{3,9},... | collective-permute-start | bytes 393224 | tf_op jit(solution)/shard_map/ppermute | solution.py:58
  104.8 7.7 %collective-permute-start.26 = (bf16[256,256]{1,0:T(8,128)(2,1)S(1)}, bf16[256,256]{1,0:T(8,128)(2,1)S(1)}, u32[]{:S(2)}, u32[]{:S(2)}) collective-permute-start(bf16[256,256]{1,0:T(8,128)(2,1)S(1)} %add_convert_fusion.refs_0_), channel_id=1, source_target_pairs={{4,0},{5,1},{6,2},{7,3},{0,4},{1,5},{2,6},{3,7},{12,8},{13,9},{14,... | collective-permute-start | bytes 393224 | tf_op jit(solution)/shard_map/ppermute | solution.py:58
  108.1 6.0 %collective-permute-start.24 = (bf16[256,256]{1,0:T(8,128)(2,1)S(1)}, bf16[256,256]{1,0:T(8,128)(2,1)S(1)}, u32[]{:S(2)}, u32[]{:S(2)}) collective-permute-start(bf16[256,256]{1,0:T(8,128)(2,1)S(1)} %add_convert_fusion.refs_0_), channel_id=1, source_target_pairs={{16,0},{17,1},{18,2},{19,3},{20,4},{21,5},{22,6},{23,7},{24,8},{25... | collective-permute-start | bytes 393224 | tf_op jit(solution)/shard_map/ppermute | solution.py:58
  123.9 5.6 %collective-permute-start.30 = (bf16[256,256]{1,0:T(8,128)(2,1)S(1)}, bf16[256,256]{1,0:T(8,128)(2,1)S(1)}, u32[]{:S(2)}, u32[]{:S(2)}) collective-permute-start(bf16[256,256]{1,0:T(8,128)(2,1)S(1)} %get-tuple-element.22), channel_id=1, source_target_pairs={{8,0},{9,1},{10,2},{11,3},{12,4},{13,5},{14,6},{15,7},{0,8},{1,9},... | collective-permute-start | bytes 393224 | tf_op jit(solution)/shard_map/ppermute | solution.py:58
  124.5 6.4 %collective-permute-start.31 = (bf16[256,256]{1,0:T(8,128)(2,1)S(1)}, bf16[256,256]{1,0:T(8,128)(2,1)S(1)}, u32[]{:S(2)}, u32[]{:S(2)}) collective-permute-start(bf16[256,256]{1,0:T(8,128)(2,1)S(1)} %get-tuple-element.23), channel_id=1, source_target_pairs={{2,0},{3,1},{0,2},{1,3},{6,4},{7,5},{4,6},{5,7},{10,8},{11,9},{8,1... | collective-permute-start | bytes 393224 | tf_op jit(solution)/shard_map/ppermute | solution.py:58
  125.5 8.0 %collective-permute-start.32 = (bf16[256,256]{1,0:T(8,128)(2,1)S(1)}, bf16[256,256]{1,0:T(8,128)(2,1)S(1)}, u32[]{:S(2)}, u32[]{:S(2)}) collective-permute-start(bf16[256,256]{1,0:T(8,128)(2,1)S(1)} %get-tuple-element.24), channel_id=1, source_target_pairs={{10,0},{11,1},{8,2},{9,3},{14,4},{15,5},{12,6},{13,7},{2,8},{3,9},... | collective-permute-start | bytes 393224 | tf_op jit(solution)/shard_map/ppermute | solution.py:58
  (22 other events, 361.7 us)

commit v2 on v0

v2 whole, which is shorter than its diff:
```python
import functools
import math

import jax
import jax.numpy as jnp
from jax import lax
from jax.experimental import pallas as pl
from jax.experimental.pallas import tpu as pltpu
from jax.sharding import PartitionSpec as P

BLOCK = 128
ITERS = 2
AXES = ("row", "col")

sharpness = 30.0
mixing = 0.8
epsilon = 1e-06


def split_two(n):
    low = max(d for d in range(1, math.isqrt(n) + 1) if n % d == 0)
    return n // low, low


class Layout:
    def __init__(self, rows, cols):
        core = 2 if cols % 2 == 0 else 1
        ny, nx = split_two(rows)
        nzh, nzl = split_two(cols // core)
        self.sizes = dict(y=ny, x=nx, zh=nzh, zl=nzl, core=core)
        self.rows, self.cols = rows, cols

    def coords(self, row, col):
        s = self.sizes
        return dict(
            y=row // s["x"],
            x=row % s["x"],
            zh=col // (s["zl"] * s["core"]),
            zl=col // s["core"] % s["zl"],
            core=col % s["core"],
        )

    def moved(self, at, offset):
        return {k: (at[k] + offset.get(k, 0)) % self.sizes[k] for k in at}

    def row_col(self, at):
        s = self.sizes
        return at["y"] * s["x"] + at["x"], (at["zh"] * s["zl"] + at["zl"]) * s["core"] + at["core"]

    def fetch(self, value, **offset):
        if all(v % self.sizes[k] == 0 for k, v in offset.items()):
            return value
        pairs = []
        for row in range(self.rows):
            for col in range(self.cols):
                r, c = self.row_col(self.moved(self.coords(row, col), offset))
                pairs.append((r * self.cols + c, row * self.cols + col))
        return lax.ppermute(value, AXES, pairs)

    def device(self, offset):
        at = self.coords(lax.axis_index("row"), lax.axis_index("col"))
        row, col = self.row_col(self.moved(at, offset))
        return col * self.rows + row


def unit_kernel(emb_ref, out_ref):
    values = emb_ref[...].astype(jnp.float32)
    mean_square = jnp.mean(values * values, axis=1, keepdims=True)
    scaled = values * lax.rsqrt(mean_square + epsilon) * values.shape[1] ** (-0.5)
    out_ref[...] = scaled.astype(jnp.bfloat16)


VMEM = pl.BlockSpec(memory_space=pltpu.VMEM)


def unit_rows(embeddings):
    return pl.pallas_call(
        unit_kernel,
        out_shape=jax.ShapeDtypeStruct(embeddings.shape, jnp.bfloat16),
        in_specs=[VMEM],
        out_specs=VMEM,
    )(embeddings)


def gram_kernel(nt, ns, sub, flags, *refs):
    t_in, s_in, (kern, acc) = refs[:nt], refs[nt : nt + ns], refs[nt + ns :]
    col = 0
    for j in range(ns):
        width = s_in[j].shape[0]
        row = 0
        for i in range(nt):
            height = t_in[i].shape[0]
            scores = lax.dot_general(
                t_in[i][...],
                s_in[j][...],
                (((1,), (1,)), ((), ())),
                preferred_element_type=jnp.float32,
            )
            value = jnp.exp(sharpness * scores).astype(jnp.bfloat16).astype(jnp.float32)
            for a in range(height // sub):
                at = row + a * sub
                flag = flags[at // sub : at // sub + 1, col : col + width]
                part = jnp.where(flag > 0, value[a * sub : (a + 1) * sub], 0.0)
                kern[at : at + sub, col : col + width] = part.astype(jnp.bfloat16)
                total = part[:, :BLOCK]
                for b in range(1, width // BLOCK):
                    total = total + part[:, b * BLOCK : (b + 1) * BLOCK]
                if j > 0:
                    total = total + acc[at : at + sub, :]
                acc[at : at + sub, :] = total
            row += height
        col += width


def gram_call(flags, t_pieces, s_pieces, sub):
    rows, cols = (sum(p.shape[0] for p in pieces) for pieces in (t_pieces, s_pieces))
    d = t_pieces[0].shape[1]
    return pl.pallas_call(
        functools.partial(gram_kernel, len(t_pieces), len(s_pieces), sub),
        out_shape=[
            jax.ShapeDtypeStruct((rows, cols), jnp.bfloat16),
            jax.ShapeDtypeStruct((rows, BLOCK), jnp.float32),
        ],
        in_specs=[VMEM] * (1 + len(t_pieces) + len(s_pieces)),
        out_specs=[VMEM] * 2,
        compiler_params=pltpu.CompilerParams(vmem_limit_bytes=32 * 2**20),
        cost_estimate=pl.CostEstimate(
            flops=2 * rows * cols * d,
            bytes_accessed=2 * (rows + cols) * d,
            transcendentals=rows * cols,
        ),
    )(flags, *t_pieces, *s_pieces)


def spread_kernel(nk, na, ns, nt, m, rects, *refs):
    kerns, refs = refs[:nk], refs[nk:]
    accs, refs = refs[:na], refs[na:]
    p_in, refs = refs[:ns], refs[ns:]
    outs, pcat = refs[:-1], refs[-1]
    own_ref, other_refs = outs[0], outs[-(nt - 1) :] if nt > 1 else ()
    c = pcat.shape[1]
    at = 0
    for ref in p_in:
        pcat[at : at + ref.shape[0], :] = ref[...]
        at += ref.shape[0]
    tile = max(m, 2 * BLOCK)
    for r0 in range(0, nt * m, tile):
        part = None
        for kern, (t0, t1, c0, c1) in zip(kerns, rects):
            if t0 <= r0 < t1:
                term = jnp.dot(
                    kern[r0 - t0 : r0 - t0 + tile, :],
                    pcat[c0:c1, :],
                    preferred_element_type=jnp.float32,
                )
                part = term if part is None else part + term
        for piece in range(r0 // m, (r0 + tile) // m):
            value = part[piece * m - r0 : (piece + 1) * m - r0]
            if piece == 0:
                own_ref[...] = value
            else:
                other_refs[piece - 1][:m, :] = value.astype(jnp.bfloat16)
            if not na:
                continue
            step = min(m, BLOCK)
            for lane in range(0, m, step):
                total = None
                for acc, (t0, t1, c0, c1) in zip(accs, rects):
                    if t0 <= piece * m < t1:
                        start = piece * m - t0 + lane
                        term = acc[start : start + step, :]
                        total = term if total is None else total + term
                total = jnp.sum(total.T, axis=0, keepdims=True)
                if piece == 0:
                    outs[1][:, lane : lane + step] = total
                else:
                    high = total.astype(jnp.bfloat16).astype(jnp.float32)
                    mid = (total - high).astype(jnp.bfloat16).astype(jnp.float32)
                    low = total - high - mid
                    index = lax.broadcasted_iota(jnp.int32, (16, step), 0)
                    terms = jnp.where(index == 0, high, jnp.where(index == 1, mid, low))
                    terms = jnp.where(index < 3, terms, 0.0)
                    other_refs[piece - 1][m:, lane : lane + step] = terms.astype(jnp.bfloat16)


def spread_call(kerns, accs, p_pieces, m, nt, rects):
    c = p_pieces[0].shape[1]
    cols = sum(p.shape[0] for p in p_pieces)
    rows = nt * m
    extra = 16 if accs else 0
    outs = [jax.ShapeDtypeStruct((m, c), jnp.float32)]
    if accs:
        outs.append(jax.ShapeDtypeStruct((1, m), jnp.float32))
    outs += [jax.ShapeDtypeStruct((m + extra, c), jnp.bfloat16)] * (nt - 1)
    got = pl.pallas_call(
        functools.partial(spread_kernel, len(kerns), len(accs), len(p_pieces), nt, m, rects),
        out_shape=outs,
        in_specs=[VMEM] * (len(kerns) + len(accs) + len(p_pieces)),
        out_specs=[VMEM] * len(outs),
        scratch_shapes=[pltpu.VMEM((cols, c), jnp.bfloat16)],
        compiler_params=pltpu.CompilerParams(vmem_limit_bytes=32 * 2**20),
        cost_estimate=pl.CostEstimate(
            flops=2 * rows * cols * c,
            bytes_accessed=2 * (rows * cols + cols * c),
            transcendentals=0,
        ),
    )(*kerns, *accs, *p_pieces)
    return got if accs else [got[0], None] + list(got[1:])


def after(value, *earlier):
    return lax.optimization_barrier((value, *earlier))[0]


def on_device(embeddings, seed_labels, pattern):
    layout = Layout(lax.axis_size("row"), lax.axis_size("col"))
    size = layout.sizes
    m = embeddings.shape[0]
    sub = min(m, BLOCK)
    halves = 2 if m % (2 * BLOCK) == 0 else 1
    fetch = layout.fetch
    cores = range(size["core"])
    t_offsets = [dict(x=a, zl=b) for b in range(size["zl"]) for a in range(size["x"])]
    nt = len(t_offsets)
    half = m // halves
    near = [(dict(y=a, zh=0, core=c), 0, m) for a in range(size["y"]) for c in cores]
    far = [
        [
            (dict(y=a, zh=b, core=c), h * half, half)
            for b in range(1, size["zh"])
            for a in range(size["y"])
            for c in cores
        ]
        for h in range(halves)
    ]
    s_groups = [near] + far if size["zh"] > 1 else [near]
    s_all = [p for group in s_groups for p in group]

    t_blocks = jnp.concatenate(
        [layout.device(o) * m // BLOCK + jnp.arange(0, m, sub) // BLOCK for o in t_offsets]
    ) if m >= BLOCK else jnp.stack([layout.device(o) * m // BLOCK for o in t_offsets])
    s_blocks = jnp.concatenate(
        [
            (layout.device(o) * m + start + jnp.arange(0, rows, sub)) // BLOCK
            for o, start, rows in s_all
        ]
    )
    flags = jnp.any(pattern[t_blocks][:, None, :] == s_blocks[None, :, None], axis=2)
    flags = jnp.repeat(flags.astype(jnp.int32), sub, axis=1)

    own_seed = seed_labels.astype(jnp.float32)
    units = unit_rows(embeddings)

    def cored(value):
        return [fetch(value, core=c) for c in cores]

    t_zl = [fetch(units, zl=b) for b in range(size["zl"])]
    t_pieces = [fetch(v, x=a) for v in t_zl for a in range(size["x"])]
    s_near = [p for a in range(size["y"]) for p in cored(fetch(units, y=a))]
    s_far, sent = [], None
    for h in range(halves):
        rows = units[h * half : (h + 1) * half]
        if sent is not None:
            rows = after(rows, *sent)
        sent = [fetch(rows, zh=b) for b in range(1, size["zh"])]
        s_far.append([p for v in sent for a in range(size["y"]) for p in cored(fetch(v, y=a))])
    s_pieces = [s_near] + s_far if size["zh"] > 1 else [s_near]

    def panel_pieces(panel):
        whole = {}
        for b in range(size["zh"]):
            value = fetch(panel, zh=b)
            for a in range(size["y"]):
                for c, piece in zip(cores, cored(fetch(value, y=a))):
                    whole[a, b, c] = piece
        return [
            whole[o["y"], o["zh"], o["core"]][start : start + rows] for o, start, rows in s_all
        ]

    seeds = panel_pieces(after(seed_labels, *sent))

    def merged(pieces):
        return pieces if m >= BLOCK else [jnp.concatenate(pieces)]

    early = [i for i, o in enumerate(t_offsets) if o["x"] == 0 or o["zl"] == 0]
    if m < BLOCK or early != list(range(len(early))):
        early = list(range(nt))
    late = [i for i in range(nt) if i not in early]
    kerns, accs, rects = [], [], []
    col = 0
    for g, group in enumerate(s_pieces):
        width = sum(p.shape[0] for p in group)
        for rows in [early, late] if g == 0 and late else [list(range(nt))]:
            t0, t1 = rows[0] * m, (rows[-1] + 1) * m
            kern, acc = gram_call(
                flags[t0 // sub : t1 // sub, col : col + width],
                merged([t_pieces[i] for i in rows]),
                merged(group),
                sub,
            )
            kerns.append(kern)
            accs.append(acc)
            rects.append((t0, t1, col, col + width))
        col += width

    def home(values):
        return [fetch(v, **{k: -d for k, d in o.items()}) for v, o in zip(values, t_offsets[1:])]

    own, totals, *others = spread_call(kerns, accs, seeds, m, nt, rects)
    for sweep_index in range(ITERS):
        if sweep_index > 0:
            pieces = panel_pieces(labels.astype(jnp.bfloat16))
            own, _, *others = spread_call(kerns, [], pieces, m, nt, rects)
        numerators = own
        got = home(others)
        for value in got:
            numerators = numerators + value[:m].astype(jnp.float32)
        if sweep_index == 0:
            for value in got:
                totals = totals + jnp.sum(value[m : m + 3, :m].astype(jnp.float32), axis=0)
            totals = totals.reshape(m, 1)
        labels = mixing * numerators / totals + (1.0 - mixing) * own_seed
    return labels


def solution(mesh):
    return jax.shard_map(
        on_device,
        mesh=mesh,
        in_specs=(P(("col", "row"), None), P(("col", "row"), None), P()),
        out_specs=P(("col", "row"), None),
        check_vma=False,
    )
```

time: 214 us -> 116 us (0.54)
  waiting for transfers between devices: 126 us -> 69.5 us
  blocking collectives: 41.7 us -> 0 us
  starting transfers between devices: 0.12 us -> 28.5 us
  matrix products: 16 us -> 0 us
  Pallas kernels: 0 us -> 13.3 us
  between operations: 13.9 us -> 0.63 us
  local copies, waits for them, and re-layouts: 9.14 us -> 2.07 us
  other arithmetic: 6.53 us -> 1.44 us
    all_gather x2 -> x0, waiting for transfers between devices: 73.6 us -> none  [the longest x1 53.4 us: on_device(): col_units = lax.all_gather(unit_rows, 'col', axis=0, tiled=True)]
    ppermute x0 -> x34, waiting for transfers between devices: none -> 69.5 us  [fetch(): return lax.ppermute(value, AXES, pairs)]
    reduce_scatter x2 -> x0, waiting for transfers between devices: 52 us -> none  [on_device(): lax.psum_scatter(partial_value, 'col', scatter_dimension=0, tiled=True)]
    ppermute x0 -> x34, starting transfers between devices: none -> 28.5 us  [fetch(): return lax.ppermute(value, AXES, pairs)]
    all_gather x2 -> x0, blocking collectives: 26.9 us -> none  [on_device(): lax.all_gather(panel_rows, 'row', axis=0, tiled=True)]
    dot_general x3 -> x0, matrix products: 16 us -> none  [the longest x1 8.49 us: on_device(): jnp.einsum('id,jd->ij', col_units, row_units, preferred_element_type=jnp....]
    unnamed x1 -> x0, blocking collectives: 14.8 us -> none
    pallas_call x0 -> x7, Pallas kernels: none -> 13.3 us  [the longest x4 8.6 us: gram_call(): pl.pallas_call(functools.partial(gram_kernel, len(t_pieces), len(s_pieces...]
  transfers between devices with their start and end apart: 4 -> 34, of which waited for: 4 -> 16; matrix products, arithmetic and copies ran while one was open for 4% -> 2% of each run, Pallas kernels for 0% -> 7%
where the time goes in v2:
time: 116 us; the launch traced here: 115 us
  waiting for transfers between devices  69.5 us (60%)
  starting transfers between devices  28.5 us (25%)
  Pallas kernels  13.3 us (11%)
  local copies, waits for them, and re-layouts  2.07 us (2%)
  other arithmetic  1.44 us (1%)
    ppermute x34, waiting for transfers between devices, fetch(): return lax.ppermute(value, AXES, pairs)  69.5 us
    ppermute x34, starting transfers between devices, fetch(): return lax.ppermute(value, AXES, pairs)  28.5 us
    pallas_call x4, Pallas kernels, gram_call(): pl.pallas_call(functools.partial(gram_kernel, len(t_pieces), len(s_pieces...  8.6 us
    pallas_call x2, Pallas kernels, spread_call(): pl.pallas_call(functools.partial(spread_kernel, len(kerns), len(accs), le...  2.56 us
  transfers between devices with their start and end apart: 34, of which 16 were waited for; matrix products, arithmetic and copies ran while one was open for 2% of the time, Pallas kernels for 7%

profile of v2, /device:TPU:0, one launch (start us, length us, event | category | flops | bytes accessed | tf_op | source)
XLA Modules:
  0.0 115.4 jit_solution(2033406465975265797)
XLA Ops:
  0.0 2.2 %shard_map.37.refs_0_.refs_3_.refs_1_ = bf16[256,1152]{1,0:T(8,128)(2,1)} custom-call(bf16[256,1152]{1,0:T(8,128)(2,1)} %emb_ref.1), custom_call_target="tpu_custom_call" | custom-call | tf_op jit(solution)/shard_map/pallas_call | solution.py:77
  2.2 2.9 %collective-permute-start = (bf16[256,1152]{1,0:T(8,128)(2,1)}, bf16[256,1152]{1,0:T(8,128)(2,1)S(1)}, u32[]{:S(2)}, u32[]{:S(2)}) collective-permute-start(bf16[256,1152]{1,0:T(8,128)(2,1)} %shard_map.37.refs_0_.refs_3_.refs_1_), channel_id=1, source_target_pairs={{8,0},{9,1},{10,2},{11,3},{12,4},{13,5},{14,6},{15,7},{0,8},{1,9},... | collective-permute-start | bytes 1769480 | tf_op jit(solution)/shard_map/ppermute | solution.py:58
  5.1 1.6 %collective-permute-start.1 = (bf16[256,1152]{1,0:T(8,128)(2,1)}, bf16[256,1152]{1,0:T(8,128)(2,1)S(1)}, u32[]{:S(2)}, u32[]{:S(2)}) collective-permute-start(bf16[256,1152]{1,0:T(8,128)(2,1)} %shard_map.37.refs_0_.refs_3_.refs_1_), channel_id=1, source_target_pairs={{2,0},{3,1},{0,2},{1,3},{6,4},{7,5},{4,6},{5,7},{10,8},{11,9},{8,1... | collective-permute-start | bytes 1769480 | tf_op jit(solution)/shard_map/ppermute | solution.py:58
  6.7 1.5 %collective-permute-start.3 = (bf16[256,1152]{1,0:T(8,128)(2,1)}, bf16[256,1152]{1,0:T(8,128)(2,1)S(1)}, u32[]{:S(2)}, u32[]{:S(2)}) collective-permute-start(bf16[256,1152]{1,0:T(8,128)(2,1)} %shard_map.37.refs_0_.refs_3_.refs_1_), channel_id=1, source_target_pairs={{16,0},{17,1},{18,2},{19,3},{20,4},{21,5},{22,6},{23,7},{24,8},{25... | collective-permute-start | bytes 1769480 | tf_op jit(solution)/shard_map/ppermute | solution.py:58
  9.3 2.7 %collective-permute-start.6 = (bf16[128,1152]{1,0:T(8,128)(2,1)S(1)}, bf16[128,1152]{1,0:T(8,128)(2,1)S(1)}, u32[]{:S(2)}, u32[]{:S(2)}) collective-permute-start(bf16[128,1152]{1,0:T(8,128)(2,1)S(1)} %get-tuple-element.44), channel_id=1, source_target_pairs={{4,0},{5,1},{6,2},{7,3},{0,4},{1,5},{2,6},{3,7},{12,8},{13,9},{14,... | collective-permute-start | bytes 884744 | tf_op jit(solution)/shard_map/ppermute | solution.py:58
  13.5 12.0 %collective-permute-done.6.refs_4_ = bf16[128,1152]{1,0:T(8,128)(2,1)S(1)} collective-permute-done((bf16[128,1152]{1,0:T(8,128)(2,1)S(1)}, bf16[128,1152]{1,0:T(8,128)(2,1)S(1)}, u32[]{:S(2)}, u32[]{:S(2)}) %collective-permute-start.6) | collective-permute-done | bytes 294944 | tf_op jit(solution)/shard_map/ppermute | solution.py:58
  25.5 3.4 %collective-permute-start.10 = (bf16[128,1152]{1,0:T(8,128)(2,1)S(1)}, bf16[128,1152]{1,0:T(8,128)(2,1)S(1)}, u32[]{:S(2)}, u32[]{:S(2)}) collective-permute-start(bf16[128,1152]{1,0:T(8,128)(2,1)S(1)} %get-tuple-element.27), channel_id=1, source_target_pairs={{4,0},{5,1},{6,2},{7,3},{0,4},{1,5},{2,6},{3,7},{12,8},{13,9},{14,... | collective-permute-start | bytes 884744 | tf_op jit(solution)/shard_map/ppermute | solution.py:58
  28.9 1.5 %collective-permute-start.8 = (bf16[128,1152]{1,0:T(8,128)(2,1)S(1)}, bf16[128,1152]{1,0:T(8,128)(2,1)S(1)}, u32[]{:S(2)}, u32[]{:S(2)}) collective-permute-start(bf16[128,1152]{1,0:T(8,128)(2,1)S(1)} %collective-permute-done.6.refs_4_), channel_id=1, source_target_pairs={{16,0},{17,1},{18,2},{19,3},{20,4},{21,5},{22,6},{23,7},{24,8},{25... | collective-permute-start | bytes 884744 | tf_op jit(solution)/shard_map/ppermute | solution.py:58
  30.5 10.6 %collective-permute-done.10.refs_4_ = bf16[128,1152]{1,0:T(8,128)(2,1)S(1)} collective-permute-done((bf16[128,1152]{1,0:T(8,128)(2,1)S(1)}, bf16[128,1152]{1,0:T(8,128)(2,1)S(1)}, u32[]{:S(2)}, u32[]{:S(2)}) %collective-permute-start.10) | collective-permute-done | bytes 294944 | tf_op jit(solution)/shard_map/ppermute | solution.py:58
  41.7 8.8 %collective-permute-done.17 = bf16[256,256]{1,0:T(8,128)(2,1)S(1)} collective-permute-done((bf16[256,256]{1,0:T(8,128)(2,1)S(1)}, bf16[256,256]{1,0:T(8,128)(2,1)S(1)}, u32[]{:S(2)}, u32[]{:S(2)}) %collective-permute-start.17) | collective-permute-done | bytes 131104 | tf_op jit(solution)/shard_map/ppermute | solution.py:58
  50.5 1.5 %collective-permute-start.19 = (bf16[256,256]{1,0:T(8,128)(2,1)S(1)}, bf16[256,256]{1,0:T(8,128)(2,1)S(1)}, u32[]{:S(2)}, u32[]{:S(2)}) collective-permute-start(bf16[256,256]{1,0:T(8,128)(2,1)S(1)} %collective-permute-done.17), channel_id=1, source_target_pairs={{16,0},{17,1},{18,2},{19,3},{20,4},{21,5},{22,6},{23,7},{24,8},{25... | collective-permute-start | bytes 393224 | tf_op jit(solution)/shard_map/ppermute | solution.py:58
  53.2 2.8 %collective-permute-done.19 = bf16[256,256]{1,0:T(8,128)(2,1)S(1)} collective-permute-done((bf16[256,256]{1,0:T(8,128)(2,1)S(1)}, bf16[256,256]{1,0:T(8,128)(2,1)S(1)}, u32[]{:S(2)}, u32[]{:S(2)}) %collective-permute-start.19) | collective-permute-done | bytes 131104 | tf_op jit(solution)/shard_map/ppermute | solution.py:58
  60.7 6.5 %collective-permute-done.12.refs_6_ = bf16[128,1152]{1,0:T(8,128)(2,1)S(1)} collective-permute-done((bf16[128,1152]{1,0:T(8,128)(2,1)S(1)}, bf16[128,1152]{1,0:T(8,128)(2,1)S(1)}, u32[]{:S(2)}, u32[]{:S(2)}) %collective-permute-start.12) | collective-permute-done | bytes 294944 | tf_op jit(solution)/shard_map/ppermute | solution.py:58
  68.0 2.7 %shard_map.40 = (bf16[1024,512]{1,0:T(8,128)(2,1)S(1)}, f32[1024,128]{1,0:T(8,128)S(1)}) custom-call(s32[8,512]{1,0:T(8,128)S(1)} %get-tuple-element.62.flags, bf16[256,1152]{1,0:T(8,128)(2,1)S(1)} %copy-done, bf16[256,1152]{1,0:T(8,128)(2,1)S(1)} %collective-permute-done.refs_1_, bf16[256,1152]{1,0:T(8,128)(2,1)S(1)} %collective-permute-done.1.refs_2_, ...), custom_call_target="tpu_custom_call" | custom-call | flops 1207959552 | bytes 3538944 | tf_op jit(solution)/shard_map/pallas_call | solution.py:118
  71.3 2.4 %shard_map.38 = (bf16[768,1024]{1,0:T(8,128)(2,1)S(1)}, f32[768,128]{1,0:T(8,128)S(1)}) custom-call(s32[6,1024]{1,0:T(8,128)S(1)} %slice.114.flags, bf16[256,1152]{1,0:T(8,128)(2,1)S(1)} %copy-done, bf16[256,1152]{1,0:T(8,128)(2,1)S(1)} %collective-permute-done.refs_1_, bf16[256,1152]{1,0:T(8,128)(2,1)S(1)} %collective-permute-done.1.refs_2_, ...), custom_call_target="tpu_custom_call" | custom-call | flops 1811939328 | bytes 4128768 | tf_op jit(solution)/shard_map/pallas_call | solution.py:118
  74.6 2.6 %shard_map.41 = (bf16[1024,512]{1,0:T(8,128)(2,1)S(1)}, f32[1024,128]{1,0:T(8,128)S(1)}) custom-call(s32[8,512]{1,0:T(8,128)S(1)} %get-tuple-element.61.flags, bf16[256,1152]{1,0:T(8,128)(2,1)S(1)} %copy-done, bf16[256,1152]{1,0:T(8,128)(2,1)S(1)} %collective-permute-done.refs_1_, bf16[256,1152]{1,0:T(8,128)(2,1)S(1)} %collective-permute-done.1.refs_2_, ...), custom_call_target="tpu_custom_call" | custom-call | flops 1207959552 | bytes 3538944 | tf_op jit(solution)/shard_map/pallas_call | solution.py:118
  78.7 2.0 %collective-permute-start.22 = (bf16[272,256]{1,0:T(8,128)(2,1)S(1)}, bf16[272,256]{1,0:T(8,128)(2,1)S(1)}, u32[]{:S(2)}, u32[]{:S(2)}) collective-permute-start(bf16[272,256]{1,0:T(8,128)(2,1)S(1)} %get-tuple-element.36), channel_id=1, source_target_pairs={{2,0},{3,1},{0,2},{1,3},{6,4},{7,5},{4,6},{5,7},{10,8},{11,9},{8,1... | collective-permute-start | bytes 417800 | tf_op jit(solution)/shard_map/ppermute | solution.py:58
  82.2 3.9 %collective-permute-done.23 = bf16[272,256]{1,0:T(8,128)(2,1)S(1)} collective-permute-done((bf16[272,256]{1,0:T(8,128)(2,1)S(1)}, bf16[272,256]{1,0:T(8,128)(2,1)S(1)}, u32[]{:S(2)}, u32[]{:S(2)}) %collective-permute-start.23) | collective-permute-done | bytes 139296 | tf_op jit(solution)/shard_map/ppermute | solution.py:58
  86.1 1.5 %collective-permute-done.22 = bf16[272,256]{1,0:T(8,128)(2,1)S(1)} collective-permute-done((bf16[272,256]{1,0:T(8,128)(2,1)S(1)}, bf16[272,256]{1,0:T(8,128)(2,1)S(1)}, u32[]{:S(2)}, u32[]{:S(2)}) %collective-permute-start.22) | collective-permute-done | bytes 139296 | tf_op jit(solution)/shard_map/ppermute | solution.py:58
  89.7 7.0 %collective-permute-done.27 = bf16[256,256]{1,0:T(8,128)(2,1)S(1)} collective-permute-done((bf16[256,256]{1,0:T(8,128)(2,1)S(1)}, bf16[256,256]{1,0:T(8,128)(2,1)S(1)}, u32[]{:S(2)}, u32[]{:S(2)}) %collective-permute-start.27) | collective-permute-done | bytes 131104 | tf_op jit(solution)/shard_map/ppermute | solution.py:58
  97.7 4.9 %collective-permute-done.29 = bf16[256,256]{1,0:T(8,128)(2,1)S(1)} collective-permute-done((bf16[256,256]{1,0:T(8,128)(2,1)S(1)}, bf16[256,256]{1,0:T(8,128)(2,1)S(1)}, u32[]{:S(2)}, u32[]{:S(2)}) %collective-permute-start.29) | collective-permute-done | bytes 131104 | tf_op jit(solution)/shard_map/ppermute | solution.py:58
  105.4 2.9 %collective-permute-start.32 = (bf16[256,256]{1,0:T(8,128)(2,1)S(1)}, bf16[256,256]{1,0:T(8,128)(2,1)S(1)}, u32[]{:S(2)}, u32[]{:S(2)}) collective-permute-start(bf16[256,256]{1,0:T(8,128)(2,1)S(1)} %get-tuple-element.41), channel_id=1, source_target_pairs={{2,0},{3,1},{0,2},{1,3},{6,4},{7,5},{4,6},{5,7},{10,8},{11,9},{8,1... | collective-permute-start | bytes 393224 | tf_op jit(solution)/shard_map/ppermute | solution.py:58
  108.8 3.7 %collective-permute-done.33 = bf16[256,256]{1,0:T(8,128)(2,1)S(1)} collective-permute-done((bf16[256,256]{1,0:T(8,128)(2,1)S(1)}, bf16[256,256]{1,0:T(8,128)(2,1)S(1)}, u32[]{:S(2)}, u32[]{:S(2)}) %collective-permute-start.33) | collective-permute-done | bytes 131104 | tf_op jit(solution)/shard_map/ppermute | solution.py:58
  112.6 2.0 %collective-permute-done.32 = bf16[256,256]{1,0:T(8,128)(2,1)S(1)} collective-permute-done((bf16[256,256]{1,0:T(8,128)(2,1)S(1)}, bf16[256,256]{1,0:T(8,128)(2,1)S(1)}, u32[]{:S(2)}, u32[]{:S(2)}) %collective-permute-start.32) | collective-permute-done | bytes 131104 | tf_op jit(solution)/shard_map/ppermute | solution.py:58
  (88 shorter events, 21.2 us)
Async XLA Ops:
  2.2 38.9 %collective-permute-start = (bf16[256,1152]{1,0:T(8,128)(2,1)}, bf16[256,1152]{1,0:T(8,128)(2,1)S(1)}, u32[]{:S(2)}, u32[]{:S(2)}) collective-permute-start(bf16[256,1152]{1,0:T(8,128)(2,1)} %shard_map.37.refs_0_.refs_3_.refs_1_), channel_id=1, source_target_pairs={{8,0},{9,1},{10,2},{11,3},{12,4},{13,5},{14,6},{15,7},{0,8},{1,9},... | collective-permute-start | bytes 1769480 | tf_op jit(solution)/shard_map/ppermute | solution.py:58
  5.1 46.9 %collective-permute-start.1 = (bf16[256,1152]{1,0:T(8,128)(2,1)}, bf16[256,1152]{1,0:T(8,128)(2,1)S(1)}, u32[]{:S(2)}, u32[]{:S(2)}) collective-permute-start(bf16[256,1152]{1,0:T(8,128)(2,1)} %shard_map.37.refs_0_.refs_3_.refs_1_), channel_id=1, source_target_pairs={{2,0},{3,1},{0,2},{1,3},{6,4},{7,5},{4,6},{5,7},{10,8},{11,9},{8,1... | collective-permute-start | bytes 1769480 | tf_op jit(solution)/shard_map/ppermute | solution.py:58
  6.7 45.4 %collective-permute-start.3 = (bf16[256,1152]{1,0:T(8,128)(2,1)}, bf16[256,1152]{1,0:T(8,128)(2,1)S(1)}, u32[]{:S(2)}, u32[]{:S(2)}) collective-permute-start(bf16[256,1152]{1,0:T(8,128)(2,1)} %shard_map.37.refs_0_.refs_3_.refs_1_), channel_id=1, source_target_pairs={{16,0},{17,1},{18,2},{19,3},{20,4},{21,5},{22,6},{23,7},{24,8},{25... | collective-permute-start | bytes 1769480 | tf_op jit(solution)/shard_map/ppermute | solution.py:58
  9.3 16.2 %collective-permute-start.6 = (bf16[128,1152]{1,0:T(8,128)(2,1)S(1)}, bf16[128,1152]{1,0:T(8,128)(2,1)S(1)}, u32[]{:S(2)}, u32[]{:S(2)}) collective-permute-start(bf16[128,1152]{1,0:T(8,128)(2,1)S(1)} %get-tuple-element.44), channel_id=1, source_target_pairs={{4,0},{5,1},{6,2},{7,3},{0,4},{1,5},{2,6},{3,7},{12,8},{13,9},{14,... | collective-permute-start | bytes 884744 | tf_op jit(solution)/shard_map/ppermute | solution.py:58
  25.5 15.6 %collective-permute-start.10 = (bf16[128,1152]{1,0:T(8,128)(2,1)S(1)}, bf16[128,1152]{1,0:T(8,128)(2,1)S(1)}, u32[]{:S(2)}, u32[]{:S(2)}) collective-permute-start(bf16[128,1152]{1,0:T(8,128)(2,1)S(1)} %get-tuple-element.27), channel_id=1, source_target_pairs={{4,0},{5,1},{6,2},{7,3},{0,4},{1,5},{2,6},{3,7},{12,8},{13,9},{14,... | collective-permute-start | bytes 884744 | tf_op jit(solution)/shard_map/ppermute | solution.py:58
  28.9 12.3 %collective-permute-start.8 = (bf16[128,1152]{1,0:T(8,128)(2,1)S(1)}, bf16[128,1152]{1,0:T(8,128)(2,1)S(1)}, u32[]{:S(2)}, u32[]{:S(2)}) collective-permute-start(bf16[128,1152]{1,0:T(8,128)(2,1)S(1)} %collective-permute-done.6.refs_4_), channel_id=1, source_target_pairs={{16,0},{17,1},{18,2},{19,3},{20,4},{21,5},{22,6},{23,7},{24,8},{25... | collective-permute-start | bytes 884744 | tf_op jit(solution)/shard_map/ppermute | solution.py:58
  41.1 11.5 %collective-permute-start.7 = (bf16[128,1152]{1,0:T(8,128)(2,1)S(1)}, bf16[128,1152]{1,0:T(8,128)(2,1)S(1)}, u32[]{:S(2)}, u32[]{:S(2)}) collective-permute-start(bf16[128,1152]{1,0:T(8,128)(2,1)S(1)} %collective-permute-done.6.refs_4_), channel_id=1, source_target_pairs={{1,0},{0,1},{3,2},{2,3},{5,4},{4,5},{7,6},{6,7},{9,8},{8,9},{11,10... | collective-permute-start | bytes 884744 | tf_op jit(solution)/shard_map/ppermute | solution.py:58
  41.1 9.4 %collective-permute-start.17 = (bf16[256,256]{1,0:T(8,128)(2,1)S(1)}, bf16[256,256]{1,0:T(8,128)(2,1)S(1)}, u32[]{:S(2)}, u32[]{:S(2)}) collective-permute-start(bf16[256,256]{1,0:T(8,128)(2,1)S(1)} %copy-done.1), channel_id=1, source_target_pairs={{4,0},{5,1},{6,2},{7,3},{0,4},{1,5},{2,6},{3,7},{12,8},{13,9},{14,... | collective-permute-start | bytes 393224 | tf_op jit(solution)/shard_map/ppermute | solution.py:58
  41.2 17.6 %collective-permute-start.9 = (bf16[128,1152]{1,0:T(8,128)(2,1)S(1)}, bf16[128,1152]{1,0:T(8,128)(2,1)S(1)}, u32[]{:S(2)}, u32[]{:S(2)}) collective-permute-start(bf16[128,1152]{1,0:T(8,128)(2,1)S(1)} %collective-permute-done.8.refs_6_), channel_id=1, source_target_pairs={{1,0},{0,1},{3,2},{2,3},{5,4},{4,5},{7,6},{6,7},{9,8},{8,9},{11,10... | collective-permute-start | bytes 884744 | tf_op jit(solution)/shard_map/ppermute | solution.py:58
  52.1 18.6 %collective-permute-start.2 = (bf16[256,1152]{1,0:T(8,128)(2,1)S(1)}, bf16[256,1152]{1,0:T(8,128)(2,1)S(1)}, u32[]{:S(2)}, u32[]{:S(2)}) collective-permute-start(bf16[256,1152]{1,0:T(8,128)(2,1)S(1)} %copy-done), channel_id=1, source_target_pairs={{1,0},{0,1},{3,2},{2,3},{5,4},{4,5},{7,6},{6,7},{9,8},{8,9},{11,10... | collective-permute-start | bytes 1769480 | tf_op jit(solution)/shard_map/ppermute | solution.py:58
  52.1 19.1 %collective-permute-start.4 = (bf16[256,1152]{1,0:T(8,128)(2,1)S(1)}, bf16[256,1152]{1,0:T(8,128)(2,1)S(1)}, u32[]{:S(2)}, u32[]{:S(2)}) collective-permute-start(bf16[256,1152]{1,0:T(8,128)(2,1)S(1)} %collective-permute-done.3.refs_5_.refs_3_), channel_id=1, source_target_pairs={{1,0},{0,1},{3,2},{2,3},{5,4},{4,5},{7,6},{6,7},{9,8},{8,9},{11,10... | collective-permute-start | bytes 1769480 | tf_op jit(solution)/shard_map/ppermute | solution.py:58
  52.6 15.3 %collective-permute-start.5 = (bf16[256,1152]{1,0:T(8,128)(2,1)S(1)}, bf16[256,1152]{1,0:T(8,128)(2,1)S(1)}, u32[]{:S(2)}, u32[]{:S(2)}) collective-permute-start(bf16[256,1152]{1,0:T(8,128)(2,1)S(1)} %collective-permute-done.1.refs_2_), channel_id=1, source_target_pairs={{8,0},{9,1},{10,2},{11,3},{12,4},{13,5},{14,6},{15,7},{0,8},{1,9},... | collective-permute-start | bytes 1769480 | tf_op jit(solution)/shard_map/ppermute | solution.py:58
  57.3 9.9 %collective-permute-start.12 = (bf16[128,1152]{1,0:T(8,128)(2,1)S(1)}, bf16[128,1152]{1,0:T(8,128)(2,1)S(1)}, u32[]{:S(2)}, u32[]{:S(2)}) collective-permute-start(bf16[128,1152]{1,0:T(8,128)(2,1)S(1)} %collective-permute-done.10.refs_4_), channel_id=1, source_target_pairs={{16,0},{17,1},{18,2},{19,3},{20,4},{21,5},{22,6},{23,7},{24,8},{25... | collective-permute-start | bytes 884744 | tf_op jit(solution)/shard_map/ppermute | solution.py:58
  60.2 11.0 %collective-permute-start.15 = (bf16[256,256]{1,0:T(8,128)(2,1)S(1)}, bf16[256,256]{1,0:T(8,128)(2,1)S(1)}, u32[]{:S(2)}, u32[]{:S(2)}) collective-permute-start(bf16[256,256]{1,0:T(8,128)(2,1)S(1)} %copy-done.1), channel_id=1, source_target_pairs={{16,0},{17,1},{18,2},{19,3},{20,4},{21,5},{22,6},{23,7},{24,8},{25... | collective-permute-start | bytes 393224 | tf_op jit(solution)/shard_map/ppermute | solution.py:58
  67.2 7.4 %collective-permute-start.11 = (bf16[128,1152]{1,0:T(8,128)(2,1)S(1)}, bf16[128,1152]{1,0:T(8,128)(2,1)S(1)}, u32[]{:S(2)}, u32[]{:S(2)}) collective-permute-start(bf16[128,1152]{1,0:T(8,128)(2,1)S(1)} %collective-permute-done.10.refs_4_), channel_id=1, source_target_pairs={{1,0},{0,1},{3,2},{2,3},{5,4},{4,5},{7,6},{6,7},{9,8},{8,9},{11,10... | collective-permute-start | bytes 884744 | tf_op jit(solution)/shard_map/ppermute | solution.py:58
  68.0 6.7 %collective-permute-start.13 = (bf16[128,1152]{1,0:T(8,128)(2,1)S(1)}, bf16[128,1152]{1,0:T(8,128)(2,1)S(1)}, u32[]{:S(2)}, u32[]{:S(2)}) collective-permute-start(bf16[128,1152]{1,0:T(8,128)(2,1)S(1)} %collective-permute-done.12.refs_6_), channel_id=1, source_target_pairs={{1,0},{0,1},{3,2},{2,3},{5,4},{4,5},{7,6},{6,7},{9,8},{8,9},{11,10... | collective-permute-start | bytes 884744 | tf_op jit(solution)/shard_map/ppermute | solution.py:58
  78.6 7.5 %collective-permute-start.23 = (bf16[272,256]{1,0:T(8,128)(2,1)S(1)}, bf16[272,256]{1,0:T(8,128)(2,1)S(1)}, u32[]{:S(2)}, u32[]{:S(2)}) collective-permute-start(bf16[272,256]{1,0:T(8,128)(2,1)S(1)} %get-tuple-element.37), channel_id=1, source_target_pairs={{10,0},{11,1},{8,2},{9,3},{14,4},{15,5},{12,6},{13,7},{2,8},{3,9},... | collective-permute-start | bytes 417800 | tf_op jit(solution)/shard_map/ppermute | solution.py:58
  78.7 9.0 %collective-permute-start.22 = (bf16[272,256]{1,0:T(8,128)(2,1)S(1)}, bf16[272,256]{1,0:T(8,128)(2,1)S(1)}, u32[]{:S(2)}, u32[]{:S(2)}) collective-permute-start(bf16[272,256]{1,0:T(8,128)(2,1)S(1)} %get-tuple-element.36), channel_id=1, source_target_pairs={{2,0},{3,1},{0,2},{1,3},{6,4},{7,5},{4,6},{5,7},{10,8},{11,9},{8,1... | collective-permute-start | bytes 417800 | tf_op jit(solution)/shard_map/ppermute | solution.py:58
  80.7 7.9 %collective-permute-start.21 = (bf16[272,256]{1,0:T(8,128)(2,1)S(1)}, bf16[272,256]{1,0:T(8,128)(2,1)S(1)}, u32[]{:S(2)}, u32[]{:S(2)}) collective-permute-start(bf16[272,256]{1,0:T(8,128)(2,1)S(1)} %get-tuple-element.35), channel_id=1, source_target_pairs={{8,0},{9,1},{10,2},{11,3},{12,4},{13,5},{14,6},{15,7},{0,8},{1,9},... | collective-permute-start | bytes 417800 | tf_op jit(solution)/shard_map/ppermute | solution.py:58
  88.7 8.0 %collective-permute-start.27 = (bf16[256,256]{1,0:T(8,128)(2,1)S(1)}, bf16[256,256]{1,0:T(8,128)(2,1)S(1)}, u32[]{:S(2)}, u32[]{:S(2)}) collective-permute-start(bf16[256,256]{1,0:T(8,128)(2,1)S(1)} %add_convert_fusion.refs_4_), channel_id=1, source_target_pairs={{4,0},{5,1},{6,2},{7,3},{0,4},{1,5},{2,6},{3,7},{12,8},{13,9},{14,... | collective-permute-start | bytes 393224 | tf_op jit(solution)/shard_map/ppermute | solution.py:58
  88.8 8.7 %collective-permute-start.25 = (bf16[256,256]{1,0:T(8,128)(2,1)S(1)}, bf16[256,256]{1,0:T(8,128)(2,1)S(1)}, u32[]{:S(2)}, u32[]{:S(2)}) collective-permute-start(bf16[256,256]{1,0:T(8,128)(2,1)S(1)} %add_convert_fusion.refs_4_), channel_id=1, source_target_pairs={{16,0},{17,1},{18,2},{19,3},{20,4},{21,5},{22,6},{23,7},{24,8},{25... | collective-permute-start | bytes 393224 | tf_op jit(solution)/shard_map/ppermute | solution.py:58
  89.7 14.3 %collective-permute-start.24 = (bf16[256,256]{1,0:T(8,128)(2,1)S(1)}, bf16[256,256]{1,0:T(8,128)(2,1)S(1)}, u32[]{:S(2)}, u32[]{:S(2)}) collective-permute-start(bf16[256,256]{1,0:T(8,128)(2,1)S(1)} %add_convert_fusion.refs_4_), channel_id=1, source_target_pairs={{1,0},{0,1},{3,2},{2,3},{5,4},{4,5},{7,6},{6,7},{9,8},{8,9},{11,10... | collective-permute-start | bytes 393224 | tf_op jit(solution)/shard_map/ppermute | solution.py:58
  105.3 7.3 %collective-permute-start.33 = (bf16[256,256]{1,0:T(8,128)(2,1)S(1)}, bf16[256,256]{1,0:T(8,128)(2,1)S(1)}, u32[]{:S(2)}, u32[]{:S(2)}) collective-permute-start(bf16[256,256]{1,0:T(8,128)(2,1)S(1)} %get-tuple-element.42), channel_id=1, source_target_pairs={{10,0},{11,1},{8,2},{9,3},{14,4},{15,5},{12,6},{13,7},{2,8},{3,9},... | collective-permute-start | bytes 393224 | tf_op jit(solution)/shard_map/ppermute | solution.py:58
  105.4 9.3 %collective-permute-start.32 = (bf16[256,256]{1,0:T(8,128)(2,1)S(1)}, bf16[256,256]{1,0:T(8,128)(2,1)S(1)}, u32[]{:S(2)}, u32[]{:S(2)}) collective-permute-start(bf16[256,256]{1,0:T(8,128)(2,1)S(1)} %get-tuple-element.41), channel_id=1, source_target_pairs={{2,0},{3,1},{0,2},{1,3},{6,4},{7,5},{4,6},{5,7},{10,8},{11,9},{8,1... | collective-permute-start | bytes 393224 | tf_op jit(solution)/shard_map/ppermute | solution.py:58
  (13 other events, 150.2 us)

commit v3 on v2

v3 whole, which is shorter than its diff:
```python
import functools
import math

import jax
import jax.numpy as jnp
from jax import lax
from jax.experimental import pallas as pl
from jax.experimental.pallas import tpu as pltpu
from jax.sharding import PartitionSpec as P

BLOCK = 128
AXES = ("row", "col")

sharpness = 30.0
mixing = 0.8
epsilon = 1e-06


def split_two(n):
    low = max(d for d in range(1, math.isqrt(n) + 1) if n % d == 0)
    return n // low, low


class Layout:
    def __init__(self, rows, cols):
        core = 2 if cols % 2 == 0 else 1
        ny, nx = split_two(rows)
        nzh, nzl = split_two(cols // core)
        self.sizes = dict(y=ny, x=nx, zh=nzh, zl=nzl, core=core)
        self.rows, self.cols = rows, cols

    def coords(self, row, col):
        s = self.sizes
        return dict(
            y=row // s["x"],
            x=row % s["x"],
            zh=col // (s["zl"] * s["core"]),
            zl=col // s["core"] % s["zl"],
            core=col % s["core"],
        )

    def moved(self, at, offset):
        return {k: (at[k] + offset.get(k, 0)) % self.sizes[k] for k in at}

    def row_col(self, at):
        s = self.sizes
        return at["y"] * s["x"] + at["x"], (at["zh"] * s["zl"] + at["zl"]) * s["core"] + at["core"]

    def fetch(self, value, **offset):
        if all(v % self.sizes[k] == 0 for k, v in offset.items()):
            return value
        pairs = []
        for row in range(self.rows):
            for col in range(self.cols):
                r, c = self.row_col(self.moved(self.coords(row, col), offset))
                pairs.append((r * self.cols + c, row * self.cols + col))
        return lax.ppermute(value, AXES, pairs)

    def device(self, offset):
        at = self.coords(lax.axis_index("row"), lax.axis_index("col"))
        row, col = self.row_col(self.moved(at, offset))
        return col * self.rows + row


VMEM = pl.BlockSpec(memory_space=pltpu.VMEM)


def limits(mib=32):
    return pltpu.CompilerParams(vmem_limit_bytes=mib * 2**20)


def unit_kernel(t_chunks, s_chunks, emb_ref, seed_ref, *outs):
    values = emb_ref[...].astype(jnp.float32)
    d = values.shape[1]
    mean_square = jnp.mean(values * values, axis=1, keepdims=True)
    scaled = values * lax.rsqrt(mean_square + epsilon) * d ** (-0.5)
    unit = scaled.astype(jnp.bfloat16)
    outs[0][...] = unit
    outs[1][:, :d] = unit
    outs[1][:, d:] = seed_ref[...]
    for out, (start, rows) in zip(outs[2:], t_chunks + s_chunks):
        out[...] = unit[start : start + rows]


def unit_rows(embeddings, seeds, t_chunks, s_chunks):
    m, d = embeddings.shape
    shapes = [(m, d), (m, d + seeds.shape[1])] + [(rows, d) for _, rows in t_chunks + s_chunks]
    got = pl.pallas_call(
        functools.partial(unit_kernel, t_chunks, s_chunks),
        out_shape=[jax.ShapeDtypeStruct(s, jnp.bfloat16) for s in shapes],
        in_specs=[VMEM] * 2,
        out_specs=[VMEM] * len(shapes),
        compiler_params=limits(),
    )(embeddings, seeds)
    return got[0], got[1], got[2 : 2 + len(t_chunks)], got[2 + len(t_chunks) :]


def gram_kernel(nt, ns, sub, d, flags, *refs):
    t_in, s_in, (kern, acc), scratch = refs[:nt], refs[nt : nt + ns], refs[nt + ns : nt + ns + 2], refs[nt + ns + 2 :]
    if scratch:
        at = 0
        for ref in s_in:
            scratch[0][at : at + ref.shape[0], :] = ref[:, :d]
            at += ref.shape[0]
        width = 2 * BLOCK if at % (2 * BLOCK) == 0 else BLOCK if at % BLOCK == 0 else at
        tiles = [(scratch[0], k, width) for k in range(0, at, width)]
    else:
        tiles = [(ref, 0, ref.shape[0]) for ref in s_in]
    col = 0
    for s_ref, s_at, width in tiles:
        row = 0
        for i in range(nt):
            height = t_in[i].shape[0]
            scores = lax.dot_general(
                t_in[i][...],
                s_ref[s_at : s_at + width, :d],
                (((1,), (1,)), ((), ())),
                preferred_element_type=jnp.float32,
            )
            value = jnp.exp(sharpness * scores).astype(jnp.bfloat16).astype(jnp.float32)
            for a in range(height // sub):
                at = row + a * sub
                flag = flags[at // sub : at // sub + 1, col : col + width]
                part = jnp.where(flag > 0, value[a * sub : (a + 1) * sub], 0.0)
                kern[at : at + sub, col : col + width] = part.astype(jnp.bfloat16)
                total = part[:, :BLOCK]
                for b in range(1, width // BLOCK):
                    total = total + part[:, b * BLOCK : (b + 1) * BLOCK]
                if col > 0:
                    total = total + acc[at : at + sub, :]
                acc[at : at + sub, :] = total
            row += height
        col += width


def gram_call(flags, t_pieces, s_pieces, sub):
    rows, cols = (sum(p.shape[0] for p in pieces) for pieces in (t_pieces, s_pieces))
    d = t_pieces[0].shape[1]
    direct = all(p.shape[0] == 2 * BLOCK for p in s_pieces)
    return pl.pallas_call(
        functools.partial(gram_kernel, len(t_pieces), len(s_pieces), sub, d),
        out_shape=[
            jax.ShapeDtypeStruct((rows, cols), jnp.bfloat16),
            jax.ShapeDtypeStruct((rows, BLOCK), jnp.float32),
        ],
        in_specs=[VMEM] * (1 + len(t_pieces) + len(s_pieces)),
        out_specs=[VMEM] * 2,
        scratch_shapes=[] if direct else [pltpu.VMEM((cols, d), jnp.bfloat16)],
        compiler_params=limits(),
        cost_estimate=pl.CostEstimate(
            flops=2 * rows * cols * d,
            bytes_accessed=2 * (rows + cols) * d,
            transcendentals=rows * cols,
        ),
    )(flags, *t_pieces, *s_pieces)


def spread_kernel(plan, nk, na, ns, *refs):
    m, t_layout, rects, p_map = plan
    kerns, refs = refs[:nk], refs[nk:]
    accs, refs = refs[:na], refs[na:]
    p_in, refs = refs[:ns], refs[ns:]
    outs, pcat = refs[:-1], refs[-1]
    own_ref, other_refs = outs[0], outs[2:] if na else outs[1:]
    c = pcat.shape[1]
    at = 0
    for index, start, rows in p_map:
        ref = p_in[index]
        pcat[at : at + rows, :] = ref[start : start + rows, ref.shape[1] - c :]
        at += rows
    row = 0
    for piece, start, rows in t_layout:
        part = None
        for kern, (t0, t1, c0, c1) in zip(kerns, rects):
            if t0 <= row < t1:
                term = jnp.dot(
                    kern[row - t0 : row - t0 + rows, :],
                    pcat[c0:c1, :],
                    preferred_element_type=jnp.float32,
                )
                part = term if part is None else part + term
        if piece == 0:
            own_ref[start : start + rows, :] = part
        else:
            other_refs[piece - 1][start : start + rows, :] = part.astype(jnp.bfloat16)
        step = min(rows, BLOCK)
        for lane in range(0, rows if na else 0, step):
            total = None
            for acc, (t0, t1, c0, c1) in zip(accs, rects):
                if t0 <= row < t1:
                    first = row - t0 + lane
                    term = acc[first : first + step, :]
                    total = term if total is None else total + term
            total = jnp.sum(total.T, axis=0, keepdims=True)
            lanes = slice(start + lane, start + lane + step)
            if piece == 0:
                outs[1][:, lanes] = total
            else:
                high = total.astype(jnp.bfloat16).astype(jnp.float32)
                mid = (total - high).astype(jnp.bfloat16).astype(jnp.float32)
                low = total - high - mid
                index = lax.broadcasted_iota(jnp.int32, (16, step), 0)
                terms = jnp.where(index == 0, high, jnp.where(index == 1, mid, low))
                terms = jnp.where(index < 3, terms, 0.0)
                other_refs[piece - 1][m:, lanes] = terms.astype(jnp.bfloat16)
        row += rows


def spread_call(kerns, accs, p_pieces, c, plan):
    m, t_layout, rects, p_map = plan
    nt = 1 + max(piece for piece, _, _ in t_layout)
    cols = sum(rows for _, _, rows in p_map)
    extra = 16 if accs else 0
    outs = [jax.ShapeDtypeStruct((m, c), jnp.float32)]
    if accs:
        outs.append(jax.ShapeDtypeStruct((1, m), jnp.float32))
    outs += [jax.ShapeDtypeStruct((m + extra, c), jnp.bfloat16)] * (nt - 1)
    return pl.pallas_call(
        functools.partial(spread_kernel, plan, len(kerns), len(accs), len(p_pieces)),
        out_shape=outs,
        in_specs=[VMEM] * (len(kerns) + len(accs) + len(p_pieces)),
        out_specs=[VMEM] * len(outs),
        scratch_shapes=[pltpu.VMEM((cols, c), jnp.bfloat16)],
        compiler_params=limits(),
        cost_estimate=pl.CostEstimate(
            flops=2 * nt * m * cols * c,
            bytes_accessed=2 * (nt * m * cols + cols * c),
            transcendentals=0,
        ),
    )(*kerns, *accs, *p_pieces)


def first_update_kernel(seed_ref, own_ref, own_total_ref, *refs):
    got, (panel_ref, total_ref) = refs[:-2], refs[-2:]
    m = seed_ref.shape[0]
    numerators = own_ref[...]
    for ref in got:
        numerators = numerators + ref[:m, :].astype(jnp.float32)
    totals = own_total_ref[...]
    for ref in got:
        terms = ref[m:, :m].astype(jnp.float32)
        totals = totals + jnp.sum(terms, axis=0, keepdims=True)
    step = min(m, BLOCK)
    for k in range(0, m, step):
        total_ref[k : k + step, :] = jnp.broadcast_to(totals[:, k : k + step], (BLOCK, step)).T
    for k in range(0, seed_ref.shape[1], BLOCK):
        labels = mixing * numerators[:, k : k + BLOCK] / total_ref[...] + (
            1.0 - mixing
        ) * seed_ref[:, k : k + BLOCK].astype(jnp.float32)
        panel_ref[:, k : k + BLOCK] = labels.astype(jnp.bfloat16)


def last_update_kernel(seed_ref, own_ref, total_ref, *refs):
    got, out_ref = refs[:-1], refs[-1]
    numerators = own_ref[...]
    for ref in got:
        numerators = numerators + ref[...].astype(jnp.float32)
    for k in range(0, seed_ref.shape[1], BLOCK):
        out_ref[:, k : k + BLOCK] = mixing * numerators[:, k : k + BLOCK] / total_ref[...] + (
            1.0 - mixing
        ) * seed_ref[:, k : k + BLOCK].astype(jnp.float32)


def update(kernel, seeds, own, totals, got, out_shape):
    return pl.pallas_call(
        kernel,
        out_shape=out_shape,
        in_specs=[VMEM] * (3 + len(got)),
        out_specs=jax.tree.map(lambda _: VMEM, out_shape),
        compiler_params=limits(),
    )(seeds, own, totals, *got)


def after(value, *earlier):
    return lax.optimization_barrier((value, *earlier))[0]


def on_device(embeddings, seed_labels, pattern):
    layout = Layout(lax.axis_size("row"), lax.axis_size("col"))
    size = layout.sizes
    m, c = embeddings.shape[0], seed_labels.shape[1]
    sub = min(m, BLOCK)
    fetch = layout.fetch
    cores, ys = range(size["core"]), range(size["y"])
    chunked = m % (2 * BLOCK) == 0
    t_chunks = [(0, m // 2), (m // 2, m // 2)] if chunked else [(0, m)]
    s_chunks = [(0, 3 * m // 4), (3 * m // 4, m // 4)] if chunked else [(0, m)]

    t_index = {(b, a): b * size["x"] + a for b in range(size["zl"]) for a in range(size["x"])}
    t_layout = [(t_index[0, a], 0, m) for a in range(size["x"])]
    ends = [size["x"] * m]
    for start, rows in t_chunks:
        for a in range(size["x"]):
            t_layout += [(t_index[b, a], start, rows) for b in range(1, size["zl"])]
            ends.append(ends[-1] + (size["zl"] - 1) * rows)
    near = [dict(y=a, core=k) for a in ys for k in cores]
    far = [dict(zh=b, y=a, core=k) for b in range(1, size["zh"]) for a in ys for k in cores]
    s_layout = [(i, o, 0, m) for i, o in enumerate(near)]
    columns = [len(near) * m]
    for start, rows in s_chunks:
        s_layout += [(len(near) + i, o, start, rows) for i, o in enumerate(far)]
        columns.append(columns[-1] + len(far) * rows)
    p_map = [(i, start, rows) for i, _, start, rows in s_layout]

    t_offsets = [dict(zl=b, x=a) for b, a in t_index]
    t_blocks = jnp.concatenate(
        [
            (layout.device(t_offsets[i]) * m + start + jnp.arange(0, rows, sub)) // BLOCK
            for i, start, rows in t_layout
        ]
    )
    s_blocks = jnp.concatenate(
        [(layout.device(o) * m + start + jnp.arange(rows)) // BLOCK for _, o, start, rows in s_layout]
    )
    flags = jnp.any(pattern[t_blocks][:, :, None] == s_blocks[None, None, :], axis=1)
    flags = flags.astype(jnp.int32)

    units, packed, t_parts, s_parts = unit_rows(embeddings, seed_labels, t_chunks, s_chunks)

    def cored(value):
        return [fetch(value, core=k) for k in cores]

    by_x = [fetch(units, x=a) for a in range(size["x"])]
    by_y = [fetch(packed, y=a) for a in ys]
    t_pieces, held = list(by_x), ()
    for part in t_parts:
        by_zl = [fetch(after(part, *held), zl=b) for b in range(1, size["zl"])]
        held = by_zl
        t_pieces += [fetch(v, x=a) for a in range(size["x"]) for v in by_zl]
    s_near = cored(after(packed, *by_y[1:])) + [p for v in by_y[1:] for p in cored(v)]
    by_zh, held = [], ()
    for part in s_parts:
        by_zh.append([fetch(after(part, *held), zh=b) for b in range(1, size["zh"])])
        held = by_zh[-1] + by_x[1:] + by_y[1:]
    s_far = []

    def near_panels(panel):
        return [p for a in ys for p in cored(fetch(panel, y=a))]

    def far_panels(panel):
        by_zh = [fetch(panel, zh=b) for b in range(1, size["zh"])]
        return [p for v in by_zh for a in ys for p in cored(fetch(v, y=a))]

    t_ends = [ends[1], ends[2], ends[-1]] if chunked and size["x"] == 2 else [ends[-1]]
    kerns, accs, rects = [], [], []

    def rectangle(t0, t1, g):
        row, pieces = 0, []
        for piece, (_, _, rows) in zip(t_pieces, t_layout):
            if t0 <= row < t1:
                pieces.append(piece)
            row += rows
        c0, c1 = ([0] + columns)[g : g + 2]
        kern, acc = gram_call(
            flags[t0 // sub : t1 // sub, c0:c1], pieces, ([s_near] + s_far)[g], sub
        )
        kerns.append(kern)
        accs.append(acc)
        rects.append((t0, t1, c0, c1))

    def onward(g, *earlier):
        values = [after(v, *earlier) for v in by_zh[g]]
        s_far.append([p for v in values for a in ys for p in cored(fetch(v, y=a))])

    if len(t_ends) == 3 and far:
        onward(0)
        rectangle(0, t_ends[0], 0)
        onward(1, accs[0])
        rectangle(t_ends[0], t_ends[1], 0)
        rectangle(0, t_ends[1], 1)
        rectangle(t_ends[1], t_ends[2], 0)
        rectangle(t_ends[1], t_ends[2], 1)
        rectangle(0, t_ends[2], 2)
    else:
        for g in range(len(s_chunks) if far else 0):
            onward(g)
        for g in range(1 + len(s_far)):
            rectangle(0, ends[-1], g)
    plan = (m, t_layout, rects, p_map)

    def home(values):
        return [fetch(v, **{k: -d for k, d in o.items()}) for v, o in zip(values, t_offsets[1:])]

    seeds = s_near + far_panels(after(seed_labels, *held))
    own, totals, *others = spread_call(kerns, accs, seeds, c, plan)
    panel, totals = update(
        first_update_kernel,
        seed_labels,
        own,
        totals,
        home(others),
        [
            jax.ShapeDtypeStruct((m, c), jnp.bfloat16),
            jax.ShapeDtypeStruct((m, BLOCK), jnp.float32),
        ],
    )
    own, *others = spread_call(kerns, [], near_panels(panel) + far_panels(panel), c, plan)
    return update(
        last_update_kernel,
        seed_labels,
        own,
        totals,
        home(others),
        jax.ShapeDtypeStruct((m, c), jnp.float32),
    )


def solution(mesh):
    return jax.shard_map(
        on_device,
        mesh=mesh,
        in_specs=(P(("col", "row"), None), P(("col", "row"), None), P()),
        out_specs=P(("col", "row"), None),
        check_vma=False,
    )
```

time: 116 us -> 113 us (0.974)
  waiting for transfers between devices: 69.5 us -> 53.2 us
  Pallas kernels: 13.3 us -> 20.4 us
  local copies, waits for them, and re-layouts: 2.07 us -> 5.83 us
  starting transfers between devices: 28.5 us -> 31.9 us
    ppermute x34 -> x33, waiting for transfers between devices: 69.5 us -> 53.2 us  [fetch(): return lax.ppermute(value, AXES, pairs)]
    pallas_call x4 -> x6, Pallas kernels: 8.6 us -> 15.6 us  [gram_call(): pl.pallas_call(functools.partial(gram_kernel, len(t_pieces), len(s_pieces...]
    unnamed x7 -> x17, local copies, waits for them, and re-layouts: 0.09 us -> 4.4 us
    ppermute x34 -> x33, starting transfers between devices: 28.5 us -> 31.9 us  [fetch(): return lax.ppermute(value, AXES, pairs)]
    slice x12 -> x6, local copies, waits for them, and re-layouts: 1.19 us -> 0.03 us  [rectangle(): flags[t0 // sub:t1 // sub, c0:c1]]
    pallas_call x3 -> x5, Pallas kernels: 4.72 us -> 4.8 us  [the longest x2 2.55 us: spread_call(): pl.pallas_call(functools.partial(spread_kernel, plan, len(kerns), len(acc...]
  transfers between devices with their start and end apart: 34 -> 33, of which waited for: 16 -> 14; matrix products, arithmetic and copies ran while one was open for 2% -> 3% of each run, Pallas kernels for 7% -> 14%
where the time goes in v3:
time: 113 us
  waiting for transfers between devices  53.2 us (47%)
  starting transfers between devices  31.9 us (28%)
  Pallas kernels  20.4 us (18%)
  local copies, waits for them, and re-layouts  5.83 us (5%)
  other arithmetic  1.41 us (1%)
    ppermute x33, waiting for transfers between devices, fetch(): return lax.ppermute(value, AXES, pairs)  53.2 us
    ppermute x33, starting transfers between devices, fetch(): return lax.ppermute(value, AXES, pairs)  31.9 us
    pallas_call x6, Pallas kernels, gram_call(): pl.pallas_call(functools.partial(gram_kernel, len(t_pieces), len(s_pieces...  15.6 us
    unnamed x17, local copies, waits for them, and re-layouts  4.4 us
    pallas_call x2, Pallas kernels, spread_call(): pl.pallas_call(functools.partial(spread_kernel, plan, len(kerns), len(acc...  2.55 us
  transfers between devices with their start and end apart: 33, of which 14 were waited for; matrix products, arithmetic and copies ran while one was open for 3% of the time, Pallas kernels for 14%

profile of v3, /device:TPU:0, one launch (start us, length us, event | category | flops | bytes accessed | tf_op | source)
XLA Modules:
  0.0 113.1 jit_solution(16979783750809524696)
XLA Ops:
  3.9 3.0 %collective-permute-start.2 = (bf16[256,1408]{1,0:T(8,128)(2,1)S(1)}, bf16[256,1408]{1,0:T(8,128)(2,1)S(1)}, u32[]{:S(2)}, u32[]{:S(2)}) collective-permute-start(bf16[256,1408]{1,0:T(8,128)(2,1)S(1)} %get-tuple-element.42.refs_3_.refs_1_.refs_2_.refs_12_), channel_id=1, source_target_pairs={{16,0},{17,1},{18,2},{19,3},{20,4},{21,5},{22,6},{23,7},{24,8},{25... | collective-permute-start | bytes 2162696 | tf_op jit(solution)/shard_map/ppermute | solution.py:57
  8.4 1.6 %collective-permute-start.1 = (bf16[128,1152]{1,0:T(8,128)(2,1)}, bf16[128,1152]{1,0:T(8,128)(2,1)S(1)}, u32[]{:S(2)}, u32[]{:S(2)}) collective-permute-start(bf16[128,1152]{1,0:T(8,128)(2,1)} %get-tuple-element.40), channel_id=1, source_target_pairs={{2,0},{3,1},{0,2},{1,3},{6,4},{7,5},{4,6},{5,7},{10,8},{11,9},{8,1... | collective-permute-start | bytes 884744 | tf_op jit(solution)/shard_map/ppermute | solution.py:57
  10.0 2.6 %collective-permute-start.6 = (bf16[192,1152]{1,0:T(8,128)(2,1)}, bf16[192,1152]{1,0:T(8,128)(2,1)}, u32[]{:S(2)}, u32[]{:S(2)}) collective-permute-start(bf16[192,1152]{1,0:T(8,128)(2,1)} %get-tuple-element.45), channel_id=1, source_target_pairs={{4,0},{5,1},{6,2},{7,3},{0,4},{1,5},{2,6},{3,7},{12,8},{13,9},{14,... | collective-permute-start | bytes 1327112 | tf_op jit(solution)/shard_map/ppermute | solution.py:57
  12.7 10.3 %collective-permute-done.2.refs_5_.refs_3_.refs_4_.refs_14_ = bf16[256,1408]{1,0:T(8,128)(2,1)S(1)} collective-permute-done((bf16[256,1408]{1,0:T(8,128)(2,1)S(1)}, bf16[256,1408]{1,0:T(8,128)(2,1)S(1)}, u32[]{:S(2)}, u32[]{:S(2)}) %collective-permute-start.2) | collective-permute-done | bytes 720928 | tf_op jit(solution)/shard_map/ppermute | solution.py:57
  23.6 8.2 %collective-permute-done.6.refs_4_.refs_2_ = bf16[192,1152]{1,0:T(8,128)(2,1)} collective-permute-done((bf16[192,1152]{1,0:T(8,128)(2,1)}, bf16[192,1152]{1,0:T(8,128)(2,1)}, u32[]{:S(2)}, u32[]{:S(2)}) %collective-permute-start.6) | collective-permute-done | bytes 442400 | tf_op jit(solution)/shard_map/ppermute | solution.py:57
  33.1 3.1 %collective-permute-start.12 = (bf16[64,1152]{1,0:T(8,128)(2,1)}, bf16[64,1152]{1,0:T(8,128)(2,1)}, u32[]{:S(2)}, u32[]{:S(2)}) collective-permute-start(bf16[64,1152]{1,0:T(8,128)(2,1)} %copy-done.6), channel_id=1, source_target_pairs={{4,0},{5,1},{6,2},{7,3},{0,4},{1,5},{2,6},{3,7},{12,8},{13,9},{14,... | collective-permute-start | bytes 442376 | tf_op jit(solution)/shard_map/ppermute | solution.py:57
  36.7 6.3 %collective-permute-done.10.refs_0_.refs_4_ = bf16[128,1152]{1,0:T(8,128)(2,1)S(1)} collective-permute-done((bf16[128,1152]{1,0:T(8,128)(2,1)S(1)}, bf16[128,1152]{1,0:T(8,128)(2,1)S(1)}, u32[]{:S(2)}, u32[]{:S(2)}) %collective-permute-start.10) | collective-permute-done | bytes 294944 | tf_op jit(solution)/shard_map/ppermute | solution.py:57
  49.3 3.6 %shard_map.38 = (bf16[640,1024]{1,0:T(8,128)(2,1)S(1)}, f32[640,128]{1,0:T(8,128)S(1)}) custom-call(s32[5,1024]{1,0:T(8,128)S(1)} %slice.26.flags, bf16[256,1152]{1,0:T(8,128)(2,1)} %get-tuple-element.39.refs_0_, bf16[256,1152]{1,0:T(8,128)(2,1)} %collective-permute-done.refs_1_, bf16[128,1152]{1,0:T(8,128)(2,1)S(1)} %copy-done.4, ...), custom_call_target="tpu_custom_call" | custom-call | flops 1509949440 | bytes 3833856 | tf_op jit(solution)/shard_map/pallas_call | solution.py:140
  52.9 1.6 %collective-permute-start.14 = (bf16[64,1152]{1,0:T(8,128)(2,1)}, bf16[64,1152]{1,0:T(8,128)(2,1)S(1)}, u32[]{:S(2)}, u32[]{:S(2)}) collective-permute-start(bf16[64,1152]{1,0:T(8,128)(2,1)} %collective-permute-done.12.refs_6_), channel_id=1, source_target_pairs={{16,0},{17,1},{18,2},{19,3},{20,4},{21,5},{22,6},{23,7},{24,8},{25... | collective-permute-start | bytes 442376 | tf_op jit(solution)/shard_map/ppermute | solution.py:57
  54.5 2.2 %collective-permute-done.16.refs_16_ = bf16[256,256]{1,0:T(8,128)(2,1)S(1)} collective-permute-done((bf16[256,256]{1,0:T(8,128)(2,1)}, bf16[256,256]{1,0:T(8,128)(2,1)S(1)}, u32[]{:S(2)}, u32[]{:S(2)}) %collective-permute-start.16) | collective-permute-done | bytes 131104 | tf_op jit(solution)/shard_map/ppermute | solution.py:57
  58.4 3.8 %collective-permute-done.18.refs_18_ = bf16[256,256]{1,0:T(8,128)(2,1)S(1)} collective-permute-done((bf16[256,256]{1,0:T(8,128)(2,1)S(1)}, bf16[256,256]{1,0:T(8,128)(2,1)S(1)}, u32[]{:S(2)}, u32[]{:S(2)}) %collective-permute-start.18) | collective-permute-done | bytes 131104 | tf_op jit(solution)/shard_map/ppermute | solution.py:57
  62.8 4.1 %shard_map.40 = (bf16[768,768]{1,0:T(8,128)(2,1)S(1)}, f32[768,128]{1,0:T(8,128)S(1)}) custom-call(s32[6,768]{1,0:T(8,128)S(1)} %slice.28.flags, bf16[256,1152]{1,0:T(8,128)(2,1)} %get-tuple-element.39.refs_0_, bf16[256,1152]{1,0:T(8,128)(2,1)} %collective-permute-done.refs_1_, bf16[128,1152]{1,0:T(8,128)(2,1)S(1)} %copy-done.5, ...), custom_call_target="tpu_custom_call" | custom-call | flops 1358954496 | bytes 3538944 | tf_op jit(solution)/shard_map/pallas_call | solution.py:140
  66.9 2.7 %shard_map.42 = (bf16[256,768]{1,0:T(8,128)(2,1)S(1)}, f32[256,128]{1,0:T(8,128)S(1)}) custom-call(s32[2,768]{1,0:T(2,128)S(1)} %slice.30.flags, bf16[128,1152]{1,0:T(8,128)(2,1)S(1)} %collective-permute-done.10.refs_0_.refs_4_, bf16[128,1152]{1,0:T(8,128)(2,1)S(1)} %collective-permute-done.11.refs_1_.refs_5_, ...), custom_call_target="tpu_custom_call" | custom-call | flops 452984832 | bytes 2359296 | tf_op jit(solution)/shard_map/pallas_call | solution.py:140
  70.6 1.7 %shard_map.41 = (bf16[256,1024]{1,0:T(8,128)(2,1)S(1)}, f32[256,128]{1,0:T(8,128)S(1)}) custom-call(s32[2,1024]{1,0:T(2,128)S(1)} %slice.29.flags, bf16[128,1152]{1,0:T(8,128)(2,1)S(1)} %collective-permute-done.10.refs_0_.refs_4_, bf16[128,1152]{1,0:T(8,128)(2,1)S(1)} %collective-permute-done.11.refs_1_.refs_5_, ...), custom_call_target="tpu_custom_call" | custom-call | flops 603979776 | bytes 2949120 | tf_op jit(solution)/shard_map/pallas_call | solution.py:140
  72.3 2.5 %shard_map.43 = (bf16[1024,256]{1,0:T(8,128)(2,1)S(1)}, f32[1024,128]{1,0:T(8,128)S(1)}) custom-call(s32[8,256]{1,0:T(8,128)S(1)} %slice.31.flags, bf16[256,1152]{1,0:T(8,128)(2,1)} %get-tuple-element.39.refs_0_, bf16[256,1152]{1,0:T(8,128)(2,1)} %collective-permute-done.refs_1_, bf16[128,1152]{1,0:T(8,128)(2,1)S(1)} %copy-done.5, ...), custom_call_target="tpu_custom_call" | custom-call | flops 603979776 | bytes 2949120 | tf_op jit(solution)/shard_map/pallas_call | solution.py:140
  76.7 1.7 %collective-permute-start.21 = (bf16[272,256]{1,0:T(8,128)(2,1)S(1)}, bf16[272,256]{1,0:T(8,128)(2,1)S(1)}, u32[]{:S(2)}, u32[]{:S(2)}) collective-permute-start(bf16[272,256]{1,0:T(8,128)(2,1)S(1)} %get-tuple-element.65), channel_id=1, source_target_pairs={{2,0},{3,1},{0,2},{1,3},{6,4},{7,5},{4,6},{5,7},{10,8},{11,9},{8,1... | collective-permute-start | bytes 417800 | tf_op jit(solution)/shard_map/ppermute | solution.py:57
  79.7 2.5 %collective-permute-done.20.refs_0_ = bf16[272,256]{1,0:T(8,128)(2,1)S(1)} collective-permute-done((bf16[272,256]{1,0:T(8,128)(2,1)S(1)}, bf16[272,256]{1,0:T(8,128)(2,1)S(1)}, u32[]{:S(2)}, u32[]{:S(2)}) %collective-permute-start.20) | collective-permute-done | bytes 139296 | tf_op jit(solution)/shard_map/ppermute | solution.py:57
  83.0 3.4 %collective-permute-done.22.refs_2_ = bf16[272,256]{1,0:T(8,128)(2,1)S(1)} collective-permute-done((bf16[272,256]{1,0:T(8,128)(2,1)S(1)}, bf16[272,256]{1,0:T(8,128)(2,1)S(1)}, u32[]{:S(2)}, u32[]{:S(2)}) %collective-permute-start.22) | collective-permute-done | bytes 139296 | tf_op jit(solution)/shard_map/ppermute | solution.py:57
  86.6 1.6 %collective-permute-start.26 = (bf16[256,256]{1,0:T(8,128)(2,1)S(1)}, bf16[256,256]{1,0:T(8,128)(2,1)S(1)}, u32[]{:S(2)}, u32[]{:S(2)}) collective-permute-start(bf16[256,256]{1,0:T(8,128)(2,1)S(1)} %get-tuple-element.67.refs_6_), channel_id=1, source_target_pairs={{4,0},{5,1},{6,2},{7,3},{0,4},{1,5},{2,6},{3,7},{12,8},{13,9},{14,... | collective-permute-start | bytes 393224 | tf_op jit(solution)/shard_map/ppermute | solution.py:57
  89.6 5.4 %collective-permute-done.26.refs_10_ = bf16[256,256]{1,0:T(8,128)(2,1)S(1)} collective-permute-done((bf16[256,256]{1,0:T(8,128)(2,1)S(1)}, bf16[256,256]{1,0:T(8,128)(2,1)S(1)}, u32[]{:S(2)}, u32[]{:S(2)}) %collective-permute-start.26) | collective-permute-done | bytes 131104 | tf_op jit(solution)/shard_map/ppermute | solution.py:57
  97.1 2.9 %collective-permute-done.28.refs_12_ = bf16[256,256]{1,0:T(8,128)(2,1)S(1)} collective-permute-done((bf16[256,256]{1,0:T(8,128)(2,1)S(1)}, bf16[256,256]{1,0:T(8,128)(2,1)S(1)}, u32[]{:S(2)}, u32[]{:S(2)}) %collective-permute-start.28) | collective-permute-done | bytes 131104 | tf_op jit(solution)/shard_map/ppermute | solution.py:57
  103.4 2.8 %collective-permute-start.32 = (bf16[256,256]{1,0:T(8,128)(2,1)S(1)}, bf16[256,256]{1,0:T(8,128)(2,1)S(1)}, u32[]{:S(2)}, u32[]{:S(2)}) collective-permute-start(bf16[256,256]{1,0:T(8,128)(2,1)S(1)} %get-tuple-element.72), channel_id=1, source_target_pairs={{10,0},{11,1},{8,2},{9,3},{14,4},{15,5},{12,6},{13,7},{2,8},{3,9},... | collective-permute-start | bytes 393224 | tf_op jit(solution)/shard_map/ppermute | solution.py:57
  106.2 2.1 %collective-permute-done.30.refs_0_ = bf16[256,256]{1,0:T(8,128)(2,1)S(1)} collective-permute-done((bf16[256,256]{1,0:T(8,128)(2,1)S(1)}, bf16[256,256]{1,0:T(8,128)(2,1)S(1)}, u32[]{:S(2)}, u32[]{:S(2)}) %collective-permute-start.30) | collective-permute-done | bytes 131104 | tf_op jit(solution)/shard_map/ppermute | solution.py:57
  109.8 2.5 %collective-permute-done.32.refs_2_ = bf16[256,256]{1,0:T(8,128)(2,1)S(1)} collective-permute-done((bf16[256,256]{1,0:T(8,128)(2,1)S(1)}, bf16[256,256]{1,0:T(8,128)(2,1)S(1)}, u32[]{:S(2)}, u32[]{:S(2)}) %collective-permute-start.32) | collective-permute-done | bytes 131104 | tf_op jit(solution)/shard_map/ppermute | solution.py:57
  (90 shorter events, 30.6 us)
Async XLA Ops:
  3.9 19.1 %collective-permute-start.2 = (bf16[256,1408]{1,0:T(8,128)(2,1)S(1)}, bf16[256,1408]{1,0:T(8,128)(2,1)S(1)}, u32[]{:S(2)}, u32[]{:S(2)}) collective-permute-start(bf16[256,1408]{1,0:T(8,128)(2,1)S(1)} %get-tuple-element.42.refs_3_.refs_1_.refs_2_.refs_12_), channel_id=1, source_target_pairs={{16,0},{17,1},{18,2},{19,3},{20,4},{21,5},{22,6},{23,7},{24,8},{25... | collective-permute-start | bytes 2162696 | tf_op jit(solution)/shard_map/ppermute | solution.py:57
  6.9 26.2 %collective-permute-start = (bf16[256,1152]{1,0:T(8,128)(2,1)}, bf16[256,1152]{1,0:T(8,128)(2,1)}, u32[]{:S(2)}, u32[]{:S(2)}) collective-permute-start(bf16[256,1152]{1,0:T(8,128)(2,1)} %get-tuple-element.39.refs_0_), channel_id=1, source_target_pairs={{8,0},{9,1},{10,2},{11,3},{12,4},{13,5},{14,6},{15,7},{0,8},{1,9},... | collective-permute-start | bytes 1769480 | tf_op jit(solution)/shard_map/ppermute | solution.py:57
  8.4 23.9 %collective-permute-start.1 = (bf16[128,1152]{1,0:T(8,128)(2,1)}, bf16[128,1152]{1,0:T(8,128)(2,1)S(1)}, u32[]{:S(2)}, u32[]{:S(2)}) collective-permute-start(bf16[128,1152]{1,0:T(8,128)(2,1)} %get-tuple-element.40), channel_id=1, source_target_pairs={{2,0},{3,1},{0,2},{1,3},{6,4},{7,5},{4,6},{5,7},{10,8},{11,9},{8,1... | collective-permute-start | bytes 884744 | tf_op jit(solution)/shard_map/ppermute | solution.py:57
  10.0 21.8 %collective-permute-start.6 = (bf16[192,1152]{1,0:T(8,128)(2,1)}, bf16[192,1152]{1,0:T(8,128)(2,1)}, u32[]{:S(2)}, u32[]{:S(2)}) collective-permute-start(bf16[192,1152]{1,0:T(8,128)(2,1)} %get-tuple-element.45), channel_id=1, source_target_pairs={{4,0},{5,1},{6,2},{7,3},{0,4},{1,5},{2,6},{3,7},{12,8},{13,9},{14,... | collective-permute-start | bytes 1327112 | tf_op jit(solution)/shard_map/ppermute | solution.py:57
  23.0 23.2 %collective-permute-start.3 = (bf16[256,1408]{1,0:T(8,128)(2,1)S(1)}, bf16[256,1408]{1,0:T(8,128)(2,1)S(1)}, u32[]{:S(2)}, u32[]{:S(2)}) collective-permute-start(bf16[256,1408]{1,0:T(8,128)(2,1)S(1)} %get-tuple-element.42.refs_3_.refs_1_.refs_2_.refs_12_), channel_id=1, source_target_pairs={{1,0},{0,1},{3,2},{2,3},{5,4},{4,5},{7,6},{6,7},{9,8},{8,9},{11,10... | collective-permute-start | bytes 2162696 | tf_op jit(solution)/shard_map/ppermute | solution.py:57
  23.0 24.8 %collective-permute-start.4 = (bf16[256,1408]{1,0:T(8,128)(2,1)S(1)}, bf16[256,1408]{1,0:T(8,128)(2,1)S(1)}, u32[]{:S(2)}, u32[]{:S(2)}) collective-permute-start(bf16[256,1408]{1,0:T(8,128)(2,1)S(1)} %collective-permute-done.2.refs_5_.refs_3_.refs_4_.refs_14_), channel_id=1, source_target_pairs={{1,0},{0,1},{3,2},{2,3},{5,4},{4,5},{7,6},{6,7},{9,8},{8,9},{11,10... | collective-permute-start | bytes 2162696 | tf_op jit(solution)/shard_map/ppermute | solution.py:57
  31.8 11.7 %collective-permute-start.8 = (bf16[192,1152]{1,0:T(8,128)(2,1)}, bf16[192,1152]{1,0:T(8,128)(2,1)}, u32[]{:S(2)}, u32[]{:S(2)}) collective-permute-start(bf16[192,1152]{1,0:T(8,128)(2,1)} %collective-permute-done.6.refs_4_.refs_2_), channel_id=1, source_target_pairs={{16,0},{17,1},{18,2},{19,3},{20,4},{21,5},{22,6},{23,7},{24,8},{25... | collective-permute-start | bytes 1327112 | tf_op jit(solution)/shard_map/ppermute | solution.py:57
  33.0 9.9 %collective-permute-start.10 = (bf16[128,1152]{1,0:T(8,128)(2,1)S(1)}, bf16[128,1152]{1,0:T(8,128)(2,1)S(1)}, u32[]{:S(2)}, u32[]{:S(2)}) collective-permute-start(bf16[128,1152]{1,0:T(8,128)(2,1)S(1)} %get-tuple-element.48), channel_id=1, source_target_pairs={{2,0},{3,1},{0,2},{1,3},{6,4},{7,5},{4,6},{5,7},{10,8},{11,9},{8,1... | collective-permute-start | bytes 884744 | tf_op jit(solution)/shard_map/ppermute | solution.py:57
  33.1 10.4 %collective-permute-start.12 = (bf16[64,1152]{1,0:T(8,128)(2,1)}, bf16[64,1152]{1,0:T(8,128)(2,1)}, u32[]{:S(2)}, u32[]{:S(2)}) collective-permute-start(bf16[64,1152]{1,0:T(8,128)(2,1)} %copy-done.6), channel_id=1, source_target_pairs={{4,0},{5,1},{6,2},{7,3},{0,4},{1,5},{2,6},{3,7},{12,8},{13,9},{14,... | collective-permute-start | bytes 442376 | tf_op jit(solution)/shard_map/ppermute | solution.py:57
  42.9 10.0 %collective-permute-start.5 = (bf16[128,1152]{1,0:T(8,128)(2,1)}, bf16[128,1152]{1,0:T(8,128)(2,1)S(1)}, u32[]{:S(2)}, u32[]{:S(2)}) collective-permute-start(bf16[128,1152]{1,0:T(8,128)(2,1)} %copy-done.3), channel_id=1, source_target_pairs={{8,0},{9,1},{10,2},{11,3},{12,4},{13,5},{14,6},{15,7},{0,8},{1,9},... | collective-permute-start | bytes 884744 | tf_op jit(solution)/shard_map/ppermute | solution.py:57
  43.5 14.8 %collective-permute-start.7 = (bf16[192,1152]{1,0:T(8,128)(2,1)}, bf16[192,1152]{1,0:T(8,128)(2,1)}, u32[]{:S(2)}, u32[]{:S(2)}) collective-permute-start(bf16[192,1152]{1,0:T(8,128)(2,1)} %collective-permute-done.6.refs_4_.refs_2_), channel_id=1, source_target_pairs={{1,0},{0,1},{3,2},{2,3},{5,4},{4,5},{7,6},{6,7},{9,8},{8,9},{11,10... | collective-permute-start | bytes 1327112 | tf_op jit(solution)/shard_map/ppermute | solution.py:57
  43.5 18.7 %collective-permute-start.9 = (bf16[192,1152]{1,0:T(8,128)(2,1)}, bf16[192,1152]{1,0:T(8,128)(2,1)}, u32[]{:S(2)}, u32[]{:S(2)}) collective-permute-start(bf16[192,1152]{1,0:T(8,128)(2,1)} %collective-permute-done.8.refs_6_.refs_4_), channel_id=1, source_target_pairs={{1,0},{0,1},{3,2},{2,3},{5,4},{4,5},{7,6},{6,7},{9,8},{8,9},{11,10... | collective-permute-start | bytes 1327112 | tf_op jit(solution)/shard_map/ppermute | solution.py:57
  46.2 20.6 %collective-permute-start.11 = (bf16[128,1152]{1,0:T(8,128)(2,1)S(1)}, bf16[128,1152]{1,0:T(8,128)(2,1)S(1)}, u32[]{:S(2)}, u32[]{:S(2)}) collective-permute-start(bf16[128,1152]{1,0:T(8,128)(2,1)S(1)} %collective-permute-done.10.refs_0_.refs_4_), channel_id=1, source_target_pairs={{8,0},{9,1},{10,2},{11,3},{12,4},{13,5},{14,6},{15,7},{0,8},{1,9},... | collective-permute-start | bytes 884744 | tf_op jit(solution)/shard_map/ppermute | solution.py:57
  47.8 8.9 %collective-permute-start.16 = (bf16[256,256]{1,0:T(8,128)(2,1)}, bf16[256,256]{1,0:T(8,128)(2,1)S(1)}, u32[]{:S(2)}, u32[]{:S(2)}) collective-permute-start(bf16[256,256]{1,0:T(8,128)(2,1)} %seed_ref.5), channel_id=1, source_target_pairs={{4,0},{5,1},{6,2},{7,3},{0,4},{1,5},{2,6},{3,7},{12,8},{13,9},{14,... | collective-permute-start | bytes 393224 | tf_op jit(solution)/shard_map/ppermute | solution.py:57
  52.9 9.8 %collective-permute-start.14 = (bf16[64,1152]{1,0:T(8,128)(2,1)}, bf16[64,1152]{1,0:T(8,128)(2,1)S(1)}, u32[]{:S(2)}, u32[]{:S(2)}) collective-permute-start(bf16[64,1152]{1,0:T(8,128)(2,1)} %collective-permute-done.12.refs_6_), channel_id=1, source_target_pairs={{16,0},{17,1},{18,2},{19,3},{20,4},{21,5},{22,6},{23,7},{24,8},{25... | collective-permute-start | bytes 442376 | tf_op jit(solution)/shard_map/ppermute | solution.py:57
  58.3 16.5 %collective-permute-start.17 = (bf16[256,256]{1,0:T(8,128)(2,1)S(1)}, bf16[256,256]{1,0:T(8,128)(2,1)S(1)}, u32[]{:S(2)}, u32[]{:S(2)}) collective-permute-start(bf16[256,256]{1,0:T(8,128)(2,1)S(1)} %collective-permute-done.16.refs_16_), channel_id=1, source_target_pairs={{1,0},{0,1},{3,2},{2,3},{5,4},{4,5},{7,6},{6,7},{9,8},{8,9},{11,10... | collective-permute-start | bytes 393224 | tf_op jit(solution)/shard_map/ppermute | solution.py:57
  62.2 12.7 %collective-permute-start.19 = (bf16[256,256]{1,0:T(8,128)(2,1)S(1)}, bf16[256,256]{1,0:T(8,128)(2,1)S(1)}, u32[]{:S(2)}, u32[]{:S(2)}) collective-permute-start(bf16[256,256]{1,0:T(8,128)(2,1)S(1)} %collective-permute-done.18.refs_18_), channel_id=1, source_target_pairs={{1,0},{0,1},{3,2},{2,3},{5,4},{4,5},{7,6},{6,7},{9,8},{8,9},{11,10... | collective-permute-start | bytes 393224 | tf_op jit(solution)/shard_map/ppermute | solution.py:57
  62.2 10.1 %collective-permute-start.13 = (bf16[64,1152]{1,0:T(8,128)(2,1)}, bf16[64,1152]{1,0:T(8,128)(2,1)S(1)}, u32[]{:S(2)}, u32[]{:S(2)}) collective-permute-start(bf16[64,1152]{1,0:T(8,128)(2,1)} %collective-permute-done.12.refs_6_), channel_id=1, source_target_pairs={{1,0},{0,1},{3,2},{2,3},{5,4},{4,5},{7,6},{6,7},{9,8},{8,9},{11,10... | collective-permute-start | bytes 442376 | tf_op jit(solution)/shard_map/ppermute | solution.py:57
  62.7 9.6 %collective-permute-start.15 = (bf16[64,1152]{1,0:T(8,128)(2,1)S(1)}, bf16[64,1152]{1,0:T(8,128)(2,1)S(1)}, u32[]{:S(2)}, u32[]{:S(2)}) collective-permute-start(bf16[64,1152]{1,0:T(8,128)(2,1)S(1)} %collective-permute-done.14.refs_8_), channel_id=1, source_target_pairs={{1,0},{0,1},{3,2},{2,3},{5,4},{4,5},{7,6},{6,7},{9,8},{8,9},{11,10... | collective-permute-start | bytes 442376 | tf_op jit(solution)/shard_map/ppermute | solution.py:57
  78.4 8.1 %collective-permute-start.22 = (bf16[272,256]{1,0:T(8,128)(2,1)S(1)}, bf16[272,256]{1,0:T(8,128)(2,1)S(1)}, u32[]{:S(2)}, u32[]{:S(2)}) collective-permute-start(bf16[272,256]{1,0:T(8,128)(2,1)S(1)} %get-tuple-element.66), channel_id=1, source_target_pairs={{10,0},{11,1},{8,2},{9,3},{14,4},{15,5},{12,6},{13,7},{2,8},{3,9},... | collective-permute-start | bytes 417800 | tf_op jit(solution)/shard_map/ppermute | solution.py:57
  86.6 8.5 %collective-permute-start.26 = (bf16[256,256]{1,0:T(8,128)(2,1)S(1)}, bf16[256,256]{1,0:T(8,128)(2,1)S(1)}, u32[]{:S(2)}, u32[]{:S(2)}) collective-permute-start(bf16[256,256]{1,0:T(8,128)(2,1)S(1)} %get-tuple-element.67.refs_6_), channel_id=1, source_target_pairs={{4,0},{5,1},{6,2},{7,3},{0,4},{1,5},{2,6},{3,7},{12,8},{13,9},{14,... | collective-permute-start | bytes 393224 | tf_op jit(solution)/shard_map/ppermute | solution.py:57
  88.1 9.0 %collective-permute-start.24 = (bf16[256,256]{1,0:T(8,128)(2,1)S(1)}, bf16[256,256]{1,0:T(8,128)(2,1)S(1)}, u32[]{:S(2)}, u32[]{:S(2)}) collective-permute-start(bf16[256,256]{1,0:T(8,128)(2,1)S(1)} %get-tuple-element.67.refs_6_), channel_id=1, source_target_pairs={{16,0},{17,1},{18,2},{19,3},{20,4},{21,5},{22,6},{23,7},{24,8},{25... | collective-permute-start | bytes 393224 | tf_op jit(solution)/shard_map/ppermute | solution.py:57
  103.4 6.4 %collective-permute-start.31 = (bf16[256,256]{1,0:T(8,128)(2,1)S(1)}, bf16[256,256]{1,0:T(8,128)(2,1)S(1)}, u32[]{:S(2)}, u32[]{:S(2)}) collective-permute-start(bf16[256,256]{1,0:T(8,128)(2,1)S(1)} %get-tuple-element.71), channel_id=1, source_target_pairs={{2,0},{3,1},{0,2},{1,3},{6,4},{7,5},{4,6},{5,7},{10,8},{11,9},{8,1... | collective-permute-start | bytes 393224 | tf_op jit(solution)/shard_map/ppermute | solution.py:57
  103.4 8.9 %collective-permute-start.32 = (bf16[256,256]{1,0:T(8,128)(2,1)S(1)}, bf16[256,256]{1,0:T(8,128)(2,1)S(1)}, u32[]{:S(2)}, u32[]{:S(2)}) collective-permute-start(bf16[256,256]{1,0:T(8,128)(2,1)S(1)} %get-tuple-element.72), channel_id=1, source_target_pairs={{10,0},{11,1},{8,2},{9,3},{14,4},{15,5},{12,6},{13,7},{2,8},{3,9},... | collective-permute-start | bytes 393224 | tf_op jit(solution)/shard_map/ppermute | solution.py:57
  (17 other events, 111.5 us)

commit v4 on v3

--- a/solution.py
+++ b/solution.py
@@ -69,56 +69,84 @@
     return pltpu.CompilerParams(vmem_limit_bytes=mib * 2**20)
 
 
-def unit_kernel(t_chunks, s_chunks, emb_ref, seed_ref, *outs):
-    values = emb_ref[...].astype(jnp.float32)
-    d = values.shape[1]
+def unit_of(values):
+    values = values.astype(jnp.float32)
     mean_square = jnp.mean(values * values, axis=1, keepdims=True)
-    scaled = values * lax.rsqrt(mean_square + epsilon) * d ** (-0.5)
-    unit = scaled.astype(jnp.bfloat16)
-    outs[0][...] = unit
-    outs[1][:, :d] = unit
-    outs[1][:, d:] = seed_ref[...]
-    for out, (start, rows) in zip(outs[2:], t_chunks + s_chunks):
-        out[...] = unit[start : start + rows]
-
-
-def unit_rows(embeddings, seeds, t_chunks, s_chunks):
-    m, d = embeddings.shape
-    shapes = [(m, d), (m, d + seeds.shape[1])] + [(rows, d) for _, rows in t_chunks + s_chunks]
-    got = pl.pallas_call(
-        functools.partial(unit_kernel, t_chunks, s_chunks),
+    scaled = values * lax.rsqrt(mean_square + epsilon) * values.shape[1] ** (-0.5)
+    return scaled.astype(jnp.bfloat16)
+
+
+def first_unit_kernel(emb_ref, out_ref):
+    out_ref[...] = unit_of(emb_ref[: out_ref.shape[0], :])
+
+
+def unit_kernel(emb_ref, seed_ref, first_ref, unit_ref, packed_ref, *second):
+    d, head = emb_ref.shape[1], first_ref.shape[0]
+    packed_ref[:, d:] = seed_ref[...]
+    unit_ref[:head, :] = first_ref[...]
+    packed_ref[:head, :d] = first_ref[...]
+    if second:
+        rest = unit_of(emb_ref[head:, :])
+        unit_ref[head:, :] = rest
+        packed_ref[head:, :d] = rest
+        second[0][...] = rest
+
+
+def unit_rows(embeddings, seeds, chunks):
+    (m, d), c = embeddings.shape, seeds.shape[1]
+    head = chunks[0][1]
+    first = pl.pallas_call(
+        first_unit_kernel,
+        out_shape=jax.ShapeDtypeStruct((head, d), jnp.bfloat16),
+        in_specs=[VMEM],
+        out_specs=VMEM,
+        compiler_params=limits(),
+    )(embeddings)
+    shapes = [(m, d), (m, d + c)] + [(rows, d) for _, rows in chunks[1:]]
+    units, packed, *second = pl.pallas_call(
+        unit_kernel,
         out_shape=[jax.ShapeDtypeStruct(s, jnp.bfloat16) for s in shapes],
-        in_specs=[VMEM] * 2,
+        in_specs=[VMEM] * 3,
         out_specs=[VMEM] * len(shapes),
         compiler_params=limits(),
-    )(embeddings, seeds)
-    return got[0], got[1], got[2 : 2 + len(t_chunks)], got[2 + len(t_chunks) :]
-
-
-def gram_kernel(nt, ns, sub, d, flags, *refs):
-    t_in, s_in, (kern, acc), scratch = refs[:nt], refs[nt : nt + ns], refs[nt + ns : nt + ns + 2], refs[nt + ns + 2 :]
-    if scratch:
-        at = 0
-        for ref in s_in:
-            scratch[0][at : at + ref.shape[0], :] = ref[:, :d]
-            at += ref.shape[0]
-        width = 2 * BLOCK if at % (2 * BLOCK) == 0 else BLOCK if at % BLOCK == 0 else at
-        tiles = [(scratch[0], k, width) for k in range(0, at, width)]
+    )(embeddings, seeds, first)
+    return units, packed, [first] + second
+
+
+def joined(refs, scratch, d):
+    if scratch is None:
+        return refs[0]
+    at = 0
+    for ref in refs:
+        scratch[at : at + ref.shape[0], :] = ref[:, :d]
+        at += ref.shape[0]
+    return scratch
+
+
+def gram_kernel(nt, ns, sub, d, join_t, join_s, flags, *refs):
+    t_in, s_in, refs = refs[:nt], refs[nt : nt + ns], refs[nt + ns :]
+    (kern, acc), scratch = refs[:2], list(refs[2:])
+    t_ref = joined(t_in, scratch.pop(0) if join_t else None, d)
+    if join_s:
+        s_ref = joined(s_in, scratch.pop(0), d)
+        total = s_ref.shape[0]
+        width = next(w for w in (2 * BLOCK, BLOCK, total) if total % w == 0)
+        tiles = [(s_ref, k, width) for k in range(0, total, width)]
     else:
         tiles = [(ref, 0, ref.shape[0]) for ref in s_in]
+    rows = kern.shape[0]
+    tall = next(h for h in (512, 384, 256, 128, rows) if rows % h == 0)
     col = 0
     for s_ref, s_at, width in tiles:
-        row = 0
-        for i in range(nt):
-            height = t_in[i].shape[0]
+        for row in range(0, rows, tall):
             scores = lax.dot_general(
-                t_in[i][...],
+                t_ref[row : row + tall, :],
                 s_ref[s_at : s_at + width, :d],
                 (((1,), (1,)), ((), ())),
                 preferred_element_type=jnp.float32,
             )
             value = jnp.exp(sharpness * scores).astype(jnp.bfloat16).astype(jnp.float32)
-            for a in range(height // sub):
+            for a in range(tall // sub):
                 at = row + a * sub
                 flag = flags[at // sub : at // sub + 1, col : col + width]
                 part = jnp.where(flag > 0, value[a * sub : (a + 1) * sub], 0.0)
@@ -129,23 +157,24 @@
                 if col > 0:
                     total = total + acc[at : at + sub, :]
                 acc[at : at + sub, :] = total
-            row += height
         col += width
 
 
 def gram_call(flags, t_pieces, s_pieces, sub):
     rows, cols = (sum(p.shape[0] for p in pieces) for pieces in (t_pieces, s_pieces))
     d = t_pieces[0].shape[1]
-    direct = all(p.shape[0] == 2 * BLOCK for p in s_pieces)
+    join_t = len(t_pieces) > 1
+    join_s = any(p.shape[0] != 2 * BLOCK for p in s_pieces)
     return pl.pallas_call(
-        functools.partial(gram_kernel, len(t_pieces), len(s_pieces), sub, d),
+        functools.partial(gram_kernel, len(t_pieces), len(s_pieces), sub, d, join_t, join_s),
         out_shape=[
             jax.ShapeDtypeStruct((rows, cols), jnp.bfloat16),
             jax.ShapeDtypeStruct((rows, BLOCK), jnp.float32),
         ],
         in_specs=[VMEM] * (1 + len(t_pieces) + len(s_pieces)),
         out_specs=[VMEM] * 2,
-        scratch_shapes=[] if direct else [pltpu.VMEM((cols, d), jnp.bfloat16)],
+        scratch_shapes=[pltpu.VMEM((rows, d), jnp.bfloat16)] * join_t
+        + [pltpu.VMEM((cols, d), jnp.bfloat16)] * join_s,
         compiler_params=limits(),
         cost_estimate=pl.CostEstimate(
             flops=2 * rows * cols * d,
@@ -280,27 +309,36 @@
     size = layout.sizes
     m, c = embeddings.shape[0], seed_labels.shape[1]
     sub = min(m, BLOCK)
-    fetch = layout.fetch
-    cores, ys = range(size["core"]), range(size["y"])
-    chunked = m % (2 * BLOCK) == 0
-    t_chunks = [(0, m // 2), (m // 2, m // 2)] if chunked else [(0, m)]
-    s_chunks = [(0, 3 * m // 4), (3 * m // 4, m // 4)] if chunked else [(0, m)]
+    other = {k: range(1, size[k]) for k in size}
+    chunks = [(0, m // 2), (m // 2, m // 2)] if m % (2 * BLOCK) == 0 else [(0, m)]
+
+    def fetch(values, axis, *earlier):
+        return [
+            layout.fetch(after(v, *earlier), **{axis: k}) for k in other[axis] for v in values
+        ]
+
+    units, packed, parts = unit_rows(embeddings, seed_labels, chunks)
 
     t_index = {(b, a): b * size["x"] + a for b in range(size["zl"]) for a in range(size["x"])}
     t_layout = [(t_index[0, a], 0, m) for a in range(size["x"])]
-    ends = [size["x"] * m]
-    for start, rows in t_chunks:
-        for a in range(size["x"]):
-            t_layout += [(t_index[b, a], start, rows) for b in range(1, size["zl"])]
-            ends.append(ends[-1] + (size["zl"] - 1) * rows)
-    near = [dict(y=a, core=k) for a in ys for k in cores]
-    far = [dict(zh=b, y=a, core=k) for b in range(1, size["zh"]) for a in ys for k in cores]
-    s_layout = [(i, o, 0, m) for i, o in enumerate(near)]
-    columns = [len(near) * m]
-    for start, rows in s_chunks:
-        s_layout += [(len(near) + i, o, start, rows) for i, o in enumerate(far)]
-        columns.append(columns[-1] + len(far) * rows)
-    p_map = [(i, start, rows) for i, _, start, rows in s_layout]
+    t_groups = [len(t_layout)]
+    for start, rows in chunks:
+        t_layout += [(t_index[b, 0], start, rows) for b in other["zl"]]
+        t_groups.append(len(t_layout))
+        t_layout += [(t_index[b, a], start, rows) for a in other["x"] for b in other["zl"]]
+        t_groups.append(len(t_layout))
+    both = [0] + list(other["core"])
+    groups = [[(0, a, k, 0, m) for a in range(size["y"]) for k in both]]
+    for start, rows in chunks:
+        groups.append([(b, 0, k, start, rows) for k in both for b in other["zh"]])
+        groups.append(
+            [(b, a, k, start, rows) for k in both for a in other["y"] for b in other["zh"]]
+        )
+    s_layout = [piece for group in groups for piece in group]
+    whole = [(0, a, k) for a in range(size["y"]) for k in both]
+    whole += [(b, 0, k) for k in both for b in other["zh"]]
+    whole += [(b, a, k) for k in both for a in other["y"] for b in other["zh"]]
+    p_map = [(whole.index(piece[:3]), *piece[3:]) for piece in s_layout]
 
     t_offsets = [dict(zl=b, x=a) for b, a in t_index]
     t_blocks = jnp.concatenate(
@@ -310,78 +348,88 @@
         ]
     )
     s_blocks = jnp.concatenate(
-        [(layout.device(o) * m + start + jnp.arange(rows)) // BLOCK for _, o, start, rows in s_layout]
+        [
+            (layout.device(dict(zh=b, y=a, core=k)) * m + start + jnp.arange(rows)) // BLOCK
+            for b, a, k, start, rows in s_layout
+        ]
     )
     flags = jnp.any(pattern[t_blocks][:, :, None] == s_blocks[None, None, :], axis=1)
     flags = flags.astype(jnp.int32)
 
-    units, packed, t_parts, s_parts = unit_rows(embeddings, seed_labels, t_chunks, s_chunks)
-
-    def cored(value):
-        return [fetch(value, core=k) for k in cores]
-
-    by_x = [fetch(units, x=a) for a in range(size["x"])]
-    by_y = [fetch(packed, y=a) for a in ys]
-    t_pieces, held = list(by_x), ()
-    for part in t_parts:
-        by_zl = [fetch(after(part, *held), zl=b) for b in range(1, size["zl"])]
-        held = by_zl
-        t_pieces += [fetch(v, x=a) for a in range(size["x"]) for v in by_zl]
-    s_near = cored(after(packed, *by_y[1:])) + [p for v in by_y[1:] for p in cored(v)]
-    by_zh, held = [], ()
-    for part in s_parts:
-        by_zh.append([fetch(after(part, *held), zh=b) for b in range(1, size["zh"])])
-        held = by_zh[-1] + by_x[1:] + by_y[1:]
-    s_far = []
-
-    def near_panels(panel):
-        return [p for a in ys for p in cored(fetch(panel, y=a))]
-
-    def far_panels(panel):
-        by_zh = [fetch(panel, zh=b) for b in range(1, size["zh"])]
-        return [p for v in by_zh for a in ys for p in cored(fetch(v, y=a))]
-
-    t_ends = [ends[1], ends[2], ends[-1]] if chunked and size["x"] == 2 else [ends[-1]]
-    kerns, accs, rects = [], [], []
-
-    def rectangle(t0, t1, g):
-        row, pieces = 0, []
-        for piece, (_, _, rows) in zip(t_pieces, t_layout):
-            if t0 <= row < t1:
-                pieces.append(piece)
-            row += rows
-        c0, c1 = ([0] + columns)[g : g + 2]
+    t_pieces, kerns, accs, rects = [], [], [], []
+    s_pieces = [None] * len(groups)
+
+    def rectangle(first, last, g0, g1):
+        t0, t1 = (sum(rows for _, _, rows in t_layout[:i]) for i in (first, last))
+        c0, c1 = (sum(p[4] for group in groups[:g] for p in group) for g in (g0, g1))
+        if t0 == t1 or c0 == c1:
+            return []
         kern, acc = gram_call(
-            flags[t0 // sub : t1 // sub, c0:c1], pieces, ([s_near] + s_far)[g], sub
+            flags[t0 // sub : t1 // sub, c0:c1],
+            t_pieces[first:last],
+            [p for g in range(g0, g1) for p in s_pieces[g]],
+            sub,
         )
         kerns.append(kern)
         accs.append(acc)
         rects.append((t0, t1, c0, c1))
-
-    def onward(g, *earlier):
-        values = [after(v, *earlier) for v in by_zh[g]]
-        s_far.append([p for v in values for a in ys for p in cored(fetch(v, y=a))])
-
-    if len(t_ends) == 3 and far:
-        onward(0)
-        rectangle(0, t_ends[0], 0)
-        onward(1, accs[0])
-        rectangle(t_ends[0], t_ends[1], 0)
-        rectangle(0, t_ends[1], 1)
-        rectangle(t_ends[1], t_ends[2], 0)
-        rectangle(t_ends[1], t_ends[2], 1)
-        rectangle(0, t_ends[2], 2)
+        return [acc]
+
+    zh, zl = fetch(parts[:1], "zh"), fetch(parts[:1], "zl")
+    x, y = fetch([units], "x"), fetch([packed], "y")
+    own_core = fetch([packed], "core")
+    done = zh + zl + x + y + own_core
+    t_pieces += [units] + x + zl
+    zh_next, zl_next = fetch(parts[1:], "zh", *done), fetch(parts[1:], "zl", *done)
+    zh_y, zl_x = fetch(zh, "y", *done), fetch(zl, "x", *done)
+    y_core = [fetch([v], "core", *done) for v in y]
+    t_pieces += zl_x
+    s_pieces[0] = [packed] + own_core + [p for v, w in zip(y, y_core) for p in [v] + w]
+    first = rectangle(0, t_groups[1], 0, 1)
+    zh_core = fetch(zh, "core", *done, *[p for w in y_core for p in w])
+    s_pieces[1] = zh + zh_core
+    done = zh_next + zl_next + zh_y + zl_x + zh_core + first
+    seeds_zh = fetch([seed_labels], "zh", *done)
+    zh_y_core = fetch(zh_y, "core", *done)
+    s_pieces[2] = zh_y + zh_y_core
+    if parts[1:]:
+        zh_next_y, zl_next_x = fetch(zh_next, "y", *done), fetch(zl_next, "x", *done)
+        zh_next_core = fetch(zh_next, "core", *done)
+        t_pieces += zl_next + zl_next_x
+        second = rectangle(t_groups[1], t_groups[2], 0, 1) + rectangle(0, t_groups[2], 1, 3)
+        done = zh_next_y + zl_next_x + zh_next_core + zh_y_core + seeds_zh + second
+        zh_next_y_core = fetch(zh_next_y, "core", *done)
+        s_pieces[3] = zh_next + zh_next_core
+        s_pieces[4] = zh_next_y + zh_next_y_core
     else:
-        for g in range(len(s_chunks) if far else 0):
-            onward(g)
-        for g in range(1 + len(s_far)):
-            rectangle(0, ends[-1], g)
+        done = zh_y_core + seeds_zh
+    seeds_y, seeds_core = fetch(seeds_zh, "y", *done), fetch(seeds_zh, "core", *done)
+    seeds_y_core = fetch(seeds_y, "core")
+    last = len(t_pieces)
+    if parts[1:]:
+        rectangle(t_groups[2], last, 0, 1)
+        rectangle(t_groups[2], last, 1, 3)
+        rectangle(0, last, 3, 4)
+        rectangle(0, last, 4, 5)
+    else:
+        rectangle(t_groups[1], last, 0, 1)
+        rectangle(0, last, 1, 2)
+        rectangle(0, last, 2, 3)
     plan = (m, t_layout, rects, p_map)
 
     def home(values):
-        return [fetch(v, **{k: -d for k, d in o.items()}) for v, o in zip(values, t_offsets[1:])]
-
-    seeds = s_near + far_panels(after(seed_labels, *held))
+        return [
+            layout.fetch(v, **{k: -d for k, d in o.items()})
+            for v, o in zip(values, t_offsets[1:])
+        ]
+
+    def panels(panel):
+        far, near = fetch([panel], "zh"), fetch([panel], "y")
+        far_y = fetch(far, "y")
+        near = [p for v in [panel] + near for p in [v] + fetch([v], "core")]
+        return near + far + fetch(far, "core") + far_y + fetch(far_y, "core")
+
+    seeds = s_pieces[0] + seeds_zh + seeds_core + seeds_y + seeds_y_core
     own, totals, *others = spread_call(kerns, accs, seeds, c, plan)
     panel, totals = update(
         first_update_kernel,
@@ -394,7 +442,7 @@
             jax.ShapeDtypeStruct((m, BLOCK), jnp.float32),
         ],
     )
-    own, *others = spread_call(kerns, [], near_panels(panel) + far_panels(panel), c, plan)
+    own, *others = spread_call(kerns, [], panels(panel), c, plan)
     return update(
         last_update_kernel,
         seed_labels,

time: 113 us -> 106 us (0.938)
  starting transfers between devices: 31.9 us -> 27.5 us
  waiting for transfers between devices: 53.2 us -> 49.1 us
  local copies, waits for them, and re-layouts: 5.83 us -> 7.44 us
    ppermute x33, starting transfers between devices: 31.9 us -> 27.5 us  [fetch(): return lax.ppermute(value, AXES, pairs)]
    ppermute x33, waiting for transfers between devices: 53.2 us -> 49.1 us  [fetch(): return lax.ppermute(value, AXES, pairs)]
    unnamed x17 -> x23, local copies, waits for them, and re-layouts: 4.4 us -> 6.76 us
    pallas_call x6 -> x7, Pallas kernels: 15.6 us -> 15.2 us  [gram_call(): pl.pallas_call(functools.partial(gram_kernel, len(t_pieces), len(s_pieces...]
  transfers between devices with their start and end apart: 33 -> 33, of which waited for: 14 -> 18; matrix products, arithmetic and copies ran while one was open for 3% -> 1% of each run, Pallas kernels for 14% -> 15%
where the time goes in v4:
time: 106 us
  waiting for transfers between devices  49.1 us (46%)
  starting transfers between devices  27.5 us (26%)
  Pallas kernels  20.7 us (20%)
  local copies, waits for them, and re-layouts  7.44 us (7%)
    ppermute x33, waiting for transfers between devices, fetch(): return lax.ppermute(value, AXES, pairs)  49.1 us
    ppermute x33, starting transfers between devices, fetch(): return lax.ppermute(value, AXES, pairs)  27.5 us
    pallas_call x7, Pallas kernels, gram_call(): pl.pallas_call(functools.partial(gram_kernel, len(t_pieces), len(s_pieces...  15.2 us
    unnamed x23, local copies, waits for them, and re-layouts  6.76 us
    pallas_call x2, Pallas kernels, spread_call(): pl.pallas_call(functools.partial(spread_kernel, plan, len(kerns), len(acc...  2.5 us
  transfers between devices with their start and end apart: 33, of which 18 were waited for; matrix products, arithmetic and copies ran while one was open for 1% of the time, Pallas kernels for 15%

profile of v4, /device:TPU:0, one launch (start us, length us, event | category | flops | bytes accessed | tf_op | source)
XLA Modules:
  0.0 105.7 jit_solution(12125536865527531752)
XLA Ops:
  2.0 4.0 %collective-permute-start.4 = (bf16[128,1152]{1,0:T(8,128)(2,1)}, bf16[128,1152]{1,0:T(8,128)(2,1)}, u32[]{:S(2)}, u32[]{:S(2)}) collective-permute-start(bf16[128,1152]{1,0:T(8,128)(2,1)} %shard_map.37.first_ref), channel_id=1, source_target_pairs={{4,0},{5,1},{6,2},{7,3},{0,4},{1,5},{2,6},{3,7},{12,8},{13,9},{14,... | collective-permute-start | bytes 884744 | tf_op jit(solution)/shard_map/ppermute | solution.py:57
  6.0 1.6 %collective-permute-start.1 = (bf16[128,1152]{1,0:T(8,128)(2,1)}, bf16[128,1152]{1,0:T(8,128)(2,1)}, u32[]{:S(2)}, u32[]{:S(2)}) collective-permute-start(bf16[128,1152]{1,0:T(8,128)(2,1)} %shard_map.37.first_ref), channel_id=1, source_target_pairs={{2,0},{3,1},{0,2},{1,3},{6,4},{7,5},{4,6},{5,7},{10,8},{11,9},{8,1... | collective-permute-start | bytes 884744 | tf_op jit(solution)/shard_map/ppermute | solution.py:57
  10.4 1.5 %collective-permute-start.3 = (bf16[256,1408]{1,0:T(8,128)(2,1)S(1)}, bf16[256,1408]{1,0:T(8,128)(2,1)S(1)}, u32[]{:S(2)}, u32[]{:S(2)}) collective-permute-start(bf16[256,1408]{1,0:T(8,128)(2,1)S(1)} %get-tuple-element.45.refs_3_.refs_1_.refs_2_.refs_14_), channel_id=1, source_target_pairs={{16,0},{17,1},{18,2},{19,3},{20,4},{21,5},{22,6},{23,7},{24,8},{25... | collective-permute-start | bytes 2162696 | tf_op jit(solution)/shard_map/ppermute | solution.py:57
  14.4 5.3 %collective-permute-done.4.refs_4_.refs_2_ = bf16[128,1152]{1,0:T(8,128)(2,1)} collective-permute-done((bf16[128,1152]{1,0:T(8,128)(2,1)}, bf16[128,1152]{1,0:T(8,128)(2,1)}, u32[]{:S(2)}, u32[]{:S(2)}) %collective-permute-start.4) | collective-permute-done | bytes 294944 | tf_op jit(solution)/shard_map/ppermute | solution.py:57
  19.9 7.7 %collective-permute-done.refs_1_ = bf16[256,1152]{1,0:T(8,128)(2,1)S(1)} collective-permute-done((bf16[256,1152]{1,0:T(8,128)(2,1)S(1)}, bf16[256,1152]{1,0:T(8,128)(2,1)S(1)}, u32[]{:S(2)}, u32[]{:S(2)}) %collective-permute-start) | collective-permute-done | bytes 589856 | tf_op jit(solution)/shard_map/ppermute | solution.py:57
  29.7 1.5 %collective-permute-start.6 = (bf16[128,1152]{1,0:T(8,128)(2,1)}, bf16[128,1152]{1,0:T(8,128)(2,1)S(1)}, u32[]{:S(2)}, u32[]{:S(2)}) collective-permute-start(bf16[128,1152]{1,0:T(8,128)(2,1)} %collective-permute-done.1.refs_2_), channel_id=1, source_target_pairs={{8,0},{9,1},{10,2},{11,3},{12,4},{13,5},{14,6},{15,7},{0,8},{1,9},... | collective-permute-start | bytes 884744 | tf_op jit(solution)/shard_map/ppermute | solution.py:57
  35.0 4.9 %shard_map.39 = (bf16[640,1024]{1,0:T(8,128)(2,1)S(1)}, f32[640,128]{1,0:T(8,128)S(1)}) custom-call(s32[5,1024]{1,0:T(8,128)S(1)} %slice.30.flags, bf16[256,1152]{1,0:T(8,128)(2,1)S(1)} %copy-done.2, bf16[256,1152]{1,0:T(8,128)(2,1)S(1)} %copy-done.5, bf16[128,1152]{1,0:T(8,128)(2,1)} %collective-permute-done.1.refs_2_, ...), custom_call_target="tpu_custom_call" | custom-call | flops 1509949440 | bytes 3833856 | tf_op jit(solution)/shard_map/pallas_call | solution.py:168
  40.1 3.5 %collective-permute-done.10.refs_0_.refs_4_ = bf16[128,1152]{1,0:T(8,128)(2,1)S(1)} collective-permute-done((bf16[128,1152]{1,0:T(8,128)(2,1)}, bf16[128,1152]{1,0:T(8,128)(2,1)S(1)}, u32[]{:S(2)}, u32[]{:S(2)}) %collective-permute-start.10) | collective-permute-done | bytes 294944 | tf_op jit(solution)/shard_map/ppermute | solution.py:57
  43.6 2.5 %collective-permute-done.9.refs_6_ = bf16[128,1152]{1,0:T(8,128)(2,1)} collective-permute-done((bf16[128,1152]{1,0:T(8,128)(2,1)}, bf16[128,1152]{1,0:T(8,128)(2,1)}, u32[]{:S(2)}, u32[]{:S(2)}) %collective-permute-start.9) | collective-permute-done | bytes 294944 | tf_op jit(solution)/shard_map/ppermute | solution.py:57
  46.1 1.5 %collective-permute-start.12 = (bf16[128,1152]{1,0:T(8,128)(2,1)S(1)}, bf16[128,1152]{1,0:T(8,128)(2,1)S(1)}, u32[]{:S(2)}, u32[]{:S(2)}) collective-permute-start(bf16[128,1152]{1,0:T(8,128)(2,1)S(1)} %collective-permute-done.10.refs_0_.refs_4_), channel_id=1, source_target_pairs={{8,0},{9,1},{10,2},{11,3},{12,4},{13,5},{14,6},{15,7},{0,8},{1,9},... | collective-permute-start | bytes 884744 | tf_op jit(solution)/shard_map/ppermute | solution.py:57
  49.7 2.6 %shard_map.41 = (bf16[768,512]{1,0:T(8,128)(2,1)S(1)}, f32[768,128]{1,0:T(8,128)S(1)}) custom-call(s32[6,512]{1,0:T(8,128)S(1)} %slice.32.flags, bf16[256,1152]{1,0:T(8,128)(2,1)S(1)} %copy-done.2, bf16[256,1152]{1,0:T(8,128)(2,1)S(1)} %copy-done.6, bf16[128,1152]{1,0:T(8,128)(2,1)} %collective-permute-done.1.refs_2_, ...), custom_call_target="tpu_custom_call" | custom-call | flops 905969664 | bytes 2949120 | tf_op jit(solution)/shard_map/pallas_call | solution.py:168
  52.3 4.3 %collective-permute-done.15.refs_18_ = bf16[256,256]{1,0:T(8,128)(2,1)S(1)} collective-permute-done((bf16[256,256]{1,0:T(8,128)(2,1)S(1)}, bf16[256,256]{1,0:T(8,128)(2,1)S(1)}, u32[]{:S(2)}, u32[]{:S(2)}) %collective-permute-start.15) | collective-permute-done | bytes 131104 | tf_op jit(solution)/shard_map/ppermute | solution.py:57
  58.6 2.0 %shard_map.44 = (bf16[1024,256]{1,0:T(8,128)(2,1)S(1)}, f32[1024,128]{1,0:T(8,128)S(1)}) custom-call(s32[8,256]{1,0:T(8,128)S(1)} %get-tuple-element.84.flags, bf16[256,1152]{1,0:T(8,128)(2,1)S(1)} %copy-done.2, bf16[256,1152]{1,0:T(8,128)(2,1)S(1)} %copy-done.6, bf16[128,1152]{1,0:T(8,128)(2,1)} %collective-permute-done.1.refs_2_, ...), custom_call_target="tpu_custom_call" | custom-call | flops 603979776 | bytes 2949120 | tf_op jit(solution)/shard_map/pallas_call | solution.py:168
  60.7 1.5 %collective-permute-done.18.refs_20_ = bf16[256,256]{1,0:T(8,128)(2,1)S(1)} collective-permute-done((bf16[256,256]{1,0:T(8,128)(2,1)S(1)}, bf16[256,256]{1,0:T(8,128)(2,1)S(1)}, u32[]{:S(2)}, u32[]{:S(2)}) %collective-permute-start.18) | collective-permute-done | bytes 131104 | tf_op jit(solution)/shard_map/ppermute | solution.py:57
  62.2 1.7 %shard_map.43 = (bf16[256,512]{1,0:T(8,128)(2,1)S(1)}, f32[256,128]{1,0:T(8,128)S(1)}) custom-call(s32[2,512]{1,0:T(2,128)S(1)} %slice.34.flags, bf16[128,1152]{1,0:T(8,128)(2,1)S(1)} %collective-permute-done.10.refs_0_.refs_4_, bf16[128,1152]{1,0:T(8,128)(2,1)S(1)} %collective-permute-done.12.refs_1_.refs_5_, ...), custom_call_target="tpu_custom_call" | custom-call | flops 301989888 | bytes 1769472 | tf_op jit(solution)/shard_map/pallas_call | solution.py:168
  65.0 2.0 %shard_map.45 = (bf16[1024,256]{1,0:T(8,128)(2,1)S(1)}, f32[1024,128]{1,0:T(8,128)S(1)}) custom-call(s32[8,256]{1,0:T(8,128)S(1)} %get-tuple-element.83.flags, bf16[256,1152]{1,0:T(8,128)(2,1)S(1)} %copy-done.3, bf16[256,1152]{1,0:T(8,128)(2,1)S(1)} %copy-done.6, bf16[128,1152]{1,0:T(8,128)(2,1)} %collective-permute-done.1.refs_2_, ...), custom_call_target="tpu_custom_call" | custom-call | flops 603979776 | bytes 2949120 | tf_op jit(solution)/shard_map/pallas_call | solution.py:168
  68.9 3.0 %collective-permute-start.22 = (bf16[272,256]{1,0:T(8,128)(2,1)S(1)}, bf16[272,256]{1,0:T(8,128)(2,1)S(1)}, u32[]{:S(2)}, u32[]{:S(2)}) collective-permute-start(bf16[272,256]{1,0:T(8,128)(2,1)S(1)} %get-tuple-element.76), channel_id=1, source_target_pairs={{10,0},{11,1},{8,2},{9,3},{14,4},{15,5},{12,6},{13,7},{2,8},{3,9},... | collective-permute-start | bytes 417800 | tf_op jit(solution)/shard_map/ppermute | solution.py:57
  71.8 2.6 %collective-permute-done.20.refs_0_ = bf16[272,256]{1,0:T(8,128)(2,1)S(1)} collective-permute-done((bf16[272,256]{1,0:T(8,128)(2,1)S(1)}, bf16[272,256]{1,0:T(8,128)(2,1)S(1)}, u32[]{:S(2)}, u32[]{:S(2)}) %collective-permute-start.20) | collective-permute-done | bytes 139296 | tf_op jit(solution)/shard_map/ppermute | solution.py:57
  75.4 3.2 %collective-permute-done.22.refs_2_ = bf16[272,256]{1,0:T(8,128)(2,1)S(1)} collective-permute-done((bf16[272,256]{1,0:T(8,128)(2,1)S(1)}, bf16[272,256]{1,0:T(8,128)(2,1)S(1)}, u32[]{:S(2)}, u32[]{:S(2)}) %collective-permute-start.22) | collective-permute-done | bytes 139296 | tf_op jit(solution)/shard_map/ppermute | solution.py:57
  81.4 5.9 %collective-permute-done.26.refs_11_ = bf16[256,256]{1,0:T(8,128)(2,1)S(1)} collective-permute-done((bf16[256,256]{1,0:T(8,128)(2,1)S(1)}, bf16[256,256]{1,0:T(8,128)(2,1)S(1)}, u32[]{:S(2)}, u32[]{:S(2)}) %collective-permute-start.26) | collective-permute-done | bytes 131104 | tf_op jit(solution)/shard_map/ppermute | solution.py:57
  89.2 3.5 %collective-permute-done.28.refs_13_ = bf16[256,256]{1,0:T(8,128)(2,1)S(1)} collective-permute-done((bf16[256,256]{1,0:T(8,128)(2,1)S(1)}, bf16[256,256]{1,0:T(8,128)(2,1)S(1)}, u32[]{:S(2)}, u32[]{:S(2)}) %collective-permute-start.28) | collective-permute-done | bytes 131104 | tf_op jit(solution)/shard_map/ppermute | solution.py:57
  95.9 3.0 %collective-permute-start.32 = (bf16[256,256]{1,0:T(8,128)(2,1)S(1)}, bf16[256,256]{1,0:T(8,128)(2,1)S(1)}, u32[]{:S(2)}, u32[]{:S(2)}) collective-permute-start(bf16[256,256]{1,0:T(8,128)(2,1)S(1)} %get-tuple-element.82), channel_id=1, source_target_pairs={{10,0},{11,1},{8,2},{9,3},{14,4},{15,5},{12,6},{13,7},{2,8},{3,9},... | collective-permute-start | bytes 393224 | tf_op jit(solution)/shard_map/ppermute | solution.py:57
  98.9 2.1 %collective-permute-done.30.refs_0_ = bf16[256,256]{1,0:T(8,128)(2,1)S(1)} collective-permute-done((bf16[256,256]{1,0:T(8,128)(2,1)S(1)}, bf16[256,256]{1,0:T(8,128)(2,1)S(1)}, u32[]{:S(2)}, u32[]{:S(2)}) %collective-permute-start.30) | collective-permute-done | bytes 131104 | tf_op jit(solution)/shard_map/ppermute | solution.py:57
  102.3 2.7 %collective-permute-done.32.refs_2_ = bf16[256,256]{1,0:T(8,128)(2,1)S(1)} collective-permute-done((bf16[256,256]{1,0:T(8,128)(2,1)S(1)}, bf16[256,256]{1,0:T(8,128)(2,1)S(1)}, u32[]{:S(2)}, u32[]{:S(2)}) %collective-permute-start.32) | collective-permute-done | bytes 131104 | tf_op jit(solution)/shard_map/ppermute | solution.py:57
  (104 shorter events, 31.0 us)
Async XLA Ops:
  2.0 17.8 %collective-permute-start.4 = (bf16[128,1152]{1,0:T(8,128)(2,1)}, bf16[128,1152]{1,0:T(8,128)(2,1)}, u32[]{:S(2)}, u32[]{:S(2)}) collective-permute-start(bf16[128,1152]{1,0:T(8,128)(2,1)} %shard_map.37.first_ref), channel_id=1, source_target_pairs={{4,0},{5,1},{6,2},{7,3},{0,4},{1,5},{2,6},{3,7},{12,8},{13,9},{14,... | collective-permute-start | bytes 884744 | tf_op jit(solution)/shard_map/ppermute | solution.py:57
  6.0 13.9 %collective-permute-start.1 = (bf16[128,1152]{1,0:T(8,128)(2,1)}, bf16[128,1152]{1,0:T(8,128)(2,1)}, u32[]{:S(2)}, u32[]{:S(2)}) collective-permute-start(bf16[128,1152]{1,0:T(8,128)(2,1)} %shard_map.37.first_ref), channel_id=1, source_target_pairs={{2,0},{3,1},{0,2},{1,3},{6,4},{7,5},{4,6},{5,7},{10,8},{11,9},{8,1... | collective-permute-start | bytes 884744 | tf_op jit(solution)/shard_map/ppermute | solution.py:57
  10.4 18.1 %collective-permute-start.3 = (bf16[256,1408]{1,0:T(8,128)(2,1)S(1)}, bf16[256,1408]{1,0:T(8,128)(2,1)S(1)}, u32[]{:S(2)}, u32[]{:S(2)}) collective-permute-start(bf16[256,1408]{1,0:T(8,128)(2,1)S(1)} %get-tuple-element.45.refs_3_.refs_1_.refs_2_.refs_14_), channel_id=1, source_target_pairs={{16,0},{17,1},{18,2},{19,3},{20,4},{21,5},{22,6},{23,7},{24,8},{25... | collective-permute-start | bytes 2162696 | tf_op jit(solution)/shard_map/ppermute | solution.py:57
  11.9 16.6 %collective-permute-start.2 = (bf16[256,1408]{1,0:T(8,128)(2,1)S(1)}, bf16[256,1408]{1,0:T(8,128)(2,1)S(1)}, u32[]{:S(2)}, u32[]{:S(2)}) collective-permute-start(bf16[256,1408]{1,0:T(8,128)(2,1)S(1)} %get-tuple-element.45.refs_3_.refs_1_.refs_2_.refs_14_), channel_id=1, source_target_pairs={{1,0},{0,1},{3,2},{2,3},{5,4},{4,5},{7,6},{6,7},{9,8},{8,9},{11,10... | collective-permute-start | bytes 2162696 | tf_op jit(solution)/shard_map/ppermute | solution.py:57
  11.9 15.7 %collective-permute-start = (bf16[256,1152]{1,0:T(8,128)(2,1)S(1)}, bf16[256,1152]{1,0:T(8,128)(2,1)S(1)}, u32[]{:S(2)}, u32[]{:S(2)}) collective-permute-start(bf16[256,1152]{1,0:T(8,128)(2,1)S(1)} %get-tuple-element.44.refs_0_), channel_id=1, source_target_pairs={{8,0},{9,1},{10,2},{11,3},{12,4},{13,5},{14,6},{15,7},{0,8},{1,9},... | collective-permute-start | bytes 1769480 | tf_op jit(solution)/shard_map/ppermute | solution.py:57
  28.8 14.8 %collective-permute-start.10 = (bf16[128,1152]{1,0:T(8,128)(2,1)}, bf16[128,1152]{1,0:T(8,128)(2,1)S(1)}, u32[]{:S(2)}, u32[]{:S(2)}) collective-permute-start(bf16[128,1152]{1,0:T(8,128)(2,1)} %copy-done.9), channel_id=1, source_target_pairs={{2,0},{3,1},{0,2},{1,3},{6,4},{7,5},{4,6},{5,7},{10,8},{11,9},{8,1... | collective-permute-start | bytes 884744 | tf_op jit(solution)/shard_map/ppermute | solution.py:57
  29.3 16.7 %collective-permute-start.9 = (bf16[128,1152]{1,0:T(8,128)(2,1)}, bf16[128,1152]{1,0:T(8,128)(2,1)}, u32[]{:S(2)}, u32[]{:S(2)}) collective-permute-start(bf16[128,1152]{1,0:T(8,128)(2,1)} %copy-done.9), channel_id=1, source_target_pairs={{4,0},{5,1},{6,2},{7,3},{0,4},{1,5},{2,6},{3,7},{12,8},{13,9},{14,... | collective-permute-start | bytes 884744 | tf_op jit(solution)/shard_map/ppermute | solution.py:57
  29.7 10.2 %collective-permute-start.6 = (bf16[128,1152]{1,0:T(8,128)(2,1)}, bf16[128,1152]{1,0:T(8,128)(2,1)S(1)}, u32[]{:S(2)}, u32[]{:S(2)}) collective-permute-start(bf16[128,1152]{1,0:T(8,128)(2,1)} %collective-permute-done.1.refs_2_), channel_id=1, source_target_pairs={{8,0},{9,1},{10,2},{11,3},{12,4},{13,5},{14,6},{15,7},{0,8},{1,9},... | collective-permute-start | bytes 884744 | tf_op jit(solution)/shard_map/ppermute | solution.py:57
  31.2 8.9 %collective-permute-start.8 = (bf16[128,1152]{1,0:T(8,128)(2,1)}, bf16[128,1152]{1,0:T(8,128)(2,1)}, u32[]{:S(2)}, u32[]{:S(2)}) collective-permute-start(bf16[128,1152]{1,0:T(8,128)(2,1)} %collective-permute-done.4.refs_4_.refs_2_), channel_id=1, source_target_pairs={{16,0},{17,1},{18,2},{19,3},{20,4},{21,5},{22,6},{23,7},{24,8},{25... | collective-permute-start | bytes 884744 | tf_op jit(solution)/shard_map/ppermute | solution.py:57
  31.9 14.2 %collective-permute-start.7 = (bf16[128,1152]{1,0:T(8,128)(2,1)}, bf16[128,1152]{1,0:T(8,128)(2,1)}, u32[]{:S(2)}, u32[]{:S(2)}) collective-permute-start(bf16[128,1152]{1,0:T(8,128)(2,1)} %collective-permute-done.4.refs_4_.refs_2_), channel_id=1, source_target_pairs={{1,0},{0,1},{3,2},{2,3},{5,4},{4,5},{7,6},{6,7},{9,8},{8,9},{11,10... | collective-permute-start | bytes 884744 | tf_op jit(solution)/shard_map/ppermute | solution.py:57
  46.1 10.6 %collective-permute-start.12 = (bf16[128,1152]{1,0:T(8,128)(2,1)S(1)}, bf16[128,1152]{1,0:T(8,128)(2,1)S(1)}, u32[]{:S(2)}, u32[]{:S(2)}) collective-permute-start(bf16[128,1152]{1,0:T(8,128)(2,1)S(1)} %collective-permute-done.10.refs_0_.refs_4_), channel_id=1, source_target_pairs={{8,0},{9,1},{10,2},{11,3},{12,4},{13,5},{14,6},{15,7},{0,8},{1,9},... | collective-permute-start | bytes 884744 | tf_op jit(solution)/shard_map/ppermute | solution.py:57
  47.5 9.4 %collective-permute-start.14 = (bf16[128,1152]{1,0:T(8,128)(2,1)}, bf16[128,1152]{1,0:T(8,128)(2,1)S(1)}, u32[]{:S(2)}, u32[]{:S(2)}) collective-permute-start(bf16[128,1152]{1,0:T(8,128)(2,1)} %collective-permute-done.9.refs_6_), channel_id=1, source_target_pairs={{16,0},{17,1},{18,2},{19,3},{20,4},{21,5},{22,6},{23,7},{24,8},{25... | collective-permute-start | bytes 884744 | tf_op jit(solution)/shard_map/ppermute | solution.py:57
  48.3 8.6 %collective-permute-start.13 = (bf16[128,1152]{1,0:T(8,128)(2,1)}, bf16[128,1152]{1,0:T(8,128)(2,1)S(1)}, u32[]{:S(2)}, u32[]{:S(2)}) collective-permute-start(bf16[128,1152]{1,0:T(8,128)(2,1)} %collective-permute-done.9.refs_6_), channel_id=1, source_target_pairs={{1,0},{0,1},{3,2},{2,3},{5,4},{4,5},{7,6},{6,7},{9,8},{8,9},{11,10... | collective-permute-start | bytes 884744 | tf_op jit(solution)/shard_map/ppermute | solution.py:57
  48.3 8.4 %collective-permute-start.15 = (bf16[256,256]{1,0:T(8,128)(2,1)S(1)}, bf16[256,256]{1,0:T(8,128)(2,1)S(1)}, u32[]{:S(2)}, u32[]{:S(2)}) collective-permute-start(bf16[256,256]{1,0:T(8,128)(2,1)S(1)} %copy-done.8), channel_id=1, source_target_pairs={{4,0},{5,1},{6,2},{7,3},{0,4},{1,5},{2,6},{3,7},{12,8},{13,9},{14,... | collective-permute-start | bytes 393224 | tf_op jit(solution)/shard_map/ppermute | solution.py:57
  58.0 6.9 %collective-permute-start.16 = (bf16[128,1152]{1,0:T(8,128)(2,1)S(1)}, bf16[128,1152]{1,0:T(8,128)(2,1)S(1)}, u32[]{:S(2)}, u32[]{:S(2)}) collective-permute-start(bf16[128,1152]{1,0:T(8,128)(2,1)S(1)} %collective-permute-done.14.refs_6_), channel_id=1, source_target_pairs={{1,0},{0,1},{3,2},{2,3},{5,4},{4,5},{7,6},{6,7},{9,8},{8,9},{11,10... | collective-permute-start | bytes 884744 | tf_op jit(solution)/shard_map/ppermute | solution.py:57
  58.1 8.9 %collective-permute-start.17 = (bf16[256,256]{1,0:T(8,128)(2,1)S(1)}, bf16[256,256]{1,0:T(8,128)(2,1)S(1)}, u32[]{:S(2)}, u32[]{:S(2)}) collective-permute-start(bf16[256,256]{1,0:T(8,128)(2,1)S(1)} %collective-permute-done.15.refs_18_), channel_id=1, source_target_pairs={{1,0},{0,1},{3,2},{2,3},{5,4},{4,5},{7,6},{6,7},{9,8},{8,9},{11,10... | collective-permute-start | bytes 393224 | tf_op jit(solution)/shard_map/ppermute | solution.py:57
  68.3 6.2 %collective-permute-start.20 = (bf16[272,256]{1,0:T(8,128)(2,1)S(1)}, bf16[272,256]{1,0:T(8,128)(2,1)S(1)}, u32[]{:S(2)}, u32[]{:S(2)}) collective-permute-start(bf16[272,256]{1,0:T(8,128)(2,1)S(1)} %get-tuple-element.74), channel_id=1, source_target_pairs={{8,0},{9,1},{10,2},{11,3},{12,4},{13,5},{14,6},{15,7},{0,8},{1,9},... | collective-permute-start | bytes 417800 | tf_op jit(solution)/shard_map/ppermute | solution.py:57
  68.9 6.5 %collective-permute-start.21 = (bf16[272,256]{1,0:T(8,128)(2,1)S(1)}, bf16[272,256]{1,0:T(8,128)(2,1)S(1)}, u32[]{:S(2)}, u32[]{:S(2)}) collective-permute-start(bf16[272,256]{1,0:T(8,128)(2,1)S(1)} %get-tuple-element.75), channel_id=1, source_target_pairs={{2,0},{3,1},{0,2},{1,3},{6,4},{7,5},{4,6},{5,7},{10,8},{11,9},{8,1... | collective-permute-start | bytes 417800 | tf_op jit(solution)/shard_map/ppermute | solution.py:57
  68.9 9.7 %collective-permute-start.22 = (bf16[272,256]{1,0:T(8,128)(2,1)S(1)}, bf16[272,256]{1,0:T(8,128)(2,1)S(1)}, u32[]{:S(2)}, u32[]{:S(2)}) collective-permute-start(bf16[272,256]{1,0:T(8,128)(2,1)S(1)} %get-tuple-element.76), channel_id=1, source_target_pairs={{10,0},{11,1},{8,2},{9,3},{14,4},{15,5},{12,6},{13,7},{2,8},{3,9},... | collective-permute-start | bytes 417800 | tf_op jit(solution)/shard_map/ppermute | solution.py:57
  78.7 8.6 %collective-permute-start.26 = (bf16[256,256]{1,0:T(8,128)(2,1)S(1)}, bf16[256,256]{1,0:T(8,128)(2,1)S(1)}, u32[]{:S(2)}, u32[]{:S(2)}) collective-permute-start(bf16[256,256]{1,0:T(8,128)(2,1)S(1)} %get-tuple-element.77.refs_7_), channel_id=1, source_target_pairs={{4,0},{5,1},{6,2},{7,3},{0,4},{1,5},{2,6},{3,7},{12,8},{13,9},{14,... | collective-permute-start | bytes 393224 | tf_op jit(solution)/shard_map/ppermute | solution.py:57
  80.1 9.1 %collective-permute-start.24 = (bf16[256,256]{1,0:T(8,128)(2,1)S(1)}, bf16[256,256]{1,0:T(8,128)(2,1)S(1)}, u32[]{:S(2)}, u32[]{:S(2)}) collective-permute-start(bf16[256,256]{1,0:T(8,128)(2,1)S(1)} %get-tuple-element.77.refs_7_), channel_id=1, source_target_pairs={{16,0},{17,1},{18,2},{19,3},{20,4},{21,5},{22,6},{23,7},{24,8},{25... | collective-permute-start | bytes 393224 | tf_op jit(solution)/shard_map/ppermute | solution.py:57
  95.3 5.6 %collective-permute-start.30 = (bf16[256,256]{1,0:T(8,128)(2,1)S(1)}, bf16[256,256]{1,0:T(8,128)(2,1)S(1)}, u32[]{:S(2)}, u32[]{:S(2)}) collective-permute-start(bf16[256,256]{1,0:T(8,128)(2,1)S(1)} %get-tuple-element.80), channel_id=1, source_target_pairs={{8,0},{9,1},{10,2},{11,3},{12,4},{13,5},{14,6},{15,7},{0,8},{1,9},... | collective-permute-start | bytes 393224 | tf_op jit(solution)/shard_map/ppermute | solution.py:57
  95.9 6.4 %collective-permute-start.31 = (bf16[256,256]{1,0:T(8,128)(2,1)S(1)}, bf16[256,256]{1,0:T(8,128)(2,1)S(1)}, u32[]{:S(2)}, u32[]{:S(2)}) collective-permute-start(bf16[256,256]{1,0:T(8,128)(2,1)S(1)} %get-tuple-element.81), channel_id=1, source_target_pairs={{2,0},{3,1},{0,2},{1,3},{6,4},{7,5},{4,6},{5,7},{10,8},{11,9},{8,1... | collective-permute-start | bytes 393224 | tf_op jit(solution)/shard_map/ppermute | solution.py:57
  95.9 9.0 %collective-permute-start.32 = (bf16[256,256]{1,0:T(8,128)(2,1)S(1)}, bf16[256,256]{1,0:T(8,128)(2,1)S(1)}, u32[]{:S(2)}, u32[]{:S(2)}) collective-permute-start(bf16[256,256]{1,0:T(8,128)(2,1)S(1)} %get-tuple-element.82), channel_id=1, source_target_pairs={{10,0},{11,1},{8,2},{9,3},{14,4},{15,5},{12,6},{13,7},{2,8},{3,9},... | collective-permute-start | bytes 393224 | tf_op jit(solution)/shard_map/ppermute | solution.py:57
  (20 other events, 88.2 us)

commit v5 on v4

--- a/solution.py
+++ b/solution.py
@@ -65,8 +65,13 @@
 VMEM = pl.BlockSpec(memory_space=pltpu.VMEM)
 
 
-def limits(mib=32):
-    return pltpu.CompilerParams(vmem_limit_bytes=mib * 2**20)
+def limits(*arrays, mib=3):
+    total = sum(max(math.prod(a.shape), 8 * BLOCK) * a.dtype.itemsize for a in arrays)
+    return pltpu.CompilerParams(vmem_limit_bytes=total * 5 // 4 + mib * 2**20)
+
+
+def shape(dims, dtype=jnp.bfloat16):
+    return jax.ShapeDtypeStruct(dims, dtype)
 
 
 def unit_of(values):
@@ -82,65 +87,97 @@
 
 def unit_kernel(emb_ref, seed_ref, first_ref, unit_ref, packed_ref, *second):
     d, head = emb_ref.shape[1], first_ref.shape[0]
-    packed_ref[:, d:] = seed_ref[...]
     unit_ref[:head, :] = first_ref[...]
     packed_ref[:head, :d] = first_ref[...]
+    packed_ref[:, d:] = seed_ref[...]
     if second:
-        rest = unit_of(emb_ref[head:, :])
-        unit_ref[head:, :] = rest
-        packed_ref[head:, :d] = rest
-        second[0][...] = rest
+        unit = unit_of(emb_ref[head:, :])
+        unit_ref[head:, :] = unit
+        packed_ref[head:, :d] = unit
+        second[0][...] = unit
 
 
 def unit_rows(embeddings, seeds, chunks):
     (m, d), c = embeddings.shape, seeds.shape[1]
-    head = chunks[0][1]
     first = pl.pallas_call(
         first_unit_kernel,
-        out_shape=jax.ShapeDtypeStruct((head, d), jnp.bfloat16),
+        out_shape=shape((chunks[0][1], d)),
         in_specs=[VMEM],
         out_specs=VMEM,
-        compiler_params=limits(),
+        compiler_params=limits(embeddings, mib=16),
     )(embeddings)
-    shapes = [(m, d), (m, d + c)] + [(rows, d) for _, rows in chunks[1:]]
+    outs = [shape((m, d)), shape((m, d + c))] + [shape((rows, d)) for _, rows in chunks[1:]]
     units, packed, *second = pl.pallas_call(
         unit_kernel,
-        out_shape=[jax.ShapeDtypeStruct(s, jnp.bfloat16) for s in shapes],
+        out_shape=outs,
         in_specs=[VMEM] * 3,
-        out_specs=[VMEM] * len(shapes),
-        compiler_params=limits(),
+        out_specs=[VMEM] * len(outs),
+        compiler_params=limits(embeddings, seeds, *outs, *outs, mib=16),
     )(embeddings, seeds, first)
-    return units, packed, [first] + second
-
-
-def joined(refs, scratch, d):
-    if scratch is None:
-        return refs[0]
-    at = 0
+    return units, packed, [[first], second]
+
+
+def flags_kernel(layout, m, t_parts, s_parts, unit, place_ref, pattern_ref, out_ref, block_ref):
+    at = layout.coords(place_ref[0], place_ref[1])
+
+    def block(offset, start):
+        row, col = layout.row_col(layout.moved(at, offset))
+        return ((col * layout.rows + row) * m + start) // BLOCK
+
+    for k, (offset, start) in enumerate(s_parts):
+        block_ref[:, k * unit : (k + 1) * unit] = jnp.full((1, unit), block(offset, start), jnp.int32)
+    blocks = block_ref[...]
+    for r, (offset, start) in enumerate(t_parts):
+        target = block(offset, start)
+        hits = blocks == pattern_ref[0, target]
+        for k in range(1, pattern_ref.shape[0]):
+            hits = hits | (blocks == pattern_ref[k, target])
+        out_ref[r : r + 1, :] = jnp.where(hits, 1, 0)
+
+
+def flags_call(layout, m, t_parts, s_parts, unit, pattern):
+    place = jnp.stack([lax.axis_index("row"), lax.axis_index("col")]).astype(jnp.int32)
+    out = shape((len(t_parts), len(s_parts) * unit), jnp.int32)
+    smem = pl.BlockSpec(memory_space=pltpu.SMEM)
+    return pl.pallas_call(
+        functools.partial(flags_kernel, layout, m, t_parts, s_parts, unit),
+        out_shape=out,
+        in_specs=[smem] * 2,
+        out_specs=VMEM,
+        scratch_shapes=[pltpu.VMEM((1, out.shape[1]), jnp.int32)],
+        compiler_params=limits(out, out),
+        cost_estimate=pl.CostEstimate(flops=0, bytes_accessed=32 * 2**20, transcendentals=0),
+    )(place, pattern.T)
+
+
+def tiles_of(refs, scratch, d):
+    tiles, held = [], 0
     for ref in refs:
-        scratch[at : at + ref.shape[0], :] = ref[:, :d]
-        at += ref.shape[0]
-    return scratch
-
-
-def gram_kernel(nt, ns, sub, d, join_t, join_s, flags, *refs):
+        rows = ref.shape[0]
+        if rows % (2 * BLOCK) == 0:
+            tiles += [(ref, k, 2 * BLOCK) for k in range(0, rows, 2 * BLOCK)]
+        else:
+            scratch[held : held + rows, :] = ref[:, :d]
+            held += rows
+    k = 0
+    while k < held:
+        rows = min(2 * BLOCK, held - k)
+        tiles.append((scratch, k, rows))
+        k += rows
+    return tiles
+
+
+def gram_kernel(nt, ns, sub, d, t_first, s_first, flags, *refs):
     t_in, s_in, refs = refs[:nt], refs[nt : nt + ns], refs[nt + ns :]
-    (kern, acc), scratch = refs[:2], list(refs[2:])
-    t_ref = joined(t_in, scratch.pop(0) if join_t else None, d)
-    if join_s:
-        s_ref = joined(s_in, scratch.pop(0), d)
-        total = s_ref.shape[0]
-        width = next(w for w in (2 * BLOCK, BLOCK, total) if total % w == 0)
-        tiles = [(s_ref, k, width) for k in range(0, total, width)]
-    else:
-        tiles = [(ref, 0, ref.shape[0]) for ref in s_in]
-    rows = kern.shape[0]
-    tall = next(h for h in (512, 384, 256, 128, rows) if rows % h == 0)
+    kern, acc, t_join, s_join = refs
+    t_tiles, s_tiles = tiles_of(t_in, t_join, d), tiles_of(s_in, s_join, d)
+    rows, cols = kern.shape
     col = 0
-    for s_ref, s_at, width in tiles:
-        for row in range(0, rows, tall):
+    for s_ref, s_at, width in s_tiles:
+        row = 0
+        for t_ref, t_at, tall in t_tiles:
             scores = lax.dot_general(
-                t_ref[row : row + tall, :],
+                t_ref[t_at : t_at + tall, :],
                 s_ref[s_at : s_at + width, :d],
                 (((1,), (1,)), ((), ())),
                 preferred_element_type=jnp.float32,
@@ -148,7 +185,10 @@
             value = jnp.exp(sharpness * scores).astype(jnp.bfloat16).astype(jnp.float32)
             for a in range(tall // sub):
                 at = row + a * sub
-                flag = flags[at // sub : at // sub + 1, col : col + width]
+                flag = flags[
+                    (t_first + at) // sub : (t_first + at) // sub + 1,
+                    s_first + col : s_first + col + width,
+                ]
                 part = jnp.where(flag > 0, value[a * sub : (a + 1) * sub], 0.0)
                 kern[at : at + sub, col : col + width] = part.astype(jnp.bfloat16)
                 total = part[:, :BLOCK]
@@ -157,25 +197,27 @@
                 if col > 0:
                     total = total + acc[at : at + sub, :]
                 acc[at : at + sub, :] = total
+            row += tall
         col += width
 
 
-def gram_call(flags, t_pieces, s_pieces, sub):
+def gram_call(flags, t_pieces, s_pieces, sub, t_first, s_first):
     rows, cols = (sum(p.shape[0] for p in pieces) for pieces in (t_pieces, s_pieces))
     d = t_pieces[0].shape[1]
-    join_t = len(t_pieces) > 1
-    join_s = any(p.shape[0] != 2 * BLOCK for p in s_pieces)
+    join = [
+        shape((max(16, sum(p.shape[0] for p in pieces if p.shape[0] % (2 * BLOCK))), d))
+        for pieces in (t_pieces, s_pieces)
+    ]
+    outs = [shape((rows, cols)), shape((rows, BLOCK), jnp.float32)]
     return pl.pallas_call(
-        functools.partial(gram_kernel, len(t_pieces), len(s_pieces), sub, d, join_t, join_s),
-        out_shape=[
-            jax.ShapeDtypeStruct((rows, cols), jnp.bfloat16),
-            jax.ShapeDtypeStruct((rows, BLOCK), jnp.float32),
-        ],
+        functools.partial(
+            gram_kernel, len(t_pieces), len(s_pieces), sub, d, t_first, s_first
+        ),
+        out_shape=outs,
         in_specs=[VMEM] * (1 + len(t_pieces) + len(s_pieces)),
         out_specs=[VMEM] * 2,
-        scratch_shapes=[pltpu.VMEM((rows, d), jnp.bfloat16)] * join_t
-        + [pltpu.VMEM((cols, d), jnp.bfloat16)] * join_s,
-        compiler_params=limits(),
+        scratch_shapes=[pltpu.VMEM(j.shape, j.dtype) for j in join],
+        compiler_params=limits(flags, *t_pieces, *s_pieces, *outs, *join),
         cost_estimate=pl.CostEstimate(
             flops=2 * rows * cols * d,
             bytes_accessed=2 * (rows + cols) * d,
@@ -212,7 +254,7 @@
             own_ref[start : start + rows, :] = part
         else:
             other_refs[piece - 1][start : start + rows, :] = part.astype(jnp.bfloat16)
-        step = min(rows, BLOCK)
+        step = math.gcd(rows, BLOCK)
         for lane in range(0, rows if na else 0, step):
             total = None
             for acc, (t0, t1, c0, c1) in zip(accs, rects):
@@ -250,7 +292,7 @@
         in_specs=[VMEM] * (len(kerns) + len(accs) + len(p_pieces)),
         out_specs=[VMEM] * len(outs),
         scratch_shapes=[pltpu.VMEM((cols, c), jnp.bfloat16)],
-        compiler_params=limits(),
+        compiler_params=limits(*kerns, *accs, *p_pieces, *outs, shape((cols, c))),
         cost_estimate=pl.CostEstimate(
             flops=2 * nt * m * cols * c,
             bytes_accessed=2 * (nt * m * cols + cols * c),
@@ -296,7 +338,7 @@
         out_shape=out_shape,
         in_specs=[VMEM] * (3 + len(got)),
         out_specs=jax.tree.map(lambda _: VMEM, out_shape),
-        compiler_params=limits(),
+        compiler_params=limits(seeds, own, totals, *got, own, own),
     )(seeds, own, totals, *got)
 
 
@@ -308,9 +350,9 @@
     layout = Layout(lax.axis_size("row"), lax.axis_size("col"))
     size = layout.sizes
     m, c = embeddings.shape[0], seed_labels.shape[1]
-    sub = min(m, BLOCK)
+    sub = math.gcd(BLOCK, m // 4) if m % (2 * BLOCK) == 0 else min(m, BLOCK)
     other = {k: range(1, size[k]) for k in size}
-    chunks = [(0, m // 2), (m // 2, m // 2)] if m % (2 * BLOCK) == 0 else [(0, m)]
+    chunks = [(0, 3 * m // 4), (3 * m // 4, m // 4)] if m % (2 * BLOCK) == 0 else [(0, m)]
 
     def fetch(values, axis, *earlier):
         return [
@@ -330,10 +372,9 @@
     both = [0] + list(other["core"])
     groups = [[(0, a, k, 0, m) for a in range(size["y"]) for k in both]]
     for start, rows in chunks:
-        groups.append([(b, 0, k, start, rows) for k in both for b in other["zh"]])
-        groups.append(
-            [(b, a, k, start, rows) for k in both for a in other["y"] for b in other["zh"]]
-        )
+        group = [(b, 0, k, start, rows) for k in both for b in other["zh"]]
+        group += [(b, a, k, start, rows) for k in both for a in other["y"] for b in other["zh"]]
+        groups.append(group)
     s_layout = [piece for group in groups for piece in group]
     whole = [(0, a, k) for a in range(size["y"]) for k in both]
     whole += [(b, 0, k) for k in both for b in other["zh"]]
@@ -341,21 +382,15 @@
     p_map = [(whole.index(piece[:3]), *piece[3:]) for piece in s_layout]
 
     t_offsets = [dict(zl=b, x=a) for b, a in t_index]
-    t_blocks = jnp.concatenate(
-        [
-            (layout.device(t_offsets[i]) * m + start + jnp.arange(0, rows, sub)) // BLOCK
-            for i, start, rows in t_layout
-        ]
-    )
-    s_blocks = jnp.concatenate(
-        [
-            (layout.device(dict(zh=b, y=a, core=k)) * m + start + jnp.arange(rows)) // BLOCK
-            for b, a, k, start, rows in s_layout
-        ]
-    )
-    flags = jnp.any(pattern[t_blocks][:, :, None] == s_blocks[None, None, :], axis=1)
-    flags = flags.astype(jnp.int32)
-
+    unit = sub
+    t_parts = [
+        (t_offsets[i], start + k) for i, start, rows in t_layout for k in range(0, rows, sub)
+    ]
+    s_parts = [
+        (dict(zh=b, y=a, core=k), start + at)
+        for b, a, k, start, rows in s_layout
+        for at in range(0, rows, unit)
+    ]
     t_pieces, kerns, accs, rects = [], [], [], []
     s_pieces = [None] * len(groups)
 
@@ -365,56 +400,53 @@
         if t0 == t1 or c0 == c1:
             return []
         kern, acc = gram_call(
-            flags[t0 // sub : t1 // sub, c0:c1],
+            flags,
             t_pieces[first:last],
             [p for g in range(g0, g1) for p in s_pieces[g]],
             sub,
+            t0,
+            c0,
         )
         kerns.append(kern)
         accs.append(acc)
         rects.append((t0, t1, c0, c1))
         return [acc]
 
-    zh, zl = fetch(parts[:1], "zh"), fetch(parts[:1], "zl")
+    zh, zl = fetch(parts[0], "zh"), fetch(parts[0], "zl")
     x, y = fetch([units], "x"), fetch([packed], "y")
     own_core = fetch([packed], "core")
-    done = zh + zl + x + y + own_core
     t_pieces += [units] + x + zl
-    zh_next, zl_next = fetch(parts[1:], "zh", *done), fetch(parts[1:], "zl", *done)
+    flags = flags_call(layout, m, t_parts, s_parts, unit, after(pattern, *zh, *zl))
+    done = zh + zl + x + y + own_core + [flags]
+    zh_next, zl_next = fetch(parts[1], "zh", *done), fetch(parts[1], "zl", *done)
     zh_y, zl_x = fetch(zh, "y", *done), fetch(zl, "x", *done)
     y_core = [fetch([v], "core", *done) for v in y]
     t_pieces += zl_x
     s_pieces[0] = [packed] + own_core + [p for v, w in zip(y, y_core) for p in [v] + w]
     first = rectangle(0, t_groups[1], 0, 1)
     zh_core = fetch(zh, "core", *done, *[p for w in y_core for p in w])
-    s_pieces[1] = zh + zh_core
-    done = zh_next + zl_next + zh_y + zl_x + zh_core + first
-    seeds_zh = fetch([seed_labels], "zh", *done)
-    zh_y_core = fetch(zh_y, "core", *done)
-    s_pieces[2] = zh_y + zh_y_core
-    if parts[1:]:
+    last = len(t_layout)
+    if zh_next:
+        done = zh_next + zl_next + zh_y + zl_x + zh_core + first
         zh_next_y, zl_next_x = fetch(zh_next, "y", *done), fetch(zl_next, "x", *done)
-        zh_next_core = fetch(zh_next, "core", *done)
+        zh_y_core, zh_next_core = fetch(zh_y, "core", *done), fetch(zh_next, "core", *done)
+        seeds_zh = fetch([seed_labels], "zh", *done)
         t_pieces += zl_next + zl_next_x
-        second = rectangle(t_groups[1], t_groups[2], 0, 1) + rectangle(0, t_groups[2], 1, 3)
-        done = zh_next_y + zl_next_x + zh_next_core + zh_y_core + seeds_zh + second
+        s_pieces[1] = zh + zh_core + zh_y + zh_y_core
+        second = rectangle(t_groups[1], t_groups[2], 0, 1) + rectangle(0, t_groups[2], 1, 2)
+        done = zh_next_y + zl_next_x + zh_next_core + zh_y_core + second
         zh_next_y_core = fetch(zh_next_y, "core", *done)
-        s_pieces[3] = zh_next + zh_next_core
-        s_pieces[4] = zh_next_y + zh_next_y_core
+        s_pieces[2] = zh_next + zh_next_core + zh_next_y + zh_next_y_core
+        rectangle(t_groups[2], last, 0, 2)
+        rectangle(0, last, 2, 3)
     else:
-        done = zh_y_core + seeds_zh
+        seeds_zh, zh_y_core = fetch([seed_labels], "zh", *done), fetch(zh_y, "core", *done)
+        s_pieces[1] = zh + zh_core + zh_y + zh_y_core
+        rectangle(t_groups[1], last, 0, 1)
+        rectangle(0, last, 1, 2)
+        done = []
     seeds_y, seeds_core = fetch(seeds_zh, "y", *done), fetch(seeds_zh, "core", *done)
     seeds_y_core = fetch(seeds_y, "core")
-    last = len(t_pieces)
-    if parts[1:]:
-        rectangle(t_groups[2], last, 0, 1)
-        rectangle(t_groups[2], last, 1, 3)
-        rectangle(0, last, 3, 4)
-        rectangle(0, last, 4, 5)
-    else:
-        rectangle(t_groups[1], last, 0, 1)
-        rectangle(0, last, 1, 2)
-        rectangle(0, last, 2, 3)
     plan = (m, t_layout, rects, p_map)
 
     def home(values):

time: 106 us -> 107 us (level)
  waiting for transfers between devices: 49.1 us -> 56.8 us
  local copies, waits for them, and re-layouts: 7.44 us -> 3.03 us
  Pallas kernels: 20.7 us -> 17.9 us
  starting transfers between devices: 27.5 us -> 28.7 us
    ppermute x33, waiting for transfers between devices: 49.1 us -> 56.8 us  [fetch(): return lax.ppermute(value, AXES, pairs)]
    unnamed x23 -> x10, local copies, waits for them, and re-layouts: 6.76 us -> 3.03 us
    pallas_call x7 -> x5, Pallas kernels: 15.2 us -> 12.5 us  [gram_call(): pl.pallas_call(functools.partial(gram_kernel, len(t_pieces), len(s_pieces...]
    ppermute x33, starting transfers between devices: 27.5 us -> 28.7 us  [fetch(): return lax.ppermute(value, AXES, pairs)]
  transfers between devices with their start and end apart: 33 -> 33, of which waited for: 18 -> 18; matrix products, arithmetic and copies ran while one was open for 1% -> 0% of each run, Pallas kernels for 15% -> 13%
where the time goes in v5:
time: 107 us
  waiting for transfers between devices  56.8 us (53%)
  starting transfers between devices  28.7 us (27%)
  Pallas kernels  17.9 us (17%)
  local copies, waits for them, and re-layouts  3.03 us (3%)
    ppermute x33, waiting for transfers between devices, fetch(): return lax.ppermute(value, AXES, pairs)  56.8 us
    ppermute x33, starting transfers between devices, fetch(): return lax.ppermute(value, AXES, pairs)  28.7 us
    pallas_call x5, Pallas kernels, gram_call(): pl.pallas_call(functools.partial(gram_kernel, len(t_pieces), len(s_pieces...  12.5 us
    unnamed x10, local copies, waits for them, and re-layouts  3.03 us
    pallas_call x2, Pallas kernels, spread_call(): pl.pallas_call(functools.partial(spread_kernel, plan, len(kerns), len(acc...  2.91 us
  transfers between devices with their start and end apart: 33, of which 18 were waited for; matrix products, arithmetic and copies ran while one was open for 0% of the time, Pallas kernels for 13%

profile of v5, /device:TPU:0, one launch (start us, length us, event | category | flops | bytes accessed | tf_op | source)
XLA Modules:
  0.0 106.6 jit_solution(7464121381148419864)
XLA Ops:
  3.4 3.0 %collective-permute-start.4 = (bf16[256,1408]{1,0:T(8,128)(2,1)S(1)}, bf16[256,1408]{1,0:T(8,128)(2,1)S(1)}, u32[]{:S(2)}, u32[]{:S(2)}) collective-permute-start(bf16[256,1408]{1,0:T(8,128)(2,1)S(1)} %get-tuple-element.43.refs_3_.refs_1_.refs_2_.refs_10_), channel_id=1, source_target_pairs={{16,0},{17,1},{18,2},{19,3},{20,4},{21,5},{22,6},{23,7},{24,8},{25... | collective-permute-start | bytes 2162696 | tf_op jit(solution)/shard_map/ppermute | solution.py:57
  9.5 2.6 %collective-permute-start = (bf16[192,1152]{1,0:T(8,128)(2,1)S(1)}, bf16[192,1152]{1,0:T(8,128)(2,1)}, u32[]{:S(2)}, u32[]{:S(2)}) collective-permute-start(bf16[192,1152]{1,0:T(8,128)(2,1)S(1)} %shard_map.37.first_ref), channel_id=1, source_target_pairs={{4,0},{5,1},{6,2},{7,3},{0,4},{1,5},{2,6},{3,7},{12,8},{13,9},{14,... | collective-permute-start | bytes 1327112 | tf_op jit(solution)/shard_map/ppermute | solution.py:57
  12.1 17.5 %collective-permute-done.1.refs_2_ = bf16[192,1152]{1,0:T(8,128)(2,1)} collective-permute-done((bf16[192,1152]{1,0:T(8,128)(2,1)S(1)}, bf16[192,1152]{1,0:T(8,128)(2,1)}, u32[]{:S(2)}, u32[]{:S(2)}) %collective-permute-start.1) | collective-permute-done | bytes 442400 | tf_op jit(solution)/shard_map/ppermute | solution.py:57
  29.7 2.4 %collective-permute-done.refs_4_.refs_6_ = bf16[192,1152]{1,0:T(8,128)(2,1)} collective-permute-done((bf16[192,1152]{1,0:T(8,128)(2,1)S(1)}, bf16[192,1152]{1,0:T(8,128)(2,1)}, u32[]{:S(2)}, u32[]{:S(2)}) %collective-permute-start) | collective-permute-done | bytes 442400 | tf_op jit(solution)/shard_map/ppermute | solution.py:57
  36.1 2.6 %collective-permute-start.9 = (bf16[64,1152]{1,0:T(8,128)(2,1)S(1)}, bf16[64,1152]{1,0:T(8,128)(2,1)S(1)}, u32[]{:S(2)}, u32[]{:S(2)}) collective-permute-start(bf16[64,1152]{1,0:T(8,128)(2,1)S(1)} %get-tuple-element.51), channel_id=1, source_target_pairs={{4,0},{5,1},{6,2},{7,3},{0,4},{1,5},{2,6},{3,7},{12,8},{13,9},{14,... | collective-permute-start | bytes 442376 | tf_op jit(solution)/shard_map/ppermute | solution.py:57
  38.7 3.5 %shard_map.40 = (bf16[704,1024]{1,0:T(8,128)(2,1)S(1)}, f32[704,128]{1,0:T(8,128)S(1)}) custom-call(s32[16,2048]{1,0:T(8,128)S(1)} %shard_map.38.flags, bf16[256,1152]{1,0:T(8,128)(2,1)S(1)} %get-tuple-element.42.refs_0_, bf16[256,1152]{1,0:T(8,128)(2,1)} %collective-permute-done.2.refs_1_, bf16[192,1152]{1,0:T(8,128)(2,1)} %collective-permute-done.1.refs_2_, ...), custom_call_target="tpu_custom_call" | custom-call | flops 1660944384 | bytes 3981312 | tf_op jit(solution)/shard_map/pallas_call | solution.py:212
  42.2 2.4 %collective-permute-done.10.refs_0_.refs_4_ = bf16[64,1152]{1,0:T(8,128)(2,1)S(1)} collective-permute-done((bf16[64,1152]{1,0:T(8,128)(2,1)S(1)}, bf16[64,1152]{1,0:T(8,128)(2,1)S(1)}, u32[]{:S(2)}, u32[]{:S(2)}) %collective-permute-start.10) | collective-permute-done | bytes 147488 | tf_op jit(solution)/shard_map/ppermute | solution.py:57
  50.0 3.6 %shard_map.42 = (bf16[896,768]{1,0:T(8,128)(2,1)S(1)}, f32[896,128]{1,0:T(8,128)S(1)}) custom-call(s32[16,2048]{1,0:T(8,128)S(1)} %shard_map.38.flags, bf16[256,1152]{1,0:T(8,128)(2,1)S(1)} %get-tuple-element.42.refs_0_, bf16[256,1152]{1,0:T(8,128)(2,1)} %collective-permute-done.2.refs_1_, bf16[192,1152]{1,0:T(8,128)(2,1)} %collective-permute-done.1.refs_2_, ...), custom_call_target="tpu_custom_call" | custom-call | flops 1585446912 | bytes 3833856 | tf_op jit(solution)/shard_map/pallas_call | solution.py:212
  53.5 3.9 %collective-permute-done.16.refs_14_ = bf16[256,256]{1,0:T(8,128)(2,1)S(1)} collective-permute-done((bf16[256,256]{1,0:T(8,128)(2,1)S(1)}, bf16[256,256]{1,0:T(8,128)(2,1)S(1)}, u32[]{:S(2)}, u32[]{:S(2)}) %collective-permute-start.16) | collective-permute-done | bytes 131104 | tf_op jit(solution)/shard_map/ppermute | solution.py:57
  57.5 1.6 %collective-permute-start.18 = (bf16[256,256]{1,0:T(8,128)(2,1)S(1)}, bf16[256,256]{1,0:T(8,128)(2,1)S(1)}, u32[]{:S(2)}, u32[]{:S(2)}) collective-permute-start(bf16[256,256]{1,0:T(8,128)(2,1)S(1)} %collective-permute-done.16.refs_14_), channel_id=1, source_target_pairs={{16,0},{17,1},{18,2},{19,3},{20,4},{21,5},{22,6},{23,7},{24,8},{25... | collective-permute-start | bytes 393224 | tf_op jit(solution)/shard_map/ppermute | solution.py:57
  59.5 3.4 %collective-permute-done.18.refs_16_ = bf16[256,256]{1,0:T(8,128)(2,1)S(1)} collective-permute-done((bf16[256,256]{1,0:T(8,128)(2,1)S(1)}, bf16[256,256]{1,0:T(8,128)(2,1)S(1)}, u32[]{:S(2)}, u32[]{:S(2)}) %collective-permute-start.18) | collective-permute-done | bytes 131104 | tf_op jit(solution)/shard_map/ppermute | solution.py:57
  63.0 2.3 %shard_map.43 = (bf16[128,1792]{1,0:T(8,128)(2,1)S(1)}, f32[128,128]{1,0:T(8,128)S(1)}) custom-call(s32[16,2048]{1,0:T(8,128)S(1)} %shard_map.38.flags, bf16[64,1152]{1,0:T(8,128)(2,1)S(1)} %collective-permute-done.10.refs_0_.refs_4_, bf16[64,1152]{1,0:T(8,128)(2,1)S(1)} %collective-permute-done.12.refs_1_.refs_5_, ...), custom_call_target="tpu_custom_call" | custom-call | flops 528482304 | bytes 4423680 | tf_op jit(solution)/shard_map/pallas_call | solution.py:212
  65.3 2.2 %shard_map.44 = (bf16[1024,256]{1,0:T(8,128)(2,1)S(1)}, f32[1024,128]{1,0:T(8,128)S(1)}) custom-call(s32[16,2048]{1,0:T(8,128)S(1)} %shard_map.38.flags, bf16[256,1152]{1,0:T(8,128)(2,1)S(1)} %get-tuple-element.42.refs_0_, bf16[256,1152]{1,0:T(8,128)(2,1)} %collective-permute-done.2.refs_1_, bf16[192,1152]{1,0:T(8,128)(2,1)} %collective-permute-done.1.refs_2_, ...), custom_call_target="tpu_custom_call" | custom-call | flops 603979776 | bytes 2949120 | tf_op jit(solution)/shard_map/pallas_call | solution.py:212
  70.5 2.0 %collective-permute-start.22 = (bf16[272,256]{1,0:T(8,128)(2,1)S(1)}, bf16[272,256]{1,0:T(8,128)(2,1)S(1)}, u32[]{:S(2)}, u32[]{:S(2)}) collective-permute-start(bf16[272,256]{1,0:T(8,128)(2,1)S(1)} %get-tuple-element.70), channel_id=1, source_target_pairs={{10,0},{11,1},{8,2},{9,3},{14,4},{15,5},{12,6},{13,7},{2,8},{3,9},... | collective-permute-start | bytes 417800 | tf_op jit(solution)/shard_map/ppermute | solution.py:57
  72.5 2.6 %collective-permute-done.20.refs_0_ = bf16[272,256]{1,0:T(8,128)(2,1)S(1)} collective-permute-done((bf16[272,256]{1,0:T(8,128)(2,1)S(1)}, bf16[272,256]{1,0:T(8,128)(2,1)S(1)}, u32[]{:S(2)}, u32[]{:S(2)}) %collective-permute-start.20) | collective-permute-done | bytes 139296 | tf_op jit(solution)/shard_map/ppermute | solution.py:57
  75.1 1.9 %collective-permute-done.21.refs_1_ = bf16[272,256]{1,0:T(8,128)(2,1)S(1)} collective-permute-done((bf16[272,256]{1,0:T(8,128)(2,1)S(1)}, bf16[272,256]{1,0:T(8,128)(2,1)S(1)}, u32[]{:S(2)}, u32[]{:S(2)}) %collective-permute-start.21) | collective-permute-done | bytes 139296 | tf_op jit(solution)/shard_map/ppermute | solution.py:57
  77.0 2.3 %collective-permute-done.22.refs_2_ = bf16[272,256]{1,0:T(8,128)(2,1)S(1)} collective-permute-done((bf16[272,256]{1,0:T(8,128)(2,1)S(1)}, bf16[272,256]{1,0:T(8,128)(2,1)S(1)}, u32[]{:S(2)}, u32[]{:S(2)}) %collective-permute-start.22) | collective-permute-done | bytes 139296 | tf_op jit(solution)/shard_map/ppermute | solution.py:57
  81.2 6.8 %collective-permute-done.26.refs_9_ = bf16[256,256]{1,0:T(8,128)(2,1)S(1)} collective-permute-done((bf16[256,256]{1,0:T(8,128)(2,1)S(1)}, bf16[256,256]{1,0:T(8,128)(2,1)S(1)}, u32[]{:S(2)}, u32[]{:S(2)}) %collective-permute-start.26) | collective-permute-done | bytes 131104 | tf_op jit(solution)/shard_map/ppermute | solution.py:57
  90.0 3.4 %collective-permute-done.28.refs_11_ = bf16[256,256]{1,0:T(8,128)(2,1)S(1)} collective-permute-done((bf16[256,256]{1,0:T(8,128)(2,1)S(1)}, bf16[256,256]{1,0:T(8,128)(2,1)S(1)}, u32[]{:S(2)}, u32[]{:S(2)}) %collective-permute-start.28) | collective-permute-done | bytes 131104 | tf_op jit(solution)/shard_map/ppermute | solution.py:57
  96.2 1.6 %collective-permute-start.30 = (bf16[256,256]{1,0:T(8,128)(2,1)S(1)}, bf16[256,256]{1,0:T(8,128)(2,1)S(1)}, u32[]{:S(2)}, u32[]{:S(2)}) collective-permute-start(bf16[256,256]{1,0:T(8,128)(2,1)S(1)} %get-tuple-element.74), channel_id=1, source_target_pairs={{8,0},{9,1},{10,2},{11,3},{12,4},{13,5},{14,6},{15,7},{0,8},{1,9},... | collective-permute-start | bytes 393224 | tf_op jit(solution)/shard_map/ppermute | solution.py:57
  97.8 2.0 %collective-permute-start.32 = (bf16[256,256]{1,0:T(8,128)(2,1)S(1)}, bf16[256,256]{1,0:T(8,128)(2,1)S(1)}, u32[]{:S(2)}, u32[]{:S(2)}) collective-permute-start(bf16[256,256]{1,0:T(8,128)(2,1)S(1)} %get-tuple-element.76), channel_id=1, source_target_pairs={{10,0},{11,1},{8,2},{9,3},{14,4},{15,5},{12,6},{13,7},{2,8},{3,9},... | collective-permute-start | bytes 393224 | tf_op jit(solution)/shard_map/ppermute | solution.py:57
  99.7 2.1 %collective-permute-done.30.refs_0_ = bf16[256,256]{1,0:T(8,128)(2,1)S(1)} collective-permute-done((bf16[256,256]{1,0:T(8,128)(2,1)S(1)}, bf16[256,256]{1,0:T(8,128)(2,1)S(1)}, u32[]{:S(2)}, u32[]{:S(2)}) %collective-permute-start.30) | collective-permute-done | bytes 131104 | tf_op jit(solution)/shard_map/ppermute | solution.py:57
  101.8 2.4 %collective-permute-done.31.refs_1_ = bf16[256,256]{1,0:T(8,128)(2,1)S(1)} collective-permute-done((bf16[256,256]{1,0:T(8,128)(2,1)S(1)}, bf16[256,256]{1,0:T(8,128)(2,1)S(1)}, u32[]{:S(2)}, u32[]{:S(2)}) %collective-permute-start.31) | collective-permute-done | bytes 131104 | tf_op jit(solution)/shard_map/ppermute | solution.py:57
  104.1 1.6 %collective-permute-done.32.refs_2_ = bf16[256,256]{1,0:T(8,128)(2,1)S(1)} collective-permute-done((bf16[256,256]{1,0:T(8,128)(2,1)S(1)}, bf16[256,256]{1,0:T(8,128)(2,1)S(1)}, u32[]{:S(2)}, u32[]{:S(2)}) %collective-permute-start.32) | collective-permute-done | bytes 131104 | tf_op jit(solution)/shard_map/ppermute | solution.py:57
  (65 shorter events, 26.9 us)
Async XLA Ops:
  3.4 29.8 %collective-permute-start.4 = (bf16[256,1408]{1,0:T(8,128)(2,1)S(1)}, bf16[256,1408]{1,0:T(8,128)(2,1)S(1)}, u32[]{:S(2)}, u32[]{:S(2)}) collective-permute-start(bf16[256,1408]{1,0:T(8,128)(2,1)S(1)} %get-tuple-element.43.refs_3_.refs_1_.refs_2_.refs_10_), channel_id=1, source_target_pairs={{16,0},{17,1},{18,2},{19,3},{20,4},{21,5},{22,6},{23,7},{24,8},{25... | collective-permute-start | bytes 2162696 | tf_op jit(solution)/shard_map/ppermute | solution.py:57
  6.4 26.8 %collective-permute-start.3 = (bf16[256,1408]{1,0:T(8,128)(2,1)S(1)}, bf16[256,1408]{1,0:T(8,128)(2,1)S(1)}, u32[]{:S(2)}, u32[]{:S(2)}) collective-permute-start(bf16[256,1408]{1,0:T(8,128)(2,1)S(1)} %get-tuple-element.43.refs_3_.refs_1_.refs_2_.refs_10_), channel_id=1, source_target_pairs={{1,0},{0,1},{3,2},{2,3},{5,4},{4,5},{7,6},{6,7},{9,8},{8,9},{11,10... | collective-permute-start | bytes 2162696 | tf_op jit(solution)/shard_map/ppermute | solution.py:57
  6.4 26.8 %collective-permute-start.2 = (bf16[256,1152]{1,0:T(8,128)(2,1)S(1)}, bf16[256,1152]{1,0:T(8,128)(2,1)}, u32[]{:S(2)}, u32[]{:S(2)}) collective-permute-start(bf16[256,1152]{1,0:T(8,128)(2,1)S(1)} %get-tuple-element.42.refs_0_), channel_id=1, source_target_pairs={{8,0},{9,1},{10,2},{11,3},{12,4},{13,5},{14,6},{15,7},{0,8},{1,9},... | collective-permute-start | bytes 1769480 | tf_op jit(solution)/shard_map/ppermute | solution.py:57
  7.9 21.8 %collective-permute-start.1 = (bf16[192,1152]{1,0:T(8,128)(2,1)S(1)}, bf16[192,1152]{1,0:T(8,128)(2,1)}, u32[]{:S(2)}, u32[]{:S(2)}) collective-permute-start(bf16[192,1152]{1,0:T(8,128)(2,1)S(1)} %shard_map.37.first_ref), channel_id=1, source_target_pairs={{2,0},{3,1},{0,2},{1,3},{6,4},{7,5},{4,6},{5,7},{10,8},{11,9},{8,1... | collective-permute-start | bytes 1327112 | tf_op jit(solution)/shard_map/ppermute | solution.py:57
  9.5 22.6 %collective-permute-start = (bf16[192,1152]{1,0:T(8,128)(2,1)S(1)}, bf16[192,1152]{1,0:T(8,128)(2,1)}, u32[]{:S(2)}, u32[]{:S(2)}) collective-permute-start(bf16[192,1152]{1,0:T(8,128)(2,1)S(1)} %shard_map.37.first_ref), channel_id=1, source_target_pairs={{4,0},{5,1},{6,2},{7,3},{0,4},{1,5},{2,6},{3,7},{12,8},{13,9},{14,... | collective-permute-start | bytes 1327112 | tf_op jit(solution)/shard_map/ppermute | solution.py:57
  33.3 12.8 %collective-permute-start.6 = (bf16[192,1152]{1,0:T(8,128)(2,1)}, bf16[192,1152]{1,0:T(8,128)(2,1)S(1)}, u32[]{:S(2)}, u32[]{:S(2)}) collective-permute-start(bf16[192,1152]{1,0:T(8,128)(2,1)} %collective-permute-done.1.refs_2_), channel_id=1, source_target_pairs={{8,0},{9,1},{10,2},{11,3},{12,4},{13,5},{14,6},{15,7},{0,8},{1,9},... | collective-permute-start | bytes 1327112 | tf_op jit(solution)/shard_map/ppermute | solution.py:57
  33.9 12.4 %collective-permute-start.8 = (bf16[192,1152]{1,0:T(8,128)(2,1)}, bf16[192,1152]{1,0:T(8,128)(2,1)S(1)}, u32[]{:S(2)}, u32[]{:S(2)}) collective-permute-start(bf16[192,1152]{1,0:T(8,128)(2,1)} %collective-permute-done.refs_4_.refs_6_), channel_id=1, source_target_pairs={{16,0},{17,1},{18,2},{19,3},{20,4},{21,5},{22,6},{23,7},{24,8},{25... | collective-permute-start | bytes 1327112 | tf_op jit(solution)/shard_map/ppermute | solution.py:57
  35.5 10.9 %collective-permute-start.7 = (bf16[192,1152]{1,0:T(8,128)(2,1)}, bf16[192,1152]{1,0:T(8,128)(2,1)S(1)}, u32[]{:S(2)}, u32[]{:S(2)}) collective-permute-start(bf16[192,1152]{1,0:T(8,128)(2,1)} %collective-permute-done.refs_4_.refs_6_), channel_id=1, source_target_pairs={{1,0},{0,1},{3,2},{2,3},{5,4},{4,5},{7,6},{6,7},{9,8},{8,9},{11,10... | collective-permute-start | bytes 1327112 | tf_op jit(solution)/shard_map/ppermute | solution.py:57
  35.6 9.0 %collective-permute-start.10 = (bf16[64,1152]{1,0:T(8,128)(2,1)S(1)}, bf16[64,1152]{1,0:T(8,128)(2,1)S(1)}, u32[]{:S(2)}, u32[]{:S(2)}) collective-permute-start(bf16[64,1152]{1,0:T(8,128)(2,1)S(1)} %get-tuple-element.51), channel_id=1, source_target_pairs={{2,0},{3,1},{0,2},{1,3},{6,4},{7,5},{4,6},{5,7},{10,8},{11,9},{8,1... | collective-permute-start | bytes 442376 | tf_op jit(solution)/shard_map/ppermute | solution.py:57
  36.1 9.9 %collective-permute-start.9 = (bf16[64,1152]{1,0:T(8,128)(2,1)S(1)}, bf16[64,1152]{1,0:T(8,128)(2,1)S(1)}, u32[]{:S(2)}, u32[]{:S(2)}) collective-permute-start(bf16[64,1152]{1,0:T(8,128)(2,1)S(1)} %get-tuple-element.51), channel_id=1, source_target_pairs={{4,0},{5,1},{6,2},{7,3},{0,4},{1,5},{2,6},{3,7},{12,8},{13,9},{14,... | collective-permute-start | bytes 442376 | tf_op jit(solution)/shard_map/ppermute | solution.py:57
  47.4 10.1 %collective-permute-start.14 = (bf16[64,1152]{1,0:T(8,128)(2,1)S(1)}, bf16[64,1152]{1,0:T(8,128)(2,1)S(1)}, u32[]{:S(2)}, u32[]{:S(2)}) collective-permute-start(bf16[64,1152]{1,0:T(8,128)(2,1)S(1)} %collective-permute-done.9.refs_6_), channel_id=1, source_target_pairs={{16,0},{17,1},{18,2},{19,3},{20,4},{21,5},{22,6},{23,7},{24,8},{25... | collective-permute-start | bytes 442376 | tf_op jit(solution)/shard_map/ppermute | solution.py:57
  47.9 9.5 %collective-permute-start.13 = (bf16[64,1152]{1,0:T(8,128)(2,1)S(1)}, bf16[64,1152]{1,0:T(8,128)(2,1)S(1)}, u32[]{:S(2)}, u32[]{:S(2)}) collective-permute-start(bf16[64,1152]{1,0:T(8,128)(2,1)S(1)} %collective-permute-done.9.refs_6_), channel_id=1, source_target_pairs={{1,0},{0,1},{3,2},{2,3},{5,4},{4,5},{7,6},{6,7},{9,8},{8,9},{11,10... | collective-permute-start | bytes 442376 | tf_op jit(solution)/shard_map/ppermute | solution.py:57
  48.1 9.3 %collective-permute-start.16 = (bf16[256,256]{1,0:T(8,128)(2,1)S(1)}, bf16[256,256]{1,0:T(8,128)(2,1)S(1)}, u32[]{:S(2)}, u32[]{:S(2)}) collective-permute-start(bf16[256,256]{1,0:T(8,128)(2,1)S(1)} %copy-done.3), channel_id=1, source_target_pairs={{4,0},{5,1},{6,2},{7,3},{0,4},{1,5},{2,6},{3,7},{12,8},{13,9},{14,... | collective-permute-start | bytes 393224 | tf_op jit(solution)/shard_map/ppermute | solution.py:57
  48.5 9.0 %collective-permute-start.12 = (bf16[64,1152]{1,0:T(8,128)(2,1)S(1)}, bf16[64,1152]{1,0:T(8,128)(2,1)S(1)}, u32[]{:S(2)}, u32[]{:S(2)}) collective-permute-start(bf16[64,1152]{1,0:T(8,128)(2,1)S(1)} %collective-permute-done.10.refs_0_.refs_4_), channel_id=1, source_target_pairs={{8,0},{9,1},{10,2},{11,3},{12,4},{13,5},{14,6},{15,7},{0,8},{1,9},... | collective-permute-start | bytes 442376 | tf_op jit(solution)/shard_map/ppermute | solution.py:57
  59.0 6.2 %collective-permute-start.15 = (bf16[64,1152]{1,0:T(8,128)(2,1)S(1)}, bf16[64,1152]{1,0:T(8,128)(2,1)S(1)}, u32[]{:S(2)}, u32[]{:S(2)}) collective-permute-start(bf16[64,1152]{1,0:T(8,128)(2,1)S(1)} %collective-permute-done.14.refs_8_), channel_id=1, source_target_pairs={{1,0},{0,1},{3,2},{2,3},{5,4},{4,5},{7,6},{6,7},{9,8},{8,9},{11,10... | collective-permute-start | bytes 442376 | tf_op jit(solution)/shard_map/ppermute | solution.py:57
  59.0 8.4 %collective-permute-start.17 = (bf16[256,256]{1,0:T(8,128)(2,1)S(1)}, bf16[256,256]{1,0:T(8,128)(2,1)S(1)}, u32[]{:S(2)}, u32[]{:S(2)}) collective-permute-start(bf16[256,256]{1,0:T(8,128)(2,1)S(1)} %collective-permute-done.16.refs_14_), channel_id=1, source_target_pairs={{1,0},{0,1},{3,2},{2,3},{5,4},{4,5},{7,6},{6,7},{9,8},{8,9},{11,10... | collective-permute-start | bytes 393224 | tf_op jit(solution)/shard_map/ppermute | solution.py:57
  69.0 6.1 %collective-permute-start.20 = (bf16[272,256]{1,0:T(8,128)(2,1)S(1)}, bf16[272,256]{1,0:T(8,128)(2,1)S(1)}, u32[]{:S(2)}, u32[]{:S(2)}) collective-permute-start(bf16[272,256]{1,0:T(8,128)(2,1)S(1)} %get-tuple-element.68), channel_id=1, source_target_pairs={{8,0},{9,1},{10,2},{11,3},{12,4},{13,5},{14,6},{15,7},{0,8},{1,9},... | collective-permute-start | bytes 417800 | tf_op jit(solution)/shard_map/ppermute | solution.py:57
  70.5 6.5 %collective-permute-start.21 = (bf16[272,256]{1,0:T(8,128)(2,1)S(1)}, bf16[272,256]{1,0:T(8,128)(2,1)S(1)}, u32[]{:S(2)}, u32[]{:S(2)}) collective-permute-start(bf16[272,256]{1,0:T(8,128)(2,1)S(1)} %get-tuple-element.69), channel_id=1, source_target_pairs={{2,0},{3,1},{0,2},{1,3},{6,4},{7,5},{4,6},{5,7},{10,8},{11,9},{8,1... | collective-permute-start | bytes 417800 | tf_op jit(solution)/shard_map/ppermute | solution.py:57
  70.5 8.8 %collective-permute-start.22 = (bf16[272,256]{1,0:T(8,128)(2,1)S(1)}, bf16[272,256]{1,0:T(8,128)(2,1)S(1)}, u32[]{:S(2)}, u32[]{:S(2)}) collective-permute-start(bf16[272,256]{1,0:T(8,128)(2,1)S(1)} %get-tuple-element.70), channel_id=1, source_target_pairs={{10,0},{11,1},{8,2},{9,3},{14,4},{15,5},{12,6},{13,7},{2,8},{3,9},... | collective-permute-start | bytes 417800 | tf_op jit(solution)/shard_map/ppermute | solution.py:57
  79.4 8.5 %collective-permute-start.26 = (bf16[256,256]{1,0:T(8,128)(2,1)S(1)}, bf16[256,256]{1,0:T(8,128)(2,1)S(1)}, u32[]{:S(2)}, u32[]{:S(2)}) collective-permute-start(bf16[256,256]{1,0:T(8,128)(2,1)S(1)} %get-tuple-element.71.refs_5_), channel_id=1, source_target_pairs={{4,0},{5,1},{6,2},{7,3},{0,4},{1,5},{2,6},{3,7},{12,8},{13,9},{14,... | collective-permute-start | bytes 393224 | tf_op jit(solution)/shard_map/ppermute | solution.py:57
  79.7 10.3 %collective-permute-start.24 = (bf16[256,256]{1,0:T(8,128)(2,1)S(1)}, bf16[256,256]{1,0:T(8,128)(2,1)S(1)}, u32[]{:S(2)}, u32[]{:S(2)}) collective-permute-start(bf16[256,256]{1,0:T(8,128)(2,1)S(1)} %get-tuple-element.71.refs_5_), channel_id=1, source_target_pairs={{16,0},{17,1},{18,2},{19,3},{20,4},{21,5},{22,6},{23,7},{24,8},{25... | collective-permute-start | bytes 393224 | tf_op jit(solution)/shard_map/ppermute | solution.py:57
  96.2 5.6 %collective-permute-start.30 = (bf16[256,256]{1,0:T(8,128)(2,1)S(1)}, bf16[256,256]{1,0:T(8,128)(2,1)S(1)}, u32[]{:S(2)}, u32[]{:S(2)}) collective-permute-start(bf16[256,256]{1,0:T(8,128)(2,1)S(1)} %get-tuple-element.74), channel_id=1, source_target_pairs={{8,0},{9,1},{10,2},{11,3},{12,4},{13,5},{14,6},{15,7},{0,8},{1,9},... | collective-permute-start | bytes 393224 | tf_op jit(solution)/shard_map/ppermute | solution.py:57
  97.8 6.4 %collective-permute-start.31 = (bf16[256,256]{1,0:T(8,128)(2,1)S(1)}, bf16[256,256]{1,0:T(8,128)(2,1)S(1)}, u32[]{:S(2)}, u32[]{:S(2)}) collective-permute-start(bf16[256,256]{1,0:T(8,128)(2,1)S(1)} %get-tuple-element.75), channel_id=1, source_target_pairs={{2,0},{3,1},{0,2},{1,3},{6,4},{7,5},{4,6},{5,7},{10,8},{11,9},{8,1... | collective-permute-start | bytes 393224 | tf_op jit(solution)/shard_map/ppermute | solution.py:57
  97.8 8.0 %collective-permute-start.32 = (bf16[256,256]{1,0:T(8,128)(2,1)S(1)}, bf16[256,256]{1,0:T(8,128)(2,1)S(1)}, u32[]{:S(2)}, u32[]{:S(2)}) collective-permute-start(bf16[256,256]{1,0:T(8,128)(2,1)S(1)} %get-tuple-element.76), channel_id=1, source_target_pairs={{10,0},{11,1},{8,2},{9,3},{14,4},{15,5},{12,6},{13,7},{2,8},{3,9},... | collective-permute-start | bytes 393224 | tf_op jit(solution)/shard_map/ppermute | solution.py:57
  (14 other events, 69.7 us)

commit v6 on v5

--- a/solution.py
+++ b/solution.py
@@ -81,40 +81,23 @@
     return scaled.astype(jnp.bfloat16)
 
 
-def first_unit_kernel(emb_ref, out_ref):
-    out_ref[...] = unit_of(emb_ref[: out_ref.shape[0], :])
-
-
-def unit_kernel(emb_ref, seed_ref, first_ref, unit_ref, packed_ref, *second):
-    d, head = emb_ref.shape[1], first_ref.shape[0]
-    unit_ref[:head, :] = first_ref[...]
-    packed_ref[:head, :d] = first_ref[...]
+def unit_kernel(emb_ref, seed_ref, unit_ref, packed_ref):
+    d = emb_ref.shape[1]
+    unit = unit_of(emb_ref[...])
+    unit_ref[...] = unit
+    packed_ref[:, :d] = unit
     packed_ref[:, d:] = seed_ref[...]
-    if second:
-        unit = unit_of(emb_ref[head:, :])
-        unit_ref[head:, :] = unit
-        packed_ref[head:, :d] = unit
-        second[0][...] = unit
-
-
-def unit_rows(embeddings, seeds, chunks):
+
+
+def unit_rows(embeddings, seeds):
     (m, d), c = embeddings.shape, seeds.shape[1]
-    first = pl.pallas_call(
-        first_unit_kernel,
-        out_shape=shape((chunks[0][1], d)),
-        in_specs=[VMEM],
-        out_specs=VMEM,
-        compiler_params=limits(embeddings, mib=16),
-    )(embeddings)
-    outs = [shape((m, d)), shape((m, d + c))] + [shape((rows, d)) for _, rows in chunks[1:]]
-    units, packed, *second = pl.pallas_call(
+    outs = [shape((m, d)), shape((m, d + c))]
+    return pl.pallas_call(
         unit_kernel,
         out_shape=outs,
-        in_specs=[VMEM] * 3,
-        out_specs=[VMEM] * len(outs),
-        compiler_params=limits(embeddings, seeds, *outs, *outs, mib=16),
-    )(embeddings, seeds, first)
-    return units, packed, [[first], second]
+        out_specs=[VMEM] * 2,
+        compiler_params=limits(embeddings, embeddings, seeds, seeds, *outs, embeddings),
+    )(embeddings, seeds)
 
 
 def flags_kernel(layout, m, t_parts, s_parts, unit, place_ref, pattern_ref, out_ref, block_ref):
@@ -146,7 +129,7 @@
         out_specs=VMEM,
         scratch_shapes=[pltpu.VMEM((1, out.shape[1]), jnp.int32)],
         compiler_params=limits(out, out),
-        cost_estimate=pl.CostEstimate(flops=0, bytes_accessed=32 * 2**20, transcendentals=0),
+        cost_estimate=pl.CostEstimate(flops=0, bytes_accessed=256 * 2**20, transcendentals=0),
     )(place, pattern.T)
 
 
@@ -161,7 +144,7 @@
             held += rows
     k = 0
     while k < held:
-        rows = min(2 * BLOCK, held - k)
+        rows = next(w for w in (2 * BLOCK, BLOCK, BLOCK // 2) if held - k >= w)
         tiles.append((scratch, k, rows))
         k += rows
     return tiles
@@ -191,6 +174,11 @@
                 ]
                 part = jnp.where(flag > 0, value[a * sub : (a + 1) * sub], 0.0)
                 kern[at : at + sub, col : col + width] = part.astype(jnp.bfloat16)
+                if width % BLOCK:
+                    if col == 0:
+                        acc[at : at + sub, :] = jnp.zeros((sub, BLOCK), jnp.float32)
+                    acc[at : at + sub, :width] += part
+                    continue
                 total = part[:, :BLOCK]
                 for b in range(1, width // BLOCK):
                     total = total + part[:, b * BLOCK : (b + 1) * BLOCK]
@@ -350,53 +338,37 @@
     layout = Layout(lax.axis_size("row"), lax.axis_size("col"))
     size = layout.sizes
     m, c = embeddings.shape[0], seed_labels.shape[1]
-    sub = math.gcd(BLOCK, m // 4) if m % (2 * BLOCK) == 0 else min(m, BLOCK)
+    sub = min(m, BLOCK)
     other = {k: range(1, size[k]) for k in size}
-    chunks = [(0, 3 * m // 4), (3 * m // 4, m // 4)] if m % (2 * BLOCK) == 0 else [(0, m)]
 
     def fetch(values, axis, *earlier):
         return [
             layout.fetch(after(v, *earlier), **{axis: k}) for k in other[axis] for v in values
         ]
 
-    units, packed, parts = unit_rows(embeddings, seed_labels, chunks)
-
-    t_index = {(b, a): b * size["x"] + a for b in range(size["zl"]) for a in range(size["x"])}
-    t_layout = [(t_index[0, a], 0, m) for a in range(size["x"])]
-    t_groups = [len(t_layout)]
-    for start, rows in chunks:
-        t_layout += [(t_index[b, 0], start, rows) for b in other["zl"]]
-        t_groups.append(len(t_layout))
-        t_layout += [(t_index[b, a], start, rows) for a in other["x"] for b in other["zl"]]
-        t_groups.append(len(t_layout))
+    t_offsets = [dict(zl=b, x=a) for b in range(size["zl"]) for a in range(size["x"])]
+    near_t = [i for i, o in enumerate(t_offsets) if o["x"] == 0 or o["zl"] == 0]
+    t_order = near_t + [i for i in range(len(t_offsets)) if i not in near_t]
+    t_layout = [(i, 0, m) for i in t_order]
     both = [0] + list(other["core"])
-    groups = [[(0, a, k, 0, m) for a in range(size["y"]) for k in both]]
-    for start, rows in chunks:
-        group = [(b, 0, k, start, rows) for k in both for b in other["zh"]]
-        group += [(b, a, k, start, rows) for k in both for a in other["y"] for b in other["zh"]]
-        groups.append(group)
-    s_layout = [piece for group in groups for piece in group]
-    whole = [(0, a, k) for a in range(size["y"]) for k in both]
-    whole += [(b, 0, k) for k in both for b in other["zh"]]
-    whole += [(b, a, k) for k in both for a in other["y"] for b in other["zh"]]
-    p_map = [(whole.index(piece[:3]), *piece[3:]) for piece in s_layout]
-
-    t_offsets = [dict(zl=b, x=a) for b, a in t_index]
-    unit = sub
-    t_parts = [
-        (t_offsets[i], start + k) for i, start, rows in t_layout for k in range(0, rows, sub)
+    groups = [
+        [(0, a, k) for a in range(size["y"]) for k in both],
+        [(b, 0, k) for k in both for b in other["zh"]],
+        [(b, a, 0) for a in other["y"] for b in other["zh"]],
+        [(b, a, k) for k in other["core"] for a in other["y"] for b in other["zh"]],
     ]
-    s_parts = [
-        (dict(zh=b, y=a, core=k), start + at)
-        for b, a, k, start, rows in s_layout
-        for at in range(0, rows, unit)
-    ]
+    s_layout = [dict(zh=b, y=a, core=k) for group in groups for b, a, k in group]
+    p_map = [(i, 0, m) for i in range(len(s_layout))]
+    t_parts = [(t_offsets[i], k) for i in t_order for k in range(0, m, sub)]
+    s_parts = [(o, k) for o in s_layout for k in range(0, m, sub)]
+    units, packed = unit_rows(embeddings, seed_labels)
+
     t_pieces, kerns, accs, rects = [], [], [], []
     s_pieces = [None] * len(groups)
 
     def rectangle(first, last, g0, g1):
-        t0, t1 = (sum(rows for _, _, rows in t_layout[:i]) for i in (first, last))
-        c0, c1 = (sum(p[4] for group in groups[:g] for p in group) for g in (g0, g1))
+        t0, t1 = first * m, last * m
+        c0, c1 = (m * sum(len(group) for group in groups[:g]) for g in (g0, g1))
         if t0 == t1 or c0 == c1:
             return []
         kern, acc = gram_call(
@@ -412,41 +384,32 @@
         rects.append((t0, t1, c0, c1))
         return [acc]
 
-    zh, zl = fetch(parts[0], "zh"), fetch(parts[0], "zl")
-    x, y = fetch([units], "x"), fetch([packed], "y")
-    own_core = fetch([packed], "core")
-    t_pieces += [units] + x + zl
-    flags = flags_call(layout, m, t_parts, s_parts, unit, after(pattern, *zh, *zl))
+    zh, zl, x = fetch([units], "zh"), fetch([units], "zl"), fetch([units], "x")
+    y, own_core = fetch([packed], "y"), fetch([packed], "core")
+    flags = flags_call(layout, m, t_parts, s_parts, sub, after(pattern, *zh))
     done = zh + zl + x + y + own_core + [flags]
-    zh_next, zl_next = fetch(parts[1], "zh", *done), fetch(parts[1], "zl", *done)
     zh_y, zl_x = fetch(zh, "y", *done), fetch(zl, "x", *done)
     y_core = [fetch([v], "core", *done) for v in y]
-    t_pieces += zl_x
+    zh_core = fetch(zh, "core", *done)
+    seeds_zh = fetch([seed_labels], "zh", *done)
+    by_offset = {(0, 0): units}
+    by_offset.update({(0, a): v for a, v in zip(other["x"], x)})
+    by_offset.update({(b, 0): v for b, v in zip(other["zl"], zl)})
+    by_offset.update({(b, a): v for (a, b), v in zip([(a, b) for a in other["x"] for b in other["zl"]], zl_x)})
+    t_pieces += [by_offset[t_offsets[i]["zl"], t_offsets[i]["x"]] for i in t_order]
     s_pieces[0] = [packed] + own_core + [p for v, w in zip(y, y_core) for p in [v] + w]
-    first = rectangle(0, t_groups[1], 0, 1)
-    zh_core = fetch(zh, "core", *done, *[p for w in y_core for p in w])
-    last = len(t_layout)
-    if zh_next:
-        done = zh_next + zl_next + zh_y + zl_x + zh_core + first
-        zh_next_y, zl_next_x = fetch(zh_next, "y", *done), fetch(zl_next, "x", *done)
-        zh_y_core, zh_next_core = fetch(zh_y, "core", *done), fetch(zh_next, "core", *done)
-        seeds_zh = fetch([seed_labels], "zh", *done)
-        t_pieces += zl_next + zl_next_x
-        s_pieces[1] = zh + zh_core + zh_y + zh_y_core
-        second = rectangle(t_groups[1], t_groups[2], 0, 1) + rectangle(0, t_groups[2], 1, 2)
-        done = zh_next_y + zl_next_x + zh_next_core + zh_y_core + second
-        zh_next_y_core = fetch(zh_next_y, "core", *done)
-        s_pieces[2] = zh_next + zh_next_core + zh_next_y + zh_next_y_core
-        rectangle(t_groups[2], last, 0, 2)
-        rectangle(0, last, 2, 3)
-    else:
-        seeds_zh, zh_y_core = fetch([seed_labels], "zh", *done), fetch(zh_y, "core", *done)
-        s_pieces[1] = zh + zh_core + zh_y + zh_y_core
-        rectangle(t_groups[1], last, 0, 1)
-        rectangle(0, last, 1, 2)
-        done = []
+    s_pieces[1] = zh + zh_core
+    s_pieces[2] = zh_y
+    early, last = len(near_t), len(t_order)
+    gram = rectangle(0, early, 0, 1) + rectangle(0, early, 1, 2)
+    done = zh_y + zl_x + zh_core + seeds_zh + gram
+    zh_y_core = fetch(zh_y, "core", *done)
+    s_pieces[3] = zh_y_core
     seeds_y, seeds_core = fetch(seeds_zh, "y", *done), fetch(seeds_zh, "core", *done)
     seeds_y_core = fetch(seeds_y, "core")
+    rectangle(early, last, 0, 2)
+    rectangle(0, last, 2, 3)
+    rectangle(0, last, 3, 4)
     plan = (m, t_layout, rects, p_map)
 
     def home(values):

time: 107 us -> 102 us (0.953)
  starting transfers between devices: 28.7 us -> 26.1 us
  waiting for transfers between devices: 56.8 us -> 55.2 us
    ppermute x33 -> x27, starting transfers between devices: 28.7 us -> 26.1 us  [fetch(): return lax.ppermute(value, AXES, pairs)]
    ppermute x33 -> x27, waiting for transfers between devices: 56.8 us -> 55.2 us  [fetch(): return lax.ppermute(value, AXES, pairs)]
    unnamed x10 -> x8, local copies, waits for them, and re-layouts: 3.03 us -> 2.67 us
  transfers between devices with their start and end apart: 33 -> 27, of which waited for: 18 -> 14; matrix products, arithmetic and copies ran while one was open for 0% -> 0% of each run, Pallas kernels for 13% -> 13%
where the time goes in v6:
time: 102 us; the launch traced here: 101 us
  waiting for transfers between devices  55.2 us (54%)
  starting transfers between devices  26.1 us (26%)
  Pallas kernels  17.1 us (17%)
  local copies, waits for them, and re-layouts  2.67 us (3%)
    ppermute x27, waiting for transfers between devices, fetch(): return lax.ppermute(value, AXES, pairs)  55.2 us
    ppermute x27, starting transfers between devices, fetch(): return lax.ppermute(value, AXES, pairs)  26.1 us
    pallas_call x5, Pallas kernels, gram_call(): pl.pallas_call(functools.partial(gram_kernel, len(t_pieces), len(s_pieces...  12.4 us
    unnamed x8, local copies, waits for them, and re-layouts  2.67 us
    pallas_call x2, Pallas kernels, spread_call(): pl.pallas_call(functools.partial(spread_kernel, plan, len(kerns), len(acc...  2.52 us
  transfers between devices with their start and end apart: 27, of which 14 were waited for; matrix products, arithmetic and copies ran while one was open for 0% of the time, Pallas kernels for 13%

profile of v6, /device:TPU:0, one launch (start us, length us, event | category | flops | bytes accessed | tf_op | source)
XLA Modules:
  0.0 101.2 jit_solution(18189719206872223459)
XLA Ops:
  2.2 3.0 %collective-permute-start.4 = (bf16[256,1408]{1,0:T(8,128)(2,1)S(1)}, bf16[256,1408]{1,0:T(8,128)(2,1)S(1)}, u32[]{:S(2)}, u32[]{:S(2)}) collective-permute-start(bf16[256,1408]{1,0:T(8,128)(2,1)S(1)} %get-tuple-element.37.refs_3_.refs_1_.refs_10_), channel_id=1, source_target_pairs={{16,0},{17,1},{18,2},{19,3},{20,4},{21,5},{22,6},{23,7},{24,8},{25... | collective-permute-start | bytes 2162696 | tf_op jit(solution)/shard_map/ppermute | solution.py:57
  5.3 2.6 %collective-permute-start = (bf16[256,1152]{1,0:T(8,128)(2,1)S(1)}, bf16[256,1152]{1,0:T(8,128)(2,1)}, u32[]{:S(2)}, u32[]{:S(2)}) collective-permute-start(bf16[256,1152]{1,0:T(8,128)(2,1)S(1)} %get-tuple-element.35.refs_0_), channel_id=1, source_target_pairs={{4,0},{5,1},{6,2},{7,3},{0,4},{1,5},{2,6},{3,7},{12,8},{13,9},{14,... | collective-permute-start | bytes 1769480 | tf_op jit(solution)/shard_map/ppermute | solution.py:57
  7.9 1.6 %collective-permute-start.2 = (bf16[256,1152]{1,0:T(8,128)(2,1)S(1)}, bf16[256,1152]{1,0:T(8,128)(2,1)S(1)}, u32[]{:S(2)}, u32[]{:S(2)}) collective-permute-start(bf16[256,1152]{1,0:T(8,128)(2,1)S(1)} %get-tuple-element.35.refs_0_), channel_id=1, source_target_pairs={{2,0},{3,1},{0,2},{1,3},{6,4},{7,5},{4,6},{5,7},{10,8},{11,9},{8,1... | collective-permute-start | bytes 1769480 | tf_op jit(solution)/shard_map/ppermute | solution.py:57
  11.0 23.8 %collective-permute-done.refs_3_.refs_5_ = bf16[256,1152]{1,0:T(8,128)(2,1)} collective-permute-done((bf16[256,1152]{1,0:T(8,128)(2,1)S(1)}, bf16[256,1152]{1,0:T(8,128)(2,1)}, u32[]{:S(2)}, u32[]{:S(2)}) %collective-permute-start) | collective-permute-done | bytes 589856 | tf_op jit(solution)/shard_map/ppermute | solution.py:57
  39.8 2.6 %shard_map.40 = (bf16[768,512]{1,0:T(8,128)(2,1)S(1)}, f32[768,128]{1,0:T(8,128)S(1)}) custom-call(s32[8,2048]{1,0:T(8,128)S(1)} %shard_map.38.flags, bf16[256,1152]{1,0:T(8,128)(2,1)S(1)} %get-tuple-element.35.refs_0_, bf16[256,1152]{1,0:T(8,128)(2,1)} %collective-permute-done.1.refs_1_, bf16[256,1152]{1,0:T(8,128)(2,1)S(1)} %collective-permute-done.2.refs_2_, ...), custom_call_target="tpu_custom_call" | custom-call | flops 905969664 | bytes 2949120 | tf_op jit(solution)/shard_map/pallas_call | solution.py:200
  42.3 3.4 %shard_map.39 = (bf16[768,1024]{1,0:T(8,128)(2,1)S(1)}, f32[768,128]{1,0:T(8,128)S(1)}) custom-call(s32[8,2048]{1,0:T(8,128)S(1)} %shard_map.38.flags, bf16[256,1152]{1,0:T(8,128)(2,1)S(1)} %get-tuple-element.35.refs_0_, bf16[256,1152]{1,0:T(8,128)(2,1)} %collective-permute-done.1.refs_1_, bf16[256,1152]{1,0:T(8,128)(2,1)S(1)} %collective-permute-done.2.refs_2_, ...), custom_call_target="tpu_custom_call" | custom-call | flops 1811939328 | bytes 4128768 | tf_op jit(solution)/shard_map/pallas_call | solution.py:200
  45.8 2.1 %collective-permute-done.9.refs_14_ = bf16[256,256]{1,0:T(8,128)(2,1)S(1)} collective-permute-done((bf16[256,256]{1,0:T(8,128)(2,1)}, bf16[256,256]{1,0:T(8,128)(2,1)S(1)}, u32[]{:S(2)}, u32[]{:S(2)}) %collective-permute-start.9) | collective-permute-done | bytes 131104 | tf_op jit(solution)/shard_map/ppermute | solution.py:57
  47.9 4.7 %collective-permute-done.8.refs_4_ = bf16[256,1152]{1,0:T(8,128)(2,1)S(1)} collective-permute-done((bf16[256,1152]{1,0:T(8,128)(2,1)}, bf16[256,1152]{1,0:T(8,128)(2,1)S(1)}, u32[]{:S(2)}, u32[]{:S(2)}) %collective-permute-start.8) | collective-permute-done | bytes 589856 | tf_op jit(solution)/shard_map/ppermute | solution.py:57
  54.1 2.0 %shard_map.42 = (bf16[1024,256]{1,0:T(8,128)(2,1)S(1)}, f32[1024,128]{1,0:T(8,128)S(1)}) custom-call(s32[8,2048]{1,0:T(8,128)S(1)} %shard_map.38.flags, bf16[256,1152]{1,0:T(8,128)(2,1)S(1)} %get-tuple-element.35.refs_0_, bf16[256,1152]{1,0:T(8,128)(2,1)} %collective-permute-done.1.refs_1_, bf16[256,1152]{1,0:T(8,128)(2,1)S(1)} %collective-permute-done.2.refs_2_, ...), custom_call_target="tpu_custom_call" | custom-call | flops 603979776 | bytes 2949120 | tf_op jit(solution)/shard_map/pallas_call | solution.py:200
  56.4 2.1 %collective-permute-done.12.refs_16_ = bf16[256,256]{1,0:T(8,128)(2,1)S(1)} collective-permute-done((bf16[256,256]{1,0:T(8,128)(2,1)S(1)}, bf16[256,256]{1,0:T(8,128)(2,1)S(1)}, u32[]{:S(2)}, u32[]{:S(2)}) %collective-permute-start.12) | collective-permute-done | bytes 131104 | tf_op jit(solution)/shard_map/ppermute | solution.py:57
  58.5 2.4 %shard_map.41 = (bf16[256,1536]{1,0:T(8,128)(2,1)S(1)}, f32[256,128]{1,0:T(8,128)S(1)}) custom-call(s32[8,2048]{1,0:T(8,128)S(1)} %shard_map.38.flags, bf16[256,1152]{1,0:T(8,128)(2,1)S(1)} %collective-permute-done.7.refs_0_.refs_3_, bf16[256,1408]{1,0:T(8,128)(2,1)S(1)} %get-tuple-element.37.refs_3_.refs_1_.refs_10_, ...), custom_call_target="tpu_custom_call" | custom-call | flops 905969664 | bytes 4128768 | tf_op jit(solution)/shard_map/pallas_call | solution.py:200
  60.8 2.0 %shard_map.43 = (bf16[1024,256]{1,0:T(8,128)(2,1)S(1)}, f32[1024,128]{1,0:T(8,128)S(1)}) custom-call(s32[8,2048]{1,0:T(8,128)S(1)} %shard_map.38.flags, bf16[256,1152]{1,0:T(8,128)(2,1)S(1)} %get-tuple-element.35.refs_0_, bf16[256,1152]{1,0:T(8,128)(2,1)} %collective-permute-done.1.refs_1_, bf16[256,1152]{1,0:T(8,128)(2,1)S(1)} %collective-permute-done.2.refs_2_, ...), custom_call_target="tpu_custom_call" | custom-call | flops 603979776 | bytes 2949120 | tf_op jit(solution)/shard_map/pallas_call | solution.py:200
  64.2 1.6 %collective-permute-start.14 = (bf16[272,256]{1,0:T(8,128)(2,1)S(1)}, bf16[272,256]{1,0:T(8,128)(2,1)S(1)}, u32[]{:S(2)}, u32[]{:S(2)}) collective-permute-start(bf16[272,256]{1,0:T(8,128)(2,1)S(1)} %get-tuple-element.56), channel_id=1, source_target_pairs={{8,0},{9,1},{10,2},{11,3},{12,4},{13,5},{14,6},{15,7},{0,8},{1,9},... | collective-permute-start | bytes 417800 | tf_op jit(solution)/shard_map/ppermute | solution.py:57
  67.7 2.6 %collective-permute-done.14.refs_0_ = bf16[272,256]{1,0:T(8,128)(2,1)S(1)} collective-permute-done((bf16[272,256]{1,0:T(8,128)(2,1)S(1)}, bf16[272,256]{1,0:T(8,128)(2,1)S(1)}, u32[]{:S(2)}, u32[]{:S(2)}) %collective-permute-start.14) | collective-permute-done | bytes 139296 | tf_op jit(solution)/shard_map/ppermute | solution.py:57
  70.3 1.9 %collective-permute-done.15.refs_1_ = bf16[272,256]{1,0:T(8,128)(2,1)S(1)} collective-permute-done((bf16[272,256]{1,0:T(8,128)(2,1)S(1)}, bf16[272,256]{1,0:T(8,128)(2,1)S(1)}, u32[]{:S(2)}, u32[]{:S(2)}) %collective-permute-start.15) | collective-permute-done | bytes 139296 | tf_op jit(solution)/shard_map/ppermute | solution.py:57
  72.2 2.2 %collective-permute-done.16.refs_2_ = bf16[272,256]{1,0:T(8,128)(2,1)S(1)} collective-permute-done((bf16[272,256]{1,0:T(8,128)(2,1)S(1)}, bf16[272,256]{1,0:T(8,128)(2,1)S(1)}, u32[]{:S(2)}, u32[]{:S(2)}) %collective-permute-start.16) | collective-permute-done | bytes 139296 | tf_op jit(solution)/shard_map/ppermute | solution.py:57
  74.6 2.3 %collective-permute-start.20 = (bf16[256,256]{1,0:T(8,128)(2,1)S(1)}, bf16[256,256]{1,0:T(8,128)(2,1)S(1)}, u32[]{:S(2)}, u32[]{:S(2)}) collective-permute-start(bf16[256,256]{1,0:T(8,128)(2,1)S(1)} %get-tuple-element.59.refs_5_), channel_id=1, source_target_pairs={{4,0},{5,1},{6,2},{7,3},{0,4},{1,5},{2,6},{3,7},{12,8},{13,9},{14,... | collective-permute-start | bytes 393224 | tf_op jit(solution)/shard_map/ppermute | solution.py:57
  78.4 4.8 %collective-permute-done.20.refs_9_ = bf16[256,256]{1,0:T(8,128)(2,1)S(1)} collective-permute-done((bf16[256,256]{1,0:T(8,128)(2,1)S(1)}, bf16[256,256]{1,0:T(8,128)(2,1)S(1)}, u32[]{:S(2)}, u32[]{:S(2)}) %collective-permute-start.20) | collective-permute-done | bytes 131104 | tf_op jit(solution)/shard_map/ppermute | solution.py:57
  83.2 1.5 %collective-permute-start.22 = (bf16[256,256]{1,0:T(8,128)(2,1)S(1)}, bf16[256,256]{1,0:T(8,128)(2,1)S(1)}, u32[]{:S(2)}, u32[]{:S(2)}) collective-permute-start(bf16[256,256]{1,0:T(8,128)(2,1)S(1)} %collective-permute-done.20.refs_9_), channel_id=1, source_target_pairs={{16,0},{17,1},{18,2},{19,3},{20,4},{21,5},{22,6},{23,7},{24,8},{25... | collective-permute-start | bytes 393224 | tf_op jit(solution)/shard_map/ppermute | solution.py:57
  85.3 2.9 %collective-permute-done.22.refs_11_ = bf16[256,256]{1,0:T(8,128)(2,1)S(1)} collective-permute-done((bf16[256,256]{1,0:T(8,128)(2,1)S(1)}, bf16[256,256]{1,0:T(8,128)(2,1)S(1)}, u32[]{:S(2)}, u32[]{:S(2)}) %collective-permute-start.22) | collective-permute-done | bytes 131104 | tf_op jit(solution)/shard_map/ppermute | solution.py:57
  90.8 1.6 %collective-permute-start.24 = (bf16[256,256]{1,0:T(8,128)(2,1)S(1)}, bf16[256,256]{1,0:T(8,128)(2,1)S(1)}, u32[]{:S(2)}, u32[]{:S(2)}) collective-permute-start(bf16[256,256]{1,0:T(8,128)(2,1)S(1)} %get-tuple-element.62), channel_id=1, source_target_pairs={{8,0},{9,1},{10,2},{11,3},{12,4},{13,5},{14,6},{15,7},{0,8},{1,9},... | collective-permute-start | bytes 393224 | tf_op jit(solution)/shard_map/ppermute | solution.py:57
  94.3 2.1 %collective-permute-done.24.refs_0_ = bf16[256,256]{1,0:T(8,128)(2,1)S(1)} collective-permute-done((bf16[256,256]{1,0:T(8,128)(2,1)S(1)}, bf16[256,256]{1,0:T(8,128)(2,1)S(1)}, u32[]{:S(2)}, u32[]{:S(2)}) %collective-permute-start.24) | collective-permute-done | bytes 131104 | tf_op jit(solution)/shard_map/ppermute | solution.py:57
  96.4 2.3 %collective-permute-done.25.refs_1_ = bf16[256,256]{1,0:T(8,128)(2,1)S(1)} collective-permute-done((bf16[256,256]{1,0:T(8,128)(2,1)S(1)}, bf16[256,256]{1,0:T(8,128)(2,1)S(1)}, u32[]{:S(2)}, u32[]{:S(2)}) %collective-permute-start.25) | collective-permute-done | bytes 131104 | tf_op jit(solution)/shard_map/ppermute | solution.py:57
  98.8 1.6 %collective-permute-done.26.refs_2_ = bf16[256,256]{1,0:T(8,128)(2,1)S(1)} collective-permute-done((bf16[256,256]{1,0:T(8,128)(2,1)S(1)}, bf16[256,256]{1,0:T(8,128)(2,1)S(1)}, u32[]{:S(2)}, u32[]{:S(2)}) %collective-permute-start.26) | collective-permute-done | bytes 131104 | tf_op jit(solution)/shard_map/ppermute | solution.py:57
  (50 shorter events, 21.4 us)
Async XLA Ops:
  2.2 34.2 %collective-permute-start.4 = (bf16[256,1408]{1,0:T(8,128)(2,1)S(1)}, bf16[256,1408]{1,0:T(8,128)(2,1)S(1)}, u32[]{:S(2)}, u32[]{:S(2)}) collective-permute-start(bf16[256,1408]{1,0:T(8,128)(2,1)S(1)} %get-tuple-element.37.refs_3_.refs_1_.refs_10_), channel_id=1, source_target_pairs={{16,0},{17,1},{18,2},{19,3},{20,4},{21,5},{22,6},{23,7},{24,8},{25... | collective-permute-start | bytes 2162696 | tf_op jit(solution)/shard_map/ppermute | solution.py:57
  5.3 31.2 %collective-permute-start.3 = (bf16[256,1408]{1,0:T(8,128)(2,1)S(1)}, bf16[256,1408]{1,0:T(8,128)(2,1)S(1)}, u32[]{:S(2)}, u32[]{:S(2)}) collective-permute-start(bf16[256,1408]{1,0:T(8,128)(2,1)S(1)} %get-tuple-element.37.refs_3_.refs_1_.refs_10_), channel_id=1, source_target_pairs={{1,0},{0,1},{3,2},{2,3},{5,4},{4,5},{7,6},{6,7},{9,8},{8,9},{11,10... | collective-permute-start | bytes 2162696 | tf_op jit(solution)/shard_map/ppermute | solution.py:57
  5.3 29.5 %collective-permute-start = (bf16[256,1152]{1,0:T(8,128)(2,1)S(1)}, bf16[256,1152]{1,0:T(8,128)(2,1)}, u32[]{:S(2)}, u32[]{:S(2)}) collective-permute-start(bf16[256,1152]{1,0:T(8,128)(2,1)S(1)} %get-tuple-element.35.refs_0_), channel_id=1, source_target_pairs={{4,0},{5,1},{6,2},{7,3},{0,4},{1,5},{2,6},{3,7},{12,8},{13,9},{14,... | collective-permute-start | bytes 1769480 | tf_op jit(solution)/shard_map/ppermute | solution.py:57
  7.9 28.5 %collective-permute-start.2 = (bf16[256,1152]{1,0:T(8,128)(2,1)S(1)}, bf16[256,1152]{1,0:T(8,128)(2,1)S(1)}, u32[]{:S(2)}, u32[]{:S(2)}) collective-permute-start(bf16[256,1152]{1,0:T(8,128)(2,1)S(1)} %get-tuple-element.35.refs_0_), channel_id=1, source_target_pairs={{2,0},{3,1},{0,2},{1,3},{6,4},{7,5},{4,6},{5,7},{10,8},{11,9},{8,1... | collective-permute-start | bytes 1769480 | tf_op jit(solution)/shard_map/ppermute | solution.py:57
  9.4 27.0 %collective-permute-start.1 = (bf16[256,1152]{1,0:T(8,128)(2,1)S(1)}, bf16[256,1152]{1,0:T(8,128)(2,1)}, u32[]{:S(2)}, u32[]{:S(2)}) collective-permute-start(bf16[256,1152]{1,0:T(8,128)(2,1)S(1)} %get-tuple-element.35.refs_0_), channel_id=1, source_target_pairs={{8,0},{9,1},{10,2},{11,3},{12,4},{13,5},{14,6},{15,7},{0,8},{1,9},... | collective-permute-start | bytes 1769480 | tf_op jit(solution)/shard_map/ppermute | solution.py:57
  36.4 5.9 %collective-permute-start.5 = (bf16[256,1408]{1,0:T(8,128)(2,1)S(1)}, bf16[256,1408]{1,0:T(8,128)(2,1)S(1)}, u32[]{:S(2)}, u32[]{:S(2)}) collective-permute-start(bf16[256,1408]{1,0:T(8,128)(2,1)S(1)} %collective-permute-done.4.refs_5_.refs_3_.refs_12_), channel_id=1, source_target_pairs={{1,0},{0,1},{3,2},{2,3},{5,4},{4,5},{7,6},{6,7},{9,8},{8,9},{11,10... | collective-permute-start | bytes 2162696 | tf_op jit(solution)/shard_map/ppermute | solution.py:57
  37.0 15.5 %collective-permute-start.8 = (bf16[256,1152]{1,0:T(8,128)(2,1)}, bf16[256,1152]{1,0:T(8,128)(2,1)S(1)}, u32[]{:S(2)}, u32[]{:S(2)}) collective-permute-start(bf16[256,1152]{1,0:T(8,128)(2,1)} %collective-permute-done.refs_3_.refs_5_), channel_id=1, source_target_pairs={{16,0},{17,1},{18,2},{19,3},{20,4},{21,5},{22,6},{23,7},{24,8},{25... | collective-permute-start | bytes 1769480 | tf_op jit(solution)/shard_map/ppermute | solution.py:57
  37.5 15.1 %collective-permute-start.7 = (bf16[256,1152]{1,0:T(8,128)(2,1)S(1)}, bf16[256,1152]{1,0:T(8,128)(2,1)S(1)}, u32[]{:S(2)}, u32[]{:S(2)}) collective-permute-start(bf16[256,1152]{1,0:T(8,128)(2,1)S(1)} %collective-permute-done.2.refs_2_), channel_id=1, source_target_pairs={{8,0},{9,1},{10,2},{11,3},{12,4},{13,5},{14,6},{15,7},{0,8},{1,9},... | collective-permute-start | bytes 1769480 | tf_op jit(solution)/shard_map/ppermute | solution.py:57
  39.0 8.8 %collective-permute-start.9 = (bf16[256,256]{1,0:T(8,128)(2,1)}, bf16[256,256]{1,0:T(8,128)(2,1)S(1)}, u32[]{:S(2)}, u32[]{:S(2)}) collective-permute-start(bf16[256,256]{1,0:T(8,128)(2,1)} %seed_ref.5), channel_id=1, source_target_pairs={{4,0},{5,1},{6,2},{7,3},{0,4},{1,5},{2,6},{3,7},{12,8},{13,9},{14,... | collective-permute-start | bytes 393224 | tf_op jit(solution)/shard_map/ppermute | solution.py:57
  52.5 8.3 %collective-permute-start.10 = (bf16[256,1152]{1,0:T(8,128)(2,1)S(1)}, bf16[256,1152]{1,0:T(8,128)(2,1)S(1)}, u32[]{:S(2)}, u32[]{:S(2)}) collective-permute-start(bf16[256,1152]{1,0:T(8,128)(2,1)S(1)} %collective-permute-done.8.refs_4_), channel_id=1, source_target_pairs={{1,0},{0,1},{3,2},{2,3},{5,4},{4,5},{7,6},{6,7},{9,8},{8,9},{11,10... | collective-permute-start | bytes 1769480 | tf_op jit(solution)/shard_map/ppermute | solution.py:57
  52.5 5.9 %collective-permute-start.12 = (bf16[256,256]{1,0:T(8,128)(2,1)S(1)}, bf16[256,256]{1,0:T(8,128)(2,1)S(1)}, u32[]{:S(2)}, u32[]{:S(2)}) collective-permute-start(bf16[256,256]{1,0:T(8,128)(2,1)S(1)} %collective-permute-done.9.refs_14_), channel_id=1, source_target_pairs={{16,0},{17,1},{18,2},{19,3},{20,4},{21,5},{22,6},{23,7},{24,8},{25... | collective-permute-start | bytes 393224 | tf_op jit(solution)/shard_map/ppermute | solution.py:57
  56.1 6.8 %collective-permute-start.11 = (bf16[256,256]{1,0:T(8,128)(2,1)S(1)}, bf16[256,256]{1,0:T(8,128)(2,1)S(1)}, u32[]{:S(2)}, u32[]{:S(2)}) collective-permute-start(bf16[256,256]{1,0:T(8,128)(2,1)S(1)} %collective-permute-done.9.refs_14_), channel_id=1, source_target_pairs={{1,0},{0,1},{3,2},{2,3},{5,4},{4,5},{7,6},{6,7},{9,8},{8,9},{11,10... | collective-permute-start | bytes 393224 | tf_op jit(solution)/shard_map/ppermute | solution.py:57
  58.5 4.4 %collective-permute-start.13 = (bf16[256,256]{1,0:T(8,128)(2,1)S(1)}, bf16[256,256]{1,0:T(8,128)(2,1)S(1)}, u32[]{:S(2)}, u32[]{:S(2)}) collective-permute-start(bf16[256,256]{1,0:T(8,128)(2,1)S(1)} %collective-permute-done.12.refs_16_), channel_id=1, source_target_pairs={{1,0},{0,1},{3,2},{2,3},{5,4},{4,5},{7,6},{6,7},{9,8},{8,9},{11,10... | collective-permute-start | bytes 393224 | tf_op jit(solution)/shard_map/ppermute | solution.py:57
  64.2 6.1 %collective-permute-start.14 = (bf16[272,256]{1,0:T(8,128)(2,1)S(1)}, bf16[272,256]{1,0:T(8,128)(2,1)S(1)}, u32[]{:S(2)}, u32[]{:S(2)}) collective-permute-start(bf16[272,256]{1,0:T(8,128)(2,1)S(1)} %get-tuple-element.56), channel_id=1, source_target_pairs={{8,0},{9,1},{10,2},{11,3},{12,4},{13,5},{14,6},{15,7},{0,8},{1,9},... | collective-permute-start | bytes 417800 | tf_op jit(solution)/shard_map/ppermute | solution.py:57
  65.7 6.5 %collective-permute-start.15 = (bf16[272,256]{1,0:T(8,128)(2,1)S(1)}, bf16[272,256]{1,0:T(8,128)(2,1)S(1)}, u32[]{:S(2)}, u32[]{:S(2)}) collective-permute-start(bf16[272,256]{1,0:T(8,128)(2,1)S(1)} %get-tuple-element.57), channel_id=1, source_target_pairs={{2,0},{3,1},{0,2},{1,3},{6,4},{7,5},{4,6},{5,7},{10,8},{11,9},{8,1... | collective-permute-start | bytes 417800 | tf_op jit(solution)/shard_map/ppermute | solution.py:57
  66.2 8.3 %collective-permute-start.16 = (bf16[272,256]{1,0:T(8,128)(2,1)S(1)}, bf16[272,256]{1,0:T(8,128)(2,1)S(1)}, u32[]{:S(2)}, u32[]{:S(2)}) collective-permute-start(bf16[272,256]{1,0:T(8,128)(2,1)S(1)} %get-tuple-element.58), channel_id=1, source_target_pairs={{10,0},{11,1},{8,2},{9,3},{14,4},{15,5},{12,6},{13,7},{2,8},{3,9},... | collective-permute-start | bytes 417800 | tf_op jit(solution)/shard_map/ppermute | solution.py:57
  74.6 8.6 %collective-permute-start.20 = (bf16[256,256]{1,0:T(8,128)(2,1)S(1)}, bf16[256,256]{1,0:T(8,128)(2,1)S(1)}, u32[]{:S(2)}, u32[]{:S(2)}) collective-permute-start(bf16[256,256]{1,0:T(8,128)(2,1)S(1)} %get-tuple-element.59.refs_5_), channel_id=1, source_target_pairs={{4,0},{5,1},{6,2},{7,3},{0,4},{1,5},{2,6},{3,7},{12,8},{13,9},{14,... | collective-permute-start | bytes 393224 | tf_op jit(solution)/shard_map/ppermute | solution.py:57
  76.9 8.4 %collective-permute-start.18 = (bf16[256,256]{1,0:T(8,128)(2,1)S(1)}, bf16[256,256]{1,0:T(8,128)(2,1)S(1)}, u32[]{:S(2)}, u32[]{:S(2)}) collective-permute-start(bf16[256,256]{1,0:T(8,128)(2,1)S(1)} %get-tuple-element.59.refs_5_), channel_id=1, source_target_pairs={{16,0},{17,1},{18,2},{19,3},{20,4},{21,5},{22,6},{23,7},{24,8},{25... | collective-permute-start | bytes 393224 | tf_op jit(solution)/shard_map/ppermute | solution.py:57
  83.2 5.0 %collective-permute-start.22 = (bf16[256,256]{1,0:T(8,128)(2,1)S(1)}, bf16[256,256]{1,0:T(8,128)(2,1)S(1)}, u32[]{:S(2)}, u32[]{:S(2)}) collective-permute-start(bf16[256,256]{1,0:T(8,128)(2,1)S(1)} %collective-permute-done.20.refs_9_), channel_id=1, source_target_pairs={{16,0},{17,1},{18,2},{19,3},{20,4},{21,5},{22,6},{23,7},{24,8},{25... | collective-permute-start | bytes 393224 | tf_op jit(solution)/shard_map/ppermute | solution.py:57
  84.8 3.4 %collective-permute-start.17 = (bf16[256,256]{1,0:T(8,128)(2,1)S(1)}, bf16[256,256]{1,0:T(8,128)(2,1)S(1)}, u32[]{:S(2)}, u32[]{:S(2)}) collective-permute-start(bf16[256,256]{1,0:T(8,128)(2,1)S(1)} %get-tuple-element.59.refs_5_), channel_id=1, source_target_pairs={{1,0},{0,1},{3,2},{2,3},{5,4},{4,5},{7,6},{6,7},{9,8},{8,9},{11,10... | collective-permute-start | bytes 393224 | tf_op jit(solution)/shard_map/ppermute | solution.py:57
  84.8 3.4 %collective-permute-start.21 = (bf16[256,256]{1,0:T(8,128)(2,1)S(1)}, bf16[256,256]{1,0:T(8,128)(2,1)S(1)}, u32[]{:S(2)}, u32[]{:S(2)}) collective-permute-start(bf16[256,256]{1,0:T(8,128)(2,1)S(1)} %collective-permute-done.20.refs_9_), channel_id=1, source_target_pairs={{1,0},{0,1},{3,2},{2,3},{5,4},{4,5},{7,6},{6,7},{9,8},{8,9},{11,10... | collective-permute-start | bytes 393224 | tf_op jit(solution)/shard_map/ppermute | solution.py:57
  90.8 5.6 %collective-permute-start.24 = (bf16[256,256]{1,0:T(8,128)(2,1)S(1)}, bf16[256,256]{1,0:T(8,128)(2,1)S(1)}, u32[]{:S(2)}, u32[]{:S(2)}) collective-permute-start(bf16[256,256]{1,0:T(8,128)(2,1)S(1)} %get-tuple-element.62), channel_id=1, source_target_pairs={{8,0},{9,1},{10,2},{11,3},{12,4},{13,5},{14,6},{15,7},{0,8},{1,9},... | collective-permute-start | bytes 393224 | tf_op jit(solution)/shard_map/ppermute | solution.py:57
  92.4 6.4 %collective-permute-start.25 = (bf16[256,256]{1,0:T(8,128)(2,1)S(1)}, bf16[256,256]{1,0:T(8,128)(2,1)S(1)}, u32[]{:S(2)}, u32[]{:S(2)}) collective-permute-start(bf16[256,256]{1,0:T(8,128)(2,1)S(1)} %get-tuple-element.63), channel_id=1, source_target_pairs={{2,0},{3,1},{0,2},{1,3},{6,4},{7,5},{4,6},{5,7},{10,8},{11,9},{8,1... | collective-permute-start | bytes 393224 | tf_op jit(solution)/shard_map/ppermute | solution.py:57
  93.4 7.0 %collective-permute-start.26 = (bf16[256,256]{1,0:T(8,128)(2,1)S(1)}, bf16[256,256]{1,0:T(8,128)(2,1)S(1)}, u32[]{:S(2)}, u32[]{:S(2)}) collective-permute-start(bf16[256,256]{1,0:T(8,128)(2,1)S(1)} %get-tuple-element.64), channel_id=1, source_target_pairs={{10,0},{11,1},{8,2},{9,3},{14,4},{15,5},{12,6},{13,7},{2,8},{3,9},... | collective-permute-start | bytes 393224 | tf_op jit(solution)/shard_map/ppermute | solution.py:57
  (7 other events, 21.8 us)

commit v7 on v5

--- a/solution.py
+++ b/solution.py
@@ -81,40 +81,32 @@
     return scaled.astype(jnp.bfloat16)
 
 
-def first_unit_kernel(emb_ref, out_ref):
-    out_ref[...] = unit_of(emb_ref[: out_ref.shape[0], :])
-
-
-def unit_kernel(emb_ref, seed_ref, first_ref, unit_ref, packed_ref, *second):
-    d, head = emb_ref.shape[1], first_ref.shape[0]
-    unit_ref[:head, :] = first_ref[...]
-    packed_ref[:head, :d] = first_ref[...]
+def unit_kernel(chunks, emb_ref, seed_ref, unit_ref, packed_ref, *outs):
+    d = emb_ref.shape[1]
+    unit = unit_of(emb_ref[...])
+    unit_ref[...] = unit
+    packed_ref[:, :d] = unit
     packed_ref[:, d:] = seed_ref[...]
-    if second:
-        unit = unit_of(emb_ref[head:, :])
-        unit_ref[head:, :] = unit
-        packed_ref[head:, :d] = unit
-        second[0][...] = unit
-
-
-def unit_rows(embeddings, seeds, chunks):
+    for out, (start, rows) in zip(outs, chunks):
+        out[:, :d] = unit_ref[start : start + rows, :]
+        for k in range((out.shape[1] - d) // seed_ref.shape[1]):
+            at = d + k * seed_ref.shape[1]
+            out[:, at : at + seed_ref.shape[1]] = seed_ref[k * rows : (k + 1) * rows, :]
+
+
+def unit_rows(embeddings, seeds, chunks, carrier):
     (m, d), c = embeddings.shape, seeds.shape[1]
-    first = pl.pallas_call(
-        first_unit_kernel,
-        out_shape=shape((chunks[0][1], d)),
-        in_specs=[VMEM],
-        out_specs=VMEM,
-        compiler_params=limits(embeddings, mib=16),
-    )(embeddings)
-    outs = [shape((m, d)), shape((m, d + c))] + [shape((rows, d)) for _, rows in chunks[1:]]
-    units, packed, *second = pl.pallas_call(
-        unit_kernel,
+    outs = [shape((m, d)), shape((m, d + c))]
+    outs += [
+        shape((rows, d + m // rows * c if i == carrier else d)) for i, (_, rows) in enumerate(chunks)
+    ]
+    units, packed, *parts = pl.pallas_call(
+        functools.partial(unit_kernel, chunks),
         out_shape=outs,
-        in_specs=[VMEM] * 3,
         out_specs=[VMEM] * len(outs),
-        compiler_params=limits(embeddings, seeds, *outs, *outs, mib=16),
-    )(embeddings, seeds, first)
-    return units, packed, [[first], second]
+        compiler_params=limits(*[embeddings, seeds] * 2, *outs, embeddings),
+    )(embeddings, seeds)
+    return units, packed, parts
 
 
 def flags_kernel(layout, m, t_parts, s_parts, unit, place_ref, pattern_ref, out_ref, block_ref):
@@ -146,7 +138,6 @@
         out_specs=VMEM,
         scratch_shapes=[pltpu.VMEM((1, out.shape[1]), jnp.int32)],
         compiler_params=limits(out, out),
-        cost_estimate=pl.CostEstimate(flops=0, bytes_accessed=32 * 2**20, transcendentals=0),
     )(place, pattern.T)
 
 
@@ -161,7 +152,7 @@
             held += rows
     k = 0
     while k < held:
-        rows = min(2 * BLOCK, held - k)
+        rows = next(w for w in (2 * BLOCK, BLOCK, BLOCK // 2) if held - k >= w)
         tiles.append((scratch, k, rows))
         k += rows
     return tiles
@@ -191,6 +182,11 @@
                 ]
                 part = jnp.where(flag > 0, value[a * sub : (a + 1) * sub], 0.0)
                 kern[at : at + sub, col : col + width] = part.astype(jnp.bfloat16)
+                if width % BLOCK:
+                    if col == 0:
+                        acc[at : at + sub, :] = jnp.zeros((sub, BLOCK), jnp.float32)
+                    acc[at : at + sub, :width] += part
+                    continue
                 total = part[:, :BLOCK]
                 for b in range(1, width // BLOCK):
                     total = total + part[:, b * BLOCK : (b + 1) * BLOCK]
@@ -235,9 +231,8 @@
     own_ref, other_refs = outs[0], outs[2:] if na else outs[1:]
     c = pcat.shape[1]
     at = 0
-    for index, start, rows in p_map:
-        ref = p_in[index]
-        pcat[at : at + rows, :] = ref[start : start + rows, ref.shape[1] - c :]
+    for index, start, rows, lane in p_map:
+        pcat[at : at + rows, :] = p_in[index][start : start + rows, lane : lane + c]
         at += rows
     row = 0
     for piece, start, rows in t_layout:
@@ -280,7 +275,7 @@
 def spread_call(kerns, accs, p_pieces, c, plan):
     m, t_layout, rects, p_map = plan
     nt = 1 + max(piece for piece, _, _ in t_layout)
-    cols = sum(rows for _, _, rows in p_map)
+    cols = sum(rows for _, _, rows, _ in p_map)
     extra = 16 if accs else 0
     outs = [jax.ShapeDtypeStruct((m, c), jnp.float32)]
     if accs:
@@ -350,28 +345,35 @@
     layout = Layout(lax.axis_size("row"), lax.axis_size("col"))
     size = layout.sizes
     m, c = embeddings.shape[0], seed_labels.shape[1]
-    sub = math.gcd(BLOCK, m // 4) if m % (2 * BLOCK) == 0 else min(m, BLOCK)
+    zh_chunks = zl_chunks = [(0, m)]
+    sub = min(m, BLOCK)
+    if m % (2 * BLOCK) == 0:
+        zh_chunks = [(0, 3 * m // 4), (3 * m // 4, m // 4)]
+        zl_chunks = [(0, m // 2), (m // 2, m // 2)]
+        sub = math.gcd(BLOCK, m // 4)
     other = {k: range(1, size[k]) for k in size}
-    chunks = [(0, 3 * m // 4), (3 * m // 4, m // 4)] if m % (2 * BLOCK) == 0 else [(0, m)]
 
     def fetch(values, axis, *earlier):
         return [
             layout.fetch(after(v, *earlier), **{axis: k}) for k in other[axis] for v in values
         ]
 
-    units, packed, parts = unit_rows(embeddings, seed_labels, chunks)
+    units, packed, parts = unit_rows(
+        embeddings, seed_labels, zh_chunks + zl_chunks, len(zh_chunks) - 1
+    )
+    zh_parts, zl_parts = parts[: len(zh_chunks)], parts[len(zh_chunks) :]
 
     t_index = {(b, a): b * size["x"] + a for b in range(size["zl"]) for a in range(size["x"])}
     t_layout = [(t_index[0, a], 0, m) for a in range(size["x"])]
     t_groups = [len(t_layout)]
-    for start, rows in chunks:
+    for start, rows in zl_chunks:
         t_layout += [(t_index[b, 0], start, rows) for b in other["zl"]]
         t_groups.append(len(t_layout))
         t_layout += [(t_index[b, a], start, rows) for a in other["x"] for b in other["zl"]]
         t_groups.append(len(t_layout))
     both = [0] + list(other["core"])
     groups = [[(0, a, k, 0, m) for a in range(size["y"]) for k in both]]
-    for start, rows in chunks:
+    for start, rows in zh_chunks:
         group = [(b, 0, k, start, rows) for k in both for b in other["zh"]]
         group += [(b, a, k, start, rows) for k in both for a in other["y"] for b in other["zh"]]
         groups.append(group)
@@ -379,7 +381,16 @@
     whole = [(0, a, k) for a in range(size["y"]) for k in both]
     whole += [(b, 0, k) for k in both for b in other["zh"]]
     whole += [(b, a, k) for k in both for a in other["y"] for b in other["zh"]]
-    p_map = [(whole.index(piece[:3]), *piece[3:]) for piece in s_layout]
+    d, tail = embeddings.shape[1], zh_chunks[-1][1]
+    p_map = [(whole.index(piece[:3]), *piece[3:], 0) for piece in s_layout]
+    seeds_map = []
+    for piece in s_layout:
+        index, (start, rows) = whole.index(piece[:3]), piece[3:]
+        if index < len(groups[0]):
+            seeds_map.append((index, start, rows, d))
+        else:
+            blocks = range(start // tail, (start + rows) // tail)
+            seeds_map += [(index, 0, tail, d + k * c) for k in blocks]
 
     t_offsets = [dict(zl=b, x=a) for b, a in t_index]
     unit = sub
@@ -412,42 +423,34 @@
         rects.append((t0, t1, c0, c1))
         return [acc]
 
-    zh, zl = fetch(parts[0], "zh"), fetch(parts[0], "zl")
+    flags = flags_call(layout, m, t_parts, s_parts, sub, pattern)
+    zh, zl = fetch(zh_parts[:1], "zh"), fetch(zl_parts[:1], "zl")
     x, y = fetch([units], "x"), fetch([packed], "y")
     own_core = fetch([packed], "core")
     t_pieces += [units] + x + zl
-    flags = flags_call(layout, m, t_parts, s_parts, unit, after(pattern, *zh, *zl))
-    done = zh + zl + x + y + own_core + [flags]
-    zh_next, zl_next = fetch(parts[1], "zh", *done), fetch(parts[1], "zl", *done)
+    done = zh + zl + x + y + own_core
+    zh_next, zl_next = fetch(zh_parts[1:], "zh", *done), fetch(zl_parts[1:], "zl", *done)
     zh_y, zl_x = fetch(zh, "y", *done), fetch(zl, "x", *done)
     y_core = [fetch([v], "core", *done) for v in y]
     t_pieces += zl_x
     s_pieces[0] = [packed] + own_core + [p for v, w in zip(y, y_core) for p in [v] + w]
-    first = rectangle(0, t_groups[1], 0, 1)
+    gram = rectangle(0, t_groups[1], 0, 1) + rectangle(t_groups[1], t_groups[2], 0, 1)
     zh_core = fetch(zh, "core", *done, *[p for w in y_core for p in w])
     last = len(t_layout)
+    done = zh_next + zl_next + zh_y + zl_x + zh_core + gram
+    zh_y_core = fetch(zh_y, "core", *done)
+    s_pieces[1] = zh + zh_core + zh_y + zh_y_core
+    gram = rectangle(0, t_groups[2], 1, 2)
     if zh_next:
-        done = zh_next + zl_next + zh_y + zl_x + zh_core + first
         zh_next_y, zl_next_x = fetch(zh_next, "y", *done), fetch(zl_next, "x", *done)
-        zh_y_core, zh_next_core = fetch(zh_y, "core", *done), fetch(zh_next, "core", *done)
-        seeds_zh = fetch([seed_labels], "zh", *done)
+        zh_next_core = fetch(zh_next, "core", *done)
         t_pieces += zl_next + zl_next_x
-        s_pieces[1] = zh + zh_core + zh_y + zh_y_core
-        second = rectangle(t_groups[1], t_groups[2], 0, 1) + rectangle(0, t_groups[2], 1, 2)
-        done = zh_next_y + zl_next_x + zh_next_core + zh_y_core + second
+        done = zh_next_y + zl_next_x + zh_next_core + zh_y_core + gram
         zh_next_y_core = fetch(zh_next_y, "core", *done)
         s_pieces[2] = zh_next + zh_next_core + zh_next_y + zh_next_y_core
         rectangle(t_groups[2], last, 0, 2)
         rectangle(0, last, 2, 3)
-    else:
-        seeds_zh, zh_y_core = fetch([seed_labels], "zh", *done), fetch(zh_y, "core", *done)
-        s_pieces[1] = zh + zh_core + zh_y + zh_y_core
-        rectangle(t_groups[1], last, 0, 1)
-        rectangle(0, last, 1, 2)
-        done = []
-    seeds_y, seeds_core = fetch(seeds_zh, "y", *done), fetch(seeds_zh, "core", *done)
-    seeds_y_core = fetch(seeds_y, "core")
-    plan = (m, t_layout, rects, p_map)
+    plan = (m, t_layout, rects)
 
     def home(values):
         return [
@@ -461,8 +464,8 @@
         near = [p for v in [panel] + near for p in [v] + fetch([v], "core")]
         return near + far + fetch(far, "core") + far_y + fetch(far_y, "core")
 
-    seeds = s_pieces[0] + seeds_zh + seeds_core + seeds_y + seeds_y_core
-    own, totals, *others = spread_call(kerns, accs, seeds, c, plan)
+    seeds = s_pieces[0] + s_pieces[-1]
+    own, totals, *others = spread_call(kerns, accs, seeds, c, (*plan, seeds_map))
     panel, totals = update(
         first_update_kernel,
         seed_labels,
@@ -474,7 +477,7 @@
             jax.ShapeDtypeStruct((m, BLOCK), jnp.float32),
         ],
     )
-    own, *others = spread_call(kerns, [], panels(panel), c, plan)
+    own, *others = spread_call(kerns, [], panels(panel), c, (*plan, p_map))
     return update(
         last_update_kernel,
         seed_labels,

time: 107 us -> 103 us (0.963)
  waiting for transfers between devices: 56.8 us -> 51.3 us
  local copies, waits for them, and re-layouts: 3.03 us -> 4.34 us
    ppermute x33 -> x29, waiting for transfers between devices: 56.8 us -> 51.3 us  [fetch(): return lax.ppermute(value, AXES, pairs)]
    unnamed x10 -> x18, local copies, waits for them, and re-layouts: 3.03 us -> 4.34 us
    ppermute x33 -> x29, starting transfers between devices: 28.7 us -> 29.4 us  [fetch(): return lax.ppermute(value, AXES, pairs)]
  transfers between devices with their start and end apart: 33 -> 29, of which waited for: 18 -> 16; matrix products, arithmetic and copies ran while one was open for 0% -> 0% of each run, Pallas kernels for 13% -> 11%
where the time goes in v7:
time: 103 us
  waiting for transfers between devices  51.3 us (50%)
  starting transfers between devices  29.4 us (29%)
  Pallas kernels  17.8 us (17%)
  local copies, waits for them, and re-layouts  4.34 us (4%)
    ppermute x29, waiting for transfers between devices, fetch(): return lax.ppermute(value, AXES, pairs)  51.3 us
    ppermute x29, starting transfers between devices, fetch(): return lax.ppermute(value, AXES, pairs)  29.4 us
    pallas_call x5, Pallas kernels, gram_call(): pl.pallas_call(functools.partial(gram_kernel, len(t_pieces), len(s_pieces...  12.1 us
    unnamed x18, local copies, waits for them, and re-layouts  4.34 us
    pallas_call x2, Pallas kernels, spread_call(): pl.pallas_call(functools.partial(spread_kernel, plan, len(kerns), len(acc...  2.57 us
  transfers between devices with their start and end apart: 29, of which 16 were waited for; matrix products, arithmetic and copies ran while one was open for 0% of the time, Pallas kernels for 11%

profile of v7, /device:TPU:0, one launch (start us, length us, event | category | flops | bytes accessed | tf_op | source)
XLA Modules:
  0.0 103.0 jit_solution(14850535884469625995)
XLA Ops:
  3.4 2.5 %collective-permute-start.3 = (bf16[256,1408]{1,0:T(8,128)(2,1)S(1)}, bf16[256,1408]{1,0:T(8,128)(2,1)S(1)}, u32[]{:S(2)}, u32[]{:S(2)}) collective-permute-start(bf16[256,1408]{1,0:T(8,128)(2,1)S(1)} %get-tuple-element.44.refs_3_.refs_1_.refs_2_.refs_10_), channel_id=1, source_target_pairs={{16,0},{17,1},{18,2},{19,3},{20,4},{21,5},{22,6},{23,7},{24,8},{25... | collective-permute-start | bytes 2162696 | tf_op jit(solution)/shard_map/ppermute | solution.py:57
  8.2 2.6 %collective-permute-start.4 = (bf16[192,1152]{1,0:T(8,128)(2,1)S(1)}, bf16[192,1152]{1,0:T(8,128)(2,1)}, u32[]{:S(2)}, u32[]{:S(2)}) collective-permute-start(bf16[192,1152]{1,0:T(8,128)(2,1)S(1)} %get-tuple-element.45), channel_id=1, source_target_pairs={{4,0},{5,1},{6,2},{7,3},{0,4},{1,5},{2,6},{3,7},{12,8},{13,9},{14,... | collective-permute-start | bytes 1327112 | tf_op jit(solution)/shard_map/ppermute | solution.py:57
  10.8 1.6 %collective-permute-start.1 = (bf16[128,1152]{1,0:T(8,128)(2,1)S(1)}, bf16[128,1152]{1,0:T(8,128)(2,1)}, u32[]{:S(2)}, u32[]{:S(2)}) collective-permute-start(bf16[128,1152]{1,0:T(8,128)(2,1)S(1)} %get-tuple-element.43), channel_id=1, source_target_pairs={{2,0},{3,1},{0,2},{1,3},{6,4},{7,5},{4,6},{5,7},{10,8},{11,9},{8,1... | collective-permute-start | bytes 884744 | tf_op jit(solution)/shard_map/ppermute | solution.py:57
  12.4 14.3 %collective-permute-done.1.refs_2_ = bf16[128,1152]{1,0:T(8,128)(2,1)} collective-permute-done((bf16[128,1152]{1,0:T(8,128)(2,1)S(1)}, bf16[128,1152]{1,0:T(8,128)(2,1)}, u32[]{:S(2)}, u32[]{:S(2)}) %collective-permute-start.1) | collective-permute-done | bytes 294944 | tf_op jit(solution)/shard_map/ppermute | solution.py:57
  26.7 4.0 %collective-permute-done.4.refs_4_.refs_6_ = bf16[192,1152]{1,0:T(8,128)(2,1)} collective-permute-done((bf16[192,1152]{1,0:T(8,128)(2,1)S(1)}, bf16[192,1152]{1,0:T(8,128)(2,1)}, u32[]{:S(2)}, u32[]{:S(2)}) %collective-permute-start.4) | collective-permute-done | bytes 442400 | tf_op jit(solution)/shard_map/ppermute | solution.py:57
  34.5 3.5 %collective-permute-start.9 = (bf16[64,2176]{1,0:T(8,128)(2,1)}, bf16[64,2176]{1,0:T(8,128)(2,1)S(1)}, u32[]{:S(2)}, u32[]{:S(2)}) collective-permute-start(bf16[64,2176]{1,0:T(8,128)(2,1)} %copy-done.8), channel_id=1, source_target_pairs={{4,0},{5,1},{6,2},{7,3},{0,4},{1,5},{2,6},{3,7},{12,8},{13,9},{14,... | collective-permute-start | bytes 835592 | tf_op jit(solution)/shard_map/ppermute | solution.py:57
  42.2 3.3 %shard_map.39 = (bf16[640,1024]{1,0:T(8,128)(2,1)S(1)}, f32[640,128]{1,0:T(8,128)S(1)}) custom-call(s32[16,2048]{1,0:T(8,128)S(1)} %shard_map.37.flags, bf16[256,1152]{1,0:T(8,128)(2,1)S(1)} %copy-done.3, bf16[256,1152]{1,0:T(8,128)(2,1)S(1)} %copy-done.5, bf16[128,1152]{1,0:T(8,128)(2,1)} %collective-permute-done.1.refs_2_, ...), custom_call_target="tpu_custom_call" | custom-call | flops 1509949440 | bytes 3833856 | tf_op jit(solution)/shard_map/pallas_call | solution.py:208
  45.5 2.2 %collective-permute-done.9.refs_6_.refs_14_ = bf16[64,2176]{1,0:T(8,128)(2,1)S(1)} collective-permute-done((bf16[64,2176]{1,0:T(8,128)(2,1)}, bf16[64,2176]{1,0:T(8,128)(2,1)S(1)}, u32[]{:S(2)}, u32[]{:S(2)}) %collective-permute-start.9) | collective-permute-done | bytes 278560 | tf_op jit(solution)/shard_map/ppermute | solution.py:57
  47.6 1.8 %collective-permute-done.10.refs_0_.refs_4_ = bf16[128,1152]{1,0:T(8,128)(2,1)S(1)} collective-permute-done((bf16[128,1152]{1,0:T(8,128)(2,1)}, bf16[128,1152]{1,0:T(8,128)(2,1)S(1)}, u32[]{:S(2)}, u32[]{:S(2)}) %collective-permute-start.10) | collective-permute-done | bytes 294944 | tf_op jit(solution)/shard_map/ppermute | solution.py:57
  51.6 3.2 %shard_map.41 = (bf16[768,768]{1,0:T(8,128)(2,1)S(1)}, f32[768,128]{1,0:T(8,128)S(1)}) custom-call(s32[16,2048]{1,0:T(8,128)S(1)} %shard_map.37.flags, bf16[256,1152]{1,0:T(8,128)(2,1)S(1)} %copy-done.3, bf16[256,1152]{1,0:T(8,128)(2,1)S(1)} %copy-done.5, bf16[128,1152]{1,0:T(8,128)(2,1)} %collective-permute-done.1.refs_2_, ...), custom_call_target="tpu_custom_call" | custom-call | flops 1358954496 | bytes 3538944 | tf_op jit(solution)/shard_map/pallas_call | solution.py:208
  54.8 4.3 %collective-permute-done.14.refs_8_.refs_16_ = bf16[64,2176]{1,0:T(8,128)(2,1)S(1)} collective-permute-done((bf16[64,2176]{1,0:T(8,128)(2,1)S(1)}, bf16[64,2176]{1,0:T(8,128)(2,1)S(1)}, u32[]{:S(2)}, u32[]{:S(2)}) %collective-permute-start.14) | collective-permute-done | bytes 278560 | tf_op jit(solution)/shard_map/ppermute | solution.py:57
  59.1 2.7 %shard_map.42 = (bf16[256,1792]{1,0:T(8,128)(2,1)S(1)}, f32[256,128]{1,0:T(8,128)S(1)}) custom-call(s32[16,2048]{1,0:T(8,128)S(1)} %shard_map.37.flags, bf16[128,1152]{1,0:T(8,128)(2,1)S(1)} %collective-permute-done.10.refs_0_.refs_4_, bf16[128,1152]{1,0:T(8,128)(2,1)S(1)} %collective-permute-done.12.refs_1_.refs_5_, ...), custom_call_target="tpu_custom_call" | custom-call | flops 1056964608 | bytes 4718592 | tf_op jit(solution)/shard_map/pallas_call | solution.py:208
  61.8 2.0 %shard_map.43 = (bf16[1024,256]{1,0:T(8,128)(2,1)S(1)}, f32[1024,128]{1,0:T(8,128)S(1)}) custom-call(s32[16,2048]{1,0:T(8,128)S(1)} %shard_map.37.flags, bf16[256,1152]{1,0:T(8,128)(2,1)S(1)} %copy-done.3, bf16[256,1152]{1,0:T(8,128)(2,1)S(1)} %copy-done.5, bf16[128,1152]{1,0:T(8,128)(2,1)} %collective-permute-done.1.refs_2_, ...), custom_call_target="tpu_custom_call" | custom-call | flops 603979776 | bytes 2949120 | tf_op jit(solution)/shard_map/pallas_call | solution.py:208
  65.1 1.6 %collective-permute-start.16 = (bf16[272,256]{1,0:T(8,128)(2,1)S(1)}, bf16[272,256]{1,0:T(8,128)(2,1)S(1)}, u32[]{:S(2)}, u32[]{:S(2)}) collective-permute-start(bf16[272,256]{1,0:T(8,128)(2,1)S(1)} %get-tuple-element.70), channel_id=1, source_target_pairs={{8,0},{9,1},{10,2},{11,3},{12,4},{13,5},{14,6},{15,7},{0,8},{1,9},... | collective-permute-start | bytes 417800 | tf_op jit(solution)/shard_map/ppermute | solution.py:57
  66.7 2.4 %collective-permute-start.17 = (bf16[272,256]{1,0:T(8,128)(2,1)S(1)}, bf16[272,256]{1,0:T(8,128)(2,1)S(1)}, u32[]{:S(2)}, u32[]{:S(2)}) collective-permute-start(bf16[272,256]{1,0:T(8,128)(2,1)S(1)} %get-tuple-element.71), channel_id=1, source_target_pairs={{2,0},{3,1},{0,2},{1,3},{6,4},{7,5},{4,6},{5,7},{10,8},{11,9},{8,1... | collective-permute-start | bytes 417800 | tf_op jit(solution)/shard_map/ppermute | solution.py:57
  69.1 2.2 %collective-permute-done.16.refs_0_ = bf16[272,256]{1,0:T(8,128)(2,1)S(1)} collective-permute-done((bf16[272,256]{1,0:T(8,128)(2,1)S(1)}, bf16[272,256]{1,0:T(8,128)(2,1)S(1)}, u32[]{:S(2)}, u32[]{:S(2)}) %collective-permute-start.16) | collective-permute-done | bytes 139296 | tf_op jit(solution)/shard_map/ppermute | solution.py:57
  71.3 2.2 %collective-permute-done.17.refs_1_ = bf16[272,256]{1,0:T(8,128)(2,1)S(1)} collective-permute-done((bf16[272,256]{1,0:T(8,128)(2,1)S(1)}, bf16[272,256]{1,0:T(8,128)(2,1)S(1)}, u32[]{:S(2)}, u32[]{:S(2)}) %collective-permute-start.17) | collective-permute-done | bytes 139296 | tf_op jit(solution)/shard_map/ppermute | solution.py:57
  73.5 2.6 %collective-permute-done.18.refs_2_ = bf16[272,256]{1,0:T(8,128)(2,1)S(1)} collective-permute-done((bf16[272,256]{1,0:T(8,128)(2,1)S(1)}, bf16[272,256]{1,0:T(8,128)(2,1)S(1)}, u32[]{:S(2)}, u32[]{:S(2)}) %collective-permute-start.18) | collective-permute-done | bytes 139296 | tf_op jit(solution)/shard_map/ppermute | solution.py:57
  76.2 2.4 %collective-permute-start.22 = (bf16[256,256]{1,0:T(8,128)(2,1)S(1)}, bf16[256,256]{1,0:T(8,128)(2,1)S(1)}, u32[]{:S(2)}, u32[]{:S(2)}) collective-permute-start(bf16[256,256]{1,0:T(8,128)(2,1)S(1)} %get-tuple-element.73.refs_5_), channel_id=1, source_target_pairs={{4,0},{5,1},{6,2},{7,3},{0,4},{1,5},{2,6},{3,7},{12,8},{13,9},{14,... | collective-permute-start | bytes 393224 | tf_op jit(solution)/shard_map/ppermute | solution.py:57
  80.0 5.0 %collective-permute-done.22.refs_9_ = bf16[256,256]{1,0:T(8,128)(2,1)S(1)} collective-permute-done((bf16[256,256]{1,0:T(8,128)(2,1)S(1)}, bf16[256,256]{1,0:T(8,128)(2,1)S(1)}, u32[]{:S(2)}, u32[]{:S(2)}) %collective-permute-start.22) | collective-permute-done | bytes 131104 | tf_op jit(solution)/shard_map/ppermute | solution.py:57
  87.1 2.9 %collective-permute-done.24.refs_11_ = bf16[256,256]{1,0:T(8,128)(2,1)S(1)} collective-permute-done((bf16[256,256]{1,0:T(8,128)(2,1)S(1)}, bf16[256,256]{1,0:T(8,128)(2,1)S(1)}, u32[]{:S(2)}, u32[]{:S(2)}) %collective-permute-start.24) | collective-permute-done | bytes 131104 | tf_op jit(solution)/shard_map/ppermute | solution.py:57
  92.6 1.7 %collective-permute-start.26 = (bf16[256,256]{1,0:T(8,128)(2,1)S(1)}, bf16[256,256]{1,0:T(8,128)(2,1)S(1)}, u32[]{:S(2)}, u32[]{:S(2)}) collective-permute-start(bf16[256,256]{1,0:T(8,128)(2,1)S(1)} %get-tuple-element.76), channel_id=1, source_target_pairs={{8,0},{9,1},{10,2},{11,3},{12,4},{13,5},{14,6},{15,7},{0,8},{1,9},... | collective-permute-start | bytes 393224 | tf_op jit(solution)/shard_map/ppermute | solution.py:57
  96.2 2.1 %collective-permute-done.26.refs_0_ = bf16[256,256]{1,0:T(8,128)(2,1)S(1)} collective-permute-done((bf16[256,256]{1,0:T(8,128)(2,1)S(1)}, bf16[256,256]{1,0:T(8,128)(2,1)S(1)}, u32[]{:S(2)}, u32[]{:S(2)}) %collective-permute-start.26) | collective-permute-done | bytes 131104 | tf_op jit(solution)/shard_map/ppermute | solution.py:57
  98.2 2.4 %collective-permute-done.27.refs_1_ = bf16[256,256]{1,0:T(8,128)(2,1)S(1)} collective-permute-done((bf16[256,256]{1,0:T(8,128)(2,1)S(1)}, bf16[256,256]{1,0:T(8,128)(2,1)S(1)}, u32[]{:S(2)}, u32[]{:S(2)}) %collective-permute-start.27) | collective-permute-done | bytes 131104 | tf_op jit(solution)/shard_map/ppermute | solution.py:57
  (64 shorter events, 27.5 us)
Async XLA Ops:
  2.9 28.6 %collective-permute-start.2 = (bf16[256,1408]{1,0:T(8,128)(2,1)S(1)}, bf16[256,1408]{1,0:T(8,128)(2,1)S(1)}, u32[]{:S(2)}, u32[]{:S(2)}) collective-permute-start(bf16[256,1408]{1,0:T(8,128)(2,1)S(1)} %get-tuple-element.44.refs_3_.refs_1_.refs_2_.refs_10_), channel_id=1, source_target_pairs={{1,0},{0,1},{3,2},{2,3},{5,4},{4,5},{7,6},{6,7},{9,8},{8,9},{11,10... | collective-permute-start | bytes 2162696 | tf_op jit(solution)/shard_map/ppermute | solution.py:57
  3.4 28.2 %collective-permute-start.3 = (bf16[256,1408]{1,0:T(8,128)(2,1)S(1)}, bf16[256,1408]{1,0:T(8,128)(2,1)S(1)}, u32[]{:S(2)}, u32[]{:S(2)}) collective-permute-start(bf16[256,1408]{1,0:T(8,128)(2,1)S(1)} %get-tuple-element.44.refs_3_.refs_1_.refs_2_.refs_10_), channel_id=1, source_target_pairs={{16,0},{17,1},{18,2},{19,3},{20,4},{21,5},{22,6},{23,7},{24,8},{25... | collective-permute-start | bytes 2162696 | tf_op jit(solution)/shard_map/ppermute | solution.py:57
  5.9 24.8 %collective-permute-start = (bf16[256,1152]{1,0:T(8,128)(2,1)S(1)}, bf16[256,1152]{1,0:T(8,128)(2,1)S(1)}, u32[]{:S(2)}, u32[]{:S(2)}) collective-permute-start(bf16[256,1152]{1,0:T(8,128)(2,1)S(1)} %get-tuple-element.42.refs_0_), channel_id=1, source_target_pairs={{8,0},{9,1},{10,2},{11,3},{12,4},{13,5},{14,6},{15,7},{0,8},{1,9},... | collective-permute-start | bytes 1769480 | tf_op jit(solution)/shard_map/ppermute | solution.py:57
  8.2 22.5 %collective-permute-start.4 = (bf16[192,1152]{1,0:T(8,128)(2,1)S(1)}, bf16[192,1152]{1,0:T(8,128)(2,1)}, u32[]{:S(2)}, u32[]{:S(2)}) collective-permute-start(bf16[192,1152]{1,0:T(8,128)(2,1)S(1)} %get-tuple-element.45), channel_id=1, source_target_pairs={{4,0},{5,1},{6,2},{7,3},{0,4},{1,5},{2,6},{3,7},{12,8},{13,9},{14,... | collective-permute-start | bytes 1327112 | tf_op jit(solution)/shard_map/ppermute | solution.py:57
  10.8 15.9 %collective-permute-start.1 = (bf16[128,1152]{1,0:T(8,128)(2,1)S(1)}, bf16[128,1152]{1,0:T(8,128)(2,1)}, u32[]{:S(2)}, u32[]{:S(2)}) collective-permute-start(bf16[128,1152]{1,0:T(8,128)(2,1)S(1)} %get-tuple-element.43), channel_id=1, source_target_pairs={{2,0},{3,1},{0,2},{1,3},{6,4},{7,5},{4,6},{5,7},{10,8},{11,9},{8,1... | collective-permute-start | bytes 884744 | tf_op jit(solution)/shard_map/ppermute | solution.py:57
  31.6 9.6 %collective-permute-start.6 = (bf16[128,1152]{1,0:T(8,128)(2,1)}, bf16[128,1152]{1,0:T(8,128)(2,1)S(1)}, u32[]{:S(2)}, u32[]{:S(2)}) collective-permute-start(bf16[128,1152]{1,0:T(8,128)(2,1)} %collective-permute-done.1.refs_2_), channel_id=1, source_target_pairs={{8,0},{9,1},{10,2},{11,3},{12,4},{13,5},{14,6},{15,7},{0,8},{1,9},... | collective-permute-start | bytes 884744 | tf_op jit(solution)/shard_map/ppermute | solution.py:57
  32.2 17.2 %collective-permute-start.8 = (bf16[192,1152]{1,0:T(8,128)(2,1)}, bf16[192,1152]{1,0:T(8,128)(2,1)}, u32[]{:S(2)}, u32[]{:S(2)}) collective-permute-start(bf16[192,1152]{1,0:T(8,128)(2,1)} %collective-permute-done.4.refs_4_.refs_6_), channel_id=1, source_target_pairs={{16,0},{17,1},{18,2},{19,3},{20,4},{21,5},{22,6},{23,7},{24,8},{25... | collective-permute-start | bytes 1327112 | tf_op jit(solution)/shard_map/ppermute | solution.py:57
  33.8 15.6 %collective-permute-start.7 = (bf16[192,1152]{1,0:T(8,128)(2,1)}, bf16[192,1152]{1,0:T(8,128)(2,1)}, u32[]{:S(2)}, u32[]{:S(2)}) collective-permute-start(bf16[192,1152]{1,0:T(8,128)(2,1)} %collective-permute-done.4.refs_4_.refs_6_), channel_id=1, source_target_pairs={{1,0},{0,1},{3,2},{2,3},{5,4},{4,5},{7,6},{6,7},{9,8},{8,9},{11,10... | collective-permute-start | bytes 1327112 | tf_op jit(solution)/shard_map/ppermute | solution.py:57
  33.9 15.5 %collective-permute-start.10 = (bf16[128,1152]{1,0:T(8,128)(2,1)}, bf16[128,1152]{1,0:T(8,128)(2,1)S(1)}, u32[]{:S(2)}, u32[]{:S(2)}) collective-permute-start(bf16[128,1152]{1,0:T(8,128)(2,1)} %get-tuple-element.55), channel_id=1, source_target_pairs={{2,0},{3,1},{0,2},{1,3},{6,4},{7,5},{4,6},{5,7},{10,8},{11,9},{8,1... | collective-permute-start | bytes 884744 | tf_op jit(solution)/shard_map/ppermute | solution.py:57
  34.5 13.1 %collective-permute-start.9 = (bf16[64,2176]{1,0:T(8,128)(2,1)}, bf16[64,2176]{1,0:T(8,128)(2,1)S(1)}, u32[]{:S(2)}, u32[]{:S(2)}) collective-permute-start(bf16[64,2176]{1,0:T(8,128)(2,1)} %copy-done.8), channel_id=1, source_target_pairs={{4,0},{5,1},{6,2},{7,3},{0,4},{1,5},{2,6},{3,7},{12,8},{13,9},{14,... | collective-permute-start | bytes 835592 | tf_op jit(solution)/shard_map/ppermute | solution.py:57
  49.4 9.7 %collective-permute-start.12 = (bf16[128,1152]{1,0:T(8,128)(2,1)S(1)}, bf16[128,1152]{1,0:T(8,128)(2,1)S(1)}, u32[]{:S(2)}, u32[]{:S(2)}) collective-permute-start(bf16[128,1152]{1,0:T(8,128)(2,1)S(1)} %collective-permute-done.10.refs_0_.refs_4_), channel_id=1, source_target_pairs={{8,0},{9,1},{10,2},{11,3},{12,4},{13,5},{14,6},{15,7},{0,8},{1,9},... | collective-permute-start | bytes 884744 | tf_op jit(solution)/shard_map/ppermute | solution.py:57
  50.0 4.8 %collective-permute-start.13 = (bf16[64,2176]{1,0:T(8,128)(2,1)S(1)}, bf16[64,2176]{1,0:T(8,128)(2,1)S(1)}, u32[]{:S(2)}, u32[]{:S(2)}) collective-permute-start(bf16[64,2176]{1,0:T(8,128)(2,1)S(1)} %collective-permute-done.9.refs_6_.refs_14_), channel_id=1, source_target_pairs={{1,0},{0,1},{3,2},{2,3},{5,4},{4,5},{7,6},{6,7},{9,8},{8,9},{11,10... | collective-permute-start | bytes 835592 | tf_op jit(solution)/shard_map/ppermute | solution.py:57
  50.2 8.9 %collective-permute-start.14 = (bf16[64,2176]{1,0:T(8,128)(2,1)S(1)}, bf16[64,2176]{1,0:T(8,128)(2,1)S(1)}, u32[]{:S(2)}, u32[]{:S(2)}) collective-permute-start(bf16[64,2176]{1,0:T(8,128)(2,1)S(1)} %collective-permute-done.9.refs_6_.refs_14_), channel_id=1, source_target_pairs={{16,0},{17,1},{18,2},{19,3},{20,4},{21,5},{22,6},{23,7},{24,8},{25... | collective-permute-start | bytes 835592 | tf_op jit(solution)/shard_map/ppermute | solution.py:57
  65.1 6.2 %collective-permute-start.16 = (bf16[272,256]{1,0:T(8,128)(2,1)S(1)}, bf16[272,256]{1,0:T(8,128)(2,1)S(1)}, u32[]{:S(2)}, u32[]{:S(2)}) collective-permute-start(bf16[272,256]{1,0:T(8,128)(2,1)S(1)} %get-tuple-element.70), channel_id=1, source_target_pairs={{8,0},{9,1},{10,2},{11,3},{12,4},{13,5},{14,6},{15,7},{0,8},{1,9},... | collective-permute-start | bytes 417800 | tf_op jit(solution)/shard_map/ppermute | solution.py:57
  66.7 6.8 %collective-permute-start.17 = (bf16[272,256]{1,0:T(8,128)(2,1)S(1)}, bf16[272,256]{1,0:T(8,128)(2,1)S(1)}, u32[]{:S(2)}, u32[]{:S(2)}) collective-permute-start(bf16[272,256]{1,0:T(8,128)(2,1)S(1)} %get-tuple-element.71), channel_id=1, source_target_pairs={{2,0},{3,1},{0,2},{1,3},{6,4},{7,5},{4,6},{5,7},{10,8},{11,9},{8,1... | collective-permute-start | bytes 417800 | tf_op jit(solution)/shard_map/ppermute | solution.py:57
  69.1 7.0 %collective-permute-start.18 = (bf16[272,256]{1,0:T(8,128)(2,1)S(1)}, bf16[272,256]{1,0:T(8,128)(2,1)S(1)}, u32[]{:S(2)}, u32[]{:S(2)}) collective-permute-start(bf16[272,256]{1,0:T(8,128)(2,1)S(1)} %get-tuple-element.72), channel_id=1, source_target_pairs={{10,0},{11,1},{8,2},{9,3},{14,4},{15,5},{12,6},{13,7},{2,8},{3,9},... | collective-permute-start | bytes 417800 | tf_op jit(solution)/shard_map/ppermute | solution.py:57
  76.2 8.8 %collective-permute-start.22 = (bf16[256,256]{1,0:T(8,128)(2,1)S(1)}, bf16[256,256]{1,0:T(8,128)(2,1)S(1)}, u32[]{:S(2)}, u32[]{:S(2)}) collective-permute-start(bf16[256,256]{1,0:T(8,128)(2,1)S(1)} %get-tuple-element.73.refs_5_), channel_id=1, source_target_pairs={{4,0},{5,1},{6,2},{7,3},{0,4},{1,5},{2,6},{3,7},{12,8},{13,9},{14,... | collective-permute-start | bytes 393224 | tf_op jit(solution)/shard_map/ppermute | solution.py:57
  78.6 8.4 %collective-permute-start.20 = (bf16[256,256]{1,0:T(8,128)(2,1)S(1)}, bf16[256,256]{1,0:T(8,128)(2,1)S(1)}, u32[]{:S(2)}, u32[]{:S(2)}) collective-permute-start(bf16[256,256]{1,0:T(8,128)(2,1)S(1)} %get-tuple-element.73.refs_5_), channel_id=1, source_target_pairs={{16,0},{17,1},{18,2},{19,3},{20,4},{21,5},{22,6},{23,7},{24,8},{25... | collective-permute-start | bytes 393224 | tf_op jit(solution)/shard_map/ppermute | solution.py:57
  85.0 5.0 %collective-permute-start.24 = (bf16[256,256]{1,0:T(8,128)(2,1)S(1)}, bf16[256,256]{1,0:T(8,128)(2,1)S(1)}, u32[]{:S(2)}, u32[]{:S(2)}) collective-permute-start(bf16[256,256]{1,0:T(8,128)(2,1)S(1)} %collective-permute-done.22.refs_9_), channel_id=1, source_target_pairs={{16,0},{17,1},{18,2},{19,3},{20,4},{21,5},{22,6},{23,7},{24,8},{25... | collective-permute-start | bytes 393224 | tf_op jit(solution)/shard_map/ppermute | solution.py:57
  86.5 3.5 %collective-permute-start.19 = (bf16[256,256]{1,0:T(8,128)(2,1)S(1)}, bf16[256,256]{1,0:T(8,128)(2,1)S(1)}, u32[]{:S(2)}, u32[]{:S(2)}) collective-permute-start(bf16[256,256]{1,0:T(8,128)(2,1)S(1)} %get-tuple-element.73.refs_5_), channel_id=1, source_target_pairs={{1,0},{0,1},{3,2},{2,3},{5,4},{4,5},{7,6},{6,7},{9,8},{8,9},{11,10... | collective-permute-start | bytes 393224 | tf_op jit(solution)/shard_map/ppermute | solution.py:57
  86.5 3.5 %collective-permute-start.23 = (bf16[256,256]{1,0:T(8,128)(2,1)S(1)}, bf16[256,256]{1,0:T(8,128)(2,1)S(1)}, u32[]{:S(2)}, u32[]{:S(2)}) collective-permute-start(bf16[256,256]{1,0:T(8,128)(2,1)S(1)} %collective-permute-done.22.refs_9_), channel_id=1, source_target_pairs={{1,0},{0,1},{3,2},{2,3},{5,4},{4,5},{7,6},{6,7},{9,8},{8,9},{11,10... | collective-permute-start | bytes 393224 | tf_op jit(solution)/shard_map/ppermute | solution.py:57
  92.6 5.6 %collective-permute-start.26 = (bf16[256,256]{1,0:T(8,128)(2,1)S(1)}, bf16[256,256]{1,0:T(8,128)(2,1)S(1)}, u32[]{:S(2)}, u32[]{:S(2)}) collective-permute-start(bf16[256,256]{1,0:T(8,128)(2,1)S(1)} %get-tuple-element.76), channel_id=1, source_target_pairs={{8,0},{9,1},{10,2},{11,3},{12,4},{13,5},{14,6},{15,7},{0,8},{1,9},... | collective-permute-start | bytes 393224 | tf_op jit(solution)/shard_map/ppermute | solution.py:57
  94.3 6.4 %collective-permute-start.27 = (bf16[256,256]{1,0:T(8,128)(2,1)S(1)}, bf16[256,256]{1,0:T(8,128)(2,1)S(1)}, u32[]{:S(2)}, u32[]{:S(2)}) collective-permute-start(bf16[256,256]{1,0:T(8,128)(2,1)S(1)} %get-tuple-element.77), channel_id=1, source_target_pairs={{2,0},{3,1},{0,2},{1,3},{6,4},{7,5},{4,6},{5,7},{10,8},{11,9},{8,1... | collective-permute-start | bytes 393224 | tf_op jit(solution)/shard_map/ppermute | solution.py:57
  95.1 7.1 %collective-permute-start.28 = (bf16[256,256]{1,0:T(8,128)(2,1)S(1)}, bf16[256,256]{1,0:T(8,128)(2,1)S(1)}, u32[]{:S(2)}, u32[]{:S(2)}) collective-permute-start(bf16[256,256]{1,0:T(8,128)(2,1)S(1)} %get-tuple-element.78), channel_id=1, source_target_pairs={{10,0},{11,1},{8,2},{9,3},{14,4},{15,5},{12,6},{13,7},{2,8},{3,9},... | collective-permute-start | bytes 393224 | tf_op jit(solution)/shard_map/ppermute | solution.py:57
  (14 other events, 63.5 us)

commit v8 on v6

--- a/solution.py
+++ b/solution.py
@@ -100,6 +100,26 @@
     )(embeddings, seeds)
 
 
+def stack_kernel(seed_ref, *refs):
+    *packed, out_ref = refs
+    m, c = seed_ref.shape
+    out_ref[:m, :] = seed_ref[...]
+    for k, ref in enumerate(packed):
+        out_ref[(k + 1) * m : (k + 2) * m, :] = ref[:, ref.shape[1] - c :]
+
+
+def stack_seeds(seeds, packed):
+    m, c = seeds.shape
+    out = shape(((len(packed) + 1) * m, c))
+    return pl.pallas_call(
+        stack_kernel,
+        out_shape=out,
+        in_specs=[VMEM] * (len(packed) + 1),
+        out_specs=VMEM,
+        compiler_params=limits(seeds, *packed, out),
+    )(seeds, *packed)
+
+
 def flags_kernel(layout, m, t_parts, s_parts, unit, place_ref, pattern_ref, out_ref, block_ref):
     at = layout.coords(place_ref[0], place_ref[1])
 
@@ -118,8 +138,9 @@
         out_ref[r : r + 1, :] = jnp.where(hits, 1, 0)
 
 
-def flags_call(layout, m, t_parts, s_parts, unit, pattern):
+def flags_call(layout, m, t_parts, s_parts, unit, pattern, *earlier):
     place = jnp.stack([lax.axis_index("row"), lax.axis_index("col")]).astype(jnp.int32)
+    place = after(place, *earlier)
     out = shape((len(t_parts), len(s_parts) * unit), jnp.int32)
     smem = pl.BlockSpec(memory_space=pltpu.SMEM)
     return pl.pallas_call(
@@ -129,7 +150,7 @@
         out_specs=VMEM,
         scratch_shapes=[pltpu.VMEM((1, out.shape[1]), jnp.int32)],
         compiler_params=limits(out, out),
-        cost_estimate=pl.CostEstimate(flops=0, bytes_accessed=256 * 2**20, transcendentals=0),
+        cost_estimate=pl.CostEstimate(flops=2 * 10**10, bytes_accessed=2**20, transcendentals=0),
     )(place, pattern.T)
 
 
@@ -223,9 +244,8 @@
     own_ref, other_refs = outs[0], outs[2:] if na else outs[1:]
     c = pcat.shape[1]
     at = 0
-    for index, start, rows in p_map:
-        ref = p_in[index]
-        pcat[at : at + rows, :] = ref[start : start + rows, ref.shape[1] - c :]
+    for index, start, rows, lane in p_map:
+        pcat[at : at + rows, :] = p_in[index][start : start + rows, lane : lane + c]
         at += rows
     row = 0
     for piece, start, rows in t_layout:
@@ -268,7 +288,7 @@
 def spread_call(kerns, accs, p_pieces, c, plan):
     m, t_layout, rects, p_map = plan
     nt = 1 + max(piece for piece, _, _ in t_layout)
-    cols = sum(rows for _, _, rows in p_map)
+    cols = sum(rows for _, _, rows, _ in p_map)
     extra = 16 if accs else 0
     outs = [jax.ShapeDtypeStruct((m, c), jnp.float32)]
     if accs:
@@ -358,7 +378,14 @@
         [(b, a, k) for k in other["core"] for a in other["y"] for b in other["zh"]],
     ]
     s_layout = [dict(zh=b, y=a, core=k) for group in groups for b, a, k in group]
-    p_map = [(i, 0, m) for i in range(len(s_layout))]
+    p_map = [(i, 0, m, 0) for i in range(len(s_layout))]
+    seeds_map = []
+    for i, o in enumerate(s_layout):
+        if o["zh"] == 0:
+            seeds_map.append((i, 0, m, embeddings.shape[1]))
+        else:
+            stack = len(groups[0]) + o["core"] * (size["zh"] - 1) + o["zh"] - 1
+            seeds_map.append((stack, o["y"] * m, m, 0))
     t_parts = [(t_offsets[i], k) for i in t_order for k in range(0, m, sub)]
     s_parts = [(o, k) for o in s_layout for k in range(0, m, sub)]
     units, packed = unit_rows(embeddings, seed_labels)
@@ -386,12 +413,12 @@
 
     zh, zl, x = fetch([units], "zh"), fetch([units], "zl"), fetch([units], "x")
     y, own_core = fetch([packed], "y"), fetch([packed], "core")
-    flags = flags_call(layout, m, t_parts, s_parts, sub, after(pattern, *zh))
+    flags = flags_call(layout, m, t_parts, s_parts, sub, pattern, *zh)
     done = zh + zl + x + y + own_core + [flags]
     zh_y, zl_x = fetch(zh, "y", *done), fetch(zl, "x", *done)
     y_core = [fetch([v], "core", *done) for v in y]
     zh_core = fetch(zh, "core", *done)
-    seeds_zh = fetch([seed_labels], "zh", *done)
+    seeds_zh = fetch([stack_seeds(seed_labels, y)], "zh", *done)
     by_offset = {(0, 0): units}
     by_offset.update({(0, a): v for a, v in zip(other["x"], x)})
     by_offset.update({(b, 0): v for b, v in zip(other["zl"], zl)})
@@ -405,12 +432,11 @@
     done = zh_y + zl_x + zh_core + seeds_zh + gram
     zh_y_core = fetch(zh_y, "core", *done)
     s_pieces[3] = zh_y_core
-    seeds_y, seeds_core = fetch(seeds_zh, "y", *done), fetch(seeds_zh, "core", *done)
-    seeds_y_core = fetch(seeds_y, "core")
-    rectangle(early, last, 0, 2)
-    rectangle(0, last, 2, 3)
+    seeds_core = fetch(seeds_zh, "core", *done)
+    rectangle(early, last, 0, 3)
+    rectangle(0, early, 2, 3)
     rectangle(0, last, 3, 4)
-    plan = (m, t_layout, rects, p_map)
+    plan = (m, t_layout, rects)
 
     def home(values):
         return [
@@ -424,8 +450,8 @@
         near = [p for v in [panel] + near for p in [v] + fetch([v], "core")]
         return near + far + fetch(far, "core") + far_y + fetch(far_y, "core")
 
-    seeds = s_pieces[0] + seeds_zh + seeds_core + seeds_y + seeds_y_core
-    own, totals, *others = spread_call(kerns, accs, seeds, c, plan)
+    seeds = s_pieces[0] + seeds_zh + seeds_core
+    own, totals, *others = spread_call(kerns, accs, seeds, c, (*plan, seeds_map))
     panel, totals = update(
         first_update_kernel,
         seed_labels,
@@ -437,7 +463,7 @@
             jax.ShapeDtypeStruct((m, BLOCK), jnp.float32),
         ],
     )
-    own, *others = spread_call(kerns, [], panels(panel), c, plan)
+    own, *others = spread_call(kerns, [], panels(panel), c, (*plan, p_map))
     return update(
         last_update_kernel,
         seed_labels,

time: 102 us -> 97 us (0.951)
  starting transfers between devices: 26.1 us -> 22.9 us
  waiting for transfers between devices: 55.2 us -> 53.7 us
    ppermute x27 -> x25, starting transfers between devices: 26.1 us -> 22.9 us  [fetch(): return lax.ppermute(value, AXES, pairs)]
    ppermute x27 -> x25, waiting for transfers between devices: 55.2 us -> 53.7 us  [fetch(): return lax.ppermute(value, AXES, pairs)]
  transfers between devices with their start and end apart: 27 -> 25, of which waited for: 14 -> 11; matrix products, arithmetic and copies ran while one was open for 0% -> 0% of each run, Pallas kernels for 13% -> 14%
where the time goes in v8:
time: 97 us; the launch traced here: 96.6 us
  waiting for transfers between devices  53.7 us (55%)
  starting transfers between devices  22.9 us (24%)
  Pallas kernels  17.1 us (18%)
  local copies, waits for them, and re-layouts  2.67 us (3%)
    ppermute x25, waiting for transfers between devices, fetch(): return lax.ppermute(value, AXES, pairs)  53.7 us
    ppermute x25, starting transfers between devices, fetch(): return lax.ppermute(value, AXES, pairs)  22.9 us
    pallas_call x5, Pallas kernels, gram_call(): pl.pallas_call(functools.partial(gram_kernel, len(t_pieces), len(s_pieces...  12.4 us
    unnamed x8, local copies, waits for them, and re-layouts  2.67 us
    pallas_call x2, Pallas kernels, spread_call(): pl.pallas_call(functools.partial(spread_kernel, plan, len(kerns), len(acc...  2.52 us
  transfers between devices with their start and end apart: 25, of which 11 were waited for; matrix products, arithmetic and copies ran while one was open for 0% of the time, Pallas kernels for 14%

profile of v8, /device:TPU:0, one launch (start us, length us, event | category | flops | bytes accessed | tf_op | source)
XLA Modules:
  0.0 96.6 jit_solution(15312522007664641809)
XLA Ops:
  2.2 4.1 %collective-permute-start = (bf16[256,1152]{1,0:T(8,128)(2,1)S(1)}, bf16[256,1152]{1,0:T(8,128)(2,1)}, u32[]{:S(2)}, u32[]{:S(2)}) collective-permute-start(bf16[256,1152]{1,0:T(8,128)(2,1)S(1)} %get-tuple-element.35.refs_0_), channel_id=1, source_target_pairs={{4,0},{5,1},{6,2},{7,3},{0,4},{1,5},{2,6},{3,7},{12,8},{13,9},{14,... | collective-permute-start | bytes 1769480 | tf_op jit(solution)/shard_map/ppermute | solution.py:57
  6.3 1.6 %collective-permute-start.2 = (bf16[256,1152]{1,0:T(8,128)(2,1)S(1)}, bf16[256,1152]{1,0:T(8,128)(2,1)S(1)}, u32[]{:S(2)}, u32[]{:S(2)}) collective-permute-start(bf16[256,1152]{1,0:T(8,128)(2,1)S(1)} %get-tuple-element.35.refs_0_), channel_id=1, source_target_pairs={{2,0},{3,1},{0,2},{1,3},{6,4},{7,5},{4,6},{5,7},{10,8},{11,9},{8,1... | collective-permute-start | bytes 1769480 | tf_op jit(solution)/shard_map/ppermute | solution.py:57
  7.9 1.5 %collective-permute-start.1 = (bf16[256,1152]{1,0:T(8,128)(2,1)S(1)}, bf16[256,1152]{1,0:T(8,128)(2,1)}, u32[]{:S(2)}, u32[]{:S(2)}) collective-permute-start(bf16[256,1152]{1,0:T(8,128)(2,1)S(1)} %get-tuple-element.35.refs_0_), channel_id=1, source_target_pairs={{8,0},{9,1},{10,2},{11,3},{12,4},{13,5},{14,6},{15,7},{0,8},{1,9},... | collective-permute-start | bytes 1769480 | tf_op jit(solution)/shard_map/ppermute | solution.py:57
  9.4 1.5 %collective-permute-start.4 = (bf16[256,1408]{1,0:T(8,128)(2,1)S(1)}, bf16[256,1408]{1,0:T(8,128)(2,1)S(1)}, u32[]{:S(2)}, u32[]{:S(2)}) collective-permute-start(bf16[256,1408]{1,0:T(8,128)(2,1)S(1)} %get-tuple-element.37.refs_3_.refs_1_.refs_10_), channel_id=1, source_target_pairs={{16,0},{17,1},{18,2},{19,3},{20,4},{21,5},{22,6},{23,7},{24,8},{25... | collective-permute-start | bytes 2162696 | tf_op jit(solution)/shard_map/ppermute | solution.py:57
  11.0 21.5 %collective-permute-done.refs_3_.refs_5_ = bf16[256,1152]{1,0:T(8,128)(2,1)} collective-permute-done((bf16[256,1152]{1,0:T(8,128)(2,1)S(1)}, bf16[256,1152]{1,0:T(8,128)(2,1)}, u32[]{:S(2)}, u32[]{:S(2)}) %collective-permute-start) | collective-permute-done | bytes 589856 | tf_op jit(solution)/shard_map/ppermute | solution.py:57
  34.8 1.6 %collective-permute-start.8 = (bf16[256,1152]{1,0:T(8,128)(2,1)}, bf16[256,1152]{1,0:T(8,128)(2,1)S(1)}, u32[]{:S(2)}, u32[]{:S(2)}) collective-permute-start(bf16[256,1152]{1,0:T(8,128)(2,1)} %collective-permute-done.refs_3_.refs_5_), channel_id=1, source_target_pairs={{16,0},{17,1},{18,2},{19,3},{20,4},{21,5},{22,6},{23,7},{24,8},{25... | collective-permute-start | bytes 1769480 | tf_op jit(solution)/shard_map/ppermute | solution.py:57
  36.3 1.5 %collective-permute-start.7 = (bf16[256,1152]{1,0:T(8,128)(2,1)S(1)}, bf16[256,1152]{1,0:T(8,128)(2,1)S(1)}, u32[]{:S(2)}, u32[]{:S(2)}) collective-permute-start(bf16[256,1152]{1,0:T(8,128)(2,1)S(1)} %collective-permute-done.2.refs_2_), channel_id=1, source_target_pairs={{8,0},{9,1},{10,2},{11,3},{12,4},{13,5},{14,6},{15,7},{0,8},{1,9},... | collective-permute-start | bytes 1769480 | tf_op jit(solution)/shard_map/ppermute | solution.py:57
  37.9 2.6 %shard_map.40 = (bf16[768,512]{1,0:T(8,128)(2,1)S(1)}, f32[768,128]{1,0:T(8,128)S(1)}) custom-call(s32[8,2048]{1,0:T(8,128)S(1)} %shard_map.38.flags, bf16[256,1152]{1,0:T(8,128)(2,1)S(1)} %get-tuple-element.35.refs_0_, bf16[256,1152]{1,0:T(8,128)(2,1)} %collective-permute-done.1.refs_1_, bf16[256,1152]{1,0:T(8,128)(2,1)S(1)} %collective-permute-done.2.refs_2_, ...), custom_call_target="tpu_custom_call" | custom-call | flops 905969664 | bytes 2949120 | tf_op jit(solution)/shard_map/pallas_call | solution.py:221
  40.5 3.4 %shard_map.39 = (bf16[768,1024]{1,0:T(8,128)(2,1)S(1)}, f32[768,128]{1,0:T(8,128)S(1)}) custom-call(s32[8,2048]{1,0:T(8,128)S(1)} %shard_map.38.flags, bf16[256,1152]{1,0:T(8,128)(2,1)S(1)} %get-tuple-element.35.refs_0_, bf16[256,1152]{1,0:T(8,128)(2,1)} %collective-permute-done.1.refs_1_, bf16[256,1152]{1,0:T(8,128)(2,1)S(1)} %collective-permute-done.2.refs_2_, ...), custom_call_target="tpu_custom_call" | custom-call | flops 1811939328 | bytes 4128768 | tf_op jit(solution)/shard_map/pallas_call | solution.py:221
  44.0 8.2 %collective-permute-done.9.refs_14_ = bf16[512,256]{1,0:T(8,128)(2,1)S(1)} collective-permute-done((bf16[512,256]{1,0:T(8,128)(2,1)S(1)}, bf16[512,256]{1,0:T(8,128)(2,1)S(1)}, u32[]{:S(2)}, u32[]{:S(2)}) %collective-permute-start.9) | collective-permute-done | bytes 262176 | tf_op jit(solution)/shard_map/ppermute | solution.py:57
  52.7 1.8 %shard_map.42 = (bf16[768,256]{1,0:T(8,128)(2,1)S(1)}, f32[768,128]{1,0:T(8,128)S(1)}) custom-call(s32[8,2048]{1,0:T(8,128)S(1)} %shard_map.38.flags, bf16[256,1152]{1,0:T(8,128)(2,1)S(1)} %get-tuple-element.35.refs_0_, bf16[256,1152]{1,0:T(8,128)(2,1)} %collective-permute-done.1.refs_1_, bf16[256,1152]{1,0:T(8,128)(2,1)S(1)} %collective-permute-done.2.refs_2_, ...), custom_call_target="tpu_custom_call" | custom-call | flops 452984832 | bytes 2359296 | tf_op jit(solution)/shard_map/pallas_call | solution.py:221
  54.5 2.5 %shard_map.41 = (bf16[256,1792]{1,0:T(8,128)(2,1)S(1)}, f32[256,128]{1,0:T(8,128)S(1)}) custom-call(s32[8,2048]{1,0:T(8,128)S(1)} %shard_map.38.flags, bf16[256,1152]{1,0:T(8,128)(2,1)S(1)} %collective-permute-done.7.refs_0_.refs_3_, bf16[256,1408]{1,0:T(8,128)(2,1)S(1)} %get-tuple-element.37.refs_3_.refs_1_.refs_10_, ...), custom_call_target="tpu_custom_call" | custom-call | flops 1056964608 | bytes 4718592 | tf_op jit(solution)/shard_map/pallas_call | solution.py:221
  57.1 2.0 %shard_map.44 = (bf16[1024,256]{1,0:T(8,128)(2,1)S(1)}, f32[1024,128]{1,0:T(8,128)S(1)}) custom-call(s32[8,2048]{1,0:T(8,128)S(1)} %shard_map.38.flags, bf16[256,1152]{1,0:T(8,128)(2,1)S(1)} %get-tuple-element.35.refs_0_, bf16[256,1152]{1,0:T(8,128)(2,1)} %collective-permute-done.1.refs_1_, bf16[256,1152]{1,0:T(8,128)(2,1)S(1)} %collective-permute-done.2.refs_2_, ...), custom_call_target="tpu_custom_call" | custom-call | flops 603979776 | bytes 2949120 | tf_op jit(solution)/shard_map/pallas_call | solution.py:221
  61.6 2.3 %collective-permute-start.14 = (bf16[272,256]{1,0:T(8,128)(2,1)S(1)}, bf16[272,256]{1,0:T(8,128)(2,1)S(1)}, u32[]{:S(2)}, u32[]{:S(2)}) collective-permute-start(bf16[272,256]{1,0:T(8,128)(2,1)S(1)} %get-tuple-element.58), channel_id=1, source_target_pairs={{10,0},{11,1},{8,2},{9,3},{14,4},{15,5},{12,6},{13,7},{2,8},{3,9},... | collective-permute-start | bytes 417800 | tf_op jit(solution)/shard_map/ppermute | solution.py:57
  63.9 2.2 %collective-permute-done.12.refs_0_ = bf16[272,256]{1,0:T(8,128)(2,1)S(1)} collective-permute-done((bf16[272,256]{1,0:T(8,128)(2,1)S(1)}, bf16[272,256]{1,0:T(8,128)(2,1)S(1)}, u32[]{:S(2)}, u32[]{:S(2)}) %collective-permute-start.12) | collective-permute-done | bytes 139296 | tf_op jit(solution)/shard_map/ppermute | solution.py:57
  66.1 1.6 %collective-permute-done.13.refs_1_ = bf16[272,256]{1,0:T(8,128)(2,1)S(1)} collective-permute-done((bf16[272,256]{1,0:T(8,128)(2,1)S(1)}, bf16[272,256]{1,0:T(8,128)(2,1)S(1)}, u32[]{:S(2)}, u32[]{:S(2)}) %collective-permute-start.13) | collective-permute-done | bytes 139296 | tf_op jit(solution)/shard_map/ppermute | solution.py:57
  67.7 2.5 %collective-permute-done.14.refs_2_ = bf16[272,256]{1,0:T(8,128)(2,1)S(1)} collective-permute-done((bf16[272,256]{1,0:T(8,128)(2,1)S(1)}, bf16[272,256]{1,0:T(8,128)(2,1)S(1)}, u32[]{:S(2)}, u32[]{:S(2)}) %collective-permute-start.14) | collective-permute-done | bytes 139296 | tf_op jit(solution)/shard_map/ppermute | solution.py:57
  70.4 1.4 %collective-permute-start.18 = (bf16[256,256]{1,0:T(8,128)(2,1)S(1)}, bf16[256,256]{1,0:T(8,128)(2,1)S(1)}, u32[]{:S(2)}, u32[]{:S(2)}) collective-permute-start(bf16[256,256]{1,0:T(8,128)(2,1)S(1)} %get-tuple-element.59.refs_5_), channel_id=1, source_target_pairs={{4,0},{5,1},{6,2},{7,3},{0,4},{1,5},{2,6},{3,7},{12,8},{13,9},{14,... | collective-permute-start | bytes 393224 | tf_op jit(solution)/shard_map/ppermute | solution.py:57
  72.3 6.2 %collective-permute-done.18.refs_9_ = bf16[256,256]{1,0:T(8,128)(2,1)S(1)} collective-permute-done((bf16[256,256]{1,0:T(8,128)(2,1)S(1)}, bf16[256,256]{1,0:T(8,128)(2,1)S(1)}, u32[]{:S(2)}, u32[]{:S(2)}) %collective-permute-start.18) | collective-permute-done | bytes 131104 | tf_op jit(solution)/shard_map/ppermute | solution.py:57
  79.5 4.1 %collective-permute-done.20.refs_11_ = bf16[256,256]{1,0:T(8,128)(2,1)S(1)} collective-permute-done((bf16[256,256]{1,0:T(8,128)(2,1)S(1)}, bf16[256,256]{1,0:T(8,128)(2,1)S(1)}, u32[]{:S(2)}, u32[]{:S(2)}) %collective-permute-start.20) | collective-permute-done | bytes 131104 | tf_op jit(solution)/shard_map/ppermute | solution.py:57
  83.6 1.3 %collective-permute-done.21.refs_12_ = bf16[256,256]{1,0:T(8,128)(2,1)S(1)} collective-permute-done((bf16[256,256]{1,0:T(8,128)(2,1)S(1)}, bf16[256,256]{1,0:T(8,128)(2,1)S(1)}, u32[]{:S(2)}, u32[]{:S(2)}) %collective-permute-start.21) | collective-permute-done | bytes 131104 | tf_op jit(solution)/shard_map/ppermute | solution.py:57
  87.3 2.5 %collective-permute-start.24 = (bf16[256,256]{1,0:T(8,128)(2,1)S(1)}, bf16[256,256]{1,0:T(8,128)(2,1)S(1)}, u32[]{:S(2)}, u32[]{:S(2)}) collective-permute-start(bf16[256,256]{1,0:T(8,128)(2,1)S(1)} %get-tuple-element.64), channel_id=1, source_target_pairs={{10,0},{11,1},{8,2},{9,3},{14,4},{15,5},{12,6},{13,7},{2,8},{3,9},... | collective-permute-start | bytes 393224 | tf_op jit(solution)/shard_map/ppermute | solution.py:57
  89.8 2.1 %collective-permute-done.22.refs_0_ = bf16[256,256]{1,0:T(8,128)(2,1)S(1)} collective-permute-done((bf16[256,256]{1,0:T(8,128)(2,1)S(1)}, bf16[256,256]{1,0:T(8,128)(2,1)S(1)}, u32[]{:S(2)}, u32[]{:S(2)}) %collective-permute-start.22) | collective-permute-done | bytes 131104 | tf_op jit(solution)/shard_map/ppermute | solution.py:57
  93.1 2.8 %collective-permute-done.24.refs_2_ = bf16[256,256]{1,0:T(8,128)(2,1)S(1)} collective-permute-done((bf16[256,256]{1,0:T(8,128)(2,1)S(1)}, bf16[256,256]{1,0:T(8,128)(2,1)S(1)}, u32[]{:S(2)}, u32[]{:S(2)}) %collective-permute-start.24) | collective-permute-done | bytes 131104 | tf_op jit(solution)/shard_map/ppermute | solution.py:57
  (47 shorter events, 13.7 us)
Async XLA Ops:
  2.2 30.3 %collective-permute-start = (bf16[256,1152]{1,0:T(8,128)(2,1)S(1)}, bf16[256,1152]{1,0:T(8,128)(2,1)}, u32[]{:S(2)}, u32[]{:S(2)}) collective-permute-start(bf16[256,1152]{1,0:T(8,128)(2,1)S(1)} %get-tuple-element.35.refs_0_), channel_id=1, source_target_pairs={{4,0},{5,1},{6,2},{7,3},{0,4},{1,5},{2,6},{3,7},{12,8},{13,9},{14,... | collective-permute-start | bytes 1769480 | tf_op jit(solution)/shard_map/ppermute | solution.py:57
  6.3 27.8 %collective-permute-start.2 = (bf16[256,1152]{1,0:T(8,128)(2,1)S(1)}, bf16[256,1152]{1,0:T(8,128)(2,1)S(1)}, u32[]{:S(2)}, u32[]{:S(2)}) collective-permute-start(bf16[256,1152]{1,0:T(8,128)(2,1)S(1)} %get-tuple-element.35.refs_0_), channel_id=1, source_target_pairs={{2,0},{3,1},{0,2},{1,3},{6,4},{7,5},{4,6},{5,7},{10,8},{11,9},{8,1... | collective-permute-start | bytes 1769480 | tf_op jit(solution)/shard_map/ppermute | solution.py:57
  7.9 26.3 %collective-permute-start.1 = (bf16[256,1152]{1,0:T(8,128)(2,1)S(1)}, bf16[256,1152]{1,0:T(8,128)(2,1)}, u32[]{:S(2)}, u32[]{:S(2)}) collective-permute-start(bf16[256,1152]{1,0:T(8,128)(2,1)S(1)} %get-tuple-element.35.refs_0_), channel_id=1, source_target_pairs={{8,0},{9,1},{10,2},{11,3},{12,4},{13,5},{14,6},{15,7},{0,8},{1,9},... | collective-permute-start | bytes 1769480 | tf_op jit(solution)/shard_map/ppermute | solution.py:57
  9.4 24.8 %collective-permute-start.4 = (bf16[256,1408]{1,0:T(8,128)(2,1)S(1)}, bf16[256,1408]{1,0:T(8,128)(2,1)S(1)}, u32[]{:S(2)}, u32[]{:S(2)}) collective-permute-start(bf16[256,1408]{1,0:T(8,128)(2,1)S(1)} %get-tuple-element.37.refs_3_.refs_1_.refs_10_), channel_id=1, source_target_pairs={{16,0},{17,1},{18,2},{19,3},{20,4},{21,5},{22,6},{23,7},{24,8},{25... | collective-permute-start | bytes 2162696 | tf_op jit(solution)/shard_map/ppermute | solution.py:57
  10.9 23.3 %collective-permute-start.3 = (bf16[256,1408]{1,0:T(8,128)(2,1)S(1)}, bf16[256,1408]{1,0:T(8,128)(2,1)S(1)}, u32[]{:S(2)}, u32[]{:S(2)}) collective-permute-start(bf16[256,1408]{1,0:T(8,128)(2,1)S(1)} %get-tuple-element.37.refs_3_.refs_1_.refs_10_), channel_id=1, source_target_pairs={{1,0},{0,1},{3,2},{2,3},{5,4},{4,5},{7,6},{6,7},{9,8},{8,9},{11,10... | collective-permute-start | bytes 2162696 | tf_op jit(solution)/shard_map/ppermute | solution.py:57
  34.2 6.3 %collective-permute-start.5 = (bf16[256,1408]{1,0:T(8,128)(2,1)S(1)}, bf16[256,1408]{1,0:T(8,128)(2,1)S(1)}, u32[]{:S(2)}, u32[]{:S(2)}) collective-permute-start(bf16[256,1408]{1,0:T(8,128)(2,1)S(1)} %collective-permute-done.4.refs_5_.refs_3_.refs_0_.refs_12_), channel_id=1, source_target_pairs={{1,0},{0,1},{3,2},{2,3},{5,4},{4,5},{7,6},{6,7},{9,8},{8,9},{11,10... | collective-permute-start | bytes 2162696 | tf_op jit(solution)/shard_map/ppermute | solution.py:57
  34.3 3.7 %collective-permute-start.6 = (bf16[256,1152]{1,0:T(8,128)(2,1)}, bf16[256,1152]{1,0:T(8,128)(2,1)S(1)}, u32[]{:S(2)}, u32[]{:S(2)}) collective-permute-start(bf16[256,1152]{1,0:T(8,128)(2,1)} %collective-permute-done.refs_3_.refs_5_), channel_id=1, source_target_pairs={{1,0},{0,1},{3,2},{2,3},{5,4},{4,5},{7,6},{6,7},{9,8},{8,9},{11,10... | collective-permute-start | bytes 1769480 | tf_op jit(solution)/shard_map/ppermute | solution.py:57
  34.8 17.4 %collective-permute-start.8 = (bf16[256,1152]{1,0:T(8,128)(2,1)}, bf16[256,1152]{1,0:T(8,128)(2,1)S(1)}, u32[]{:S(2)}, u32[]{:S(2)}) collective-permute-start(bf16[256,1152]{1,0:T(8,128)(2,1)} %collective-permute-done.refs_3_.refs_5_), channel_id=1, source_target_pairs={{16,0},{17,1},{18,2},{19,3},{20,4},{21,5},{22,6},{23,7},{24,8},{25... | collective-permute-start | bytes 1769480 | tf_op jit(solution)/shard_map/ppermute | solution.py:57
  36.3 15.8 %collective-permute-start.7 = (bf16[256,1152]{1,0:T(8,128)(2,1)S(1)}, bf16[256,1152]{1,0:T(8,128)(2,1)S(1)}, u32[]{:S(2)}, u32[]{:S(2)}) collective-permute-start(bf16[256,1152]{1,0:T(8,128)(2,1)S(1)} %collective-permute-done.2.refs_2_), channel_id=1, source_target_pairs={{8,0},{9,1},{10,2},{11,3},{12,4},{13,5},{14,6},{15,7},{0,8},{1,9},... | collective-permute-start | bytes 1769480 | tf_op jit(solution)/shard_map/ppermute | solution.py:57
  37.9 14.3 %collective-permute-start.9 = (bf16[512,256]{1,0:T(8,128)(2,1)S(1)}, bf16[512,256]{1,0:T(8,128)(2,1)S(1)}, u32[]{:S(2)}, u32[]{:S(2)}) collective-permute-start(bf16[512,256]{1,0:T(8,128)(2,1)S(1)} %shard_map.43), channel_id=1, source_target_pairs={{4,0},{5,1},{6,2},{7,3},{0,4},{1,5},{2,6},{3,7},{12,8},{13,9},{14,... | collective-permute-start | bytes 786440 | tf_op jit(solution)/shard_map/ppermute | solution.py:57
  52.2 4.9 %collective-permute-start.10 = (bf16[256,1152]{1,0:T(8,128)(2,1)S(1)}, bf16[256,1152]{1,0:T(8,128)(2,1)S(1)}, u32[]{:S(2)}, u32[]{:S(2)}) collective-permute-start(bf16[256,1152]{1,0:T(8,128)(2,1)S(1)} %collective-permute-done.8.refs_7_.refs_3_), channel_id=1, source_target_pairs={{1,0},{0,1},{3,2},{2,3},{5,4},{4,5},{7,6},{6,7},{9,8},{8,9},{11,10... | collective-permute-start | bytes 1769480 | tf_op jit(solution)/shard_map/ppermute | solution.py:57
  52.2 6.9 %collective-permute-start.11 = (bf16[512,256]{1,0:T(8,128)(2,1)S(1)}, bf16[512,256]{1,0:T(8,128)(2,1)S(1)}, u32[]{:S(2)}, u32[]{:S(2)}) collective-permute-start(bf16[512,256]{1,0:T(8,128)(2,1)S(1)} %collective-permute-done.9.refs_14_), channel_id=1, source_target_pairs={{1,0},{0,1},{3,2},{2,3},{5,4},{4,5},{7,6},{6,7},{9,8},{8,9},{11,10... | collective-permute-start | bytes 786440 | tf_op jit(solution)/shard_map/ppermute | solution.py:57
  60.4 5.7 %collective-permute-start.12 = (bf16[272,256]{1,0:T(8,128)(2,1)S(1)}, bf16[272,256]{1,0:T(8,128)(2,1)S(1)}, u32[]{:S(2)}, u32[]{:S(2)}) collective-permute-start(bf16[272,256]{1,0:T(8,128)(2,1)S(1)} %get-tuple-element.56), channel_id=1, source_target_pairs={{8,0},{9,1},{10,2},{11,3},{12,4},{13,5},{14,6},{15,7},{0,8},{1,9},... | collective-permute-start | bytes 417800 | tf_op jit(solution)/shard_map/ppermute | solution.py:57
  61.1 6.6 %collective-permute-start.13 = (bf16[272,256]{1,0:T(8,128)(2,1)S(1)}, bf16[272,256]{1,0:T(8,128)(2,1)S(1)}, u32[]{:S(2)}, u32[]{:S(2)}) collective-permute-start(bf16[272,256]{1,0:T(8,128)(2,1)S(1)} %get-tuple-element.57), channel_id=1, source_target_pairs={{2,0},{3,1},{0,2},{1,3},{6,4},{7,5},{4,6},{5,7},{10,8},{11,9},{8,1... | collective-permute-start | bytes 417800 | tf_op jit(solution)/shard_map/ppermute | solution.py:57
  61.6 8.7 %collective-permute-start.14 = (bf16[272,256]{1,0:T(8,128)(2,1)S(1)}, bf16[272,256]{1,0:T(8,128)(2,1)S(1)}, u32[]{:S(2)}, u32[]{:S(2)}) collective-permute-start(bf16[272,256]{1,0:T(8,128)(2,1)S(1)} %get-tuple-element.58), channel_id=1, source_target_pairs={{10,0},{11,1},{8,2},{9,3},{14,4},{15,5},{12,6},{13,7},{2,8},{3,9},... | collective-permute-start | bytes 417800 | tf_op jit(solution)/shard_map/ppermute | solution.py:57
  70.4 8.1 %collective-permute-start.18 = (bf16[256,256]{1,0:T(8,128)(2,1)S(1)}, bf16[256,256]{1,0:T(8,128)(2,1)S(1)}, u32[]{:S(2)}, u32[]{:S(2)}) collective-permute-start(bf16[256,256]{1,0:T(8,128)(2,1)S(1)} %get-tuple-element.59.refs_5_), channel_id=1, source_target_pairs={{4,0},{5,1},{6,2},{7,3},{0,4},{1,5},{2,6},{3,7},{12,8},{13,9},{14,... | collective-permute-start | bytes 393224 | tf_op jit(solution)/shard_map/ppermute | solution.py:57
  71.8 7.7 %collective-permute-start.16 = (bf16[256,256]{1,0:T(8,128)(2,1)S(1)}, bf16[256,256]{1,0:T(8,128)(2,1)S(1)}, u32[]{:S(2)}, u32[]{:S(2)}) collective-permute-start(bf16[256,256]{1,0:T(8,128)(2,1)S(1)} %get-tuple-element.59.refs_5_), channel_id=1, source_target_pairs={{16,0},{17,1},{18,2},{19,3},{20,4},{21,5},{22,6},{23,7},{24,8},{25... | collective-permute-start | bytes 393224 | tf_op jit(solution)/shard_map/ppermute | solution.py:57
  78.5 5.1 %collective-permute-start.20 = (bf16[256,256]{1,0:T(8,128)(2,1)S(1)}, bf16[256,256]{1,0:T(8,128)(2,1)S(1)}, u32[]{:S(2)}, u32[]{:S(2)}) collective-permute-start(bf16[256,256]{1,0:T(8,128)(2,1)S(1)} %collective-permute-done.18.refs_9_), channel_id=1, source_target_pairs={{16,0},{17,1},{18,2},{19,3},{20,4},{21,5},{22,6},{23,7},{24,8},{25... | collective-permute-start | bytes 393224 | tf_op jit(solution)/shard_map/ppermute | solution.py:57
  79.0 4.6 %collective-permute-start.15 = (bf16[256,256]{1,0:T(8,128)(2,1)S(1)}, bf16[256,256]{1,0:T(8,128)(2,1)S(1)}, u32[]{:S(2)}, u32[]{:S(2)}) collective-permute-start(bf16[256,256]{1,0:T(8,128)(2,1)S(1)} %get-tuple-element.59.refs_5_), channel_id=1, source_target_pairs={{1,0},{0,1},{3,2},{2,3},{5,4},{4,5},{7,6},{6,7},{9,8},{8,9},{11,10... | collective-permute-start | bytes 393224 | tf_op jit(solution)/shard_map/ppermute | solution.py:57
  79.0 4.6 %collective-permute-start.19 = (bf16[256,256]{1,0:T(8,128)(2,1)S(1)}, bf16[256,256]{1,0:T(8,128)(2,1)S(1)}, u32[]{:S(2)}, u32[]{:S(2)}) collective-permute-start(bf16[256,256]{1,0:T(8,128)(2,1)S(1)} %collective-permute-done.18.refs_9_), channel_id=1, source_target_pairs={{1,0},{0,1},{3,2},{2,3},{5,4},{4,5},{7,6},{6,7},{9,8},{8,9},{11,10... | collective-permute-start | bytes 393224 | tf_op jit(solution)/shard_map/ppermute | solution.py:57
  79.5 4.1 %collective-permute-start.17 = (bf16[256,256]{1,0:T(8,128)(2,1)S(1)}, bf16[256,256]{1,0:T(8,128)(2,1)S(1)}, u32[]{:S(2)}, u32[]{:S(2)}) collective-permute-start(bf16[256,256]{1,0:T(8,128)(2,1)S(1)} %collective-permute-done.16.refs_7_), channel_id=1, source_target_pairs={{1,0},{0,1},{3,2},{2,3},{5,4},{4,5},{7,6},{6,7},{9,8},{8,9},{11,10... | collective-permute-start | bytes 393224 | tf_op jit(solution)/shard_map/ppermute | solution.py:57
  86.2 5.6 %collective-permute-start.22 = (bf16[256,256]{1,0:T(8,128)(2,1)S(1)}, bf16[256,256]{1,0:T(8,128)(2,1)S(1)}, u32[]{:S(2)}, u32[]{:S(2)}) collective-permute-start(bf16[256,256]{1,0:T(8,128)(2,1)S(1)} %get-tuple-element.62), channel_id=1, source_target_pairs={{8,0},{9,1},{10,2},{11,3},{12,4},{13,5},{14,6},{15,7},{0,8},{1,9},... | collective-permute-start | bytes 393224 | tf_op jit(solution)/shard_map/ppermute | solution.py:57
  86.7 6.4 %collective-permute-start.23 = (bf16[256,256]{1,0:T(8,128)(2,1)S(1)}, bf16[256,256]{1,0:T(8,128)(2,1)S(1)}, u32[]{:S(2)}, u32[]{:S(2)}) collective-permute-start(bf16[256,256]{1,0:T(8,128)(2,1)S(1)} %get-tuple-element.63), channel_id=1, source_target_pairs={{2,0},{3,1},{0,2},{1,3},{6,4},{7,5},{4,6},{5,7},{10,8},{11,9},{8,1... | collective-permute-start | bytes 393224 | tf_op jit(solution)/shard_map/ppermute | solution.py:57
  87.3 8.5 %collective-permute-start.24 = (bf16[256,256]{1,0:T(8,128)(2,1)S(1)}, bf16[256,256]{1,0:T(8,128)(2,1)S(1)}, u32[]{:S(2)}, u32[]{:S(2)}) collective-permute-start(bf16[256,256]{1,0:T(8,128)(2,1)S(1)} %get-tuple-element.64), channel_id=1, source_target_pairs={{10,0},{11,1},{8,2},{9,3},{14,4},{15,5},{12,6},{13,7},{2,8},{3,9},... | collective-permute-start | bytes 393224 | tf_op jit(solution)/shard_map/ppermute | solution.py:57
  (5 other events, 8.6 us)

commit v9 on v8

--- a/solution.py
+++ b/solution.py
@@ -108,7 +108,7 @@
         out_ref[(k + 1) * m : (k + 2) * m, :] = ref[:, ref.shape[1] - c :]
 
 
-def stack_seeds(seeds, packed):
+def stack_seeds(seeds, packed, work=0):
     m, c = seeds.shape
     out = shape(((len(packed) + 1) * m, c))
     return pl.pallas_call(
@@ -117,6 +117,7 @@
         in_specs=[VMEM] * (len(packed) + 1),
         out_specs=VMEM,
         compiler_params=limits(seeds, *packed, out),
+        cost_estimate=pl.CostEstimate(flops=work, bytes_accessed=2 * m * c, transcendentals=0),
     )(seeds, *packed)
 
 
@@ -138,9 +139,7 @@
         out_ref[r : r + 1, :] = jnp.where(hits, 1, 0)
 
 
-def flags_call(layout, m, t_parts, s_parts, unit, pattern, *earlier):
-    place = jnp.stack([lax.axis_index("row"), lax.axis_index("col")]).astype(jnp.int32)
-    place = after(place, *earlier)
+def flags_call(layout, m, t_parts, s_parts, unit, pattern, place):
     out = shape((len(t_parts), len(s_parts) * unit), jnp.int32)
     smem = pl.BlockSpec(memory_space=pltpu.SMEM)
     return pl.pallas_call(
@@ -388,7 +387,8 @@
             seeds_map.append((stack, o["y"] * m, m, 0))
     t_parts = [(t_offsets[i], k) for i in t_order for k in range(0, m, sub)]
     s_parts = [(o, k) for o in s_layout for k in range(0, m, sub)]
-    units, packed = unit_rows(embeddings, seed_labels)
+    place = jnp.stack([lax.axis_index("row"), lax.axis_index("col")]).astype(jnp.int32)
+    units, packed = unit_rows(after(embeddings, place), seed_labels)
 
     t_pieces, kerns, accs, rects = [], [], [], []
     s_pieces = [None] * len(groups)
@@ -413,7 +413,7 @@
 
     zh, zl, x = fetch([units], "zh"), fetch([units], "zl"), fetch([units], "x")
     y, own_core = fetch([packed], "y"), fetch([packed], "core")
-    flags = flags_call(layout, m, t_parts, s_parts, sub, pattern, *zh)
+    flags = flags_call(layout, m, t_parts, s_parts, sub, pattern, after(place, *zh))
     done = zh + zl + x + y + own_core + [flags]
     zh_y, zl_x = fetch(zh, "y", *done), fetch(zl, "x", *done)
     y_core = [fetch([v], "core", *done) for v in y]
@@ -429,7 +429,8 @@
     s_pieces[2] = zh_y
     early, last = len(near_t), len(t_order)
     gram = rectangle(0, early, 0, 1) + rectangle(0, early, 1, 2)
-    done = zh_y + zl_x + zh_core + seeds_zh + gram
+    seeds_zh = [stack_seeds(after(v, *gram), [], 2 * 10**10) for v in seeds_zh]
+    done = zh_y + zl_x + zh_core + gram + seeds_zh
     zh_y_core = fetch(zh_y, "core", *done)
     s_pieces[3] = zh_y_core
     seeds_core = fetch(seeds_zh, "core", *done)

time: 97 us -> 94.9 us (0.978)
  Pallas kernels: 17.1 us -> 11.7 us
  waiting for transfers between devices: 53.7 us -> 56.1 us
  starting transfers between devices: 22.9 us -> 23.9 us
    pallas_call x5, Pallas kernels: 12.4 us -> 6.96 us  [gram_call(): pl.pallas_call(functools.partial(gram_kernel, len(t_pieces), len(s_pieces...]
    ppermute x25, waiting for transfers between devices: 53.7 us -> 56.1 us  [fetch(): return lax.ppermute(value, AXES, pairs)]
    ppermute x25, starting transfers between devices: 22.9 us -> 23.9 us  [fetch(): return lax.ppermute(value, AXES, pairs)]
  transfers between devices with their start and end apart: 25 -> 25, of which waited for: 11 -> 13; matrix products, arithmetic and copies ran while one was open for 0% -> 0% of each run, Pallas kernels for 14% -> 8%
where the time goes in v9:
time: 94.9 us; the launch traced here: 94.7 us
  waiting for transfers between devices  56.1 us (59%)
  starting transfers between devices  23.9 us (25%)
  Pallas kernels  11.7 us (12%)
  local copies, waits for them, and re-layouts  2.67 us (3%)
    ppermute x25, waiting for transfers between devices, fetch(): return lax.ppermute(value, AXES, pairs)  56.1 us
    ppermute x25, starting transfers between devices, fetch(): return lax.ppermute(value, AXES, pairs)  23.9 us
    pallas_call x5, Pallas kernels, gram_call(): pl.pallas_call(functools.partial(gram_kernel, len(t_pieces), len(s_pieces...  6.96 us
    unnamed x8, local copies, waits for them, and re-layouts  2.67 us
    pallas_call x2, Pallas kernels, spread_call(): pl.pallas_call(functools.partial(spread_kernel, plan, len(kerns), len(acc...  2.57 us
  transfers between devices with their start and end apart: 25, of which 13 were waited for; matrix products, arithmetic and copies ran while one was open for 0% of the time, Pallas kernels for 8%

profile of v9, /device:TPU:0, one launch (start us, length us, event | category | flops | bytes accessed | tf_op | source)
XLA Modules:
  0.0 94.7 jit_solution(11746587596564382015)
XLA Ops:
  2.3 4.1 %collective-permute-start = (bf16[256,1152]{1,0:T(8,128)(2,1)S(1)}, bf16[256,1152]{1,0:T(8,128)(2,1)S(1)}, u32[]{:S(2)}, u32[]{:S(2)}) collective-permute-start(bf16[256,1152]{1,0:T(8,128)(2,1)S(1)} %get-tuple-element.38.refs_0_), channel_id=1, source_target_pairs={{4,0},{5,1},{6,2},{7,3},{0,4},{1,5},{2,6},{3,7},{12,8},{13,9},{14,... | collective-permute-start | bytes 1769480 | tf_op jit(solution)/shard_map/ppermute | solution.py:57
  6.4 1.6 %collective-permute-start.2 = (bf16[256,1152]{1,0:T(8,128)(2,1)S(1)}, bf16[256,1152]{1,0:T(8,128)(2,1)S(1)}, u32[]{:S(2)}, u32[]{:S(2)}) collective-permute-start(bf16[256,1152]{1,0:T(8,128)(2,1)S(1)} %get-tuple-element.38.refs_0_), channel_id=1, source_target_pairs={{2,0},{3,1},{0,2},{1,3},{6,4},{7,5},{4,6},{5,7},{10,8},{11,9},{8,1... | collective-permute-start | bytes 1769480 | tf_op jit(solution)/shard_map/ppermute | solution.py:57
  8.0 1.5 %collective-permute-start.1 = (bf16[256,1152]{1,0:T(8,128)(2,1)S(1)}, bf16[256,1152]{1,0:T(8,128)(2,1)S(1)}, u32[]{:S(2)}, u32[]{:S(2)}) collective-permute-start(bf16[256,1152]{1,0:T(8,128)(2,1)S(1)} %get-tuple-element.38.refs_0_), channel_id=1, source_target_pairs={{8,0},{9,1},{10,2},{11,3},{12,4},{13,5},{14,6},{15,7},{0,8},{1,9},... | collective-permute-start | bytes 1769480 | tf_op jit(solution)/shard_map/ppermute | solution.py:57
  9.5 1.5 %collective-permute-start.4 = (bf16[256,1408]{1,0:T(8,128)(2,1)S(1)}, bf16[256,1408]{1,0:T(8,128)(2,1)S(1)}, u32[]{:S(2)}, u32[]{:S(2)}) collective-permute-start(bf16[256,1408]{1,0:T(8,128)(2,1)S(1)} %get-tuple-element.40.refs_3_.refs_1_.refs_10_), channel_id=1, source_target_pairs={{16,0},{17,1},{18,2},{19,3},{20,4},{21,5},{22,6},{23,7},{24,8},{25... | collective-permute-start | bytes 2162696 | tf_op jit(solution)/shard_map/ppermute | solution.py:57
  11.0 21.5 %collective-permute-done.refs_3_.refs_5_ = bf16[256,1152]{1,0:T(8,128)(2,1)S(1)} collective-permute-done((bf16[256,1152]{1,0:T(8,128)(2,1)S(1)}, bf16[256,1152]{1,0:T(8,128)(2,1)S(1)}, u32[]{:S(2)}, u32[]{:S(2)}) %collective-permute-start) | collective-permute-done | bytes 589856 | tf_op jit(solution)/shard_map/ppermute | solution.py:57
  34.8 1.6 %collective-permute-start.8 = (bf16[256,1152]{1,0:T(8,128)(2,1)S(1)}, bf16[256,1152]{1,0:T(8,128)(2,1)S(1)}, u32[]{:S(2)}, u32[]{:S(2)}) collective-permute-start(bf16[256,1152]{1,0:T(8,128)(2,1)S(1)} %collective-permute-done.refs_3_.refs_5_), channel_id=1, source_target_pairs={{16,0},{17,1},{18,2},{19,3},{20,4},{21,5},{22,6},{23,7},{24,8},{25... | collective-permute-start | bytes 1769480 | tf_op jit(solution)/shard_map/ppermute | solution.py:57
  36.5 1.5 %collective-permute-start.7 = (bf16[256,1152]{1,0:T(8,128)(2,1)S(1)}, bf16[256,1152]{1,0:T(8,128)(2,1)S(1)}, u32[]{:S(2)}, u32[]{:S(2)}) collective-permute-start(bf16[256,1152]{1,0:T(8,128)(2,1)S(1)} %collective-permute-done.2.refs_2_), channel_id=1, source_target_pairs={{8,0},{9,1},{10,2},{11,3},{12,4},{13,5},{14,6},{15,7},{0,8},{1,9},... | collective-permute-start | bytes 1769480 | tf_op jit(solution)/shard_map/ppermute | solution.py:57
  38.0 1.3 %shard_map.40 = (bf16[768,512]{1,0:T(8,128)(2,1)S(1)}, f32[768,128]{1,0:T(8,128)S(1)}) custom-call(s32[8,2048]{1,0:T(8,128)S(1)} %shard_map.38.flags, bf16[256,1152]{1,0:T(8,128)(2,1)S(1)} %get-tuple-element.38.refs_0_, bf16[256,1152]{1,0:T(8,128)(2,1)S(1)} %collective-permute-done.1.refs_1_, bf16[256,1152]{1,0:T(8,128)(2,1)S(1)} %collective-permute-done.2.refs_2_, ...), custom_call_target="tpu_custom_call" | custom-call | flops 905969664 | bytes 2949120 | tf_op jit(solution)/shard_map/pallas_call | solution.py:220
  39.3 2.5 %shard_map.39 = (bf16[768,1024]{1,0:T(8,128)(2,1)S(1)}, f32[768,128]{1,0:T(8,128)S(1)}) custom-call(s32[8,2048]{1,0:T(8,128)S(1)} %shard_map.38.flags, bf16[256,1152]{1,0:T(8,128)(2,1)S(1)} %get-tuple-element.38.refs_0_, bf16[256,1152]{1,0:T(8,128)(2,1)S(1)} %collective-permute-done.1.refs_1_, bf16[256,1152]{1,0:T(8,128)(2,1)S(1)} %collective-permute-done.2.refs_2_, ...), custom_call_target="tpu_custom_call" | custom-call | flops 1811939328 | bytes 4128768 | tf_op jit(solution)/shard_map/pallas_call | solution.py:220
  41.8 7.9 %collective-permute-done.9.seed_ref = bf16[512,256]{1,0:T(8,128)(2,1)S(1)} collective-permute-done((bf16[512,256]{1,0:T(8,128)(2,1)S(1)}, bf16[512,256]{1,0:T(8,128)(2,1)S(1)}, u32[]{:S(2)}, u32[]{:S(2)}) %collective-permute-start.9) | collective-permute-done | bytes 262176 | tf_op jit(solution)/shard_map/ppermute | solution.py:57
  52.8 1.5 %shard_map.41 = (bf16[256,1792]{1,0:T(8,128)(2,1)S(1)}, f32[256,128]{1,0:T(8,128)S(1)}) custom-call(s32[8,2048]{1,0:T(8,128)S(1)} %shard_map.38.flags, bf16[256,1152]{1,0:T(8,128)(2,1)S(1)} %collective-permute-done.7.refs_0_.refs_3_, bf16[256,1408]{1,0:T(8,128)(2,1)S(1)} %get-tuple-element.40.refs_3_.refs_1_.refs_10_, ...), custom_call_target="tpu_custom_call" | custom-call | flops 1056964608 | bytes 4718592 | tf_op jit(solution)/shard_map/pallas_call | solution.py:220
  55.3 1.3 %shard_map.46 = (f32[256,256]{1,0:T(8,128)S(1)}, f32[1,256]{1,0:T(1,128)S(1)}, bf16[272,256]{1,0:T(8,128)(2,1)S(1)}, bf16[272,256]{1,0:T(8,128)(2,1)S(1)}, bf16[272,256]{1,0:T(8,128)(2,1)S(1)}) custom-call(bf16[768,1024]{1,0:T(8,128)(2,1)S(1)} %get-tuple-element.42.refs_0_, bf16[768,512]{1,0:T(8,128)(2,1)S(1)} %get-tuple-element.44.refs_1_, ...), custom_call_target="tpu_custom_call" | custom-call | flops 1073741824 | bytes 5242880 | tf_op jit(solution)/shard_map/pallas_call | solution.py:296
  56.6 1.6 %collective-permute-start.12 = (bf16[272,256]{1,0:T(8,128)(2,1)S(1)}, bf16[272,256]{1,0:T(8,128)(2,1)S(1)}, u32[]{:S(2)}, u32[]{:S(2)}) collective-permute-start(bf16[272,256]{1,0:T(8,128)(2,1)S(1)} %get-tuple-element.60), channel_id=1, source_target_pairs={{8,0},{9,1},{10,2},{11,3},{12,4},{13,5},{14,6},{15,7},{0,8},{1,9},... | collective-permute-start | bytes 417800 | tf_op jit(solution)/shard_map/ppermute | solution.py:57
  58.1 3.6 %collective-permute-start.13 = (bf16[272,256]{1,0:T(8,128)(2,1)S(1)}, bf16[272,256]{1,0:T(8,128)(2,1)S(1)}, u32[]{:S(2)}, u32[]{:S(2)}) collective-permute-start(bf16[272,256]{1,0:T(8,128)(2,1)S(1)} %get-tuple-element.61), channel_id=1, source_target_pairs={{2,0},{3,1},{0,2},{1,3},{6,4},{7,5},{4,6},{5,7},{10,8},{11,9},{8,1... | collective-permute-start | bytes 417800 | tf_op jit(solution)/shard_map/ppermute | solution.py:57
  62.2 4.0 %collective-permute-done.13.refs_1_ = bf16[272,256]{1,0:T(8,128)(2,1)S(1)} collective-permute-done((bf16[272,256]{1,0:T(8,128)(2,1)S(1)}, bf16[272,256]{1,0:T(8,128)(2,1)S(1)}, u32[]{:S(2)}, u32[]{:S(2)}) %collective-permute-start.13) | collective-permute-done | bytes 139296 | tf_op jit(solution)/shard_map/ppermute | solution.py:57
  66.2 2.0 %collective-permute-done.14.refs_2_ = bf16[272,256]{1,0:T(8,128)(2,1)S(1)} collective-permute-done((bf16[272,256]{1,0:T(8,128)(2,1)S(1)}, bf16[272,256]{1,0:T(8,128)(2,1)S(1)}, u32[]{:S(2)}, u32[]{:S(2)}) %collective-permute-start.14) | collective-permute-done | bytes 139296 | tf_op jit(solution)/shard_map/ppermute | solution.py:57
  69.6 7.0 %collective-permute-done.18.refs_9_ = bf16[256,256]{1,0:T(8,128)(2,1)S(1)} collective-permute-done((bf16[256,256]{1,0:T(8,128)(2,1)S(1)}, bf16[256,256]{1,0:T(8,128)(2,1)S(1)}, u32[]{:S(2)}, u32[]{:S(2)}) %collective-permute-start.18) | collective-permute-done | bytes 131104 | tf_op jit(solution)/shard_map/ppermute | solution.py:57
  77.7 4.0 %collective-permute-done.20.refs_11_ = bf16[256,256]{1,0:T(8,128)(2,1)S(1)} collective-permute-done((bf16[256,256]{1,0:T(8,128)(2,1)S(1)}, bf16[256,256]{1,0:T(8,128)(2,1)S(1)}, u32[]{:S(2)}, u32[]{:S(2)}) %collective-permute-start.20) | collective-permute-done | bytes 131104 | tf_op jit(solution)/shard_map/ppermute | solution.py:57
  81.7 1.3 %collective-permute-done.21.refs_12_ = bf16[256,256]{1,0:T(8,128)(2,1)S(1)} collective-permute-done((bf16[256,256]{1,0:T(8,128)(2,1)S(1)}, bf16[256,256]{1,0:T(8,128)(2,1)S(1)}, u32[]{:S(2)}, u32[]{:S(2)}) %collective-permute-start.21) | collective-permute-done | bytes 131104 | tf_op jit(solution)/shard_map/ppermute | solution.py:57
  84.3 1.6 %collective-permute-start.22 = (bf16[256,256]{1,0:T(8,128)(2,1)S(1)}, bf16[256,256]{1,0:T(8,128)(2,1)S(1)}, u32[]{:S(2)}, u32[]{:S(2)}) collective-permute-start(bf16[256,256]{1,0:T(8,128)(2,1)S(1)} %get-tuple-element.66), channel_id=1, source_target_pairs={{8,0},{9,1},{10,2},{11,3},{12,4},{13,5},{14,6},{15,7},{0,8},{1,9},... | collective-permute-start | bytes 393224 | tf_op jit(solution)/shard_map/ppermute | solution.py:57
  85.9 2.0 %collective-permute-start.24 = (bf16[256,256]{1,0:T(8,128)(2,1)S(1)}, bf16[256,256]{1,0:T(8,128)(2,1)S(1)}, u32[]{:S(2)}, u32[]{:S(2)}) collective-permute-start(bf16[256,256]{1,0:T(8,128)(2,1)S(1)} %get-tuple-element.68), channel_id=1, source_target_pairs={{10,0},{11,1},{8,2},{9,3},{14,4},{15,5},{12,6},{13,7},{2,8},{3,9},... | collective-permute-start | bytes 393224 | tf_op jit(solution)/shard_map/ppermute | solution.py:57
  87.8 2.1 %collective-permute-done.22.refs_0_ = bf16[256,256]{1,0:T(8,128)(2,1)S(1)} collective-permute-done((bf16[256,256]{1,0:T(8,128)(2,1)S(1)}, bf16[256,256]{1,0:T(8,128)(2,1)S(1)}, u32[]{:S(2)}, u32[]{:S(2)}) %collective-permute-start.22) | collective-permute-done | bytes 131104 | tf_op jit(solution)/shard_map/ppermute | solution.py:57
  89.9 2.4 %collective-permute-done.23.refs_1_ = bf16[256,256]{1,0:T(8,128)(2,1)S(1)} collective-permute-done((bf16[256,256]{1,0:T(8,128)(2,1)S(1)}, bf16[256,256]{1,0:T(8,128)(2,1)S(1)}, u32[]{:S(2)}, u32[]{:S(2)}) %collective-permute-start.23) | collective-permute-done | bytes 131104 | tf_op jit(solution)/shard_map/ppermute | solution.py:57
  92.2 1.6 %collective-permute-done.24.refs_2_ = bf16[256,256]{1,0:T(8,128)(2,1)S(1)} collective-permute-done((bf16[256,256]{1,0:T(8,128)(2,1)S(1)}, bf16[256,256]{1,0:T(8,128)(2,1)S(1)}, u32[]{:S(2)}, u32[]{:S(2)}) %collective-permute-start.24) | collective-permute-done | bytes 131104 | tf_op jit(solution)/shard_map/ppermute | solution.py:57
  (48 shorter events, 13.7 us)
Async XLA Ops:
  2.3 30.2 %collective-permute-start = (bf16[256,1152]{1,0:T(8,128)(2,1)S(1)}, bf16[256,1152]{1,0:T(8,128)(2,1)S(1)}, u32[]{:S(2)}, u32[]{:S(2)}) collective-permute-start(bf16[256,1152]{1,0:T(8,128)(2,1)S(1)} %get-tuple-element.38.refs_0_), channel_id=1, source_target_pairs={{4,0},{5,1},{6,2},{7,3},{0,4},{1,5},{2,6},{3,7},{12,8},{13,9},{14,... | collective-permute-start | bytes 1769480 | tf_op jit(solution)/shard_map/ppermute | solution.py:57
  6.4 27.7 %collective-permute-start.2 = (bf16[256,1152]{1,0:T(8,128)(2,1)S(1)}, bf16[256,1152]{1,0:T(8,128)(2,1)S(1)}, u32[]{:S(2)}, u32[]{:S(2)}) collective-permute-start(bf16[256,1152]{1,0:T(8,128)(2,1)S(1)} %get-tuple-element.38.refs_0_), channel_id=1, source_target_pairs={{2,0},{3,1},{0,2},{1,3},{6,4},{7,5},{4,6},{5,7},{10,8},{11,9},{8,1... | collective-permute-start | bytes 1769480 | tf_op jit(solution)/shard_map/ppermute | solution.py:57
  8.0 26.2 %collective-permute-start.1 = (bf16[256,1152]{1,0:T(8,128)(2,1)S(1)}, bf16[256,1152]{1,0:T(8,128)(2,1)S(1)}, u32[]{:S(2)}, u32[]{:S(2)}) collective-permute-start(bf16[256,1152]{1,0:T(8,128)(2,1)S(1)} %get-tuple-element.38.refs_0_), channel_id=1, source_target_pairs={{8,0},{9,1},{10,2},{11,3},{12,4},{13,5},{14,6},{15,7},{0,8},{1,9},... | collective-permute-start | bytes 1769480 | tf_op jit(solution)/shard_map/ppermute | solution.py:57
  9.5 24.7 %collective-permute-start.4 = (bf16[256,1408]{1,0:T(8,128)(2,1)S(1)}, bf16[256,1408]{1,0:T(8,128)(2,1)S(1)}, u32[]{:S(2)}, u32[]{:S(2)}) collective-permute-start(bf16[256,1408]{1,0:T(8,128)(2,1)S(1)} %get-tuple-element.40.refs_3_.refs_1_.refs_10_), channel_id=1, source_target_pairs={{16,0},{17,1},{18,2},{19,3},{20,4},{21,5},{22,6},{23,7},{24,8},{25... | collective-permute-start | bytes 2162696 | tf_op jit(solution)/shard_map/ppermute | solution.py:57
  11.0 23.2 %collective-permute-start.3 = (bf16[256,1408]{1,0:T(8,128)(2,1)S(1)}, bf16[256,1408]{1,0:T(8,128)(2,1)S(1)}, u32[]{:S(2)}, u32[]{:S(2)}) collective-permute-start(bf16[256,1408]{1,0:T(8,128)(2,1)S(1)} %get-tuple-element.40.refs_3_.refs_1_.refs_10_), channel_id=1, source_target_pairs={{1,0},{0,1},{3,2},{2,3},{5,4},{4,5},{7,6},{6,7},{9,8},{8,9},{11,10... | collective-permute-start | bytes 2162696 | tf_op jit(solution)/shard_map/ppermute | solution.py:57
  34.2 5.1 %collective-permute-start.5 = (bf16[256,1408]{1,0:T(8,128)(2,1)S(1)}, bf16[256,1408]{1,0:T(8,128)(2,1)S(1)}, u32[]{:S(2)}, u32[]{:S(2)}) collective-permute-start(bf16[256,1408]{1,0:T(8,128)(2,1)S(1)} %collective-permute-done.4.refs_5_.refs_3_.refs_0_.refs_12_), channel_id=1, source_target_pairs={{1,0},{0,1},{3,2},{2,3},{5,4},{4,5},{7,6},{6,7},{9,8},{8,9},{11,10... | collective-permute-start | bytes 2162696 | tf_op jit(solution)/shard_map/ppermute | solution.py:57
  34.2 3.7 %collective-permute-start.6 = (bf16[256,1152]{1,0:T(8,128)(2,1)S(1)}, bf16[256,1152]{1,0:T(8,128)(2,1)S(1)}, u32[]{:S(2)}, u32[]{:S(2)}) collective-permute-start(bf16[256,1152]{1,0:T(8,128)(2,1)S(1)} %collective-permute-done.refs_3_.refs_5_), channel_id=1, source_target_pairs={{1,0},{0,1},{3,2},{2,3},{5,4},{4,5},{7,6},{6,7},{9,8},{8,9},{11,10... | collective-permute-start | bytes 1769480 | tf_op jit(solution)/shard_map/ppermute | solution.py:57
  34.8 14.9 %collective-permute-start.9 = (bf16[512,256]{1,0:T(8,128)(2,1)S(1)}, bf16[512,256]{1,0:T(8,128)(2,1)S(1)}, u32[]{:S(2)}, u32[]{:S(2)}) collective-permute-start(bf16[512,256]{1,0:T(8,128)(2,1)S(1)} %shard_map.43), channel_id=1, source_target_pairs={{4,0},{5,1},{6,2},{7,3},{0,4},{1,5},{2,6},{3,7},{12,8},{13,9},{14,... | collective-permute-start | bytes 786440 | tf_op jit(solution)/shard_map/ppermute | solution.py:57
  34.8 15.4 %collective-permute-start.8 = (bf16[256,1152]{1,0:T(8,128)(2,1)S(1)}, bf16[256,1152]{1,0:T(8,128)(2,1)S(1)}, u32[]{:S(2)}, u32[]{:S(2)}) collective-permute-start(bf16[256,1152]{1,0:T(8,128)(2,1)S(1)} %collective-permute-done.refs_3_.refs_5_), channel_id=1, source_target_pairs={{16,0},{17,1},{18,2},{19,3},{20,4},{21,5},{22,6},{23,7},{24,8},{25... | collective-permute-start | bytes 1769480 | tf_op jit(solution)/shard_map/ppermute | solution.py:57
  36.5 15.0 %collective-permute-start.7 = (bf16[256,1152]{1,0:T(8,128)(2,1)S(1)}, bf16[256,1152]{1,0:T(8,128)(2,1)S(1)}, u32[]{:S(2)}, u32[]{:S(2)}) collective-permute-start(bf16[256,1152]{1,0:T(8,128)(2,1)S(1)} %collective-permute-done.2.refs_2_), channel_id=1, source_target_pairs={{8,0},{9,1},{10,2},{11,3},{12,4},{13,5},{14,6},{15,7},{0,8},{1,9},... | collective-permute-start | bytes 1769480 | tf_op jit(solution)/shard_map/ppermute | solution.py:57
  51.5 2.8 %collective-permute-start.10 = (bf16[256,1152]{1,0:T(8,128)(2,1)S(1)}, bf16[256,1152]{1,0:T(8,128)(2,1)S(1)}, u32[]{:S(2)}, u32[]{:S(2)}) collective-permute-start(bf16[256,1152]{1,0:T(8,128)(2,1)S(1)} %collective-permute-done.8.refs_7_.refs_3_), channel_id=1, source_target_pairs={{1,0},{0,1},{3,2},{2,3},{5,4},{4,5},{7,6},{6,7},{9,8},{8,9},{11,10... | collective-permute-start | bytes 1769480 | tf_op jit(solution)/shard_map/ppermute | solution.py:57
  51.5 3.7 %collective-permute-start.11 = (bf16[512,256]{1,0:T(8,128)(2,1)S(1)}, bf16[512,256]{1,0:T(8,128)(2,1)S(1)}, u32[]{:S(2)}, u32[]{:S(2)}) collective-permute-start(bf16[512,256]{1,0:T(8,128)(2,1)S(1)} %shard_map.44.refs_14_), channel_id=1, source_target_pairs={{1,0},{0,1},{3,2},{2,3},{5,4},{4,5},{7,6},{6,7},{9,8},{8,9},{11,10... | collective-permute-start | bytes 786440 | tf_op jit(solution)/shard_map/ppermute | solution.py:57
  56.6 5.6 %collective-permute-start.12 = (bf16[272,256]{1,0:T(8,128)(2,1)S(1)}, bf16[272,256]{1,0:T(8,128)(2,1)S(1)}, u32[]{:S(2)}, u32[]{:S(2)}) collective-permute-start(bf16[272,256]{1,0:T(8,128)(2,1)S(1)} %get-tuple-element.60), channel_id=1, source_target_pairs={{8,0},{9,1},{10,2},{11,3},{12,4},{13,5},{14,6},{15,7},{0,8},{1,9},... | collective-permute-start | bytes 417800 | tf_op jit(solution)/shard_map/ppermute | solution.py:57
  58.1 8.1 %collective-permute-start.13 = (bf16[272,256]{1,0:T(8,128)(2,1)S(1)}, bf16[272,256]{1,0:T(8,128)(2,1)S(1)}, u32[]{:S(2)}, u32[]{:S(2)}) collective-permute-start(bf16[272,256]{1,0:T(8,128)(2,1)S(1)} %get-tuple-element.61), channel_id=1, source_target_pairs={{2,0},{3,1},{0,2},{1,3},{6,4},{7,5},{4,6},{5,7},{10,8},{11,9},{8,1... | collective-permute-start | bytes 417800 | tf_op jit(solution)/shard_map/ppermute | solution.py:57
  61.7 6.5 %collective-permute-start.14 = (bf16[272,256]{1,0:T(8,128)(2,1)S(1)}, bf16[272,256]{1,0:T(8,128)(2,1)S(1)}, u32[]{:S(2)}, u32[]{:S(2)}) collective-permute-start(bf16[272,256]{1,0:T(8,128)(2,1)S(1)} %get-tuple-element.62), channel_id=1, source_target_pairs={{10,0},{11,1},{8,2},{9,3},{14,4},{15,5},{12,6},{13,7},{2,8},{3,9},... | collective-permute-start | bytes 417800 | tf_op jit(solution)/shard_map/ppermute | solution.py:57
  68.4 8.3 %collective-permute-start.18 = (bf16[256,256]{1,0:T(8,128)(2,1)S(1)}, bf16[256,256]{1,0:T(8,128)(2,1)S(1)}, u32[]{:S(2)}, u32[]{:S(2)}) collective-permute-start(bf16[256,256]{1,0:T(8,128)(2,1)S(1)} %get-tuple-element.63.refs_5_), channel_id=1, source_target_pairs={{4,0},{5,1},{6,2},{7,3},{0,4},{1,5},{2,6},{3,7},{12,8},{13,9},{14,... | collective-permute-start | bytes 393224 | tf_op jit(solution)/shard_map/ppermute | solution.py:57
  69.2 8.5 %collective-permute-start.16 = (bf16[256,256]{1,0:T(8,128)(2,1)S(1)}, bf16[256,256]{1,0:T(8,128)(2,1)S(1)}, u32[]{:S(2)}, u32[]{:S(2)}) collective-permute-start(bf16[256,256]{1,0:T(8,128)(2,1)S(1)} %get-tuple-element.63.refs_5_), channel_id=1, source_target_pairs={{16,0},{17,1},{18,2},{19,3},{20,4},{21,5},{22,6},{23,7},{24,8},{25... | collective-permute-start | bytes 393224 | tf_op jit(solution)/shard_map/ppermute | solution.py:57
  76.7 5.0 %collective-permute-start.20 = (bf16[256,256]{1,0:T(8,128)(2,1)S(1)}, bf16[256,256]{1,0:T(8,128)(2,1)S(1)}, u32[]{:S(2)}, u32[]{:S(2)}) collective-permute-start(bf16[256,256]{1,0:T(8,128)(2,1)S(1)} %collective-permute-done.18.refs_9_), channel_id=1, source_target_pairs={{16,0},{17,1},{18,2},{19,3},{20,4},{21,5},{22,6},{23,7},{24,8},{25... | collective-permute-start | bytes 393224 | tf_op jit(solution)/shard_map/ppermute | solution.py:57
  77.2 4.5 %collective-permute-start.15 = (bf16[256,256]{1,0:T(8,128)(2,1)S(1)}, bf16[256,256]{1,0:T(8,128)(2,1)S(1)}, u32[]{:S(2)}, u32[]{:S(2)}) collective-permute-start(bf16[256,256]{1,0:T(8,128)(2,1)S(1)} %get-tuple-element.63.refs_5_), channel_id=1, source_target_pairs={{1,0},{0,1},{3,2},{2,3},{5,4},{4,5},{7,6},{6,7},{9,8},{8,9},{11,10... | collective-permute-start | bytes 393224 | tf_op jit(solution)/shard_map/ppermute | solution.py:57
  77.2 4.5 %collective-permute-start.19 = (bf16[256,256]{1,0:T(8,128)(2,1)S(1)}, bf16[256,256]{1,0:T(8,128)(2,1)S(1)}, u32[]{:S(2)}, u32[]{:S(2)}) collective-permute-start(bf16[256,256]{1,0:T(8,128)(2,1)S(1)} %collective-permute-done.18.refs_9_), channel_id=1, source_target_pairs={{1,0},{0,1},{3,2},{2,3},{5,4},{4,5},{7,6},{6,7},{9,8},{8,9},{11,10... | collective-permute-start | bytes 393224 | tf_op jit(solution)/shard_map/ppermute | solution.py:57
  77.7 4.0 %collective-permute-start.17 = (bf16[256,256]{1,0:T(8,128)(2,1)S(1)}, bf16[256,256]{1,0:T(8,128)(2,1)S(1)}, u32[]{:S(2)}, u32[]{:S(2)}) collective-permute-start(bf16[256,256]{1,0:T(8,128)(2,1)S(1)} %collective-permute-done.16.refs_7_), channel_id=1, source_target_pairs={{1,0},{0,1},{3,2},{2,3},{5,4},{4,5},{7,6},{6,7},{9,8},{8,9},{11,10... | collective-permute-start | bytes 393224 | tf_op jit(solution)/shard_map/ppermute | solution.py:57
  84.3 5.6 %collective-permute-start.22 = (bf16[256,256]{1,0:T(8,128)(2,1)S(1)}, bf16[256,256]{1,0:T(8,128)(2,1)S(1)}, u32[]{:S(2)}, u32[]{:S(2)}) collective-permute-start(bf16[256,256]{1,0:T(8,128)(2,1)S(1)} %get-tuple-element.66), channel_id=1, source_target_pairs={{8,0},{9,1},{10,2},{11,3},{12,4},{13,5},{14,6},{15,7},{0,8},{1,9},... | collective-permute-start | bytes 393224 | tf_op jit(solution)/shard_map/ppermute | solution.py:57
  85.9 6.4 %collective-permute-start.23 = (bf16[256,256]{1,0:T(8,128)(2,1)S(1)}, bf16[256,256]{1,0:T(8,128)(2,1)S(1)}, u32[]{:S(2)}, u32[]{:S(2)}) collective-permute-start(bf16[256,256]{1,0:T(8,128)(2,1)S(1)} %get-tuple-element.67), channel_id=1, source_target_pairs={{2,0},{3,1},{0,2},{1,3},{6,4},{7,5},{4,6},{5,7},{10,8},{11,9},{8,1... | collective-permute-start | bytes 393224 | tf_op jit(solution)/shard_map/ppermute | solution.py:57
  85.9 8.0 %collective-permute-start.24 = (bf16[256,256]{1,0:T(8,128)(2,1)S(1)}, bf16[256,256]{1,0:T(8,128)(2,1)S(1)}, u32[]{:S(2)}, u32[]{:S(2)}) collective-permute-start(bf16[256,256]{1,0:T(8,128)(2,1)S(1)} %get-tuple-element.68), channel_id=1, source_target_pairs={{10,0},{11,1},{8,2},{9,3},{14,4},{15,5},{12,6},{13,7},{2,8},{3,9},... | collective-permute-start | bytes 393224 | tf_op jit(solution)/shard_map/ppermute | solution.py:57
  (5 other events, 17.0 us)

commit v10 on v7

--- a/solution.py
+++ b/solution.py
@@ -109,6 +109,23 @@
     return units, packed, parts
 
 
+def copy_kernel(in_ref, out_ref):
+    out_ref[...] = in_ref[...]
+
+
+def copied(value, work):
+    return pl.pallas_call(
+        copy_kernel,
+        out_shape=shape(value.shape, value.dtype),
+        in_specs=[VMEM],
+        out_specs=VMEM,
+        compiler_params=limits(value, value),
+        cost_estimate=pl.CostEstimate(
+            flops=work, bytes_accessed=4 * value.size, transcendentals=0
+        ),
+    )(value)
+
+
 def flags_kernel(layout, m, t_parts, s_parts, unit, place_ref, pattern_ref, out_ref, block_ref):
     at = layout.coords(place_ref[0], place_ref[1])
 
@@ -127,8 +144,7 @@
         out_ref[r : r + 1, :] = jnp.where(hits, 1, 0)
 
 
-def flags_call(layout, m, t_parts, s_parts, unit, pattern):
-    place = jnp.stack([lax.axis_index("row"), lax.axis_index("col")]).astype(jnp.int32)
+def flags_call(layout, m, t_parts, s_parts, unit, pattern, place):
     out = shape((len(t_parts), len(s_parts) * unit), jnp.int32)
     smem = pl.BlockSpec(memory_space=pltpu.SMEM)
     return pl.pallas_call(
@@ -358,8 +374,9 @@
             layout.fetch(after(v, *earlier), **{axis: k}) for k in other[axis] for v in values
         ]
 
+    place = jnp.stack([lax.axis_index("row"), lax.axis_index("col")]).astype(jnp.int32)
     units, packed, parts = unit_rows(
-        embeddings, seed_labels, zh_chunks + zl_chunks, len(zh_chunks) - 1
+        after(embeddings, place), seed_labels, zh_chunks + zl_chunks, len(zh_chunks) - 1
     )
     zh_parts, zl_parts = parts[: len(zh_chunks)], parts[len(zh_chunks) :]
 
@@ -423,12 +440,13 @@
         rects.append((t0, t1, c0, c1))
         return [acc]
 
-    flags = flags_call(layout, m, t_parts, s_parts, sub, pattern)
+    flags = flags_call(layout, m, t_parts, s_parts, sub, pattern, place)
     zh, zl = fetch(zh_parts[:1], "zh"), fetch(zl_parts[:1], "zl")
     x, y = fetch([units], "x"), fetch([packed], "y")
     own_core = fetch([packed], "core")
     t_pieces += [units] + x + zl
-    done = zh + zl + x + y + own_core
+    seeds = copied(after(seed_labels, *zh), 2 * 10**10)
+    done = zh + zl + x + y + own_core + [seeds]
     zh_next, zl_next = fetch(zh_parts[1:], "zh", *done), fetch(zl_parts[1:], "zl", *done)
     zh_y, zl_x = fetch(zh, "y", *done), fetch(zl, "x", *done)
     y_core = [fetch([v], "core", *done) for v in y]
@@ -437,6 +455,7 @@
     gram = rectangle(0, t_groups[1], 0, 1) + rectangle(t_groups[1], t_groups[2], 0, 1)
     zh_core = fetch(zh, "core", *done, *[p for w in y_core for p in w])
     last = len(t_layout)
+    zh_next = [copied(after(v, *gram), 2 * 10**10) for v in zh_next]
     done = zh_next + zl_next + zh_y + zl_x + zh_core + gram
     zh_y_core = fetch(zh_y, "core", *done)
     s_pieces[1] = zh + zh_core + zh_y + zh_y_core
@@ -464,11 +483,11 @@
         near = [p for v in [panel] + near for p in [v] + fetch([v], "core")]
         return near + far + fetch(far, "core") + far_y + fetch(far_y, "core")
 
-    seeds = s_pieces[0] + s_pieces[-1]
-    own, totals, *others = spread_call(kerns, accs, seeds, c, (*plan, seeds_map))
+    panels_in = s_pieces[0] + s_pieces[-1]
+    own, totals, *others = spread_call(kerns, accs, panels_in, c, (*plan, seeds_map))
     panel, totals = update(
         first_update_kernel,
-        seed_labels,
+        seeds,
         own,
         totals,
         home(others),
@@ -480,7 +499,7 @@
     own, *others = spread_call(kerns, [], panels(panel), c, (*plan, p_map))
     return update(
         last_update_kernel,
-        seed_labels,
+        seeds,
         own,
         totals,
         home(others),

time: 103 us -> 98 us (0.951)
  waiting for transfers between devices: 51.3 us -> 57.1 us
  Pallas kernels: 17.8 us -> 12.6 us
  starting transfers between devices: 29.4 us -> 25.9 us
  local copies, waits for them, and re-layouts: 4.34 us -> 1.97 us
    ppermute x29, waiting for transfers between devices: 51.3 us -> 57.1 us  [fetch(): return lax.ppermute(value, AXES, pairs)]
    pallas_call x5, Pallas kernels: 12.1 us -> 7.54 us  [gram_call(): pl.pallas_call(functools.partial(gram_kernel, len(t_pieces), len(s_pieces...]
    ppermute x29, starting transfers between devices: 29.4 us -> 25.9 us  [fetch(): return lax.ppermute(value, AXES, pairs)]
    unnamed x18 -> x6, local copies, waits for them, and re-layouts: 4.34 us -> 1.97 us
  transfers between devices with their start and end apart: 29 -> 29, of which waited for: 16 -> 17; matrix products, arithmetic and copies ran while one was open for 0% -> 0% of each run, Pallas kernels for 11% -> 8%
where the time goes in v10:
time: 98 us; the launch traced here: 97.8 us
  waiting for transfers between devices  57.1 us (58%)
  starting transfers between devices  25.9 us (26%)
  Pallas kernels  12.6 us (13%)
  local copies, waits for them, and re-layouts  1.97 us (2%)
    ppermute x29, waiting for transfers between devices, fetch(): return lax.ppermute(value, AXES, pairs)  57.1 us
    ppermute x29, starting transfers between devices, fetch(): return lax.ppermute(value, AXES, pairs)  25.9 us
    pallas_call x5, Pallas kernels, gram_call(): pl.pallas_call(functools.partial(gram_kernel, len(t_pieces), len(s_pieces...  7.54 us
    pallas_call x2, Pallas kernels, spread_call(): pl.pallas_call(functools.partial(spread_kernel, plan, len(kerns), len(acc...  2.56 us
    unnamed x6, local copies, waits for them, and re-layouts  1.97 us
  transfers between devices with their start and end apart: 29, of which 17 were waited for; matrix products, arithmetic and copies ran while one was open for 0% of the time, Pallas kernels for 8%

profile of v10, /device:TPU:0, one launch (start us, length us, event | category | flops | bytes accessed | tf_op | source)
XLA Modules:
  0.0 97.8 jit_solution(16933510055463550407)
XLA Ops:
  2.4 4.1 %collective-permute-start = (bf16[192,1152]{1,0:T(8,128)(2,1)S(1)}, bf16[192,1152]{1,0:T(8,128)(2,1)S(1)}, u32[]{:S(2)}, u32[]{:S(2)}) collective-permute-start(bf16[192,1152]{1,0:T(8,128)(2,1)S(1)} %get-tuple-element.46), channel_id=1, source_target_pairs={{4,0},{5,1},{6,2},{7,3},{0,4},{1,5},{2,6},{3,7},{12,8},{13,9},{14,... | collective-permute-start | bytes 1327112 | tf_op jit(solution)/shard_map/ppermute | solution.py:57
  6.5 1.5 %collective-permute-start.4 = (bf16[256,1408]{1,0:T(8,128)(2,1)S(1)}, bf16[256,1408]{1,0:T(8,128)(2,1)S(1)}, u32[]{:S(2)}, u32[]{:S(2)}) collective-permute-start(bf16[256,1408]{1,0:T(8,128)(2,1)S(1)} %get-tuple-element.50.refs_3_.refs_1_.refs_2_.refs_10_), channel_id=1, source_target_pairs={{16,0},{17,1},{18,2},{19,3},{20,4},{21,5},{22,6},{23,7},{24,8},{25... | collective-permute-start | bytes 2162696 | tf_op jit(solution)/shard_map/ppermute | solution.py:57
  8.0 1.5 %collective-permute-start.1 = (bf16[256,1152]{1,0:T(8,128)(2,1)S(1)}, bf16[256,1152]{1,0:T(8,128)(2,1)S(1)}, u32[]{:S(2)}, u32[]{:S(2)}) collective-permute-start(bf16[256,1152]{1,0:T(8,128)(2,1)S(1)} %get-tuple-element.48.refs_0_), channel_id=1, source_target_pairs={{8,0},{9,1},{10,2},{11,3},{12,4},{13,5},{14,6},{15,7},{0,8},{1,9},... | collective-permute-start | bytes 1769480 | tf_op jit(solution)/shard_map/ppermute | solution.py:57
  9.5 1.6 %collective-permute-start.2 = (bf16[128,1152]{1,0:T(8,128)(2,1)S(1)}, bf16[128,1152]{1,0:T(8,128)(2,1)S(1)}, u32[]{:S(2)}, u32[]{:S(2)}) collective-permute-start(bf16[128,1152]{1,0:T(8,128)(2,1)S(1)} %get-tuple-element.49), channel_id=1, source_target_pairs={{2,0},{3,1},{0,2},{1,3},{6,4},{7,5},{4,6},{5,7},{10,8},{11,9},{8,1... | collective-permute-start | bytes 884744 | tf_op jit(solution)/shard_map/ppermute | solution.py:57
  11.1 15.2 %collective-permute-done.refs_4_.refs_6_ = bf16[192,1152]{1,0:T(8,128)(2,1)S(1)} collective-permute-done((bf16[192,1152]{1,0:T(8,128)(2,1)S(1)}, bf16[192,1152]{1,0:T(8,128)(2,1)S(1)}, u32[]{:S(2)}, u32[]{:S(2)}) %collective-permute-start) | collective-permute-done | bytes 442400 | tf_op jit(solution)/shard_map/ppermute | solution.py:57
  29.1 1.6 %collective-permute-start.8 = (bf16[192,1152]{1,0:T(8,128)(2,1)S(1)}, bf16[192,1152]{1,0:T(8,128)(2,1)S(1)}, u32[]{:S(2)}, u32[]{:S(2)}) collective-permute-start(bf16[192,1152]{1,0:T(8,128)(2,1)S(1)} %collective-permute-done.refs_4_.refs_6_), channel_id=1, source_target_pairs={{16,0},{17,1},{18,2},{19,3},{20,4},{21,5},{22,6},{23,7},{24,8},{25... | collective-permute-start | bytes 1327112 | tf_op jit(solution)/shard_map/ppermute | solution.py:57
  30.6 4.0 %collective-permute-start.10 = (bf16[128,1152]{1,0:T(8,128)(2,1)S(1)}, bf16[128,1152]{1,0:T(8,128)(2,1)S(1)}, u32[]{:S(2)}, u32[]{:S(2)}) collective-permute-start(bf16[128,1152]{1,0:T(8,128)(2,1)S(1)} %get-tuple-element.63), channel_id=1, source_target_pairs={{2,0},{3,1},{0,2},{1,3},{6,4},{7,5},{4,6},{5,7},{10,8},{11,9},{8,1... | collective-permute-start | bytes 884744 | tf_op jit(solution)/shard_map/ppermute | solution.py:57
  34.7 1.5 %collective-permute-done.6.refs_0_.refs_3_ = bf16[128,1152]{1,0:T(8,128)(2,1)S(1)} collective-permute-done((bf16[128,1152]{1,0:T(8,128)(2,1)S(1)}, bf16[128,1152]{1,0:T(8,128)(2,1)S(1)}, u32[]{:S(2)}, u32[]{:S(2)}) %collective-permute-start.6) | collective-permute-done | bytes 294944 | tf_op jit(solution)/shard_map/ppermute | solution.py:57
  37.2 2.3 %shard_map.40 = (bf16[640,1024]{1,0:T(8,128)(2,1)S(1)}, f32[640,128]{1,0:T(8,128)S(1)}) custom-call(s32[16,2048]{1,0:T(8,128)S(1)} %shard_map.39.flags, bf16[256,1152]{1,0:T(8,128)(2,1)S(1)} %get-tuple-element.48.refs_0_, bf16[256,1152]{1,0:T(8,128)(2,1)S(1)} %collective-permute-done.1.refs_1_, bf16[128,1152]{1,0:T(8,128)(2,1)S(1)} %collective-permute-done.2.refs_2_, ...), custom_call_target="tpu_custom_call" | custom-call | flops 1509949440 | bytes 3833856 | tf_op jit(solution)/shard_map/pallas_call | solution.py:224
  39.5 4.1 %collective-permute-done.9.in_ref = bf16[64,2176]{1,0:T(8,128)(2,1)S(1)} collective-permute-done((bf16[64,2176]{1,0:T(8,128)(2,1)S(1)}, bf16[64,2176]{1,0:T(8,128)(2,1)S(1)}, u32[]{:S(2)}, u32[]{:S(2)}) %collective-permute-start.9) | collective-permute-done | bytes 278560 | tf_op jit(solution)/shard_map/ppermute | solution.py:57
  43.6 2.9 %collective-permute-done.10.refs_0_.refs_4_ = bf16[128,1152]{1,0:T(8,128)(2,1)S(1)} collective-permute-done((bf16[128,1152]{1,0:T(8,128)(2,1)S(1)}, bf16[128,1152]{1,0:T(8,128)(2,1)S(1)}, u32[]{:S(2)}, u32[]{:S(2)}) %collective-permute-start.10) | collective-permute-done | bytes 294944 | tf_op jit(solution)/shard_map/ppermute | solution.py:57
  48.3 1.8 %shard_map.43 = (bf16[768,768]{1,0:T(8,128)(2,1)S(1)}, f32[768,128]{1,0:T(8,128)S(1)}) custom-call(s32[16,2048]{1,0:T(8,128)S(1)} %shard_map.39.flags, bf16[256,1152]{1,0:T(8,128)(2,1)S(1)} %get-tuple-element.48.refs_0_, bf16[256,1152]{1,0:T(8,128)(2,1)S(1)} %collective-permute-done.1.refs_1_, bf16[128,1152]{1,0:T(8,128)(2,1)S(1)} %collective-permute-done.2.refs_2_, ...), custom_call_target="tpu_custom_call" | custom-call | flops 1358954496 | bytes 3538944 | tf_op jit(solution)/shard_map/pallas_call | solution.py:224
  50.1 6.5 %collective-permute-done.14.refs_8_.refs_16_ = bf16[64,2176]{1,0:T(8,128)(2,1)S(1)} collective-permute-done((bf16[64,2176]{1,0:T(8,128)(2,1)S(1)}, bf16[64,2176]{1,0:T(8,128)(2,1)S(1)}, u32[]{:S(2)}, u32[]{:S(2)}) %collective-permute-start.14) | collective-permute-done | bytes 278560 | tf_op jit(solution)/shard_map/ppermute | solution.py:57
  56.6 1.5 %shard_map.44 = (bf16[256,1792]{1,0:T(8,128)(2,1)S(1)}, f32[256,128]{1,0:T(8,128)S(1)}) custom-call(s32[16,2048]{1,0:T(8,128)S(1)} %shard_map.39.flags, bf16[128,1152]{1,0:T(8,128)(2,1)S(1)} %collective-permute-done.10.refs_0_.refs_4_, bf16[128,1152]{1,0:T(8,128)(2,1)S(1)} %collective-permute-done.12.refs_1_.refs_5_, ...), custom_call_target="tpu_custom_call" | custom-call | flops 1056964608 | bytes 4718592 | tf_op jit(solution)/shard_map/pallas_call | solution.py:224
  61.6 2.5 %collective-permute-start.18 = (bf16[272,256]{1,0:T(8,128)(2,1)S(1)}, bf16[272,256]{1,0:T(8,128)(2,1)S(1)}, u32[]{:S(2)}, u32[]{:S(2)}) collective-permute-start(bf16[272,256]{1,0:T(8,128)(2,1)S(1)} %get-tuple-element.78), channel_id=1, source_target_pairs={{10,0},{11,1},{8,2},{9,3},{14,4},{15,5},{12,6},{13,7},{2,8},{3,9},... | collective-permute-start | bytes 417800 | tf_op jit(solution)/shard_map/ppermute | solution.py:57
  64.1 2.5 %collective-permute-done.16.refs_0_ = bf16[272,256]{1,0:T(8,128)(2,1)S(1)} collective-permute-done((bf16[272,256]{1,0:T(8,128)(2,1)S(1)}, bf16[272,256]{1,0:T(8,128)(2,1)S(1)}, u32[]{:S(2)}, u32[]{:S(2)}) %collective-permute-start.16) | collective-permute-done | bytes 139296 | tf_op jit(solution)/shard_map/ppermute | solution.py:57
  66.6 1.5 %collective-permute-done.17.refs_1_ = bf16[272,256]{1,0:T(8,128)(2,1)S(1)} collective-permute-done((bf16[272,256]{1,0:T(8,128)(2,1)S(1)}, bf16[272,256]{1,0:T(8,128)(2,1)S(1)}, u32[]{:S(2)}, u32[]{:S(2)}) %collective-permute-start.17) | collective-permute-done | bytes 139296 | tf_op jit(solution)/shard_map/ppermute | solution.py:57
  68.1 2.6 %collective-permute-done.18.refs_2_ = bf16[272,256]{1,0:T(8,128)(2,1)S(1)} collective-permute-done((bf16[272,256]{1,0:T(8,128)(2,1)S(1)}, bf16[272,256]{1,0:T(8,128)(2,1)S(1)}, u32[]{:S(2)}, u32[]{:S(2)}) %collective-permute-start.18) | collective-permute-done | bytes 139296 | tf_op jit(solution)/shard_map/ppermute | solution.py:57
  72.2 7.2 %collective-permute-done.22.refs_9_ = bf16[256,256]{1,0:T(8,128)(2,1)S(1)} collective-permute-done((bf16[256,256]{1,0:T(8,128)(2,1)S(1)}, bf16[256,256]{1,0:T(8,128)(2,1)S(1)}, u32[]{:S(2)}, u32[]{:S(2)}) %collective-permute-start.22) | collective-permute-done | bytes 131104 | tf_op jit(solution)/shard_map/ppermute | solution.py:57
  80.2 4.6 %collective-permute-done.24.refs_11_ = bf16[256,256]{1,0:T(8,128)(2,1)S(1)} collective-permute-done((bf16[256,256]{1,0:T(8,128)(2,1)S(1)}, bf16[256,256]{1,0:T(8,128)(2,1)S(1)}, u32[]{:S(2)}, u32[]{:S(2)}) %collective-permute-start.24) | collective-permute-done | bytes 131104 | tf_op jit(solution)/shard_map/ppermute | solution.py:57
  88.5 2.5 %collective-permute-start.28 = (bf16[256,256]{1,0:T(8,128)(2,1)S(1)}, bf16[256,256]{1,0:T(8,128)(2,1)S(1)}, u32[]{:S(2)}, u32[]{:S(2)}) collective-permute-start(bf16[256,256]{1,0:T(8,128)(2,1)S(1)} %get-tuple-element.84), channel_id=1, source_target_pairs={{10,0},{11,1},{8,2},{9,3},{14,4},{15,5},{12,6},{13,7},{2,8},{3,9},... | collective-permute-start | bytes 393224 | tf_op jit(solution)/shard_map/ppermute | solution.py:57
  91.0 2.1 %collective-permute-done.26.refs_0_ = bf16[256,256]{1,0:T(8,128)(2,1)S(1)} collective-permute-done((bf16[256,256]{1,0:T(8,128)(2,1)S(1)}, bf16[256,256]{1,0:T(8,128)(2,1)S(1)}, u32[]{:S(2)}, u32[]{:S(2)}) %collective-permute-start.26) | collective-permute-done | bytes 131104 | tf_op jit(solution)/shard_map/ppermute | solution.py:57
  93.0 1.9 %collective-permute-done.27.refs_1_ = bf16[256,256]{1,0:T(8,128)(2,1)S(1)} collective-permute-done((bf16[256,256]{1,0:T(8,128)(2,1)S(1)}, bf16[256,256]{1,0:T(8,128)(2,1)S(1)}, u32[]{:S(2)}, u32[]{:S(2)}) %collective-permute-start.27) | collective-permute-done | bytes 131104 | tf_op jit(solution)/shard_map/ppermute | solution.py:57
  94.9 2.1 %collective-permute-done.28.refs_2_ = bf16[256,256]{1,0:T(8,128)(2,1)S(1)} collective-permute-done((bf16[256,256]{1,0:T(8,128)(2,1)S(1)}, bf16[256,256]{1,0:T(8,128)(2,1)S(1)}, u32[]{:S(2)}, u32[]{:S(2)}) %collective-permute-start.28) | collective-permute-done | bytes 131104 | tf_op jit(solution)/shard_map/ppermute | solution.py:57
  (54 shorter events, 18.1 us)
Async XLA Ops:
  2.4 23.9 %collective-permute-start = (bf16[192,1152]{1,0:T(8,128)(2,1)S(1)}, bf16[192,1152]{1,0:T(8,128)(2,1)S(1)}, u32[]{:S(2)}, u32[]{:S(2)}) collective-permute-start(bf16[192,1152]{1,0:T(8,128)(2,1)S(1)} %get-tuple-element.46), channel_id=1, source_target_pairs={{4,0},{5,1},{6,2},{7,3},{0,4},{1,5},{2,6},{3,7},{12,8},{13,9},{14,... | collective-permute-start | bytes 1327112 | tf_op jit(solution)/shard_map/ppermute | solution.py:57
  6.5 20.2 %collective-permute-start.3 = (bf16[256,1408]{1,0:T(8,128)(2,1)S(1)}, bf16[256,1408]{1,0:T(8,128)(2,1)S(1)}, u32[]{:S(2)}, u32[]{:S(2)}) collective-permute-start(bf16[256,1408]{1,0:T(8,128)(2,1)S(1)} %get-tuple-element.50.refs_3_.refs_1_.refs_2_.refs_10_), channel_id=1, source_target_pairs={{1,0},{0,1},{3,2},{2,3},{5,4},{4,5},{7,6},{6,7},{9,8},{8,9},{11,10... | collective-permute-start | bytes 2162696 | tf_op jit(solution)/shard_map/ppermute | solution.py:57
  6.5 20.2 %collective-permute-start.4 = (bf16[256,1408]{1,0:T(8,128)(2,1)S(1)}, bf16[256,1408]{1,0:T(8,128)(2,1)S(1)}, u32[]{:S(2)}, u32[]{:S(2)}) collective-permute-start(bf16[256,1408]{1,0:T(8,128)(2,1)S(1)} %get-tuple-element.50.refs_3_.refs_1_.refs_2_.refs_10_), channel_id=1, source_target_pairs={{16,0},{17,1},{18,2},{19,3},{20,4},{21,5},{22,6},{23,7},{24,8},{25... | collective-permute-start | bytes 2162696 | tf_op jit(solution)/shard_map/ppermute | solution.py:57
  8.0 18.7 %collective-permute-start.1 = (bf16[256,1152]{1,0:T(8,128)(2,1)S(1)}, bf16[256,1152]{1,0:T(8,128)(2,1)S(1)}, u32[]{:S(2)}, u32[]{:S(2)}) collective-permute-start(bf16[256,1152]{1,0:T(8,128)(2,1)S(1)} %get-tuple-element.48.refs_0_), channel_id=1, source_target_pairs={{8,0},{9,1},{10,2},{11,3},{12,4},{13,5},{14,6},{15,7},{0,8},{1,9},... | collective-permute-start | bytes 1769480 | tf_op jit(solution)/shard_map/ppermute | solution.py:57
  9.5 17.2 %collective-permute-start.2 = (bf16[128,1152]{1,0:T(8,128)(2,1)S(1)}, bf16[128,1152]{1,0:T(8,128)(2,1)S(1)}, u32[]{:S(2)}, u32[]{:S(2)}) collective-permute-start(bf16[128,1152]{1,0:T(8,128)(2,1)S(1)} %get-tuple-element.49), channel_id=1, source_target_pairs={{2,0},{3,1},{0,2},{1,3},{6,4},{7,5},{4,6},{5,7},{10,8},{11,9},{8,1... | collective-permute-start | bytes 884744 | tf_op jit(solution)/shard_map/ppermute | solution.py:57
  26.7 8.0 %collective-permute-start.5 = (bf16[256,1408]{1,0:T(8,128)(2,1)S(1)}, bf16[256,1408]{1,0:T(8,128)(2,1)S(1)}, u32[]{:S(2)}, u32[]{:S(2)}) collective-permute-start(bf16[256,1408]{1,0:T(8,128)(2,1)S(1)} %collective-permute-done.4.refs_5_.refs_3_.refs_4_.refs_12_), channel_id=1, source_target_pairs={{1,0},{0,1},{3,2},{2,3},{5,4},{4,5},{7,6},{6,7},{9,8},{8,9},{11,10... | collective-permute-start | bytes 2162696 | tf_op jit(solution)/shard_map/ppermute | solution.py:57
  26.8 9.4 %collective-permute-start.6 = (bf16[128,1152]{1,0:T(8,128)(2,1)S(1)}, bf16[128,1152]{1,0:T(8,128)(2,1)S(1)}, u32[]{:S(2)}, u32[]{:S(2)}) collective-permute-start(bf16[128,1152]{1,0:T(8,128)(2,1)S(1)} %collective-permute-done.2.refs_2_), channel_id=1, source_target_pairs={{8,0},{9,1},{10,2},{11,3},{12,4},{13,5},{14,6},{15,7},{0,8},{1,9},... | collective-permute-start | bytes 884744 | tf_op jit(solution)/shard_map/ppermute | solution.py:57
  27.9 15.7 %collective-permute-start.9 = (bf16[64,2176]{1,0:T(8,128)(2,1)S(1)}, bf16[64,2176]{1,0:T(8,128)(2,1)S(1)}, u32[]{:S(2)}, u32[]{:S(2)}) collective-permute-start(bf16[64,2176]{1,0:T(8,128)(2,1)S(1)} %get-tuple-element.58), channel_id=1, source_target_pairs={{4,0},{5,1},{6,2},{7,3},{0,4},{1,5},{2,6},{3,7},{12,8},{13,9},{14,... | collective-permute-start | bytes 835592 | tf_op jit(solution)/shard_map/ppermute | solution.py:57
  29.1 17.4 %collective-permute-start.8 = (bf16[192,1152]{1,0:T(8,128)(2,1)S(1)}, bf16[192,1152]{1,0:T(8,128)(2,1)S(1)}, u32[]{:S(2)}, u32[]{:S(2)}) collective-permute-start(bf16[192,1152]{1,0:T(8,128)(2,1)S(1)} %collective-permute-done.refs_4_.refs_6_), channel_id=1, source_target_pairs={{16,0},{17,1},{18,2},{19,3},{20,4},{21,5},{22,6},{23,7},{24,8},{25... | collective-permute-start | bytes 1327112 | tf_op jit(solution)/shard_map/ppermute | solution.py:57
  30.6 15.8 %collective-permute-start.10 = (bf16[128,1152]{1,0:T(8,128)(2,1)S(1)}, bf16[128,1152]{1,0:T(8,128)(2,1)S(1)}, u32[]{:S(2)}, u32[]{:S(2)}) collective-permute-start(bf16[128,1152]{1,0:T(8,128)(2,1)S(1)} %get-tuple-element.63), channel_id=1, source_target_pairs={{2,0},{3,1},{0,2},{1,3},{6,4},{7,5},{4,6},{5,7},{10,8},{11,9},{8,1... | collective-permute-start | bytes 884744 | tf_op jit(solution)/shard_map/ppermute | solution.py:57
  34.7 11.8 %collective-permute-start.7 = (bf16[192,1152]{1,0:T(8,128)(2,1)S(1)}, bf16[192,1152]{1,0:T(8,128)(2,1)S(1)}, u32[]{:S(2)}, u32[]{:S(2)}) collective-permute-start(bf16[192,1152]{1,0:T(8,128)(2,1)S(1)} %collective-permute-done.refs_4_.refs_6_), channel_id=1, source_target_pairs={{1,0},{0,1},{3,2},{2,3},{5,4},{4,5},{7,6},{6,7},{9,8},{8,9},{11,10... | collective-permute-start | bytes 1327112 | tf_op jit(solution)/shard_map/ppermute | solution.py:57
  46.5 10.1 %collective-permute-start.12 = (bf16[128,1152]{1,0:T(8,128)(2,1)S(1)}, bf16[128,1152]{1,0:T(8,128)(2,1)S(1)}, u32[]{:S(2)}, u32[]{:S(2)}) collective-permute-start(bf16[128,1152]{1,0:T(8,128)(2,1)S(1)} %collective-permute-done.10.refs_0_.refs_4_), channel_id=1, source_target_pairs={{8,0},{9,1},{10,2},{11,3},{12,4},{13,5},{14,6},{15,7},{0,8},{1,9},... | collective-permute-start | bytes 884744 | tf_op jit(solution)/shard_map/ppermute | solution.py:57
  47.7 8.9 %collective-permute-start.14 = (bf16[64,2176]{1,0:T(8,128)(2,1)S(1)}, bf16[64,2176]{1,0:T(8,128)(2,1)S(1)}, u32[]{:S(2)}, u32[]{:S(2)}) collective-permute-start(bf16[64,2176]{1,0:T(8,128)(2,1)S(1)} %shard_map.42.refs_6_.refs_14_), channel_id=1, source_target_pairs={{16,0},{17,1},{18,2},{19,3},{20,4},{21,5},{22,6},{23,7},{24,8},{25... | collective-permute-start | bytes 835592 | tf_op jit(solution)/shard_map/ppermute | solution.py:57
  60.5 6.1 %collective-permute-start.16 = (bf16[272,256]{1,0:T(8,128)(2,1)S(1)}, bf16[272,256]{1,0:T(8,128)(2,1)S(1)}, u32[]{:S(2)}, u32[]{:S(2)}) collective-permute-start(bf16[272,256]{1,0:T(8,128)(2,1)S(1)} %get-tuple-element.76), channel_id=1, source_target_pairs={{8,0},{9,1},{10,2},{11,3},{12,4},{13,5},{14,6},{15,7},{0,8},{1,9},... | collective-permute-start | bytes 417800 | tf_op jit(solution)/shard_map/ppermute | solution.py:57
  61.6 6.5 %collective-permute-start.17 = (bf16[272,256]{1,0:T(8,128)(2,1)S(1)}, bf16[272,256]{1,0:T(8,128)(2,1)S(1)}, u32[]{:S(2)}, u32[]{:S(2)}) collective-permute-start(bf16[272,256]{1,0:T(8,128)(2,1)S(1)} %get-tuple-element.77), channel_id=1, source_target_pairs={{2,0},{3,1},{0,2},{1,3},{6,4},{7,5},{4,6},{5,7},{10,8},{11,9},{8,1... | collective-permute-start | bytes 417800 | tf_op jit(solution)/shard_map/ppermute | solution.py:57
  61.6 9.2 %collective-permute-start.18 = (bf16[272,256]{1,0:T(8,128)(2,1)S(1)}, bf16[272,256]{1,0:T(8,128)(2,1)S(1)}, u32[]{:S(2)}, u32[]{:S(2)}) collective-permute-start(bf16[272,256]{1,0:T(8,128)(2,1)S(1)} %get-tuple-element.78), channel_id=1, source_target_pairs={{10,0},{11,1},{8,2},{9,3},{14,4},{15,5},{12,6},{13,7},{2,8},{3,9},... | collective-permute-start | bytes 417800 | tf_op jit(solution)/shard_map/ppermute | solution.py:57
  70.9 8.5 %collective-permute-start.22 = (bf16[256,256]{1,0:T(8,128)(2,1)S(1)}, bf16[256,256]{1,0:T(8,128)(2,1)S(1)}, u32[]{:S(2)}, u32[]{:S(2)}) collective-permute-start(bf16[256,256]{1,0:T(8,128)(2,1)S(1)} %get-tuple-element.79.refs_5_), channel_id=1, source_target_pairs={{4,0},{5,1},{6,2},{7,3},{0,4},{1,5},{2,6},{3,7},{12,8},{13,9},{14,... | collective-permute-start | bytes 393224 | tf_op jit(solution)/shard_map/ppermute | solution.py:57
  71.7 8.5 %collective-permute-start.20 = (bf16[256,256]{1,0:T(8,128)(2,1)S(1)}, bf16[256,256]{1,0:T(8,128)(2,1)S(1)}, u32[]{:S(2)}, u32[]{:S(2)}) collective-permute-start(bf16[256,256]{1,0:T(8,128)(2,1)S(1)} %get-tuple-element.79.refs_5_), channel_id=1, source_target_pairs={{16,0},{17,1},{18,2},{19,3},{20,4},{21,5},{22,6},{23,7},{24,8},{25... | collective-permute-start | bytes 393224 | tf_op jit(solution)/shard_map/ppermute | solution.py:57
  79.4 5.4 %collective-permute-start.24 = (bf16[256,256]{1,0:T(8,128)(2,1)S(1)}, bf16[256,256]{1,0:T(8,128)(2,1)S(1)}, u32[]{:S(2)}, u32[]{:S(2)}) collective-permute-start(bf16[256,256]{1,0:T(8,128)(2,1)S(1)} %collective-permute-done.22.refs_9_), channel_id=1, source_target_pairs={{16,0},{17,1},{18,2},{19,3},{20,4},{21,5},{22,6},{23,7},{24,8},{25... | collective-permute-start | bytes 393224 | tf_op jit(solution)/shard_map/ppermute | solution.py:57
  79.7 5.1 %collective-permute-start.19 = (bf16[256,256]{1,0:T(8,128)(2,1)S(1)}, bf16[256,256]{1,0:T(8,128)(2,1)S(1)}, u32[]{:S(2)}, u32[]{:S(2)}) collective-permute-start(bf16[256,256]{1,0:T(8,128)(2,1)S(1)} %get-tuple-element.79.refs_5_), channel_id=1, source_target_pairs={{1,0},{0,1},{3,2},{2,3},{5,4},{4,5},{7,6},{6,7},{9,8},{8,9},{11,10... | collective-permute-start | bytes 393224 | tf_op jit(solution)/shard_map/ppermute | solution.py:57
  79.7 5.1 %collective-permute-start.23 = (bf16[256,256]{1,0:T(8,128)(2,1)S(1)}, bf16[256,256]{1,0:T(8,128)(2,1)S(1)}, u32[]{:S(2)}, u32[]{:S(2)}) collective-permute-start(bf16[256,256]{1,0:T(8,128)(2,1)S(1)} %collective-permute-done.22.refs_9_), channel_id=1, source_target_pairs={{1,0},{0,1},{3,2},{2,3},{5,4},{4,5},{7,6},{6,7},{9,8},{8,9},{11,10... | collective-permute-start | bytes 393224 | tf_op jit(solution)/shard_map/ppermute | solution.py:57
  87.4 5.6 %collective-permute-start.26 = (bf16[256,256]{1,0:T(8,128)(2,1)S(1)}, bf16[256,256]{1,0:T(8,128)(2,1)S(1)}, u32[]{:S(2)}, u32[]{:S(2)}) collective-permute-start(bf16[256,256]{1,0:T(8,128)(2,1)S(1)} %get-tuple-element.82), channel_id=1, source_target_pairs={{8,0},{9,1},{10,2},{11,3},{12,4},{13,5},{14,6},{15,7},{0,8},{1,9},... | collective-permute-start | bytes 393224 | tf_op jit(solution)/shard_map/ppermute | solution.py:57
  88.5 6.4 %collective-permute-start.27 = (bf16[256,256]{1,0:T(8,128)(2,1)S(1)}, bf16[256,256]{1,0:T(8,128)(2,1)S(1)}, u32[]{:S(2)}, u32[]{:S(2)}) collective-permute-start(bf16[256,256]{1,0:T(8,128)(2,1)S(1)} %get-tuple-element.83), channel_id=1, source_target_pairs={{2,0},{3,1},{0,2},{1,3},{6,4},{7,5},{4,6},{5,7},{10,8},{11,9},{8,1... | collective-permute-start | bytes 393224 | tf_op jit(solution)/shard_map/ppermute | solution.py:57
  88.5 8.5 %collective-permute-start.28 = (bf16[256,256]{1,0:T(8,128)(2,1)S(1)}, bf16[256,256]{1,0:T(8,128)(2,1)S(1)}, u32[]{:S(2)}, u32[]{:S(2)}) collective-permute-start(bf16[256,256]{1,0:T(8,128)(2,1)S(1)} %get-tuple-element.84), channel_id=1, source_target_pairs={{10,0},{11,1},{8,2},{9,3},{14,4},{15,5},{12,6},{13,7},{2,8},{3,9},... | collective-permute-start | bytes 393224 | tf_op jit(solution)/shard_map/ppermute | solution.py:57
  (8 other events, 32.2 us)

commit v11 on v9

--- a/solution.py
+++ b/solution.py
@@ -81,23 +81,36 @@
     return scaled.astype(jnp.bfloat16)
 
 
-def unit_kernel(emb_ref, seed_ref, unit_ref, packed_ref):
-    d = emb_ref.shape[1]
-    unit = unit_of(emb_ref[...])
-    unit_ref[...] = unit
-    packed_ref[:, :d] = unit
+def unit_kernel(emb_ref, unit_ref):
+    unit_ref[...] = unit_of(emb_ref[...])
+
+
+def unit_rows(embeddings):
+    out = shape(embeddings.shape)
+    return pl.pallas_call(
+        unit_kernel,
+        out_shape=out,
+        in_specs=[VMEM],
+        out_specs=VMEM,
+        compiler_params=limits(*[out] * 4),
+    )(embeddings)
+
+
+def pack_kernel(unit_ref, seed_ref, packed_ref):
+    d = unit_ref.shape[1]
+    packed_ref[:, :d] = unit_ref[...]
     packed_ref[:, d:] = seed_ref[...]
 
 
-def unit_rows(embeddings, seeds):
-    (m, d), c = embeddings.shape, seeds.shape[1]
-    outs = [shape((m, d)), shape((m, d + c))]
-    return pl.pallas_call(
-        unit_kernel,
-        out_shape=outs,
-        out_specs=[VMEM] * 2,
-        compiler_params=limits(embeddings, embeddings, seeds, seeds, *outs, embeddings),
-    )(embeddings, seeds)
+def pack_rows(units, seeds):
+    out = shape((units.shape[0], units.shape[1] + seeds.shape[1]))
+    return pl.pallas_call(
+        pack_kernel,
+        out_shape=out,
+        in_specs=[VMEM] * 2,
+        out_specs=VMEM,
+        compiler_params=limits(out, out),
+    )(units, seeds)
 
 
 def stack_kernel(seed_ref, *refs):
@@ -149,7 +162,7 @@
         out_specs=VMEM,
         scratch_shapes=[pltpu.VMEM((1, out.shape[1]), jnp.int32)],
         compiler_params=limits(out, out),
-        cost_estimate=pl.CostEstimate(flops=2 * 10**10, bytes_accessed=2**20, transcendentals=0),
+        cost_estimate=pl.CostEstimate(flops=10**7, bytes_accessed=2**20, transcendentals=0),
     )(place, pattern.T)
 
 
@@ -388,7 +401,8 @@
     t_parts = [(t_offsets[i], k) for i in t_order for k in range(0, m, sub)]
     s_parts = [(o, k) for o in s_layout for k in range(0, m, sub)]
     place = jnp.stack([lax.axis_index("row"), lax.axis_index("col")]).astype(jnp.int32)
-    units, packed = unit_rows(after(embeddings, place), seed_labels)
+    units = unit_rows(after(embeddings, place))
+    packed = pack_rows(units, seed_labels)
 
     t_pieces, kerns, accs, rects = [], [], [], []
     s_pieces = [None] * len(groups)
@@ -413,12 +427,13 @@
 
     zh, zl, x = fetch([units], "zh"), fetch([units], "zl"), fetch([units], "x")
     y, own_core = fetch([packed], "y"), fetch([packed], "core")
-    flags = flags_call(layout, m, t_parts, s_parts, sub, pattern, after(place, *zh))
-    done = zh + zl + x + y + own_core + [flags]
+    flags = flags_call(layout, m, t_parts, s_parts, sub, pattern, place)
+    held = stack_seeds(after(seed_labels, flags, *zh), [], 2 * 10**10)
+    done = zh + zl + x + y + own_core + [held]
     zh_y, zl_x = fetch(zh, "y", *done), fetch(zl, "x", *done)
     y_core = [fetch([v], "core", *done) for v in y]
     zh_core = fetch(zh, "core", *done)
-    seeds_zh = fetch([stack_seeds(seed_labels, y)], "zh", *done)
+    seeds_zh = fetch([stack_seeds(held, y)], "zh", *done)
     by_offset = {(0, 0): units}
     by_offset.update({(0, a): v for a, v in zip(other["x"], x)})
     by_offset.update({(b, 0): v for b, v in zip(other["zl"], zl)})
@@ -455,7 +470,7 @@
     own, totals, *others = spread_call(kerns, accs, seeds, c, (*plan, seeds_map))
     panel, totals = update(
         first_update_kernel,
-        seed_labels,
+        held,
         own,
         totals,
         home(others),
@@ -467,7 +482,7 @@
     own, *others = spread_call(kerns, [], panels(panel), c, (*plan, p_map))
     return update(
         last_update_kernel,
-        seed_labels,
+        held,
         own,
         totals,
         home(others),

time: 94.9 us -> 92.3 us (0.973)
  waiting for transfers between devices: 56.1 us -> 54 us
    ppermute x25, waiting for transfers between devices: 56.1 us -> 54 us  [fetch(): return lax.ppermute(value, AXES, pairs)]
    unnamed x8 -> x6, local copies, waits for them, and re-layouts: 2.67 us -> 1.97 us
  transfers between devices with their start and end apart: 25 -> 25, of which waited for: 13 -> 14; matrix products, arithmetic and copies ran while one was open for 0% -> 0% of each run, Pallas kernels for 8% -> 9%
where the time goes in v11:
time: 92.3 us; the launch traced here: 92.1 us
  waiting for transfers between devices  54 us (59%)
  starting transfers between devices  24.2 us (26%)
  Pallas kernels  11.7 us (13%)
  local copies, waits for them, and re-layouts  1.97 us (2%)
    ppermute x25, waiting for transfers between devices, fetch(): return lax.ppermute(value, AXES, pairs)  54 us
    ppermute x25, starting transfers between devices, fetch(): return lax.ppermute(value, AXES, pairs)  24.2 us
    pallas_call x5, Pallas kernels, gram_call(): pl.pallas_call(functools.partial(gram_kernel, len(t_pieces), len(s_pieces...  6.9 us
    pallas_call x2, Pallas kernels, spread_call(): pl.pallas_call(functools.partial(spread_kernel, plan, len(kerns), len(acc...  2.57 us
    unnamed x6, local copies, waits for them, and re-layouts  1.97 us
  transfers between devices with their start and end apart: 25, of which 14 were waited for; matrix products, arithmetic and copies ran while one was open for 0% of the time, Pallas kernels for 9%

profile of v11, /device:TPU:0, one launch (start us, length us, event | category | flops | bytes accessed | tf_op | source)
XLA Modules:
  0.0 92.1 jit_solution(5143911205388612408)
XLA Ops:
  1.4 4.1 %collective-permute-start = (bf16[256,1152]{1,0:T(8,128)(2,1)S(1)}, bf16[256,1152]{1,0:T(8,128)(2,1)S(1)}, u32[]{:S(2)}, u32[]{:S(2)}) collective-permute-start(bf16[256,1152]{1,0:T(8,128)(2,1)S(1)} %shard_map.38.unit_ref.refs_0_), channel_id=1, source_target_pairs={{4,0},{5,1},{6,2},{7,3},{0,4},{1,5},{2,6},{3,7},{12,8},{13,9},{14,... | collective-permute-start | bytes 1769480 | tf_op jit(solution)/shard_map/ppermute | solution.py:57
  5.5 1.6 %collective-permute-start.2 = (bf16[256,1152]{1,0:T(8,128)(2,1)S(1)}, bf16[256,1152]{1,0:T(8,128)(2,1)S(1)}, u32[]{:S(2)}, u32[]{:S(2)}) collective-permute-start(bf16[256,1152]{1,0:T(8,128)(2,1)S(1)} %shard_map.38.unit_ref.refs_0_), channel_id=1, source_target_pairs={{2,0},{3,1},{0,2},{1,3},{6,4},{7,5},{4,6},{5,7},{10,8},{11,9},{8,1... | collective-permute-start | bytes 1769480 | tf_op jit(solution)/shard_map/ppermute | solution.py:57
  7.1 1.5 %collective-permute-start.1 = (bf16[256,1152]{1,0:T(8,128)(2,1)S(1)}, bf16[256,1152]{1,0:T(8,128)(2,1)S(1)}, u32[]{:S(2)}, u32[]{:S(2)}) collective-permute-start(bf16[256,1152]{1,0:T(8,128)(2,1)S(1)} %shard_map.38.unit_ref.refs_0_), channel_id=1, source_target_pairs={{8,0},{9,1},{10,2},{11,3},{12,4},{13,5},{14,6},{15,7},{0,8},{1,9},... | collective-permute-start | bytes 1769480 | tf_op jit(solution)/shard_map/ppermute | solution.py:57
  9.5 1.6 %collective-permute-start.4 = (bf16[256,1408]{1,0:T(8,128)(2,1)S(1)}, bf16[256,1408]{1,0:T(8,128)(2,1)S(1)}, u32[]{:S(2)}, u32[]{:S(2)}) collective-permute-start(bf16[256,1408]{1,0:T(8,128)(2,1)S(1)} %shard_map.40.refs_3_.refs_1_.refs_10_), channel_id=1, source_target_pairs={{16,0},{17,1},{18,2},{19,3},{20,4},{21,5},{22,6},{23,7},{24,8},{25... | collective-permute-start | bytes 2162696 | tf_op jit(solution)/shard_map/ppermute | solution.py:57
  12.0 19.5 %collective-permute-done.refs_3_.refs_5_ = bf16[256,1152]{1,0:T(8,128)(2,1)S(1)} collective-permute-done((bf16[256,1152]{1,0:T(8,128)(2,1)S(1)}, bf16[256,1152]{1,0:T(8,128)(2,1)S(1)}, u32[]{:S(2)}, u32[]{:S(2)}) %collective-permute-start) | collective-permute-done | bytes 589856 | tf_op jit(solution)/shard_map/ppermute | solution.py:57
  32.4 1.4 %collective-permute-start.9 = (bf16[512,256]{1,0:T(8,128)(2,1)S(1)}, bf16[512,256]{1,0:T(8,128)(2,1)S(1)}, u32[]{:S(2)}, u32[]{:S(2)}) collective-permute-start(bf16[512,256]{1,0:T(8,128)(2,1)S(1)} %shard_map.45), channel_id=1, source_target_pairs={{4,0},{5,1},{6,2},{7,3},{0,4},{1,5},{2,6},{3,7},{12,8},{13,9},{14,... | collective-permute-start | bytes 786440 | tf_op jit(solution)/shard_map/ppermute | solution.py:57
  33.8 1.5 %collective-permute-start.8 = (bf16[256,1152]{1,0:T(8,128)(2,1)S(1)}, bf16[256,1152]{1,0:T(8,128)(2,1)S(1)}, u32[]{:S(2)}, u32[]{:S(2)}) collective-permute-start(bf16[256,1152]{1,0:T(8,128)(2,1)S(1)} %collective-permute-done.refs_3_.refs_5_), channel_id=1, source_target_pairs={{16,0},{17,1},{18,2},{19,3},{20,4},{21,5},{22,6},{23,7},{24,8},{25... | collective-permute-start | bytes 1769480 | tf_op jit(solution)/shard_map/ppermute | solution.py:57
  35.3 1.5 %collective-permute-start.7 = (bf16[256,1152]{1,0:T(8,128)(2,1)S(1)}, bf16[256,1152]{1,0:T(8,128)(2,1)S(1)}, u32[]{:S(2)}, u32[]{:S(2)}) collective-permute-start(bf16[256,1152]{1,0:T(8,128)(2,1)S(1)} %collective-permute-done.2.refs_2_), channel_id=1, source_target_pairs={{8,0},{9,1},{10,2},{11,3},{12,4},{13,5},{14,6},{15,7},{0,8},{1,9},... | collective-permute-start | bytes 1769480 | tf_op jit(solution)/shard_map/ppermute | solution.py:57
  38.1 2.4 %shard_map.41 = (bf16[768,1024]{1,0:T(8,128)(2,1)S(1)}, f32[768,128]{1,0:T(8,128)S(1)}) custom-call(s32[8,2048]{1,0:T(8,128)S(1)} %shard_map.37.flags, bf16[256,1152]{1,0:T(8,128)(2,1)S(1)} %shard_map.38.unit_ref.refs_0_, bf16[256,1152]{1,0:T(8,128)(2,1)S(1)} %collective-permute-done.1.refs_1_, bf16[256,1152]{1,0:T(8,128)(2,1)S(1)} %collective-permute-done.2.refs_2_, ...), custom_call_target="tpu_custom_call" | custom-call | flops 1811939328 | bytes 4128768 | tf_op jit(solution)/shard_map/pallas_call | solution.py:233
  40.5 6.7 %collective-permute-done.9.seed_ref = bf16[512,256]{1,0:T(8,128)(2,1)S(1)} collective-permute-done((bf16[512,256]{1,0:T(8,128)(2,1)S(1)}, bf16[512,256]{1,0:T(8,128)(2,1)S(1)}, u32[]{:S(2)}, u32[]{:S(2)}) %collective-permute-start.9) | collective-permute-done | bytes 262176 | tf_op jit(solution)/shard_map/ppermute | solution.py:57
  47.3 1.6 %collective-permute-done.8.refs_7_.refs_3_ = bf16[256,1152]{1,0:T(8,128)(2,1)S(1)} collective-permute-done((bf16[256,1152]{1,0:T(8,128)(2,1)S(1)}, bf16[256,1152]{1,0:T(8,128)(2,1)S(1)}, u32[]{:S(2)}, u32[]{:S(2)}) %collective-permute-start.8) | collective-permute-done | bytes 589856 | tf_op jit(solution)/shard_map/ppermute | solution.py:57
  51.3 1.5 %shard_map.43 = (bf16[256,1792]{1,0:T(8,128)(2,1)S(1)}, f32[256,128]{1,0:T(8,128)S(1)}) custom-call(s32[8,2048]{1,0:T(8,128)S(1)} %shard_map.37.flags, bf16[256,1152]{1,0:T(8,128)(2,1)S(1)} %collective-permute-done.7.refs_0_.refs_3_, bf16[256,1408]{1,0:T(8,128)(2,1)S(1)} %shard_map.40.refs_3_.refs_1_.refs_10_, ...), custom_call_target="tpu_custom_call" | custom-call | flops 1056964608 | bytes 4718592 | tf_op jit(solution)/shard_map/pallas_call | solution.py:233
  55.1 1.6 %collective-permute-start.12 = (bf16[272,256]{1,0:T(8,128)(2,1)S(1)}, bf16[272,256]{1,0:T(8,128)(2,1)S(1)}, u32[]{:S(2)}, u32[]{:S(2)}) collective-permute-start(bf16[272,256]{1,0:T(8,128)(2,1)S(1)} %get-tuple-element.56), channel_id=1, source_target_pairs={{8,0},{9,1},{10,2},{11,3},{12,4},{13,5},{14,6},{15,7},{0,8},{1,9},... | collective-permute-start | bytes 417800 | tf_op jit(solution)/shard_map/ppermute | solution.py:57
  56.7 2.5 %collective-permute-start.13 = (bf16[272,256]{1,0:T(8,128)(2,1)S(1)}, bf16[272,256]{1,0:T(8,128)(2,1)S(1)}, u32[]{:S(2)}, u32[]{:S(2)}) collective-permute-start(bf16[272,256]{1,0:T(8,128)(2,1)S(1)} %get-tuple-element.57), channel_id=1, source_target_pairs={{2,0},{3,1},{0,2},{1,3},{6,4},{7,5},{4,6},{5,7},{10,8},{11,9},{8,1... | collective-permute-start | bytes 417800 | tf_op jit(solution)/shard_map/ppermute | solution.py:57
  59.1 1.6 %collective-permute-done.12.refs_0_ = bf16[272,256]{1,0:T(8,128)(2,1)S(1)} collective-permute-done((bf16[272,256]{1,0:T(8,128)(2,1)S(1)}, bf16[272,256]{1,0:T(8,128)(2,1)S(1)}, u32[]{:S(2)}, u32[]{:S(2)}) %collective-permute-start.12) | collective-permute-done | bytes 139296 | tf_op jit(solution)/shard_map/ppermute | solution.py:57
  60.8 2.9 %collective-permute-done.13.refs_1_ = bf16[272,256]{1,0:T(8,128)(2,1)S(1)} collective-permute-done((bf16[272,256]{1,0:T(8,128)(2,1)S(1)}, bf16[272,256]{1,0:T(8,128)(2,1)S(1)}, u32[]{:S(2)}, u32[]{:S(2)}) %collective-permute-start.13) | collective-permute-done | bytes 139296 | tf_op jit(solution)/shard_map/ppermute | solution.py:57
  63.7 2.0 %collective-permute-done.14.refs_2_ = bf16[272,256]{1,0:T(8,128)(2,1)S(1)} collective-permute-done((bf16[272,256]{1,0:T(8,128)(2,1)S(1)}, bf16[272,256]{1,0:T(8,128)(2,1)S(1)}, u32[]{:S(2)}, u32[]{:S(2)}) %collective-permute-start.14) | collective-permute-done | bytes 139296 | tf_op jit(solution)/shard_map/ppermute | solution.py:57
  67.2 6.9 %collective-permute-done.18.refs_9_ = bf16[256,256]{1,0:T(8,128)(2,1)S(1)} collective-permute-done((bf16[256,256]{1,0:T(8,128)(2,1)S(1)}, bf16[256,256]{1,0:T(8,128)(2,1)S(1)}, u32[]{:S(2)}, u32[]{:S(2)}) %collective-permute-start.18) | collective-permute-done | bytes 131104 | tf_op jit(solution)/shard_map/ppermute | solution.py:57
  75.1 4.0 %collective-permute-done.20.refs_11_ = bf16[256,256]{1,0:T(8,128)(2,1)S(1)} collective-permute-done((bf16[256,256]{1,0:T(8,128)(2,1)S(1)}, bf16[256,256]{1,0:T(8,128)(2,1)S(1)}, u32[]{:S(2)}, u32[]{:S(2)}) %collective-permute-start.20) | collective-permute-done | bytes 131104 | tf_op jit(solution)/shard_map/ppermute | solution.py:57
  81.7 1.6 %collective-permute-start.22 = (bf16[256,256]{1,0:T(8,128)(2,1)S(1)}, bf16[256,256]{1,0:T(8,128)(2,1)S(1)}, u32[]{:S(2)}, u32[]{:S(2)}) collective-permute-start(bf16[256,256]{1,0:T(8,128)(2,1)S(1)} %get-tuple-element.62), channel_id=1, source_target_pairs={{8,0},{9,1},{10,2},{11,3},{12,4},{13,5},{14,6},{15,7},{0,8},{1,9},... | collective-permute-start | bytes 393224 | tf_op jit(solution)/shard_map/ppermute | solution.py:57
  83.3 2.0 %collective-permute-start.24 = (bf16[256,256]{1,0:T(8,128)(2,1)S(1)}, bf16[256,256]{1,0:T(8,128)(2,1)S(1)}, u32[]{:S(2)}, u32[]{:S(2)}) collective-permute-start(bf16[256,256]{1,0:T(8,128)(2,1)S(1)} %get-tuple-element.64), channel_id=1, source_target_pairs={{10,0},{11,1},{8,2},{9,3},{14,4},{15,5},{12,6},{13,7},{2,8},{3,9},... | collective-permute-start | bytes 393224 | tf_op jit(solution)/shard_map/ppermute | solution.py:57
  85.3 2.1 %collective-permute-done.22.refs_0_ = bf16[256,256]{1,0:T(8,128)(2,1)S(1)} collective-permute-done((bf16[256,256]{1,0:T(8,128)(2,1)S(1)}, bf16[256,256]{1,0:T(8,128)(2,1)S(1)}, u32[]{:S(2)}, u32[]{:S(2)}) %collective-permute-start.22) | collective-permute-done | bytes 131104 | tf_op jit(solution)/shard_map/ppermute | solution.py:57
  87.3 2.3 %collective-permute-done.23.refs_1_ = bf16[256,256]{1,0:T(8,128)(2,1)S(1)} collective-permute-done((bf16[256,256]{1,0:T(8,128)(2,1)S(1)}, bf16[256,256]{1,0:T(8,128)(2,1)S(1)}, u32[]{:S(2)}, u32[]{:S(2)}) %collective-permute-start.23) | collective-permute-done | bytes 131104 | tf_op jit(solution)/shard_map/ppermute | solution.py:57
  89.6 1.7 %collective-permute-done.24.refs_2_ = bf16[256,256]{1,0:T(8,128)(2,1)S(1)} collective-permute-done((bf16[256,256]{1,0:T(8,128)(2,1)S(1)}, bf16[256,256]{1,0:T(8,128)(2,1)S(1)}, u32[]{:S(2)}, u32[]{:S(2)}) %collective-permute-start.24) | collective-permute-done | bytes 131104 | tf_op jit(solution)/shard_map/ppermute | solution.py:57
  (48 shorter events, 16.1 us)
Async XLA Ops:
  1.4 30.2 %collective-permute-start = (bf16[256,1152]{1,0:T(8,128)(2,1)S(1)}, bf16[256,1152]{1,0:T(8,128)(2,1)S(1)}, u32[]{:S(2)}, u32[]{:S(2)}) collective-permute-start(bf16[256,1152]{1,0:T(8,128)(2,1)S(1)} %shard_map.38.unit_ref.refs_0_), channel_id=1, source_target_pairs={{4,0},{5,1},{6,2},{7,3},{0,4},{1,5},{2,6},{3,7},{12,8},{13,9},{14,... | collective-permute-start | bytes 1769480 | tf_op jit(solution)/shard_map/ppermute | solution.py:57
  5.5 26.3 %collective-permute-start.2 = (bf16[256,1152]{1,0:T(8,128)(2,1)S(1)}, bf16[256,1152]{1,0:T(8,128)(2,1)S(1)}, u32[]{:S(2)}, u32[]{:S(2)}) collective-permute-start(bf16[256,1152]{1,0:T(8,128)(2,1)S(1)} %shard_map.38.unit_ref.refs_0_), channel_id=1, source_target_pairs={{2,0},{3,1},{0,2},{1,3},{6,4},{7,5},{4,6},{5,7},{10,8},{11,9},{8,1... | collective-permute-start | bytes 1769480 | tf_op jit(solution)/shard_map/ppermute | solution.py:57
  7.1 24.7 %collective-permute-start.1 = (bf16[256,1152]{1,0:T(8,128)(2,1)S(1)}, bf16[256,1152]{1,0:T(8,128)(2,1)S(1)}, u32[]{:S(2)}, u32[]{:S(2)}) collective-permute-start(bf16[256,1152]{1,0:T(8,128)(2,1)S(1)} %shard_map.38.unit_ref.refs_0_), channel_id=1, source_target_pairs={{8,0},{9,1},{10,2},{11,3},{12,4},{13,5},{14,6},{15,7},{0,8},{1,9},... | collective-permute-start | bytes 1769480 | tf_op jit(solution)/shard_map/ppermute | solution.py:57
  9.5 22.2 %collective-permute-start.4 = (bf16[256,1408]{1,0:T(8,128)(2,1)S(1)}, bf16[256,1408]{1,0:T(8,128)(2,1)S(1)}, u32[]{:S(2)}, u32[]{:S(2)}) collective-permute-start(bf16[256,1408]{1,0:T(8,128)(2,1)S(1)} %shard_map.40.refs_3_.refs_1_.refs_10_), channel_id=1, source_target_pairs={{16,0},{17,1},{18,2},{19,3},{20,4},{21,5},{22,6},{23,7},{24,8},{25... | collective-permute-start | bytes 2162696 | tf_op jit(solution)/shard_map/ppermute | solution.py:57
  11.1 20.7 %collective-permute-start.3 = (bf16[256,1408]{1,0:T(8,128)(2,1)S(1)}, bf16[256,1408]{1,0:T(8,128)(2,1)S(1)}, u32[]{:S(2)}, u32[]{:S(2)}) collective-permute-start(bf16[256,1408]{1,0:T(8,128)(2,1)S(1)} %shard_map.40.refs_3_.refs_1_.refs_10_), channel_id=1, source_target_pairs={{1,0},{0,1},{3,2},{2,3},{5,4},{4,5},{7,6},{6,7},{9,8},{8,9},{11,10... | collective-permute-start | bytes 2162696 | tf_op jit(solution)/shard_map/ppermute | solution.py:57
  31.8 6.4 %collective-permute-start.5 = (bf16[256,1408]{1,0:T(8,128)(2,1)S(1)}, bf16[256,1408]{1,0:T(8,128)(2,1)S(1)}, u32[]{:S(2)}, u32[]{:S(2)}) collective-permute-start(bf16[256,1408]{1,0:T(8,128)(2,1)S(1)} %collective-permute-done.4.refs_5_.refs_3_.refs_0_.refs_12_), channel_id=1, source_target_pairs={{1,0},{0,1},{3,2},{2,3},{5,4},{4,5},{7,6},{6,7},{9,8},{8,9},{11,10... | collective-permute-start | bytes 2162696 | tf_op jit(solution)/shard_map/ppermute | solution.py:57
  31.8 5.0 %collective-permute-start.6 = (bf16[256,1152]{1,0:T(8,128)(2,1)S(1)}, bf16[256,1152]{1,0:T(8,128)(2,1)S(1)}, u32[]{:S(2)}, u32[]{:S(2)}) collective-permute-start(bf16[256,1152]{1,0:T(8,128)(2,1)S(1)} %collective-permute-done.refs_3_.refs_5_), channel_id=1, source_target_pairs={{1,0},{0,1},{3,2},{2,3},{5,4},{4,5},{7,6},{6,7},{9,8},{8,9},{11,10... | collective-permute-start | bytes 1769480 | tf_op jit(solution)/shard_map/ppermute | solution.py:57
  32.4 14.9 %collective-permute-start.9 = (bf16[512,256]{1,0:T(8,128)(2,1)S(1)}, bf16[512,256]{1,0:T(8,128)(2,1)S(1)}, u32[]{:S(2)}, u32[]{:S(2)}) collective-permute-start(bf16[512,256]{1,0:T(8,128)(2,1)S(1)} %shard_map.45), channel_id=1, source_target_pairs={{4,0},{5,1},{6,2},{7,3},{0,4},{1,5},{2,6},{3,7},{12,8},{13,9},{14,... | collective-permute-start | bytes 786440 | tf_op jit(solution)/shard_map/ppermute | solution.py:57
  33.8 15.0 %collective-permute-start.8 = (bf16[256,1152]{1,0:T(8,128)(2,1)S(1)}, bf16[256,1152]{1,0:T(8,128)(2,1)S(1)}, u32[]{:S(2)}, u32[]{:S(2)}) collective-permute-start(bf16[256,1152]{1,0:T(8,128)(2,1)S(1)} %collective-permute-done.refs_3_.refs_5_), channel_id=1, source_target_pairs={{16,0},{17,1},{18,2},{19,3},{20,4},{21,5},{22,6},{23,7},{24,8},{25... | collective-permute-start | bytes 1769480 | tf_op jit(solution)/shard_map/ppermute | solution.py:57
  35.3 14.8 %collective-permute-start.7 = (bf16[256,1152]{1,0:T(8,128)(2,1)S(1)}, bf16[256,1152]{1,0:T(8,128)(2,1)S(1)}, u32[]{:S(2)}, u32[]{:S(2)}) collective-permute-start(bf16[256,1152]{1,0:T(8,128)(2,1)S(1)} %collective-permute-done.2.refs_2_), channel_id=1, source_target_pairs={{8,0},{9,1},{10,2},{11,3},{12,4},{13,5},{14,6},{15,7},{0,8},{1,9},... | collective-permute-start | bytes 1769480 | tf_op jit(solution)/shard_map/ppermute | solution.py:57
  50.1 2.8 %collective-permute-start.10 = (bf16[256,1152]{1,0:T(8,128)(2,1)S(1)}, bf16[256,1152]{1,0:T(8,128)(2,1)S(1)}, u32[]{:S(2)}, u32[]{:S(2)}) collective-permute-start(bf16[256,1152]{1,0:T(8,128)(2,1)S(1)} %collective-permute-done.8.refs_7_.refs_3_), channel_id=1, source_target_pairs={{1,0},{0,1},{3,2},{2,3},{5,4},{4,5},{7,6},{6,7},{9,8},{8,9},{11,10... | collective-permute-start | bytes 1769480 | tf_op jit(solution)/shard_map/ppermute | solution.py:57
  50.1 3.7 %collective-permute-start.11 = (bf16[512,256]{1,0:T(8,128)(2,1)S(1)}, bf16[512,256]{1,0:T(8,128)(2,1)S(1)}, u32[]{:S(2)}, u32[]{:S(2)}) collective-permute-start(bf16[512,256]{1,0:T(8,128)(2,1)S(1)} %shard_map.46.refs_14_), channel_id=1, source_target_pairs={{1,0},{0,1},{3,2},{2,3},{5,4},{4,5},{7,6},{6,7},{9,8},{8,9},{11,10... | collective-permute-start | bytes 786440 | tf_op jit(solution)/shard_map/ppermute | solution.py:57
  55.1 5.6 %collective-permute-start.12 = (bf16[272,256]{1,0:T(8,128)(2,1)S(1)}, bf16[272,256]{1,0:T(8,128)(2,1)S(1)}, u32[]{:S(2)}, u32[]{:S(2)}) collective-permute-start(bf16[272,256]{1,0:T(8,128)(2,1)S(1)} %get-tuple-element.56), channel_id=1, source_target_pairs={{8,0},{9,1},{10,2},{11,3},{12,4},{13,5},{14,6},{15,7},{0,8},{1,9},... | collective-permute-start | bytes 417800 | tf_op jit(solution)/shard_map/ppermute | solution.py:57
  56.7 7.0 %collective-permute-start.13 = (bf16[272,256]{1,0:T(8,128)(2,1)S(1)}, bf16[272,256]{1,0:T(8,128)(2,1)S(1)}, u32[]{:S(2)}, u32[]{:S(2)}) collective-permute-start(bf16[272,256]{1,0:T(8,128)(2,1)S(1)} %get-tuple-element.57), channel_id=1, source_target_pairs={{2,0},{3,1},{0,2},{1,3},{6,4},{7,5},{4,6},{5,7},{10,8},{11,9},{8,1... | collective-permute-start | bytes 417800 | tf_op jit(solution)/shard_map/ppermute | solution.py:57
  59.1 6.5 %collective-permute-start.14 = (bf16[272,256]{1,0:T(8,128)(2,1)S(1)}, bf16[272,256]{1,0:T(8,128)(2,1)S(1)}, u32[]{:S(2)}, u32[]{:S(2)}) collective-permute-start(bf16[272,256]{1,0:T(8,128)(2,1)S(1)} %get-tuple-element.58), channel_id=1, source_target_pairs={{10,0},{11,1},{8,2},{9,3},{14,4},{15,5},{12,6},{13,7},{2,8},{3,9},... | collective-permute-start | bytes 417800 | tf_op jit(solution)/shard_map/ppermute | solution.py:57
  65.8 8.3 %collective-permute-start.18 = (bf16[256,256]{1,0:T(8,128)(2,1)S(1)}, bf16[256,256]{1,0:T(8,128)(2,1)S(1)}, u32[]{:S(2)}, u32[]{:S(2)}) collective-permute-start(bf16[256,256]{1,0:T(8,128)(2,1)S(1)} %get-tuple-element.59.refs_5_), channel_id=1, source_target_pairs={{4,0},{5,1},{6,2},{7,3},{0,4},{1,5},{2,6},{3,7},{12,8},{13,9},{14,... | collective-permute-start | bytes 393224 | tf_op jit(solution)/shard_map/ppermute | solution.py:57
  66.8 8.4 %collective-permute-start.16 = (bf16[256,256]{1,0:T(8,128)(2,1)S(1)}, bf16[256,256]{1,0:T(8,128)(2,1)S(1)}, u32[]{:S(2)}, u32[]{:S(2)}) collective-permute-start(bf16[256,256]{1,0:T(8,128)(2,1)S(1)} %get-tuple-element.59.refs_5_), channel_id=1, source_target_pairs={{16,0},{17,1},{18,2},{19,3},{20,4},{21,5},{22,6},{23,7},{24,8},{25... | collective-permute-start | bytes 393224 | tf_op jit(solution)/shard_map/ppermute | solution.py:57
  74.1 5.0 %collective-permute-start.20 = (bf16[256,256]{1,0:T(8,128)(2,1)S(1)}, bf16[256,256]{1,0:T(8,128)(2,1)S(1)}, u32[]{:S(2)}, u32[]{:S(2)}) collective-permute-start(bf16[256,256]{1,0:T(8,128)(2,1)S(1)} %collective-permute-done.18.refs_9_), channel_id=1, source_target_pairs={{16,0},{17,1},{18,2},{19,3},{20,4},{21,5},{22,6},{23,7},{24,8},{25... | collective-permute-start | bytes 393224 | tf_op jit(solution)/shard_map/ppermute | solution.py:57
  74.6 4.5 %collective-permute-start.15 = (bf16[256,256]{1,0:T(8,128)(2,1)S(1)}, bf16[256,256]{1,0:T(8,128)(2,1)S(1)}, u32[]{:S(2)}, u32[]{:S(2)}) collective-permute-start(bf16[256,256]{1,0:T(8,128)(2,1)S(1)} %get-tuple-element.59.refs_5_), channel_id=1, source_target_pairs={{1,0},{0,1},{3,2},{2,3},{5,4},{4,5},{7,6},{6,7},{9,8},{8,9},{11,10... | collective-permute-start | bytes 393224 | tf_op jit(solution)/shard_map/ppermute | solution.py:57
  74.6 4.5 %collective-permute-start.19 = (bf16[256,256]{1,0:T(8,128)(2,1)S(1)}, bf16[256,256]{1,0:T(8,128)(2,1)S(1)}, u32[]{:S(2)}, u32[]{:S(2)}) collective-permute-start(bf16[256,256]{1,0:T(8,128)(2,1)S(1)} %collective-permute-done.18.refs_9_), channel_id=1, source_target_pairs={{1,0},{0,1},{3,2},{2,3},{5,4},{4,5},{7,6},{6,7},{9,8},{8,9},{11,10... | collective-permute-start | bytes 393224 | tf_op jit(solution)/shard_map/ppermute | solution.py:57
  75.1 4.0 %collective-permute-start.17 = (bf16[256,256]{1,0:T(8,128)(2,1)S(1)}, bf16[256,256]{1,0:T(8,128)(2,1)S(1)}, u32[]{:S(2)}, u32[]{:S(2)}) collective-permute-start(bf16[256,256]{1,0:T(8,128)(2,1)S(1)} %collective-permute-done.16.refs_7_), channel_id=1, source_target_pairs={{1,0},{0,1},{3,2},{2,3},{5,4},{4,5},{7,6},{6,7},{9,8},{8,9},{11,10... | collective-permute-start | bytes 393224 | tf_op jit(solution)/shard_map/ppermute | solution.py:57
  81.7 5.6 %collective-permute-start.22 = (bf16[256,256]{1,0:T(8,128)(2,1)S(1)}, bf16[256,256]{1,0:T(8,128)(2,1)S(1)}, u32[]{:S(2)}, u32[]{:S(2)}) collective-permute-start(bf16[256,256]{1,0:T(8,128)(2,1)S(1)} %get-tuple-element.62), channel_id=1, source_target_pairs={{8,0},{9,1},{10,2},{11,3},{12,4},{13,5},{14,6},{15,7},{0,8},{1,9},... | collective-permute-start | bytes 393224 | tf_op jit(solution)/shard_map/ppermute | solution.py:57
  83.3 6.4 %collective-permute-start.23 = (bf16[256,256]{1,0:T(8,128)(2,1)S(1)}, bf16[256,256]{1,0:T(8,128)(2,1)S(1)}, u32[]{:S(2)}, u32[]{:S(2)}) collective-permute-start(bf16[256,256]{1,0:T(8,128)(2,1)S(1)} %get-tuple-element.63), channel_id=1, source_target_pairs={{2,0},{3,1},{0,2},{1,3},{6,4},{7,5},{4,6},{5,7},{10,8},{11,9},{8,1... | collective-permute-start | bytes 393224 | tf_op jit(solution)/shard_map/ppermute | solution.py:57
  83.3 8.0 %collective-permute-start.24 = (bf16[256,256]{1,0:T(8,128)(2,1)S(1)}, bf16[256,256]{1,0:T(8,128)(2,1)S(1)}, u32[]{:S(2)}, u32[]{:S(2)}) collective-permute-start(bf16[256,256]{1,0:T(8,128)(2,1)S(1)} %get-tuple-element.64), channel_id=1, source_target_pairs={{10,0},{11,1},{8,2},{9,3},{14,4},{15,5},{12,6},{13,7},{2,8},{3,9},... | collective-permute-start | bytes 393224 | tf_op jit(solution)/shard_map/ppermute | solution.py:57
  (4 other events, 14.4 us)

commit v12 on v11

--- a/solution.py
+++ b/solution.py
@@ -247,9 +247,53 @@
     )(flags, *t_pieces, *s_pieces)
 
 
+def row_sums(kerns, rects, pcat, row, rows, lo, hi):
+    part = None
+    for kern, (t0, t1, c0, c1) in zip(kerns, rects):
+        first, last = max(c0, lo), min(c1, hi)
+        if t0 <= row < t1 and first < last:
+            term = jnp.dot(
+                kern[row - t0 : row - t0 + rows, first - c0 : last - c0],
+                pcat[first - lo : last - lo, :],
+                preferred_element_type=jnp.float32,
+            )
+            part = term if part is None else part + term
+    return part
+
+
+def base_kernel(t_layout, rects, nk, *refs):
+    kerns, p_in, (out_ref, pcat) = refs[:nk], refs[nk:-2], refs[-2:]
+    at = 0
+    for ref in p_in:
+        pcat[at : at + ref.shape[0], :] = ref[...]
+        at += ref.shape[0]
+    row = 0
+    for _, _, rows in t_layout:
+        out_ref[row : row + rows, :] = row_sums(kerns, rects, pcat, row, rows, 0, at)
+        row += rows
+
+
+def base_call(kerns, p_pieces, t_layout, rects):
+    m, c = p_pieces[0].shape
+    rows, cols = sum(r for _, _, r in t_layout), m * len(p_pieces)
+    out = shape((rows, c), jnp.float32)
+    return pl.pallas_call(
+        functools.partial(base_kernel, t_layout, rects, len(kerns)),
+        out_shape=out,
+        in_specs=[VMEM] * (len(kerns) + len(p_pieces)),
+        out_specs=VMEM,
+        scratch_shapes=[pltpu.VMEM((cols, c), jnp.bfloat16)],
+        compiler_params=limits(*kerns, *p_pieces, out, shape((cols, c))),
+        cost_estimate=pl.CostEstimate(
+            flops=2 * rows * cols * c, bytes_accessed=2 * rows * cols, transcendentals=0
+        ),
+    )(*kerns, *p_pieces)
+
+
 def spread_kernel(plan, nk, na, ns, *refs):
-    m, t_layout, rects, p_map = plan
+    m, t_layout, rects, p_map, lo = plan
     kerns, refs = refs[:nk], refs[nk:]
+    base, refs = (refs[0], refs[1:]) if lo else (None, refs)
     accs, refs = refs[:na], refs[na:]
     p_in, refs = refs[:ns], refs[ns:]
     outs, pcat = refs[:-1], refs[-1]
@@ -261,15 +305,9 @@
         at += rows
     row = 0
     for piece, start, rows in t_layout:
-        part = None
-        for kern, (t0, t1, c0, c1) in zip(kerns, rects):
-            if t0 <= row < t1:
-                term = jnp.dot(
-                    kern[row - t0 : row - t0 + rows, :],
-                    pcat[c0:c1, :],
-                    preferred_element_type=jnp.float32,
-                )
-                part = term if part is None else part + term
+        part = row_sums(kerns, rects, pcat, row, rows, lo, lo + pcat.shape[0])
+        if lo:
+            part = part + base[row : row + rows, :]
         if piece == 0:
             own_ref[start : start + rows, :] = part
         else:
@@ -297,8 +335,8 @@
         row += rows
 
 
-def spread_call(kerns, accs, p_pieces, c, plan):
-    m, t_layout, rects, p_map = plan
+def spread_call(kerns, accs, p_pieces, c, plan, base=()):
+    m, t_layout, rects, p_map, lo = plan
     nt = 1 + max(piece for piece, _, _ in t_layout)
     cols = sum(rows for _, _, rows, _ in p_map)
     extra = 16 if accs else 0
@@ -309,16 +347,16 @@
     return pl.pallas_call(
         functools.partial(spread_kernel, plan, len(kerns), len(accs), len(p_pieces)),
         out_shape=outs,
-        in_specs=[VMEM] * (len(kerns) + len(accs) + len(p_pieces)),
+        in_specs=[VMEM] * (len(kerns) + len(base) + len(accs) + len(p_pieces)),
         out_specs=[VMEM] * len(outs),
         scratch_shapes=[pltpu.VMEM((cols, c), jnp.bfloat16)],
-        compiler_params=limits(*kerns, *accs, *p_pieces, *outs, shape((cols, c))),
+        compiler_params=limits(*kerns, *base, *accs, *p_pieces, *outs, shape((cols, c))),
         cost_estimate=pl.CostEstimate(
             flops=2 * nt * m * cols * c,
             bytes_accessed=2 * (nt * m * cols + cols * c),
             transcendentals=0,
         ),
-    )(*kerns, *accs, *p_pieces)
+    )(*kerns, *base, *accs, *p_pieces)
 
 
 def first_update_kernel(seed_ref, own_ref, own_total_ref, *refs):
@@ -390,7 +428,6 @@
         [(b, a, k) for k in other["core"] for a in other["y"] for b in other["zh"]],
     ]
     s_layout = [dict(zh=b, y=a, core=k) for group in groups for b, a, k in group]
-    p_map = [(i, 0, m, 0) for i in range(len(s_layout))]
     seeds_map = []
     for i, o in enumerate(s_layout):
         if o["zh"] == 0:
@@ -445,7 +482,7 @@
     early, last = len(near_t), len(t_order)
     gram = rectangle(0, early, 0, 1) + rectangle(0, early, 1, 2)
     seeds_zh = [stack_seeds(after(v, *gram), [], 2 * 10**10) for v in seeds_zh]
-    done = zh_y + zl_x + zh_core + gram + seeds_zh
+    done = zh_y + zh_core + gram + seeds_zh
     zh_y_core = fetch(zh_y, "core", *done)
     s_pieces[3] = zh_y_core
     seeds_core = fetch(seeds_zh, "core", *done)
@@ -467,7 +504,7 @@
         return near + far + fetch(far, "core") + far_y + fetch(far_y, "core")
 
     seeds = s_pieces[0] + seeds_zh + seeds_core
-    own, totals, *others = spread_call(kerns, accs, seeds, c, (*plan, seeds_map))
+    own, totals, *others = spread_call(kerns, accs, seeds, c, (*plan, seeds_map, 0))
     panel, totals = update(
         first_update_kernel,
         held,
@@ -479,7 +516,11 @@
             jax.ShapeDtypeStruct((m, BLOCK), jnp.float32),
         ],
     )
-    own, *others = spread_call(kerns, [], panels(panel), c, (*plan, p_map))
+    pieces = panels(panel)
+    first = len(groups[0]) + len(groups[1])
+    base = base_call(kerns, pieces[:first], t_layout, rects)
+    rest = [(i, 0, m, 0) for i in range(len(pieces) - first)]
+    own, *others = spread_call(kerns, [], pieces[first:], c, (*plan, rest, first * m), [base])
     return update(
         last_update_kernel,
         held,

time: 92.3 us -> 90.2 us (0.977)
  waiting for transfers between devices: 54 us -> 49.6 us
  starting transfers between devices: 24.2 us -> 26.4 us
    ppermute x25, waiting for transfers between devices: 54 us -> 49.6 us  [fetch(): return lax.ppermute(value, AXES, pairs)]
    ppermute x25, starting transfers between devices: 24.2 us -> 26.4 us  [fetch(): return lax.ppermute(value, AXES, pairs)]
    pallas_call x0 -> x1, Pallas kernels: none -> 0.98 us  [base_call(): pl.pallas_call(functools.partial(base_kernel, t_layout, rects, len(kerns)...]
  transfers between devices with their start and end apart: 25 -> 25, of which waited for: 14 -> 13; matrix products, arithmetic and copies ran while one was open for 0% -> 0% of each run, Pallas kernels for 9% -> 10%
where the time goes in v12:
time: 90.2 us; the launch traced here: 90 us
  waiting for transfers between devices  49.6 us (55%)
  starting transfers between devices  26.4 us (29%)
  Pallas kernels  11.8 us (13%)
  local copies, waits for them, and re-layouts  1.97 us (2%)
    ppermute x25, waiting for transfers between devices, fetch(): return lax.ppermute(value, AXES, pairs)  49.6 us
    ppermute x25, starting transfers between devices, fetch(): return lax.ppermute(value, AXES, pairs)  26.4 us
    pallas_call x5, Pallas kernels, gram_call(): pl.pallas_call(functools.partial(gram_kernel, len(t_pieces), len(s_pieces...  6.87 us
    unnamed x6, local copies, waits for them, and re-layouts  1.97 us
  transfers between devices with their start and end apart: 25, of which 13 were waited for; matrix products, arithmetic and copies ran while one was open for 0% of the time, Pallas kernels for 10%

profile of v12, /device:TPU:0, one launch (start us, length us, event | category | flops | bytes accessed | tf_op | source)
XLA Modules:
  0.0 90.0 jit_solution(15277704592667249443)
XLA Ops:
  1.4 4.1 %collective-permute-start = (bf16[256,1152]{1,0:T(8,128)(2,1)S(1)}, bf16[256,1152]{1,0:T(8,128)(2,1)S(1)}, u32[]{:S(2)}, u32[]{:S(2)}) collective-permute-start(bf16[256,1152]{1,0:T(8,128)(2,1)S(1)} %shard_map.38.unit_ref.refs_0_), channel_id=1, source_target_pairs={{4,0},{5,1},{6,2},{7,3},{0,4},{1,5},{2,6},{3,7},{12,8},{13,9},{14,... | collective-permute-start | bytes 1769480 | tf_op jit(solution)/shard_map/ppermute | solution.py:57
  5.5 1.6 %collective-permute-start.2 = (bf16[256,1152]{1,0:T(8,128)(2,1)S(1)}, bf16[256,1152]{1,0:T(8,128)(2,1)S(1)}, u32[]{:S(2)}, u32[]{:S(2)}) collective-permute-start(bf16[256,1152]{1,0:T(8,128)(2,1)S(1)} %shard_map.38.unit_ref.refs_0_), channel_id=1, source_target_pairs={{2,0},{3,1},{0,2},{1,3},{6,4},{7,5},{4,6},{5,7},{10,8},{11,9},{8,1... | collective-permute-start | bytes 1769480 | tf_op jit(solution)/shard_map/ppermute | solution.py:57
  7.1 1.5 %collective-permute-start.1 = (bf16[256,1152]{1,0:T(8,128)(2,1)S(1)}, bf16[256,1152]{1,0:T(8,128)(2,1)S(1)}, u32[]{:S(2)}, u32[]{:S(2)}) collective-permute-start(bf16[256,1152]{1,0:T(8,128)(2,1)S(1)} %shard_map.38.unit_ref.refs_0_), channel_id=1, source_target_pairs={{8,0},{9,1},{10,2},{11,3},{12,4},{13,5},{14,6},{15,7},{0,8},{1,9},... | collective-permute-start | bytes 1769480 | tf_op jit(solution)/shard_map/ppermute | solution.py:57
  9.5 1.6 %collective-permute-start.4 = (bf16[256,1408]{1,0:T(8,128)(2,1)S(1)}, bf16[256,1408]{1,0:T(8,128)(2,1)S(1)}, u32[]{:S(2)}, u32[]{:S(2)}) collective-permute-start(bf16[256,1408]{1,0:T(8,128)(2,1)S(1)} %shard_map.40.refs_3_.refs_1_.refs_10_), channel_id=1, source_target_pairs={{16,0},{17,1},{18,2},{19,3},{20,4},{21,5},{22,6},{23,7},{24,8},{25... | collective-permute-start | bytes 2162696 | tf_op jit(solution)/shard_map/ppermute | solution.py:57
  12.0 19.5 %collective-permute-done.refs_3_.refs_5_ = bf16[256,1152]{1,0:T(8,128)(2,1)S(1)} collective-permute-done((bf16[256,1152]{1,0:T(8,128)(2,1)S(1)}, bf16[256,1152]{1,0:T(8,128)(2,1)S(1)}, u32[]{:S(2)}, u32[]{:S(2)}) %collective-permute-start) | collective-permute-done | bytes 589856 | tf_op jit(solution)/shard_map/ppermute | solution.py:57
  33.8 1.5 %collective-permute-start.8 = (bf16[256,1152]{1,0:T(8,128)(2,1)S(1)}, bf16[256,1152]{1,0:T(8,128)(2,1)S(1)}, u32[]{:S(2)}, u32[]{:S(2)}) collective-permute-start(bf16[256,1152]{1,0:T(8,128)(2,1)S(1)} %collective-permute-done.refs_3_.refs_5_), channel_id=1, source_target_pairs={{16,0},{17,1},{18,2},{19,3},{20,4},{21,5},{22,6},{23,7},{24,8},{25... | collective-permute-start | bytes 1769480 | tf_op jit(solution)/shard_map/ppermute | solution.py:57
  35.3 1.5 %collective-permute-start.7 = (bf16[256,1152]{1,0:T(8,128)(2,1)S(1)}, bf16[256,1152]{1,0:T(8,128)(2,1)S(1)}, u32[]{:S(2)}, u32[]{:S(2)}) collective-permute-start(bf16[256,1152]{1,0:T(8,128)(2,1)S(1)} %collective-permute-done.2.refs_2_), channel_id=1, source_target_pairs={{8,0},{9,1},{10,2},{11,3},{12,4},{13,5},{14,6},{15,7},{0,8},{1,9},... | collective-permute-start | bytes 1769480 | tf_op jit(solution)/shard_map/ppermute | solution.py:57
  38.1 2.4 %shard_map.41 = (bf16[768,1024]{1,0:T(8,128)(2,1)S(1)}, f32[768,128]{1,0:T(8,128)S(1)}) custom-call(s32[8,2048]{1,0:T(8,128)S(1)} %shard_map.37.flags, bf16[256,1152]{1,0:T(8,128)(2,1)S(1)} %shard_map.38.unit_ref.refs_0_, bf16[256,1152]{1,0:T(8,128)(2,1)S(1)} %collective-permute-done.1.refs_1_, bf16[256,1152]{1,0:T(8,128)(2,1)S(1)} %collective-permute-done.2.refs_2_, ...), custom_call_target="tpu_custom_call" | custom-call | flops 1811939328 | bytes 4128768 | tf_op jit(solution)/shard_map/pallas_call | solution.py:233
  40.5 6.7 %collective-permute-done.9.seed_ref = bf16[512,256]{1,0:T(8,128)(2,1)S(1)} collective-permute-done((bf16[512,256]{1,0:T(8,128)(2,1)S(1)}, bf16[512,256]{1,0:T(8,128)(2,1)S(1)}, u32[]{:S(2)}, u32[]{:S(2)}) %collective-permute-start.9) | collective-permute-done | bytes 262176 | tf_op jit(solution)/shard_map/ppermute | solution.py:57
  47.3 1.6 %collective-permute-done.8.refs_7_.refs_3_ = bf16[256,1152]{1,0:T(8,128)(2,1)S(1)} collective-permute-done((bf16[256,1152]{1,0:T(8,128)(2,1)S(1)}, bf16[256,1152]{1,0:T(8,128)(2,1)S(1)}, u32[]{:S(2)}, u32[]{:S(2)}) %collective-permute-start.8) | collective-permute-done | bytes 589856 | tf_op jit(solution)/shard_map/ppermute | solution.py:57
  53.8 1.6 %collective-permute-start.12 = (bf16[272,256]{1,0:T(8,128)(2,1)S(1)}, bf16[272,256]{1,0:T(8,128)(2,1)S(1)}, u32[]{:S(2)}, u32[]{:S(2)}) collective-permute-start(bf16[272,256]{1,0:T(8,128)(2,1)S(1)} %get-tuple-element.56), channel_id=1, source_target_pairs={{8,0},{9,1},{10,2},{11,3},{12,4},{13,5},{14,6},{15,7},{0,8},{1,9},... | collective-permute-start | bytes 417800 | tf_op jit(solution)/shard_map/ppermute | solution.py:57
  55.4 2.5 %collective-permute-start.13 = (bf16[272,256]{1,0:T(8,128)(2,1)S(1)}, bf16[272,256]{1,0:T(8,128)(2,1)S(1)}, u32[]{:S(2)}, u32[]{:S(2)}) collective-permute-start(bf16[272,256]{1,0:T(8,128)(2,1)S(1)} %get-tuple-element.57), channel_id=1, source_target_pairs={{2,0},{3,1},{0,2},{1,3},{6,4},{7,5},{4,6},{5,7},{10,8},{11,9},{8,1... | collective-permute-start | bytes 417800 | tf_op jit(solution)/shard_map/ppermute | solution.py:57
  57.9 1.6 %collective-permute-done.12.refs_0_ = bf16[272,256]{1,0:T(8,128)(2,1)S(1)} collective-permute-done((bf16[272,256]{1,0:T(8,128)(2,1)S(1)}, bf16[272,256]{1,0:T(8,128)(2,1)S(1)}, u32[]{:S(2)}, u32[]{:S(2)}) %collective-permute-start.12) | collective-permute-done | bytes 139296 | tf_op jit(solution)/shard_map/ppermute | solution.py:57
  59.5 2.9 %collective-permute-done.13.refs_1_ = bf16[272,256]{1,0:T(8,128)(2,1)S(1)} collective-permute-done((bf16[272,256]{1,0:T(8,128)(2,1)S(1)}, bf16[272,256]{1,0:T(8,128)(2,1)S(1)}, u32[]{:S(2)}, u32[]{:S(2)}) %collective-permute-start.13) | collective-permute-done | bytes 139296 | tf_op jit(solution)/shard_map/ppermute | solution.py:57
  62.4 2.0 %collective-permute-done.14.refs_2_ = bf16[272,256]{1,0:T(8,128)(2,1)S(1)} collective-permute-done((bf16[272,256]{1,0:T(8,128)(2,1)S(1)}, bf16[272,256]{1,0:T(8,128)(2,1)S(1)}, u32[]{:S(2)}, u32[]{:S(2)}) %collective-permute-start.14) | collective-permute-done | bytes 139296 | tf_op jit(solution)/shard_map/ppermute | solution.py:57
  65.4 1.6 %collective-permute-start.16 = (bf16[256,256]{1,0:T(8,128)(2,1)S(1)}, bf16[256,256]{1,0:T(8,128)(2,1)S(1)}, u32[]{:S(2)}, u32[]{:S(2)}) collective-permute-start(bf16[256,256]{1,0:T(8,128)(2,1)S(1)} %get-tuple-element.59.refs_5_), channel_id=1, source_target_pairs={{16,0},{17,1},{18,2},{19,3},{20,4},{21,5},{22,6},{23,7},{24,8},{25... | collective-permute-start | bytes 393224 | tf_op jit(solution)/shard_map/ppermute | solution.py:57
  67.0 5.8 %collective-permute-done.18.refs_9_ = bf16[256,256]{1,0:T(8,128)(2,1)S(1)} collective-permute-done((bf16[256,256]{1,0:T(8,128)(2,1)S(1)}, bf16[256,256]{1,0:T(8,128)(2,1)S(1)}, u32[]{:S(2)}, u32[]{:S(2)}) %collective-permute-start.18) | collective-permute-done | bytes 131104 | tf_op jit(solution)/shard_map/ppermute | solution.py:57
  72.8 1.5 %collective-permute-start.20 = (bf16[256,256]{1,0:T(8,128)(2,1)S(1)}, bf16[256,256]{1,0:T(8,128)(2,1)S(1)}, u32[]{:S(2)}, u32[]{:S(2)}) collective-permute-start(bf16[256,256]{1,0:T(8,128)(2,1)S(1)} %collective-permute-done.18.refs_9_), channel_id=1, source_target_pairs={{16,0},{17,1},{18,2},{19,3},{20,4},{21,5},{22,6},{23,7},{24,8},{25... | collective-permute-start | bytes 393224 | tf_op jit(solution)/shard_map/ppermute | solution.py:57
  74.8 2.9 %collective-permute-done.20.refs_6_ = bf16[256,256]{1,0:T(8,128)(2,1)S(1)} collective-permute-done((bf16[256,256]{1,0:T(8,128)(2,1)S(1)}, bf16[256,256]{1,0:T(8,128)(2,1)S(1)}, u32[]{:S(2)}, u32[]{:S(2)}) %collective-permute-start.20) | collective-permute-done | bytes 131104 | tf_op jit(solution)/shard_map/ppermute | solution.py:57
  79.6 1.6 %collective-permute-start.22 = (bf16[256,256]{1,0:T(8,128)(2,1)S(1)}, bf16[256,256]{1,0:T(8,128)(2,1)S(1)}, u32[]{:S(2)}, u32[]{:S(2)}) collective-permute-start(bf16[256,256]{1,0:T(8,128)(2,1)S(1)} %get-tuple-element.62), channel_id=1, source_target_pairs={{8,0},{9,1},{10,2},{11,3},{12,4},{13,5},{14,6},{15,7},{0,8},{1,9},... | collective-permute-start | bytes 393224 | tf_op jit(solution)/shard_map/ppermute | solution.py:57
  81.2 1.9 %collective-permute-start.24 = (bf16[256,256]{1,0:T(8,128)(2,1)S(1)}, bf16[256,256]{1,0:T(8,128)(2,1)S(1)}, u32[]{:S(2)}, u32[]{:S(2)}) collective-permute-start(bf16[256,256]{1,0:T(8,128)(2,1)S(1)} %get-tuple-element.64), channel_id=1, source_target_pairs={{10,0},{11,1},{8,2},{9,3},{14,4},{15,5},{12,6},{13,7},{2,8},{3,9},... | collective-permute-start | bytes 393224 | tf_op jit(solution)/shard_map/ppermute | solution.py:57
  83.1 2.1 %collective-permute-done.22.refs_0_ = bf16[256,256]{1,0:T(8,128)(2,1)S(1)} collective-permute-done((bf16[256,256]{1,0:T(8,128)(2,1)S(1)}, bf16[256,256]{1,0:T(8,128)(2,1)S(1)}, u32[]{:S(2)}, u32[]{:S(2)}) %collective-permute-start.22) | collective-permute-done | bytes 131104 | tf_op jit(solution)/shard_map/ppermute | solution.py:57
  85.2 2.3 %collective-permute-done.23.refs_1_ = bf16[256,256]{1,0:T(8,128)(2,1)S(1)} collective-permute-done((bf16[256,256]{1,0:T(8,128)(2,1)S(1)}, bf16[256,256]{1,0:T(8,128)(2,1)S(1)}, u32[]{:S(2)}, u32[]{:S(2)}) %collective-permute-start.23) | collective-permute-done | bytes 131104 | tf_op jit(solution)/shard_map/ppermute | solution.py:57
  87.5 1.6 %collective-permute-done.24.refs_2_ = bf16[256,256]{1,0:T(8,128)(2,1)S(1)} collective-permute-done((bf16[256,256]{1,0:T(8,128)(2,1)S(1)}, bf16[256,256]{1,0:T(8,128)(2,1)S(1)}, u32[]{:S(2)}, u32[]{:S(2)}) %collective-permute-start.24) | collective-permute-done | bytes 131104 | tf_op jit(solution)/shard_map/ppermute | solution.py:57
  (49 shorter events, 15.9 us)
Async XLA Ops:
  1.4 30.2 %collective-permute-start = (bf16[256,1152]{1,0:T(8,128)(2,1)S(1)}, bf16[256,1152]{1,0:T(8,128)(2,1)S(1)}, u32[]{:S(2)}, u32[]{:S(2)}) collective-permute-start(bf16[256,1152]{1,0:T(8,128)(2,1)S(1)} %shard_map.38.unit_ref.refs_0_), channel_id=1, source_target_pairs={{4,0},{5,1},{6,2},{7,3},{0,4},{1,5},{2,6},{3,7},{12,8},{13,9},{14,... | collective-permute-start | bytes 1769480 | tf_op jit(solution)/shard_map/ppermute | solution.py:57
  5.5 26.3 %collective-permute-start.2 = (bf16[256,1152]{1,0:T(8,128)(2,1)S(1)}, bf16[256,1152]{1,0:T(8,128)(2,1)S(1)}, u32[]{:S(2)}, u32[]{:S(2)}) collective-permute-start(bf16[256,1152]{1,0:T(8,128)(2,1)S(1)} %shard_map.38.unit_ref.refs_0_), channel_id=1, source_target_pairs={{2,0},{3,1},{0,2},{1,3},{6,4},{7,5},{4,6},{5,7},{10,8},{11,9},{8,1... | collective-permute-start | bytes 1769480 | tf_op jit(solution)/shard_map/ppermute | solution.py:57
  7.1 24.7 %collective-permute-start.1 = (bf16[256,1152]{1,0:T(8,128)(2,1)S(1)}, bf16[256,1152]{1,0:T(8,128)(2,1)S(1)}, u32[]{:S(2)}, u32[]{:S(2)}) collective-permute-start(bf16[256,1152]{1,0:T(8,128)(2,1)S(1)} %shard_map.38.unit_ref.refs_0_), channel_id=1, source_target_pairs={{8,0},{9,1},{10,2},{11,3},{12,4},{13,5},{14,6},{15,7},{0,8},{1,9},... | collective-permute-start | bytes 1769480 | tf_op jit(solution)/shard_map/ppermute | solution.py:57
  9.5 22.2 %collective-permute-start.4 = (bf16[256,1408]{1,0:T(8,128)(2,1)S(1)}, bf16[256,1408]{1,0:T(8,128)(2,1)S(1)}, u32[]{:S(2)}, u32[]{:S(2)}) collective-permute-start(bf16[256,1408]{1,0:T(8,128)(2,1)S(1)} %shard_map.40.refs_3_.refs_1_.refs_10_), channel_id=1, source_target_pairs={{16,0},{17,1},{18,2},{19,3},{20,4},{21,5},{22,6},{23,7},{24,8},{25... | collective-permute-start | bytes 2162696 | tf_op jit(solution)/shard_map/ppermute | solution.py:57
  11.1 20.7 %collective-permute-start.3 = (bf16[256,1408]{1,0:T(8,128)(2,1)S(1)}, bf16[256,1408]{1,0:T(8,128)(2,1)S(1)}, u32[]{:S(2)}, u32[]{:S(2)}) collective-permute-start(bf16[256,1408]{1,0:T(8,128)(2,1)S(1)} %shard_map.40.refs_3_.refs_1_.refs_10_), channel_id=1, source_target_pairs={{1,0},{0,1},{3,2},{2,3},{5,4},{4,5},{7,6},{6,7},{9,8},{8,9},{11,10... | collective-permute-start | bytes 2162696 | tf_op jit(solution)/shard_map/ppermute | solution.py:57
  31.8 6.4 %collective-permute-start.5 = (bf16[256,1408]{1,0:T(8,128)(2,1)S(1)}, bf16[256,1408]{1,0:T(8,128)(2,1)S(1)}, u32[]{:S(2)}, u32[]{:S(2)}) collective-permute-start(bf16[256,1408]{1,0:T(8,128)(2,1)S(1)} %collective-permute-done.4.refs_5_.refs_3_.refs_0_.refs_12_), channel_id=1, source_target_pairs={{1,0},{0,1},{3,2},{2,3},{5,4},{4,5},{7,6},{6,7},{9,8},{8,9},{11,10... | collective-permute-start | bytes 2162696 | tf_op jit(solution)/shard_map/ppermute | solution.py:57
  31.8 5.0 %collective-permute-start.6 = (bf16[256,1152]{1,0:T(8,128)(2,1)S(1)}, bf16[256,1152]{1,0:T(8,128)(2,1)S(1)}, u32[]{:S(2)}, u32[]{:S(2)}) collective-permute-start(bf16[256,1152]{1,0:T(8,128)(2,1)S(1)} %collective-permute-done.refs_3_.refs_5_), channel_id=1, source_target_pairs={{1,0},{0,1},{3,2},{2,3},{5,4},{4,5},{7,6},{6,7},{9,8},{8,9},{11,10... | collective-permute-start | bytes 1769480 | tf_op jit(solution)/shard_map/ppermute | solution.py:57
  32.4 14.9 %collective-permute-start.9 = (bf16[512,256]{1,0:T(8,128)(2,1)S(1)}, bf16[512,256]{1,0:T(8,128)(2,1)S(1)}, u32[]{:S(2)}, u32[]{:S(2)}) collective-permute-start(bf16[512,256]{1,0:T(8,128)(2,1)S(1)} %shard_map.45), channel_id=1, source_target_pairs={{4,0},{5,1},{6,2},{7,3},{0,4},{1,5},{2,6},{3,7},{12,8},{13,9},{14,... | collective-permute-start | bytes 786440 | tf_op jit(solution)/shard_map/ppermute | solution.py:57
  33.8 15.0 %collective-permute-start.8 = (bf16[256,1152]{1,0:T(8,128)(2,1)S(1)}, bf16[256,1152]{1,0:T(8,128)(2,1)S(1)}, u32[]{:S(2)}, u32[]{:S(2)}) collective-permute-start(bf16[256,1152]{1,0:T(8,128)(2,1)S(1)} %collective-permute-done.refs_3_.refs_5_), channel_id=1, source_target_pairs={{16,0},{17,1},{18,2},{19,3},{20,4},{21,5},{22,6},{23,7},{24,8},{25... | collective-permute-start | bytes 1769480 | tf_op jit(solution)/shard_map/ppermute | solution.py:57
  35.3 14.8 %collective-permute-start.7 = (bf16[256,1152]{1,0:T(8,128)(2,1)S(1)}, bf16[256,1152]{1,0:T(8,128)(2,1)S(1)}, u32[]{:S(2)}, u32[]{:S(2)}) collective-permute-start(bf16[256,1152]{1,0:T(8,128)(2,1)S(1)} %collective-permute-done.2.refs_2_), channel_id=1, source_target_pairs={{8,0},{9,1},{10,2},{11,3},{12,4},{13,5},{14,6},{15,7},{0,8},{1,9},... | collective-permute-start | bytes 1769480 | tf_op jit(solution)/shard_map/ppermute | solution.py:57
  48.8 2.8 %collective-permute-start.10 = (bf16[256,1152]{1,0:T(8,128)(2,1)S(1)}, bf16[256,1152]{1,0:T(8,128)(2,1)S(1)}, u32[]{:S(2)}, u32[]{:S(2)}) collective-permute-start(bf16[256,1152]{1,0:T(8,128)(2,1)S(1)} %collective-permute-done.8.refs_7_.refs_3_), channel_id=1, source_target_pairs={{1,0},{0,1},{3,2},{2,3},{5,4},{4,5},{7,6},{6,7},{9,8},{8,9},{11,10... | collective-permute-start | bytes 1769480 | tf_op jit(solution)/shard_map/ppermute | solution.py:57
  48.8 3.7 %collective-permute-start.11 = (bf16[512,256]{1,0:T(8,128)(2,1)S(1)}, bf16[512,256]{1,0:T(8,128)(2,1)S(1)}, u32[]{:S(2)}, u32[]{:S(2)}) collective-permute-start(bf16[512,256]{1,0:T(8,128)(2,1)S(1)} %shard_map.46.refs_14_), channel_id=1, source_target_pairs={{1,0},{0,1},{3,2},{2,3},{5,4},{4,5},{7,6},{6,7},{9,8},{8,9},{11,10... | collective-permute-start | bytes 786440 | tf_op jit(solution)/shard_map/ppermute | solution.py:57
  53.8 5.6 %collective-permute-start.12 = (bf16[272,256]{1,0:T(8,128)(2,1)S(1)}, bf16[272,256]{1,0:T(8,128)(2,1)S(1)}, u32[]{:S(2)}, u32[]{:S(2)}) collective-permute-start(bf16[272,256]{1,0:T(8,128)(2,1)S(1)} %get-tuple-element.56), channel_id=1, source_target_pairs={{8,0},{9,1},{10,2},{11,3},{12,4},{13,5},{14,6},{15,7},{0,8},{1,9},... | collective-permute-start | bytes 417800 | tf_op jit(solution)/shard_map/ppermute | solution.py:57
  55.4 7.0 %collective-permute-start.13 = (bf16[272,256]{1,0:T(8,128)(2,1)S(1)}, bf16[272,256]{1,0:T(8,128)(2,1)S(1)}, u32[]{:S(2)}, u32[]{:S(2)}) collective-permute-start(bf16[272,256]{1,0:T(8,128)(2,1)S(1)} %get-tuple-element.57), channel_id=1, source_target_pairs={{2,0},{3,1},{0,2},{1,3},{6,4},{7,5},{4,6},{5,7},{10,8},{11,9},{8,1... | collective-permute-start | bytes 417800 | tf_op jit(solution)/shard_map/ppermute | solution.py:57
  57.9 6.5 %collective-permute-start.14 = (bf16[272,256]{1,0:T(8,128)(2,1)S(1)}, bf16[272,256]{1,0:T(8,128)(2,1)S(1)}, u32[]{:S(2)}, u32[]{:S(2)}) collective-permute-start(bf16[272,256]{1,0:T(8,128)(2,1)S(1)} %get-tuple-element.58), channel_id=1, source_target_pairs={{10,0},{11,1},{8,2},{9,3},{14,4},{15,5},{12,6},{13,7},{2,8},{3,9},... | collective-permute-start | bytes 417800 | tf_op jit(solution)/shard_map/ppermute | solution.py:57
  64.5 8.3 %collective-permute-start.18 = (bf16[256,256]{1,0:T(8,128)(2,1)S(1)}, bf16[256,256]{1,0:T(8,128)(2,1)S(1)}, u32[]{:S(2)}, u32[]{:S(2)}) collective-permute-start(bf16[256,256]{1,0:T(8,128)(2,1)S(1)} %get-tuple-element.59.refs_5_), channel_id=1, source_target_pairs={{4,0},{5,1},{6,2},{7,3},{0,4},{1,5},{2,6},{3,7},{12,8},{13,9},{14,... | collective-permute-start | bytes 393224 | tf_op jit(solution)/shard_map/ppermute | solution.py:57
  65.4 9.4 %collective-permute-start.16 = (bf16[256,256]{1,0:T(8,128)(2,1)S(1)}, bf16[256,256]{1,0:T(8,128)(2,1)S(1)}, u32[]{:S(2)}, u32[]{:S(2)}) collective-permute-start(bf16[256,256]{1,0:T(8,128)(2,1)S(1)} %get-tuple-element.59.refs_5_), channel_id=1, source_target_pairs={{16,0},{17,1},{18,2},{19,3},{20,4},{21,5},{22,6},{23,7},{24,8},{25... | collective-permute-start | bytes 393224 | tf_op jit(solution)/shard_map/ppermute | solution.py:57
  72.8 5.0 %collective-permute-start.20 = (bf16[256,256]{1,0:T(8,128)(2,1)S(1)}, bf16[256,256]{1,0:T(8,128)(2,1)S(1)}, u32[]{:S(2)}, u32[]{:S(2)}) collective-permute-start(bf16[256,256]{1,0:T(8,128)(2,1)S(1)} %collective-permute-done.18.refs_9_), channel_id=1, source_target_pairs={{16,0},{17,1},{18,2},{19,3},{20,4},{21,5},{22,6},{23,7},{24,8},{25... | collective-permute-start | bytes 393224 | tf_op jit(solution)/shard_map/ppermute | solution.py:57
  74.3 3.4 %collective-permute-start.15 = (bf16[256,256]{1,0:T(8,128)(2,1)S(1)}, bf16[256,256]{1,0:T(8,128)(2,1)S(1)}, u32[]{:S(2)}, u32[]{:S(2)}) collective-permute-start(bf16[256,256]{1,0:T(8,128)(2,1)S(1)} %get-tuple-element.59.refs_5_), channel_id=1, source_target_pairs={{1,0},{0,1},{3,2},{2,3},{5,4},{4,5},{7,6},{6,7},{9,8},{8,9},{11,10... | collective-permute-start | bytes 393224 | tf_op jit(solution)/shard_map/ppermute | solution.py:57
  74.3 3.4 %collective-permute-start.19 = (bf16[256,256]{1,0:T(8,128)(2,1)S(1)}, bf16[256,256]{1,0:T(8,128)(2,1)S(1)}, u32[]{:S(2)}, u32[]{:S(2)}) collective-permute-start(bf16[256,256]{1,0:T(8,128)(2,1)S(1)} %collective-permute-done.18.refs_9_), channel_id=1, source_target_pairs={{1,0},{0,1},{3,2},{2,3},{5,4},{4,5},{7,6},{6,7},{9,8},{8,9},{11,10... | collective-permute-start | bytes 393224 | tf_op jit(solution)/shard_map/ppermute | solution.py:57
  74.8 2.9 %collective-permute-start.17 = (bf16[256,256]{1,0:T(8,128)(2,1)S(1)}, bf16[256,256]{1,0:T(8,128)(2,1)S(1)}, u32[]{:S(2)}, u32[]{:S(2)}) collective-permute-start(bf16[256,256]{1,0:T(8,128)(2,1)S(1)} %collective-permute-done.16.refs_7_), channel_id=1, source_target_pairs={{1,0},{0,1},{3,2},{2,3},{5,4},{4,5},{7,6},{6,7},{9,8},{8,9},{11,10... | collective-permute-start | bytes 393224 | tf_op jit(solution)/shard_map/ppermute | solution.py:57
  79.6 5.6 %collective-permute-start.22 = (bf16[256,256]{1,0:T(8,128)(2,1)S(1)}, bf16[256,256]{1,0:T(8,128)(2,1)S(1)}, u32[]{:S(2)}, u32[]{:S(2)}) collective-permute-start(bf16[256,256]{1,0:T(8,128)(2,1)S(1)} %get-tuple-element.62), channel_id=1, source_target_pairs={{8,0},{9,1},{10,2},{11,3},{12,4},{13,5},{14,6},{15,7},{0,8},{1,9},... | collective-permute-start | bytes 393224 | tf_op jit(solution)/shard_map/ppermute | solution.py:57
  81.2 6.4 %collective-permute-start.23 = (bf16[256,256]{1,0:T(8,128)(2,1)S(1)}, bf16[256,256]{1,0:T(8,128)(2,1)S(1)}, u32[]{:S(2)}, u32[]{:S(2)}) collective-permute-start(bf16[256,256]{1,0:T(8,128)(2,1)S(1)} %get-tuple-element.63), channel_id=1, source_target_pairs={{2,0},{3,1},{0,2},{1,3},{6,4},{7,5},{4,6},{5,7},{10,8},{11,9},{8,1... | collective-permute-start | bytes 393224 | tf_op jit(solution)/shard_map/ppermute | solution.py:57
  81.2 8.0 %collective-permute-start.24 = (bf16[256,256]{1,0:T(8,128)(2,1)S(1)}, bf16[256,256]{1,0:T(8,128)(2,1)S(1)}, u32[]{:S(2)}, u32[]{:S(2)}) collective-permute-start(bf16[256,256]{1,0:T(8,128)(2,1)S(1)} %get-tuple-element.64), channel_id=1, source_target_pairs={{10,0},{11,1},{8,2},{9,3},{14,4},{15,5},{12,6},{13,7},{2,8},{3,9},... | collective-permute-start | bytes 393224 | tf_op jit(solution)/shard_map/ppermute | solution.py:57
  (4 other events, 14.4 us)

commit v13 on v12

--- a/solution.py
+++ b/solution.py
@@ -291,13 +291,15 @@
 
 
 def spread_kernel(plan, nk, na, ns, *refs):
-    m, t_layout, rects, p_map, lo = plan
+    m, t_layout, rects, p_map, lo, chosen = plan
     kerns, refs = refs[:nk], refs[nk:]
     base, refs = (refs[0], refs[1:]) if lo else (None, refs)
     accs, refs = refs[:na], refs[na:]
     p_in, refs = refs[:ns], refs[ns:]
     outs, pcat = refs[:-1], refs[-1]
-    own_ref, other_refs = outs[0], outs[2:] if na else outs[1:]
+    owned = (2 if na else 1) if 0 in chosen else 0
+    own_ref = outs[0]
+    other_refs = dict(zip([p for p in chosen if p], outs[owned:]))
     c = pcat.shape[1]
     at = 0
     for index, start, rows, lane in p_map:
@@ -305,13 +307,16 @@
         at += rows
     row = 0
     for piece, start, rows in t_layout:
+        if piece not in chosen:
+            row += rows
+            continue
         part = row_sums(kerns, rects, pcat, row, rows, lo, lo + pcat.shape[0])
         if lo:
             part = part + base[row : row + rows, :]
         if piece == 0:
             own_ref[start : start + rows, :] = part
         else:
-            other_refs[piece - 1][start : start + rows, :] = part.astype(jnp.bfloat16)
+            other_refs[piece][start : start + rows, :] = part.astype(jnp.bfloat16)
         step = math.gcd(rows, BLOCK)
         for lane in range(0, rows if na else 0, step):
             total = None
@@ -331,19 +336,21 @@
                 index = lax.broadcasted_iota(jnp.int32, (16, step), 0)
                 terms = jnp.where(index == 0, high, jnp.where(index == 1, mid, low))
                 terms = jnp.where(index < 3, terms, 0.0)
-                other_refs[piece - 1][m:, lanes] = terms.astype(jnp.bfloat16)
+                other_refs[piece][m:, lanes] = terms.astype(jnp.bfloat16)
         row += rows
 
 
 def spread_call(kerns, accs, p_pieces, c, plan, base=()):
-    m, t_layout, rects, p_map, lo = plan
-    nt = 1 + max(piece for piece, _, _ in t_layout)
+    m, t_layout, rects, p_map, lo, chosen = plan
+    nt = len(chosen)
     cols = sum(rows for _, _, rows, _ in p_map)
     extra = 16 if accs else 0
-    outs = [jax.ShapeDtypeStruct((m, c), jnp.float32)]
-    if accs:
-        outs.append(jax.ShapeDtypeStruct((1, m), jnp.float32))
-    outs += [jax.ShapeDtypeStruct((m + extra, c), jnp.bfloat16)] * (nt - 1)
+    outs = []
+    if 0 in chosen:
+        outs.append(shape((m, c), jnp.float32))
+        if accs:
+            outs.append(shape((1, m), jnp.float32))
+    outs += [shape((m + extra, c)) for p in chosen if p]
     return pl.pallas_call(
         functools.partial(spread_kernel, plan, len(kerns), len(accs), len(p_pieces)),
         out_shape=outs,
@@ -504,7 +511,13 @@
         return near + far + fetch(far, "core") + far_y + fetch(far_y, "core")
 
     seeds = s_pieces[0] + seeds_zh + seeds_core
-    own, totals, *others = spread_call(kerns, accs, seeds, c, (*plan, seeds_map, 0))
+    over_x = tuple(i for i, o in enumerate(t_offsets) if o["x"])
+    along = tuple(i for i, o in enumerate(t_offsets) if not o["x"])
+    every = tuple(range(len(t_offsets)))
+    sent = spread_call(kerns, accs, seeds, c, (*plan, seeds_map, 0, over_x))
+    own, totals, *rest = spread_call(kerns, accs, seeds, c, (*plan, seeds_map, 0, along))
+    by_piece = dict(zip(over_x + along[1:], list(sent) + rest))
+    others = [by_piece[i] for i in every[1:]]
     panel, totals = update(
         first_update_kernel,
         held,
@@ -520,7 +533,7 @@
     first = len(groups[0]) + len(groups[1])
     base = base_call(kerns, pieces[:first], t_layout, rects)
     rest = [(i, 0, m, 0) for i in range(len(pieces) - first)]
-    own, *others = spread_call(kerns, [], pieces[first:], c, (*plan, rest, first * m), [base])
+    own, *others = spread_call(kerns, [], pieces[first:], c, (*plan, rest, first * m, every), [base])
     return update(
         last_update_kernel,
         held,

time: 90.2 us -> 90 us (level)
    pallas_call x2 -> x3, Pallas kernels: 1.71 us -> 1.9 us  [spread_call(): pl.pallas_call(functools.partial(spread_kernel, plan, len(kerns), len(acc...]
  transfers between devices with their start and end apart: 25 -> 25, of which waited for: 13 -> 12; matrix products, arithmetic and copies ran while one was open for 0% -> 0% of each run, Pallas kernels for 10% -> 11%
where the time goes in v13:
time: 90 us; the launch traced here: 89.8 us
  waiting for transfers between devices  49.1 us (55%)
  starting transfers between devices  26.4 us (29%)
  Pallas kernels  12 us (13%)
  local copies, waits for them, and re-layouts  1.97 us (2%)
    ppermute x25, waiting for transfers between devices, fetch(): return lax.ppermute(value, AXES, pairs)  49.1 us
    ppermute x25, starting transfers between devices, fetch(): return lax.ppermute(value, AXES, pairs)  26.4 us
    pallas_call x5, Pallas kernels, gram_call(): pl.pallas_call(functools.partial(gram_kernel, len(t_pieces), len(s_pieces...  6.95 us
    unnamed x6, local copies, waits for them, and re-layouts  1.97 us
    pallas_call x3, Pallas kernels, spread_call(): pl.pallas_call(functools.partial(spread_kernel, plan, len(kerns), len(acc...  1.9 us
  transfers between devices with their start and end apart: 25, of which 12 were waited for; matrix products, arithmetic and copies ran while one was open for 0% of the time, Pallas kernels for 11%

profile of v13, /device:TPU:0, one launch (start us, length us, event | category | flops | bytes accessed | tf_op | source)
XLA Modules:
  0.0 89.8 jit_solution(336086580980810434)
XLA Ops:
  1.4 4.1 %collective-permute-start = (bf16[256,1152]{1,0:T(8,128)(2,1)S(1)}, bf16[256,1152]{1,0:T(8,128)(2,1)S(1)}, u32[]{:S(2)}, u32[]{:S(2)}) collective-permute-start(bf16[256,1152]{1,0:T(8,128)(2,1)S(1)} %shard_map.38.unit_ref.refs_0_), channel_id=1, source_target_pairs={{4,0},{5,1},{6,2},{7,3},{0,4},{1,5},{2,6},{3,7},{12,8},{13,9},{14,... | collective-permute-start | bytes 1769480 | tf_op jit(solution)/shard_map/ppermute | solution.py:57
  5.5 1.6 %collective-permute-start.2 = (bf16[256,1152]{1,0:T(8,128)(2,1)S(1)}, bf16[256,1152]{1,0:T(8,128)(2,1)S(1)}, u32[]{:S(2)}, u32[]{:S(2)}) collective-permute-start(bf16[256,1152]{1,0:T(8,128)(2,1)S(1)} %shard_map.38.unit_ref.refs_0_), channel_id=1, source_target_pairs={{2,0},{3,1},{0,2},{1,3},{6,4},{7,5},{4,6},{5,7},{10,8},{11,9},{8,1... | collective-permute-start | bytes 1769480 | tf_op jit(solution)/shard_map/ppermute | solution.py:57
  7.1 1.5 %collective-permute-start.1 = (bf16[256,1152]{1,0:T(8,128)(2,1)S(1)}, bf16[256,1152]{1,0:T(8,128)(2,1)S(1)}, u32[]{:S(2)}, u32[]{:S(2)}) collective-permute-start(bf16[256,1152]{1,0:T(8,128)(2,1)S(1)} %shard_map.38.unit_ref.refs_0_), channel_id=1, source_target_pairs={{8,0},{9,1},{10,2},{11,3},{12,4},{13,5},{14,6},{15,7},{0,8},{1,9},... | collective-permute-start | bytes 1769480 | tf_op jit(solution)/shard_map/ppermute | solution.py:57
  9.5 1.6 %collective-permute-start.4 = (bf16[256,1408]{1,0:T(8,128)(2,1)S(1)}, bf16[256,1408]{1,0:T(8,128)(2,1)S(1)}, u32[]{:S(2)}, u32[]{:S(2)}) collective-permute-start(bf16[256,1408]{1,0:T(8,128)(2,1)S(1)} %shard_map.40.refs_3_.refs_1_.refs_10_), channel_id=1, source_target_pairs={{16,0},{17,1},{18,2},{19,3},{20,4},{21,5},{22,6},{23,7},{24,8},{25... | collective-permute-start | bytes 2162696 | tf_op jit(solution)/shard_map/ppermute | solution.py:57
  12.0 19.5 %collective-permute-done.refs_3_.refs_5_ = bf16[256,1152]{1,0:T(8,128)(2,1)S(1)} collective-permute-done((bf16[256,1152]{1,0:T(8,128)(2,1)S(1)}, bf16[256,1152]{1,0:T(8,128)(2,1)S(1)}, u32[]{:S(2)}, u32[]{:S(2)}) %collective-permute-start) | collective-permute-done | bytes 589856 | tf_op jit(solution)/shard_map/ppermute | solution.py:57
  32.4 1.4 %collective-permute-start.9 = (bf16[512,256]{1,0:T(8,128)(2,1)S(1)}, bf16[512,256]{1,0:T(8,128)(2,1)S(1)}, u32[]{:S(2)}, u32[]{:S(2)}) collective-permute-start(bf16[512,256]{1,0:T(8,128)(2,1)S(1)} %shard_map.45), channel_id=1, source_target_pairs={{4,0},{5,1},{6,2},{7,3},{0,4},{1,5},{2,6},{3,7},{12,8},{13,9},{14,... | collective-permute-start | bytes 786440 | tf_op jit(solution)/shard_map/ppermute | solution.py:57
  33.8 1.5 %collective-permute-start.8 = (bf16[256,1152]{1,0:T(8,128)(2,1)S(1)}, bf16[256,1152]{1,0:T(8,128)(2,1)S(1)}, u32[]{:S(2)}, u32[]{:S(2)}) collective-permute-start(bf16[256,1152]{1,0:T(8,128)(2,1)S(1)} %collective-permute-done.refs_3_.refs_5_), channel_id=1, source_target_pairs={{16,0},{17,1},{18,2},{19,3},{20,4},{21,5},{22,6},{23,7},{24,8},{25... | collective-permute-start | bytes 1769480 | tf_op jit(solution)/shard_map/ppermute | solution.py:57
  35.3 1.5 %collective-permute-start.7 = (bf16[256,1152]{1,0:T(8,128)(2,1)S(1)}, bf16[256,1152]{1,0:T(8,128)(2,1)S(1)}, u32[]{:S(2)}, u32[]{:S(2)}) collective-permute-start(bf16[256,1152]{1,0:T(8,128)(2,1)S(1)} %collective-permute-done.2.refs_2_), channel_id=1, source_target_pairs={{8,0},{9,1},{10,2},{11,3},{12,4},{13,5},{14,6},{15,7},{0,8},{1,9},... | collective-permute-start | bytes 1769480 | tf_op jit(solution)/shard_map/ppermute | solution.py:57
  38.2 2.4 %shard_map.41 = (bf16[768,1024]{1,0:T(8,128)(2,1)S(1)}, f32[768,128]{1,0:T(8,128)S(1)}) custom-call(s32[8,2048]{1,0:T(8,128)S(1)} %shard_map.37.flags, bf16[256,1152]{1,0:T(8,128)(2,1)S(1)} %shard_map.38.unit_ref.refs_0_, bf16[256,1152]{1,0:T(8,128)(2,1)S(1)} %collective-permute-done.1.refs_1_, bf16[256,1152]{1,0:T(8,128)(2,1)S(1)} %collective-permute-done.2.refs_2_, ...), custom_call_target="tpu_custom_call" | custom-call | flops 1811939328 | bytes 4128768 | tf_op jit(solution)/shard_map/pallas_call | solution.py:233
  40.6 6.6 %collective-permute-done.9.seed_ref = bf16[512,256]{1,0:T(8,128)(2,1)S(1)} collective-permute-done((bf16[512,256]{1,0:T(8,128)(2,1)S(1)}, bf16[512,256]{1,0:T(8,128)(2,1)S(1)}, u32[]{:S(2)}, u32[]{:S(2)}) %collective-permute-start.9) | collective-permute-done | bytes 262176 | tf_op jit(solution)/shard_map/ppermute | solution.py:57
  47.3 1.6 %collective-permute-done.8.refs_7_.refs_3_ = bf16[256,1152]{1,0:T(8,128)(2,1)S(1)} collective-permute-done((bf16[256,1152]{1,0:T(8,128)(2,1)S(1)}, bf16[256,1152]{1,0:T(8,128)(2,1)S(1)}, u32[]{:S(2)}, u32[]{:S(2)}) %collective-permute-start.8) | collective-permute-done | bytes 589856 | tf_op jit(solution)/shard_map/ppermute | solution.py:57
  50.1 1.5 %shard_map.43 = (bf16[256,1792]{1,0:T(8,128)(2,1)S(1)}, f32[256,128]{1,0:T(8,128)S(1)}) custom-call(s32[8,2048]{1,0:T(8,128)S(1)} %shard_map.37.flags, bf16[256,1152]{1,0:T(8,128)(2,1)S(1)} %collective-permute-done.7.refs_0_.refs_3_, bf16[256,1408]{1,0:T(8,128)(2,1)S(1)} %shard_map.40.refs_3_.refs_1_.refs_10_, ...), custom_call_target="tpu_custom_call" | custom-call | flops 1056964608 | bytes 4718592 | tf_op jit(solution)/shard_map/pallas_call | solution.py:233
  53.3 1.6 %collective-permute-start.12 = (bf16[272,256]{1,0:T(8,128)(2,1)S(1)}, bf16[272,256]{1,0:T(8,128)(2,1)S(1)}, u32[]{:S(2)}, u32[]{:S(2)}) collective-permute-start(bf16[272,256]{1,0:T(8,128)(2,1)S(1)} %get-tuple-element.56), channel_id=1, source_target_pairs={{8,0},{9,1},{10,2},{11,3},{12,4},{13,5},{14,6},{15,7},{0,8},{1,9},... | collective-permute-start | bytes 417800 | tf_op jit(solution)/shard_map/ppermute | solution.py:57
  54.9 2.4 %collective-permute-start.14 = (bf16[272,256]{1,0:T(8,128)(2,1)S(1)}, bf16[272,256]{1,0:T(8,128)(2,1)S(1)}, u32[]{:S(2)}, u32[]{:S(2)}) collective-permute-start(bf16[272,256]{1,0:T(8,128)(2,1)S(1)} %get-tuple-element.58), channel_id=1, source_target_pairs={{10,0},{11,1},{8,2},{9,3},{14,4},{15,5},{12,6},{13,7},{2,8},{3,9},... | collective-permute-start | bytes 417800 | tf_op jit(solution)/shard_map/ppermute | solution.py:57
  58.2 3.8 %collective-permute-done.12.refs_0_ = bf16[272,256]{1,0:T(8,128)(2,1)S(1)} collective-permute-done((bf16[272,256]{1,0:T(8,128)(2,1)S(1)}, bf16[272,256]{1,0:T(8,128)(2,1)S(1)}, u32[]{:S(2)}, u32[]{:S(2)}) %collective-permute-start.12) | collective-permute-done | bytes 139296 | tf_op jit(solution)/shard_map/ppermute | solution.py:57
  62.0 2.0 %collective-permute-done.13.refs_1_ = bf16[272,256]{1,0:T(8,128)(2,1)S(1)} collective-permute-done((bf16[272,256]{1,0:T(8,128)(2,1)S(1)}, bf16[272,256]{1,0:T(8,128)(2,1)S(1)}, u32[]{:S(2)}, u32[]{:S(2)}) %collective-permute-start.13) | collective-permute-done | bytes 139296 | tf_op jit(solution)/shard_map/ppermute | solution.py:57
  65.0 1.6 %collective-permute-start.16 = (bf16[256,256]{1,0:T(8,128)(2,1)S(1)}, bf16[256,256]{1,0:T(8,128)(2,1)S(1)}, u32[]{:S(2)}, u32[]{:S(2)}) collective-permute-start(bf16[256,256]{1,0:T(8,128)(2,1)S(1)} %get-tuple-element.59.refs_5_), channel_id=1, source_target_pairs={{16,0},{17,1},{18,2},{19,3},{20,4},{21,5},{22,6},{23,7},{24,8},{25... | collective-permute-start | bytes 393224 | tf_op jit(solution)/shard_map/ppermute | solution.py:57
  66.5 6.1 %collective-permute-done.18.refs_9_ = bf16[256,256]{1,0:T(8,128)(2,1)S(1)} collective-permute-done((bf16[256,256]{1,0:T(8,128)(2,1)S(1)}, bf16[256,256]{1,0:T(8,128)(2,1)S(1)}, u32[]{:S(2)}, u32[]{:S(2)}) %collective-permute-start.18) | collective-permute-done | bytes 131104 | tf_op jit(solution)/shard_map/ppermute | solution.py:57
  72.6 1.5 %collective-permute-start.20 = (bf16[256,256]{1,0:T(8,128)(2,1)S(1)}, bf16[256,256]{1,0:T(8,128)(2,1)S(1)}, u32[]{:S(2)}, u32[]{:S(2)}) collective-permute-start(bf16[256,256]{1,0:T(8,128)(2,1)S(1)} %collective-permute-done.18.refs_9_), channel_id=1, source_target_pairs={{16,0},{17,1},{18,2},{19,3},{20,4},{21,5},{22,6},{23,7},{24,8},{25... | collective-permute-start | bytes 393224 | tf_op jit(solution)/shard_map/ppermute | solution.py:57
  74.7 2.9 %collective-permute-done.20.refs_6_ = bf16[256,256]{1,0:T(8,128)(2,1)S(1)} collective-permute-done((bf16[256,256]{1,0:T(8,128)(2,1)S(1)}, bf16[256,256]{1,0:T(8,128)(2,1)S(1)}, u32[]{:S(2)}, u32[]{:S(2)}) %collective-permute-start.20) | collective-permute-done | bytes 131104 | tf_op jit(solution)/shard_map/ppermute | solution.py:57
  80.2 2.7 %collective-permute-start.24 = (bf16[256,256]{1,0:T(8,128)(2,1)S(1)}, bf16[256,256]{1,0:T(8,128)(2,1)S(1)}, u32[]{:S(2)}, u32[]{:S(2)}) collective-permute-start(bf16[256,256]{1,0:T(8,128)(2,1)S(1)} %get-tuple-element.64), channel_id=1, source_target_pairs={{10,0},{11,1},{8,2},{9,3},{14,4},{15,5},{12,6},{13,7},{2,8},{3,9},... | collective-permute-start | bytes 393224 | tf_op jit(solution)/shard_map/ppermute | solution.py:57
  82.9 2.1 %collective-permute-done.22.refs_0_ = bf16[256,256]{1,0:T(8,128)(2,1)S(1)} collective-permute-done((bf16[256,256]{1,0:T(8,128)(2,1)S(1)}, bf16[256,256]{1,0:T(8,128)(2,1)S(1)}, u32[]{:S(2)}, u32[]{:S(2)}) %collective-permute-start.22) | collective-permute-done | bytes 131104 | tf_op jit(solution)/shard_map/ppermute | solution.py:57
  85.0 1.6 %collective-permute-done.23.refs_1_ = bf16[256,256]{1,0:T(8,128)(2,1)S(1)} collective-permute-done((bf16[256,256]{1,0:T(8,128)(2,1)S(1)}, bf16[256,256]{1,0:T(8,128)(2,1)S(1)}, u32[]{:S(2)}, u32[]{:S(2)}) %collective-permute-start.23) | collective-permute-done | bytes 131104 | tf_op jit(solution)/shard_map/ppermute | solution.py:57
  86.6 2.4 %collective-permute-done.24.refs_2_ = bf16[256,256]{1,0:T(8,128)(2,1)S(1)} collective-permute-done((bf16[256,256]{1,0:T(8,128)(2,1)S(1)}, bf16[256,256]{1,0:T(8,128)(2,1)S(1)}, u32[]{:S(2)}, u32[]{:S(2)}) %collective-permute-start.24) | collective-permute-done | bytes 131104 | tf_op jit(solution)/shard_map/ppermute | solution.py:57
  (50 shorter events, 14.1 us)
Async XLA Ops:
  1.4 30.2 %collective-permute-start = (bf16[256,1152]{1,0:T(8,128)(2,1)S(1)}, bf16[256,1152]{1,0:T(8,128)(2,1)S(1)}, u32[]{:S(2)}, u32[]{:S(2)}) collective-permute-start(bf16[256,1152]{1,0:T(8,128)(2,1)S(1)} %shard_map.38.unit_ref.refs_0_), channel_id=1, source_target_pairs={{4,0},{5,1},{6,2},{7,3},{0,4},{1,5},{2,6},{3,7},{12,8},{13,9},{14,... | collective-permute-start | bytes 1769480 | tf_op jit(solution)/shard_map/ppermute | solution.py:57
  5.5 26.3 %collective-permute-start.2 = (bf16[256,1152]{1,0:T(8,128)(2,1)S(1)}, bf16[256,1152]{1,0:T(8,128)(2,1)S(1)}, u32[]{:S(2)}, u32[]{:S(2)}) collective-permute-start(bf16[256,1152]{1,0:T(8,128)(2,1)S(1)} %shard_map.38.unit_ref.refs_0_), channel_id=1, source_target_pairs={{2,0},{3,1},{0,2},{1,3},{6,4},{7,5},{4,6},{5,7},{10,8},{11,9},{8,1... | collective-permute-start | bytes 1769480 | tf_op jit(solution)/shard_map/ppermute | solution.py:57
  7.1 24.7 %collective-permute-start.1 = (bf16[256,1152]{1,0:T(8,128)(2,1)S(1)}, bf16[256,1152]{1,0:T(8,128)(2,1)S(1)}, u32[]{:S(2)}, u32[]{:S(2)}) collective-permute-start(bf16[256,1152]{1,0:T(8,128)(2,1)S(1)} %shard_map.38.unit_ref.refs_0_), channel_id=1, source_target_pairs={{8,0},{9,1},{10,2},{11,3},{12,4},{13,5},{14,6},{15,7},{0,8},{1,9},... | collective-permute-start | bytes 1769480 | tf_op jit(solution)/shard_map/ppermute | solution.py:57
  9.5 22.2 %collective-permute-start.4 = (bf16[256,1408]{1,0:T(8,128)(2,1)S(1)}, bf16[256,1408]{1,0:T(8,128)(2,1)S(1)}, u32[]{:S(2)}, u32[]{:S(2)}) collective-permute-start(bf16[256,1408]{1,0:T(8,128)(2,1)S(1)} %shard_map.40.refs_3_.refs_1_.refs_10_), channel_id=1, source_target_pairs={{16,0},{17,1},{18,2},{19,3},{20,4},{21,5},{22,6},{23,7},{24,8},{25... | collective-permute-start | bytes 2162696 | tf_op jit(solution)/shard_map/ppermute | solution.py:57
  11.1 20.7 %collective-permute-start.3 = (bf16[256,1408]{1,0:T(8,128)(2,1)S(1)}, bf16[256,1408]{1,0:T(8,128)(2,1)S(1)}, u32[]{:S(2)}, u32[]{:S(2)}) collective-permute-start(bf16[256,1408]{1,0:T(8,128)(2,1)S(1)} %shard_map.40.refs_3_.refs_1_.refs_10_), channel_id=1, source_target_pairs={{1,0},{0,1},{3,2},{2,3},{5,4},{4,5},{7,6},{6,7},{9,8},{8,9},{11,10... | collective-permute-start | bytes 2162696 | tf_op jit(solution)/shard_map/ppermute | solution.py:57
  31.8 6.4 %collective-permute-start.5 = (bf16[256,1408]{1,0:T(8,128)(2,1)S(1)}, bf16[256,1408]{1,0:T(8,128)(2,1)S(1)}, u32[]{:S(2)}, u32[]{:S(2)}) collective-permute-start(bf16[256,1408]{1,0:T(8,128)(2,1)S(1)} %collective-permute-done.4.refs_5_.refs_3_.refs_0_.refs_12_), channel_id=1, source_target_pairs={{1,0},{0,1},{3,2},{2,3},{5,4},{4,5},{7,6},{6,7},{9,8},{8,9},{11,10... | collective-permute-start | bytes 2162696 | tf_op jit(solution)/shard_map/ppermute | solution.py:57
  31.8 5.0 %collective-permute-start.6 = (bf16[256,1152]{1,0:T(8,128)(2,1)S(1)}, bf16[256,1152]{1,0:T(8,128)(2,1)S(1)}, u32[]{:S(2)}, u32[]{:S(2)}) collective-permute-start(bf16[256,1152]{1,0:T(8,128)(2,1)S(1)} %collective-permute-done.refs_3_.refs_5_), channel_id=1, source_target_pairs={{1,0},{0,1},{3,2},{2,3},{5,4},{4,5},{7,6},{6,7},{9,8},{8,9},{11,10... | collective-permute-start | bytes 1769480 | tf_op jit(solution)/shard_map/ppermute | solution.py:57
  32.4 14.9 %collective-permute-start.9 = (bf16[512,256]{1,0:T(8,128)(2,1)S(1)}, bf16[512,256]{1,0:T(8,128)(2,1)S(1)}, u32[]{:S(2)}, u32[]{:S(2)}) collective-permute-start(bf16[512,256]{1,0:T(8,128)(2,1)S(1)} %shard_map.45), channel_id=1, source_target_pairs={{4,0},{5,1},{6,2},{7,3},{0,4},{1,5},{2,6},{3,7},{12,8},{13,9},{14,... | collective-permute-start | bytes 786440 | tf_op jit(solution)/shard_map/ppermute | solution.py:57
  33.8 15.0 %collective-permute-start.8 = (bf16[256,1152]{1,0:T(8,128)(2,1)S(1)}, bf16[256,1152]{1,0:T(8,128)(2,1)S(1)}, u32[]{:S(2)}, u32[]{:S(2)}) collective-permute-start(bf16[256,1152]{1,0:T(8,128)(2,1)S(1)} %collective-permute-done.refs_3_.refs_5_), channel_id=1, source_target_pairs={{16,0},{17,1},{18,2},{19,3},{20,4},{21,5},{22,6},{23,7},{24,8},{25... | collective-permute-start | bytes 1769480 | tf_op jit(solution)/shard_map/ppermute | solution.py:57
  35.3 14.8 %collective-permute-start.7 = (bf16[256,1152]{1,0:T(8,128)(2,1)S(1)}, bf16[256,1152]{1,0:T(8,128)(2,1)S(1)}, u32[]{:S(2)}, u32[]{:S(2)}) collective-permute-start(bf16[256,1152]{1,0:T(8,128)(2,1)S(1)} %collective-permute-done.2.refs_2_), channel_id=1, source_target_pairs={{8,0},{9,1},{10,2},{11,3},{12,4},{13,5},{14,6},{15,7},{0,8},{1,9},... | collective-permute-start | bytes 1769480 | tf_op jit(solution)/shard_map/ppermute | solution.py:57
  48.8 2.8 %collective-permute-start.10 = (bf16[256,1152]{1,0:T(8,128)(2,1)S(1)}, bf16[256,1152]{1,0:T(8,128)(2,1)S(1)}, u32[]{:S(2)}, u32[]{:S(2)}) collective-permute-start(bf16[256,1152]{1,0:T(8,128)(2,1)S(1)} %collective-permute-done.8.refs_7_.refs_3_), channel_id=1, source_target_pairs={{1,0},{0,1},{3,2},{2,3},{5,4},{4,5},{7,6},{6,7},{9,8},{8,9},{11,10... | collective-permute-start | bytes 1769480 | tf_op jit(solution)/shard_map/ppermute | solution.py:57
  48.8 3.8 %collective-permute-start.11 = (bf16[512,256]{1,0:T(8,128)(2,1)S(1)}, bf16[512,256]{1,0:T(8,128)(2,1)S(1)}, u32[]{:S(2)}, u32[]{:S(2)}) collective-permute-start(bf16[512,256]{1,0:T(8,128)(2,1)S(1)} %shard_map.46.refs_14_), channel_id=1, source_target_pairs={{1,0},{0,1},{3,2},{2,3},{5,4},{4,5},{7,6},{6,7},{9,8},{8,9},{11,10... | collective-permute-start | bytes 786440 | tf_op jit(solution)/shard_map/ppermute | solution.py:57
  53.3 8.6 %collective-permute-start.12 = (bf16[272,256]{1,0:T(8,128)(2,1)S(1)}, bf16[272,256]{1,0:T(8,128)(2,1)S(1)}, u32[]{:S(2)}, u32[]{:S(2)}) collective-permute-start(bf16[272,256]{1,0:T(8,128)(2,1)S(1)} %get-tuple-element.56), channel_id=1, source_target_pairs={{8,0},{9,1},{10,2},{11,3},{12,4},{13,5},{14,6},{15,7},{0,8},{1,9},... | collective-permute-start | bytes 417800 | tf_op jit(solution)/shard_map/ppermute | solution.py:57
  54.9 7.1 %collective-permute-start.14 = (bf16[272,256]{1,0:T(8,128)(2,1)S(1)}, bf16[272,256]{1,0:T(8,128)(2,1)S(1)}, u32[]{:S(2)}, u32[]{:S(2)}) collective-permute-start(bf16[272,256]{1,0:T(8,128)(2,1)S(1)} %get-tuple-element.58), channel_id=1, source_target_pairs={{10,0},{11,1},{8,2},{9,3},{14,4},{15,5},{12,6},{13,7},{2,8},{3,9},... | collective-permute-start | bytes 417800 | tf_op jit(solution)/shard_map/ppermute | solution.py:57
  58.1 5.9 %collective-permute-start.13 = (bf16[272,256]{1,0:T(8,128)(2,1)S(1)}, bf16[272,256]{1,0:T(8,128)(2,1)S(1)}, u32[]{:S(2)}, u32[]{:S(2)}) collective-permute-start(bf16[272,256]{1,0:T(8,128)(2,1)S(1)} %get-tuple-element.57), channel_id=1, source_target_pairs={{2,0},{3,1},{0,2},{1,3},{6,4},{7,5},{4,6},{5,7},{10,8},{11,9},{8,1... | collective-permute-start | bytes 417800 | tf_op jit(solution)/shard_map/ppermute | solution.py:57
  64.1 8.5 %collective-permute-start.18 = (bf16[256,256]{1,0:T(8,128)(2,1)S(1)}, bf16[256,256]{1,0:T(8,128)(2,1)S(1)}, u32[]{:S(2)}, u32[]{:S(2)}) collective-permute-start(bf16[256,256]{1,0:T(8,128)(2,1)S(1)} %get-tuple-element.59.refs_5_), channel_id=1, source_target_pairs={{4,0},{5,1},{6,2},{7,3},{0,4},{1,5},{2,6},{3,7},{12,8},{13,9},{14,... | collective-permute-start | bytes 393224 | tf_op jit(solution)/shard_map/ppermute | solution.py:57
  65.0 9.7 %collective-permute-start.16 = (bf16[256,256]{1,0:T(8,128)(2,1)S(1)}, bf16[256,256]{1,0:T(8,128)(2,1)S(1)}, u32[]{:S(2)}, u32[]{:S(2)}) collective-permute-start(bf16[256,256]{1,0:T(8,128)(2,1)S(1)} %get-tuple-element.59.refs_5_), channel_id=1, source_target_pairs={{16,0},{17,1},{18,2},{19,3},{20,4},{21,5},{22,6},{23,7},{24,8},{25... | collective-permute-start | bytes 393224 | tf_op jit(solution)/shard_map/ppermute | solution.py:57
  72.6 5.0 %collective-permute-start.20 = (bf16[256,256]{1,0:T(8,128)(2,1)S(1)}, bf16[256,256]{1,0:T(8,128)(2,1)S(1)}, u32[]{:S(2)}, u32[]{:S(2)}) collective-permute-start(bf16[256,256]{1,0:T(8,128)(2,1)S(1)} %collective-permute-done.18.refs_9_), channel_id=1, source_target_pairs={{16,0},{17,1},{18,2},{19,3},{20,4},{21,5},{22,6},{23,7},{24,8},{25... | collective-permute-start | bytes 393224 | tf_op jit(solution)/shard_map/ppermute | solution.py:57
  74.1 3.4 %collective-permute-start.15 = (bf16[256,256]{1,0:T(8,128)(2,1)S(1)}, bf16[256,256]{1,0:T(8,128)(2,1)S(1)}, u32[]{:S(2)}, u32[]{:S(2)}) collective-permute-start(bf16[256,256]{1,0:T(8,128)(2,1)S(1)} %get-tuple-element.59.refs_5_), channel_id=1, source_target_pairs={{1,0},{0,1},{3,2},{2,3},{5,4},{4,5},{7,6},{6,7},{9,8},{8,9},{11,10... | collective-permute-start | bytes 393224 | tf_op jit(solution)/shard_map/ppermute | solution.py:57
  74.2 3.4 %collective-permute-start.19 = (bf16[256,256]{1,0:T(8,128)(2,1)S(1)}, bf16[256,256]{1,0:T(8,128)(2,1)S(1)}, u32[]{:S(2)}, u32[]{:S(2)}) collective-permute-start(bf16[256,256]{1,0:T(8,128)(2,1)S(1)} %collective-permute-done.18.refs_9_), channel_id=1, source_target_pairs={{1,0},{0,1},{3,2},{2,3},{5,4},{4,5},{7,6},{6,7},{9,8},{8,9},{11,10... | collective-permute-start | bytes 393224 | tf_op jit(solution)/shard_map/ppermute | solution.py:57
  74.7 2.9 %collective-permute-start.17 = (bf16[256,256]{1,0:T(8,128)(2,1)S(1)}, bf16[256,256]{1,0:T(8,128)(2,1)S(1)}, u32[]{:S(2)}, u32[]{:S(2)}) collective-permute-start(bf16[256,256]{1,0:T(8,128)(2,1)S(1)} %collective-permute-done.16.refs_7_), channel_id=1, source_target_pairs={{1,0},{0,1},{3,2},{2,3},{5,4},{4,5},{7,6},{6,7},{9,8},{8,9},{11,10... | collective-permute-start | bytes 393224 | tf_op jit(solution)/shard_map/ppermute | solution.py:57
  79.4 5.6 %collective-permute-start.22 = (bf16[256,256]{1,0:T(8,128)(2,1)S(1)}, bf16[256,256]{1,0:T(8,128)(2,1)S(1)}, u32[]{:S(2)}, u32[]{:S(2)}) collective-permute-start(bf16[256,256]{1,0:T(8,128)(2,1)S(1)} %get-tuple-element.62), channel_id=1, source_target_pairs={{8,0},{9,1},{10,2},{11,3},{12,4},{13,5},{14,6},{15,7},{0,8},{1,9},... | collective-permute-start | bytes 393224 | tf_op jit(solution)/shard_map/ppermute | solution.py:57
  80.2 6.4 %collective-permute-start.23 = (bf16[256,256]{1,0:T(8,128)(2,1)S(1)}, bf16[256,256]{1,0:T(8,128)(2,1)S(1)}, u32[]{:S(2)}, u32[]{:S(2)}) collective-permute-start(bf16[256,256]{1,0:T(8,128)(2,1)S(1)} %get-tuple-element.63), channel_id=1, source_target_pairs={{2,0},{3,1},{0,2},{1,3},{6,4},{7,5},{4,6},{5,7},{10,8},{11,9},{8,1... | collective-permute-start | bytes 393224 | tf_op jit(solution)/shard_map/ppermute | solution.py:57
  80.2 8.8 %collective-permute-start.24 = (bf16[256,256]{1,0:T(8,128)(2,1)S(1)}, bf16[256,256]{1,0:T(8,128)(2,1)S(1)}, u32[]{:S(2)}, u32[]{:S(2)}) collective-permute-start(bf16[256,256]{1,0:T(8,128)(2,1)S(1)} %get-tuple-element.64), channel_id=1, source_target_pairs={{10,0},{11,1},{8,2},{9,3},{14,4},{15,5},{12,6},{13,7},{2,8},{3,9},... | collective-permute-start | bytes 393224 | tf_op jit(solution)/shard_map/ppermute | solution.py:57
  (4 other events, 14.4 us)

commit v14 on v13

--- a/solution.py
+++ b/solution.py
@@ -485,16 +485,17 @@
     t_pieces += [by_offset[t_offsets[i]["zl"], t_offsets[i]["x"]] for i in t_order]
     s_pieces[0] = [packed] + own_core + [p for v, w in zip(y, y_core) for p in [v] + w]
     s_pieces[1] = zh + zh_core
-    s_pieces[2] = zh_y
     early, last = len(near_t), len(t_order)
     gram = rectangle(0, early, 0, 1) + rectangle(0, early, 1, 2)
-    seeds_zh = [stack_seeds(after(v, *gram), [], 2 * 10**10) for v in seeds_zh]
-    done = zh_y + zh_core + gram + seeds_zh
+    done = zh_y + zh_core + gram
+    s_pieces[2] = [after(v, *gram) for v in zh_y]
     zh_y_core = fetch(zh_y, "core", *done)
     s_pieces[3] = zh_y_core
-    seeds_core = fetch(seeds_zh, "core", *done)
+    seeds_in = seeds_zh
+    gram = rectangle(0, early, 2, 3)
+    seeds_zh = [stack_seeds(after(v, *gram), [], 2 * 10**10) for v in seeds_in]
+    seeds_core = fetch(seeds_zh, "core")
     rectangle(early, last, 0, 3)
-    rectangle(0, early, 2, 3)
     rectangle(0, last, 3, 4)
     plan = (m, t_layout, rects)
 

time: 90 us -> 88 us (0.978)
  waiting for transfers between devices: 49.1 us -> 47.4 us
    ppermute x25, waiting for transfers between devices: 49.1 us -> 47.4 us  [fetch(): return lax.ppermute(value, AXES, pairs)]
  transfers between devices with their start and end apart: 25 -> 25, of which waited for: 12 -> 14; matrix products, arithmetic and copies ran while one was open for 0% -> 0% of each run, Pallas kernels for 11% -> 11%
where the time goes in v14:
time: 88 us; the launch traced here: 87.9 us
  waiting for transfers between devices  47.4 us (54%)
  starting transfers between devices  26.3 us (30%)
  Pallas kernels  12 us (14%)
  local copies, waits for them, and re-layouts  1.97 us (2%)
    ppermute x25, waiting for transfers between devices, fetch(): return lax.ppermute(value, AXES, pairs)  47.4 us
    ppermute x25, starting transfers between devices, fetch(): return lax.ppermute(value, AXES, pairs)  26.3 us
    pallas_call x5, Pallas kernels, gram_call(): pl.pallas_call(functools.partial(gram_kernel, len(t_pieces), len(s_pieces...  6.9 us
    unnamed x6, local copies, waits for them, and re-layouts  1.97 us
    pallas_call x3, Pallas kernels, spread_call(): pl.pallas_call(functools.partial(spread_kernel, plan, len(kerns), len(acc...  1.91 us
  transfers between devices with their start and end apart: 25, of which 14 were waited for; matrix products, arithmetic and copies ran while one was open for 0% of the time, Pallas kernels for 11%

profile of v14, /device:TPU:0, one launch (start us, length us, event | category | flops | bytes accessed | tf_op | source)
XLA Modules:
  0.0 87.9 jit_solution(6711959661389539616)
XLA Ops:
  1.4 4.1 %collective-permute-start = (bf16[256,1152]{1,0:T(8,128)(2,1)S(1)}, bf16[256,1152]{1,0:T(8,128)(2,1)S(1)}, u32[]{:S(2)}, u32[]{:S(2)}) collective-permute-start(bf16[256,1152]{1,0:T(8,128)(2,1)S(1)} %shard_map.38.unit_ref.refs_0_), channel_id=1, source_target_pairs={{4,0},{5,1},{6,2},{7,3},{0,4},{1,5},{2,6},{3,7},{12,8},{13,9},{14,... | collective-permute-start | bytes 1769480 | tf_op jit(solution)/shard_map/ppermute | solution.py:57
  5.5 1.6 %collective-permute-start.2 = (bf16[256,1152]{1,0:T(8,128)(2,1)S(1)}, bf16[256,1152]{1,0:T(8,128)(2,1)S(1)}, u32[]{:S(2)}, u32[]{:S(2)}) collective-permute-start(bf16[256,1152]{1,0:T(8,128)(2,1)S(1)} %shard_map.38.unit_ref.refs_0_), channel_id=1, source_target_pairs={{2,0},{3,1},{0,2},{1,3},{6,4},{7,5},{4,6},{5,7},{10,8},{11,9},{8,1... | collective-permute-start | bytes 1769480 | tf_op jit(solution)/shard_map/ppermute | solution.py:57
  7.1 1.5 %collective-permute-start.1 = (bf16[256,1152]{1,0:T(8,128)(2,1)S(1)}, bf16[256,1152]{1,0:T(8,128)(2,1)S(1)}, u32[]{:S(2)}, u32[]{:S(2)}) collective-permute-start(bf16[256,1152]{1,0:T(8,128)(2,1)S(1)} %shard_map.38.unit_ref.refs_0_), channel_id=1, source_target_pairs={{8,0},{9,1},{10,2},{11,3},{12,4},{13,5},{14,6},{15,7},{0,8},{1,9},... | collective-permute-start | bytes 1769480 | tf_op jit(solution)/shard_map/ppermute | solution.py:57
  9.5 1.6 %collective-permute-start.4 = (bf16[256,1408]{1,0:T(8,128)(2,1)S(1)}, bf16[256,1408]{1,0:T(8,128)(2,1)S(1)}, u32[]{:S(2)}, u32[]{:S(2)}) collective-permute-start(bf16[256,1408]{1,0:T(8,128)(2,1)S(1)} %shard_map.40.refs_3_.refs_1_.refs_10_), channel_id=1, source_target_pairs={{16,0},{17,1},{18,2},{19,3},{20,4},{21,5},{22,6},{23,7},{24,8},{25... | collective-permute-start | bytes 2162696 | tf_op jit(solution)/shard_map/ppermute | solution.py:57
  12.0 19.5 %collective-permute-done.refs_3_.refs_5_ = bf16[256,1152]{1,0:T(8,128)(2,1)S(1)} collective-permute-done((bf16[256,1152]{1,0:T(8,128)(2,1)S(1)}, bf16[256,1152]{1,0:T(8,128)(2,1)S(1)}, u32[]{:S(2)}, u32[]{:S(2)}) %collective-permute-start) | collective-permute-done | bytes 589856 | tf_op jit(solution)/shard_map/ppermute | solution.py:57
  32.3 1.6 %collective-permute-start.7 = (bf16[256,1152]{1,0:T(8,128)(2,1)S(1)}, bf16[256,1152]{1,0:T(8,128)(2,1)S(1)}, u32[]{:S(2)}, u32[]{:S(2)}) collective-permute-start(bf16[256,1152]{1,0:T(8,128)(2,1)S(1)} %collective-permute-done.refs_3_.refs_5_), channel_id=1, source_target_pairs={{16,0},{17,1},{18,2},{19,3},{20,4},{21,5},{22,6},{23,7},{24,8},{25... | collective-permute-start | bytes 1769480 | tf_op jit(solution)/shard_map/ppermute | solution.py:57
  33.9 1.4 %collective-permute-start.10 = (bf16[512,256]{1,0:T(8,128)(2,1)S(1)}, bf16[512,256]{1,0:T(8,128)(2,1)S(1)}, u32[]{:S(2)}, u32[]{:S(2)}) collective-permute-start(bf16[512,256]{1,0:T(8,128)(2,1)S(1)} %shard_map.46), channel_id=1, source_target_pairs={{4,0},{5,1},{6,2},{7,3},{0,4},{1,5},{2,6},{3,7},{12,8},{13,9},{14,... | collective-permute-start | bytes 786440 | tf_op jit(solution)/shard_map/ppermute | solution.py:57
  35.3 1.5 %collective-permute-start.8 = (bf16[256,1152]{1,0:T(8,128)(2,1)S(1)}, bf16[256,1152]{1,0:T(8,128)(2,1)S(1)}, u32[]{:S(2)}, u32[]{:S(2)}) collective-permute-start(bf16[256,1152]{1,0:T(8,128)(2,1)S(1)} %collective-permute-done.2.refs_2_), channel_id=1, source_target_pairs={{8,0},{9,1},{10,2},{11,3},{12,4},{13,5},{14,6},{15,7},{0,8},{1,9},... | collective-permute-start | bytes 1769480 | tf_op jit(solution)/shard_map/ppermute | solution.py:57
  36.8 1.3 %shard_map.42 = (bf16[768,512]{1,0:T(8,128)(2,1)S(1)}, f32[768,128]{1,0:T(8,128)S(1)}) custom-call(s32[8,2048]{1,0:T(8,128)S(1)} %shard_map.37.flags, bf16[256,1152]{1,0:T(8,128)(2,1)S(1)} %shard_map.38.unit_ref.refs_0_, bf16[256,1152]{1,0:T(8,128)(2,1)S(1)} %collective-permute-done.1.refs_1_, bf16[256,1152]{1,0:T(8,128)(2,1)S(1)} %collective-permute-done.2.refs_2_, ...), custom_call_target="tpu_custom_call" | custom-call | flops 905969664 | bytes 2949120 | tf_op jit(solution)/shard_map/pallas_call | solution.py:233
  38.2 2.4 %shard_map.41 = (bf16[768,1024]{1,0:T(8,128)(2,1)S(1)}, f32[768,128]{1,0:T(8,128)S(1)}) custom-call(s32[8,2048]{1,0:T(8,128)S(1)} %shard_map.37.flags, bf16[256,1152]{1,0:T(8,128)(2,1)S(1)} %shard_map.38.unit_ref.refs_0_, bf16[256,1152]{1,0:T(8,128)(2,1)S(1)} %collective-permute-done.1.refs_1_, bf16[256,1152]{1,0:T(8,128)(2,1)S(1)} %collective-permute-done.2.refs_2_, ...), custom_call_target="tpu_custom_call" | custom-call | flops 1811939328 | bytes 4128768 | tf_op jit(solution)/shard_map/pallas_call | solution.py:233
  40.6 7.1 %collective-permute-done.7.refs_3_.refs_7_ = bf16[256,1152]{1,0:T(8,128)(2,1)S(1)} collective-permute-done((bf16[256,1152]{1,0:T(8,128)(2,1)S(1)}, bf16[256,1152]{1,0:T(8,128)(2,1)S(1)}, u32[]{:S(2)}, u32[]{:S(2)}) %collective-permute-start.7) | collective-permute-done | bytes 589856 | tf_op jit(solution)/shard_map/ppermute | solution.py:57
  50.1 1.5 %shard_map.44 = (bf16[256,1792]{1,0:T(8,128)(2,1)S(1)}, f32[256,128]{1,0:T(8,128)S(1)}) custom-call(s32[8,2048]{1,0:T(8,128)S(1)} %shard_map.37.flags, bf16[256,1152]{1,0:T(8,128)(2,1)S(1)} %collective-permute-done.8.refs_0_.refs_3_, bf16[256,1408]{1,0:T(8,128)(2,1)S(1)} %shard_map.40.refs_3_.refs_1_.refs_10_, ...), custom_call_target="tpu_custom_call" | custom-call | flops 1056964608 | bytes 4718592 | tf_op jit(solution)/shard_map/pallas_call | solution.py:233
  53.3 1.6 %collective-permute-start.12 = (bf16[272,256]{1,0:T(8,128)(2,1)S(1)}, bf16[272,256]{1,0:T(8,128)(2,1)S(1)}, u32[]{:S(2)}, u32[]{:S(2)}) collective-permute-start(bf16[272,256]{1,0:T(8,128)(2,1)S(1)} %get-tuple-element.56), channel_id=1, source_target_pairs={{8,0},{9,1},{10,2},{11,3},{12,4},{13,5},{14,6},{15,7},{0,8},{1,9},... | collective-permute-start | bytes 417800 | tf_op jit(solution)/shard_map/ppermute | solution.py:57
  54.8 2.4 %collective-permute-start.14 = (bf16[272,256]{1,0:T(8,128)(2,1)S(1)}, bf16[272,256]{1,0:T(8,128)(2,1)S(1)}, u32[]{:S(2)}, u32[]{:S(2)}) collective-permute-start(bf16[272,256]{1,0:T(8,128)(2,1)S(1)} %get-tuple-element.58), channel_id=1, source_target_pairs={{10,0},{11,1},{8,2},{9,3},{14,4},{15,5},{12,6},{13,7},{2,8},{3,9},... | collective-permute-start | bytes 417800 | tf_op jit(solution)/shard_map/ppermute | solution.py:57
  58.1 2.7 %collective-permute-done.12.refs_0_ = bf16[272,256]{1,0:T(8,128)(2,1)S(1)} collective-permute-done((bf16[272,256]{1,0:T(8,128)(2,1)S(1)}, bf16[272,256]{1,0:T(8,128)(2,1)S(1)}, u32[]{:S(2)}, u32[]{:S(2)}) %collective-permute-start.12) | collective-permute-done | bytes 139296 | tf_op jit(solution)/shard_map/ppermute | solution.py:57
  63.3 1.3 %collective-permute-start.18 = (bf16[256,256]{1,0:T(8,128)(2,1)S(1)}, bf16[256,256]{1,0:T(8,128)(2,1)S(1)}, u32[]{:S(2)}, u32[]{:S(2)}) collective-permute-start(bf16[256,256]{1,0:T(8,128)(2,1)S(1)} %get-tuple-element.59.refs_5_), channel_id=1, source_target_pairs={{4,0},{5,1},{6,2},{7,3},{0,4},{1,5},{2,6},{3,7},{12,8},{13,9},{14,... | collective-permute-start | bytes 393224 | tf_op jit(solution)/shard_map/ppermute | solution.py:57
  64.6 1.3 %collective-permute-start.16 = (bf16[256,256]{1,0:T(8,128)(2,1)S(1)}, bf16[256,256]{1,0:T(8,128)(2,1)S(1)}, u32[]{:S(2)}, u32[]{:S(2)}) collective-permute-start(bf16[256,256]{1,0:T(8,128)(2,1)S(1)} %get-tuple-element.59.refs_5_), channel_id=1, source_target_pairs={{16,0},{17,1},{18,2},{19,3},{20,4},{21,5},{22,6},{23,7},{24,8},{25... | collective-permute-start | bytes 393224 | tf_op jit(solution)/shard_map/ppermute | solution.py:57
  66.0 4.7 %collective-permute-done.18.refs_9_ = bf16[256,256]{1,0:T(8,128)(2,1)S(1)} collective-permute-done((bf16[256,256]{1,0:T(8,128)(2,1)S(1)}, bf16[256,256]{1,0:T(8,128)(2,1)S(1)}, u32[]{:S(2)}, u32[]{:S(2)}) %collective-permute-start.18) | collective-permute-done | bytes 131104 | tf_op jit(solution)/shard_map/ppermute | solution.py:57
  72.4 3.2 %collective-permute-done.20.refs_6_ = bf16[256,256]{1,0:T(8,128)(2,1)S(1)} collective-permute-done((bf16[256,256]{1,0:T(8,128)(2,1)S(1)}, bf16[256,256]{1,0:T(8,128)(2,1)S(1)}, u32[]{:S(2)}, u32[]{:S(2)}) %collective-permute-start.20) | collective-permute-done | bytes 131104 | tf_op jit(solution)/shard_map/ppermute | solution.py:57
  77.4 1.6 %collective-permute-start.22 = (bf16[256,256]{1,0:T(8,128)(2,1)S(1)}, bf16[256,256]{1,0:T(8,128)(2,1)S(1)}, u32[]{:S(2)}, u32[]{:S(2)}) collective-permute-start(bf16[256,256]{1,0:T(8,128)(2,1)S(1)} %get-tuple-element.62), channel_id=1, source_target_pairs={{8,0},{9,1},{10,2},{11,3},{12,4},{13,5},{14,6},{15,7},{0,8},{1,9},... | collective-permute-start | bytes 393224 | tf_op jit(solution)/shard_map/ppermute | solution.py:57
  79.0 2.0 %collective-permute-start.24 = (bf16[256,256]{1,0:T(8,128)(2,1)S(1)}, bf16[256,256]{1,0:T(8,128)(2,1)S(1)}, u32[]{:S(2)}, u32[]{:S(2)}) collective-permute-start(bf16[256,256]{1,0:T(8,128)(2,1)S(1)} %get-tuple-element.64), channel_id=1, source_target_pairs={{10,0},{11,1},{8,2},{9,3},{14,4},{15,5},{12,6},{13,7},{2,8},{3,9},... | collective-permute-start | bytes 393224 | tf_op jit(solution)/shard_map/ppermute | solution.py:57
  81.0 2.1 %collective-permute-done.22.refs_0_ = bf16[256,256]{1,0:T(8,128)(2,1)S(1)} collective-permute-done((bf16[256,256]{1,0:T(8,128)(2,1)S(1)}, bf16[256,256]{1,0:T(8,128)(2,1)S(1)}, u32[]{:S(2)}, u32[]{:S(2)}) %collective-permute-start.22) | collective-permute-done | bytes 131104 | tf_op jit(solution)/shard_map/ppermute | solution.py:57
  83.1 2.3 %collective-permute-done.23.refs_1_ = bf16[256,256]{1,0:T(8,128)(2,1)S(1)} collective-permute-done((bf16[256,256]{1,0:T(8,128)(2,1)S(1)}, bf16[256,256]{1,0:T(8,128)(2,1)S(1)}, u32[]{:S(2)}, u32[]{:S(2)}) %collective-permute-start.23) | collective-permute-done | bytes 131104 | tf_op jit(solution)/shard_map/ppermute | solution.py:57
  85.4 1.7 %collective-permute-done.24.refs_2_ = bf16[256,256]{1,0:T(8,128)(2,1)S(1)} collective-permute-done((bf16[256,256]{1,0:T(8,128)(2,1)S(1)}, bf16[256,256]{1,0:T(8,128)(2,1)S(1)}, u32[]{:S(2)}, u32[]{:S(2)}) %collective-permute-start.24) | collective-permute-done | bytes 131104 | tf_op jit(solution)/shard_map/ppermute | solution.py:57
  (50 shorter events, 15.8 us)
Async XLA Ops:
  1.4 30.2 %collective-permute-start = (bf16[256,1152]{1,0:T(8,128)(2,1)S(1)}, bf16[256,1152]{1,0:T(8,128)(2,1)S(1)}, u32[]{:S(2)}, u32[]{:S(2)}) collective-permute-start(bf16[256,1152]{1,0:T(8,128)(2,1)S(1)} %shard_map.38.unit_ref.refs_0_), channel_id=1, source_target_pairs={{4,0},{5,1},{6,2},{7,3},{0,4},{1,5},{2,6},{3,7},{12,8},{13,9},{14,... | collective-permute-start | bytes 1769480 | tf_op jit(solution)/shard_map/ppermute | solution.py:57
  5.5 26.3 %collective-permute-start.2 = (bf16[256,1152]{1,0:T(8,128)(2,1)S(1)}, bf16[256,1152]{1,0:T(8,128)(2,1)S(1)}, u32[]{:S(2)}, u32[]{:S(2)}) collective-permute-start(bf16[256,1152]{1,0:T(8,128)(2,1)S(1)} %shard_map.38.unit_ref.refs_0_), channel_id=1, source_target_pairs={{2,0},{3,1},{0,2},{1,3},{6,4},{7,5},{4,6},{5,7},{10,8},{11,9},{8,1... | collective-permute-start | bytes 1769480 | tf_op jit(solution)/shard_map/ppermute | solution.py:57
  7.1 24.7 %collective-permute-start.1 = (bf16[256,1152]{1,0:T(8,128)(2,1)S(1)}, bf16[256,1152]{1,0:T(8,128)(2,1)S(1)}, u32[]{:S(2)}, u32[]{:S(2)}) collective-permute-start(bf16[256,1152]{1,0:T(8,128)(2,1)S(1)} %shard_map.38.unit_ref.refs_0_), channel_id=1, source_target_pairs={{8,0},{9,1},{10,2},{11,3},{12,4},{13,5},{14,6},{15,7},{0,8},{1,9},... | collective-permute-start | bytes 1769480 | tf_op jit(solution)/shard_map/ppermute | solution.py:57
  9.5 22.2 %collective-permute-start.4 = (bf16[256,1408]{1,0:T(8,128)(2,1)S(1)}, bf16[256,1408]{1,0:T(8,128)(2,1)S(1)}, u32[]{:S(2)}, u32[]{:S(2)}) collective-permute-start(bf16[256,1408]{1,0:T(8,128)(2,1)S(1)} %shard_map.40.refs_3_.refs_1_.refs_10_), channel_id=1, source_target_pairs={{16,0},{17,1},{18,2},{19,3},{20,4},{21,5},{22,6},{23,7},{24,8},{25... | collective-permute-start | bytes 2162696 | tf_op jit(solution)/shard_map/ppermute | solution.py:57
  11.1 20.7 %collective-permute-start.3 = (bf16[256,1408]{1,0:T(8,128)(2,1)S(1)}, bf16[256,1408]{1,0:T(8,128)(2,1)S(1)}, u32[]{:S(2)}, u32[]{:S(2)}) collective-permute-start(bf16[256,1408]{1,0:T(8,128)(2,1)S(1)} %shard_map.40.refs_3_.refs_1_.refs_10_), channel_id=1, source_target_pairs={{1,0},{0,1},{3,2},{2,3},{5,4},{4,5},{7,6},{6,7},{9,8},{8,9},{11,10... | collective-permute-start | bytes 2162696 | tf_op jit(solution)/shard_map/ppermute | solution.py:57
  31.8 6.4 %collective-permute-start.5 = (bf16[256,1408]{1,0:T(8,128)(2,1)S(1)}, bf16[256,1408]{1,0:T(8,128)(2,1)S(1)}, u32[]{:S(2)}, u32[]{:S(2)}) collective-permute-start(bf16[256,1408]{1,0:T(8,128)(2,1)S(1)} %collective-permute-done.4.refs_5_.refs_3_.refs_0_.refs_12_), channel_id=1, source_target_pairs={{1,0},{0,1},{3,2},{2,3},{5,4},{4,5},{7,6},{6,7},{9,8},{8,9},{11,10... | collective-permute-start | bytes 2162696 | tf_op jit(solution)/shard_map/ppermute | solution.py:57
  31.8 5.0 %collective-permute-start.6 = (bf16[256,1152]{1,0:T(8,128)(2,1)S(1)}, bf16[256,1152]{1,0:T(8,128)(2,1)S(1)}, u32[]{:S(2)}, u32[]{:S(2)}) collective-permute-start(bf16[256,1152]{1,0:T(8,128)(2,1)S(1)} %collective-permute-done.refs_3_.refs_5_), channel_id=1, source_target_pairs={{1,0},{0,1},{3,2},{2,3},{5,4},{4,5},{7,6},{6,7},{9,8},{8,9},{11,10... | collective-permute-start | bytes 1769480 | tf_op jit(solution)/shard_map/ppermute | solution.py:57
  32.3 15.3 %collective-permute-start.7 = (bf16[256,1152]{1,0:T(8,128)(2,1)S(1)}, bf16[256,1152]{1,0:T(8,128)(2,1)S(1)}, u32[]{:S(2)}, u32[]{:S(2)}) collective-permute-start(bf16[256,1152]{1,0:T(8,128)(2,1)S(1)} %collective-permute-done.refs_3_.refs_5_), channel_id=1, source_target_pairs={{16,0},{17,1},{18,2},{19,3},{20,4},{21,5},{22,6},{23,7},{24,8},{25... | collective-permute-start | bytes 1769480 | tf_op jit(solution)/shard_map/ppermute | solution.py:57
  33.9 14.6 %collective-permute-start.10 = (bf16[512,256]{1,0:T(8,128)(2,1)S(1)}, bf16[512,256]{1,0:T(8,128)(2,1)S(1)}, u32[]{:S(2)}, u32[]{:S(2)}) collective-permute-start(bf16[512,256]{1,0:T(8,128)(2,1)S(1)} %shard_map.46), channel_id=1, source_target_pairs={{4,0},{5,1},{6,2},{7,3},{0,4},{1,5},{2,6},{3,7},{12,8},{13,9},{14,... | collective-permute-start | bytes 786440 | tf_op jit(solution)/shard_map/ppermute | solution.py:57
  35.3 14.8 %collective-permute-start.8 = (bf16[256,1152]{1,0:T(8,128)(2,1)S(1)}, bf16[256,1152]{1,0:T(8,128)(2,1)S(1)}, u32[]{:S(2)}, u32[]{:S(2)}) collective-permute-start(bf16[256,1152]{1,0:T(8,128)(2,1)S(1)} %collective-permute-done.2.refs_2_), channel_id=1, source_target_pairs={{8,0},{9,1},{10,2},{11,3},{12,4},{13,5},{14,6},{15,7},{0,8},{1,9},... | collective-permute-start | bytes 1769480 | tf_op jit(solution)/shard_map/ppermute | solution.py:57
  47.6 3.9 %collective-permute-start.9 = (bf16[256,1152]{1,0:T(8,128)(2,1)S(1)}, bf16[256,1152]{1,0:T(8,128)(2,1)S(1)}, u32[]{:S(2)}, u32[]{:S(2)}) collective-permute-start(bf16[256,1152]{1,0:T(8,128)(2,1)S(1)} %collective-permute-done.7.refs_3_.refs_7_), channel_id=1, source_target_pairs={{1,0},{0,1},{3,2},{2,3},{5,4},{4,5},{7,6},{6,7},{9,8},{8,9},{11,10... | collective-permute-start | bytes 1769480 | tf_op jit(solution)/shard_map/ppermute | solution.py:57
  48.5 4.0 %collective-permute-start.11 = (bf16[512,256]{1,0:T(8,128)(2,1)S(1)}, bf16[512,256]{1,0:T(8,128)(2,1)S(1)}, u32[]{:S(2)}, u32[]{:S(2)}) collective-permute-start(bf16[512,256]{1,0:T(8,128)(2,1)S(1)} %shard_map.47.refs_14_), channel_id=1, source_target_pairs={{1,0},{0,1},{3,2},{2,3},{5,4},{4,5},{7,6},{6,7},{9,8},{8,9},{11,10... | collective-permute-start | bytes 786440 | tf_op jit(solution)/shard_map/ppermute | solution.py:57
  53.3 7.6 %collective-permute-start.12 = (bf16[272,256]{1,0:T(8,128)(2,1)S(1)}, bf16[272,256]{1,0:T(8,128)(2,1)S(1)}, u32[]{:S(2)}, u32[]{:S(2)}) collective-permute-start(bf16[272,256]{1,0:T(8,128)(2,1)S(1)} %get-tuple-element.56), channel_id=1, source_target_pairs={{8,0},{9,1},{10,2},{11,3},{12,4},{13,5},{14,6},{15,7},{0,8},{1,9},... | collective-permute-start | bytes 417800 | tf_op jit(solution)/shard_map/ppermute | solution.py:57
  54.8 7.1 %collective-permute-start.14 = (bf16[272,256]{1,0:T(8,128)(2,1)S(1)}, bf16[272,256]{1,0:T(8,128)(2,1)S(1)}, u32[]{:S(2)}, u32[]{:S(2)}) collective-permute-start(bf16[272,256]{1,0:T(8,128)(2,1)S(1)} %get-tuple-element.58), channel_id=1, source_target_pairs={{10,0},{11,1},{8,2},{9,3},{14,4},{15,5},{12,6},{13,7},{2,8},{3,9},... | collective-permute-start | bytes 417800 | tf_op jit(solution)/shard_map/ppermute | solution.py:57
  58.0 5.2 %collective-permute-start.13 = (bf16[272,256]{1,0:T(8,128)(2,1)S(1)}, bf16[272,256]{1,0:T(8,128)(2,1)S(1)}, u32[]{:S(2)}, u32[]{:S(2)}) collective-permute-start(bf16[272,256]{1,0:T(8,128)(2,1)S(1)} %get-tuple-element.57), channel_id=1, source_target_pairs={{2,0},{3,1},{0,2},{1,3},{6,4},{7,5},{4,6},{5,7},{10,8},{11,9},{8,1... | collective-permute-start | bytes 417800 | tf_op jit(solution)/shard_map/ppermute | solution.py:57
  63.3 7.4 %collective-permute-start.18 = (bf16[256,256]{1,0:T(8,128)(2,1)S(1)}, bf16[256,256]{1,0:T(8,128)(2,1)S(1)}, u32[]{:S(2)}, u32[]{:S(2)}) collective-permute-start(bf16[256,256]{1,0:T(8,128)(2,1)S(1)} %get-tuple-element.59.refs_5_), channel_id=1, source_target_pairs={{4,0},{5,1},{6,2},{7,3},{0,4},{1,5},{2,6},{3,7},{12,8},{13,9},{14,... | collective-permute-start | bytes 393224 | tf_op jit(solution)/shard_map/ppermute | solution.py:57
  64.6 7.8 %collective-permute-start.16 = (bf16[256,256]{1,0:T(8,128)(2,1)S(1)}, bf16[256,256]{1,0:T(8,128)(2,1)S(1)}, u32[]{:S(2)}, u32[]{:S(2)}) collective-permute-start(bf16[256,256]{1,0:T(8,128)(2,1)S(1)} %get-tuple-element.59.refs_5_), channel_id=1, source_target_pairs={{16,0},{17,1},{18,2},{19,3},{20,4},{21,5},{22,6},{23,7},{24,8},{25... | collective-permute-start | bytes 393224 | tf_op jit(solution)/shard_map/ppermute | solution.py:57
  70.7 5.0 %collective-permute-start.20 = (bf16[256,256]{1,0:T(8,128)(2,1)S(1)}, bf16[256,256]{1,0:T(8,128)(2,1)S(1)}, u32[]{:S(2)}, u32[]{:S(2)}) collective-permute-start(bf16[256,256]{1,0:T(8,128)(2,1)S(1)} %collective-permute-done.18.refs_9_), channel_id=1, source_target_pairs={{16,0},{17,1},{18,2},{19,3},{20,4},{21,5},{22,6},{23,7},{24,8},{25... | collective-permute-start | bytes 393224 | tf_op jit(solution)/shard_map/ppermute | solution.py:57
  71.9 3.8 %collective-permute-start.15 = (bf16[256,256]{1,0:T(8,128)(2,1)S(1)}, bf16[256,256]{1,0:T(8,128)(2,1)S(1)}, u32[]{:S(2)}, u32[]{:S(2)}) collective-permute-start(bf16[256,256]{1,0:T(8,128)(2,1)S(1)} %get-tuple-element.59.refs_5_), channel_id=1, source_target_pairs={{1,0},{0,1},{3,2},{2,3},{5,4},{4,5},{7,6},{6,7},{9,8},{8,9},{11,10... | collective-permute-start | bytes 393224 | tf_op jit(solution)/shard_map/ppermute | solution.py:57
  71.9 3.8 %collective-permute-start.19 = (bf16[256,256]{1,0:T(8,128)(2,1)S(1)}, bf16[256,256]{1,0:T(8,128)(2,1)S(1)}, u32[]{:S(2)}, u32[]{:S(2)}) collective-permute-start(bf16[256,256]{1,0:T(8,128)(2,1)S(1)} %collective-permute-done.18.refs_9_), channel_id=1, source_target_pairs={{1,0},{0,1},{3,2},{2,3},{5,4},{4,5},{7,6},{6,7},{9,8},{8,9},{11,10... | collective-permute-start | bytes 393224 | tf_op jit(solution)/shard_map/ppermute | solution.py:57
  72.4 3.3 %collective-permute-start.17 = (bf16[256,256]{1,0:T(8,128)(2,1)S(1)}, bf16[256,256]{1,0:T(8,128)(2,1)S(1)}, u32[]{:S(2)}, u32[]{:S(2)}) collective-permute-start(bf16[256,256]{1,0:T(8,128)(2,1)S(1)} %collective-permute-done.16.refs_7_), channel_id=1, source_target_pairs={{1,0},{0,1},{3,2},{2,3},{5,4},{4,5},{7,6},{6,7},{9,8},{8,9},{11,10... | collective-permute-start | bytes 393224 | tf_op jit(solution)/shard_map/ppermute | solution.py:57
  77.4 5.6 %collective-permute-start.22 = (bf16[256,256]{1,0:T(8,128)(2,1)S(1)}, bf16[256,256]{1,0:T(8,128)(2,1)S(1)}, u32[]{:S(2)}, u32[]{:S(2)}) collective-permute-start(bf16[256,256]{1,0:T(8,128)(2,1)S(1)} %get-tuple-element.62), channel_id=1, source_target_pairs={{8,0},{9,1},{10,2},{11,3},{12,4},{13,5},{14,6},{15,7},{0,8},{1,9},... | collective-permute-start | bytes 393224 | tf_op jit(solution)/shard_map/ppermute | solution.py:57
  79.0 6.4 %collective-permute-start.23 = (bf16[256,256]{1,0:T(8,128)(2,1)S(1)}, bf16[256,256]{1,0:T(8,128)(2,1)S(1)}, u32[]{:S(2)}, u32[]{:S(2)}) collective-permute-start(bf16[256,256]{1,0:T(8,128)(2,1)S(1)} %get-tuple-element.63), channel_id=1, source_target_pairs={{2,0},{3,1},{0,2},{1,3},{6,4},{7,5},{4,6},{5,7},{10,8},{11,9},{8,1... | collective-permute-start | bytes 393224 | tf_op jit(solution)/shard_map/ppermute | solution.py:57
  79.0 8.1 %collective-permute-start.24 = (bf16[256,256]{1,0:T(8,128)(2,1)S(1)}, bf16[256,256]{1,0:T(8,128)(2,1)S(1)}, u32[]{:S(2)}, u32[]{:S(2)}) collective-permute-start(bf16[256,256]{1,0:T(8,128)(2,1)S(1)} %get-tuple-element.64), channel_id=1, source_target_pairs={{10,0},{11,1},{8,2},{9,3},{14,4},{15,5},{12,6},{13,7},{2,8},{3,9},... | collective-permute-start | bytes 393224 | tf_op jit(solution)/shard_map/ppermute | solution.py:57
  (4 other events, 14.4 us)

commit v15 on v14

--- a/solution.py
+++ b/solution.py
@@ -512,8 +512,8 @@
         return near + far + fetch(far, "core") + far_y + fetch(far_y, "core")
 
     seeds = s_pieces[0] + seeds_zh + seeds_core
-    over_x = tuple(i for i, o in enumerate(t_offsets) if o["x"])
-    along = tuple(i for i, o in enumerate(t_offsets) if not o["x"])
+    over_x = tuple(i for i, o in enumerate(t_offsets) if o["x"] and not o["zl"])
+    along = tuple(i for i in range(len(t_offsets)) if i not in over_x)
     every = tuple(range(len(t_offsets)))
     sent = spread_call(kerns, accs, seeds, c, (*plan, seeds_map, 0, over_x))
     own, totals, *rest = spread_call(kerns, accs, seeds, c, (*plan, seeds_map, 0, along))

time: 88 us -> 89.1 us (1.012)
  starting transfers between devices: 26.3 us -> 28.4 us
  waiting for transfers between devices: 47.4 us -> 46.3 us
    ppermute x25, starting transfers between devices: 26.3 us -> 28.4 us  [fetch(): return lax.ppermute(value, AXES, pairs)]
    ppermute x25, waiting for transfers between devices: 47.4 us -> 46.3 us  [fetch(): return lax.ppermute(value, AXES, pairs)]
where the time goes in v15:
time: 89.1 us; the launch traced here: 88.9 us
  waiting for transfers between devices  46.3 us (52%)
  starting transfers between devices  28.4 us (32%)
  Pallas kernels  12 us (13%)
  local copies, waits for them, and re-layouts  1.97 us (2%)
    ppermute x25, waiting for transfers between devices, fetch(): return lax.ppermute(value, AXES, pairs)  46.3 us
    ppermute x25, starting transfers between devices, fetch(): return lax.ppermute(value, AXES, pairs)  28.4 us
    pallas_call x5, Pallas kernels, gram_call(): pl.pallas_call(functools.partial(gram_kernel, len(t_pieces), len(s_pieces...  6.86 us
    unnamed x6, local copies, waits for them, and re-layouts  1.97 us
    pallas_call x3, Pallas kernels, spread_call(): pl.pallas_call(functools.partial(spread_kernel, plan, len(kerns), len(acc...  1.9 us
  transfers between devices with their start and end apart: 25, of which 14 were waited for; matrix products, arithmetic and copies ran while one was open for 0% of the time, Pallas kernels for 11%

profile of v15, /device:TPU:0, one launch (start us, length us, event | category | flops | bytes accessed | tf_op | source)
XLA Modules:
  0.0 88.9 jit_solution(13502169607673000397)
XLA Ops:
  1.4 4.1 %collective-permute-start = (bf16[256,1152]{1,0:T(8,128)(2,1)S(1)}, bf16[256,1152]{1,0:T(8,128)(2,1)S(1)}, u32[]{:S(2)}, u32[]{:S(2)}) collective-permute-start(bf16[256,1152]{1,0:T(8,128)(2,1)S(1)} %shard_map.38.unit_ref.refs_0_), channel_id=1, source_target_pairs={{4,0},{5,1},{6,2},{7,3},{0,4},{1,5},{2,6},{3,7},{12,8},{13,9},{14,... | collective-permute-start | bytes 1769480 | tf_op jit(solution)/shard_map/ppermute | solution.py:57
  5.5 1.6 %collective-permute-start.2 = (bf16[256,1152]{1,0:T(8,128)(2,1)S(1)}, bf16[256,1152]{1,0:T(8,128)(2,1)S(1)}, u32[]{:S(2)}, u32[]{:S(2)}) collective-permute-start(bf16[256,1152]{1,0:T(8,128)(2,1)S(1)} %shard_map.38.unit_ref.refs_0_), channel_id=1, source_target_pairs={{2,0},{3,1},{0,2},{1,3},{6,4},{7,5},{4,6},{5,7},{10,8},{11,9},{8,1... | collective-permute-start | bytes 1769480 | tf_op jit(solution)/shard_map/ppermute | solution.py:57
  7.1 1.5 %collective-permute-start.1 = (bf16[256,1152]{1,0:T(8,128)(2,1)S(1)}, bf16[256,1152]{1,0:T(8,128)(2,1)S(1)}, u32[]{:S(2)}, u32[]{:S(2)}) collective-permute-start(bf16[256,1152]{1,0:T(8,128)(2,1)S(1)} %shard_map.38.unit_ref.refs_0_), channel_id=1, source_target_pairs={{8,0},{9,1},{10,2},{11,3},{12,4},{13,5},{14,6},{15,7},{0,8},{1,9},... | collective-permute-start | bytes 1769480 | tf_op jit(solution)/shard_map/ppermute | solution.py:57
  9.5 1.6 %collective-permute-start.4 = (bf16[256,1408]{1,0:T(8,128)(2,1)S(1)}, bf16[256,1408]{1,0:T(8,128)(2,1)S(1)}, u32[]{:S(2)}, u32[]{:S(2)}) collective-permute-start(bf16[256,1408]{1,0:T(8,128)(2,1)S(1)} %shard_map.40.refs_3_.refs_1_.refs_10_), channel_id=1, source_target_pairs={{16,0},{17,1},{18,2},{19,3},{20,4},{21,5},{22,6},{23,7},{24,8},{25... | collective-permute-start | bytes 2162696 | tf_op jit(solution)/shard_map/ppermute | solution.py:57
  12.0 19.5 %collective-permute-done.refs_3_.refs_5_ = bf16[256,1152]{1,0:T(8,128)(2,1)S(1)} collective-permute-done((bf16[256,1152]{1,0:T(8,128)(2,1)S(1)}, bf16[256,1152]{1,0:T(8,128)(2,1)S(1)}, u32[]{:S(2)}, u32[]{:S(2)}) %collective-permute-start) | collective-permute-done | bytes 589856 | tf_op jit(solution)/shard_map/ppermute | solution.py:57
  32.3 1.6 %collective-permute-start.7 = (bf16[256,1152]{1,0:T(8,128)(2,1)S(1)}, bf16[256,1152]{1,0:T(8,128)(2,1)S(1)}, u32[]{:S(2)}, u32[]{:S(2)}) collective-permute-start(bf16[256,1152]{1,0:T(8,128)(2,1)S(1)} %collective-permute-done.refs_3_.refs_5_), channel_id=1, source_target_pairs={{16,0},{17,1},{18,2},{19,3},{20,4},{21,5},{22,6},{23,7},{24,8},{25... | collective-permute-start | bytes 1769480 | tf_op jit(solution)/shard_map/ppermute | solution.py:57
  33.9 1.4 %collective-permute-start.10 = (bf16[512,256]{1,0:T(8,128)(2,1)S(1)}, bf16[512,256]{1,0:T(8,128)(2,1)S(1)}, u32[]{:S(2)}, u32[]{:S(2)}) collective-permute-start(bf16[512,256]{1,0:T(8,128)(2,1)S(1)} %shard_map.46), channel_id=1, source_target_pairs={{4,0},{5,1},{6,2},{7,3},{0,4},{1,5},{2,6},{3,7},{12,8},{13,9},{14,... | collective-permute-start | bytes 786440 | tf_op jit(solution)/shard_map/ppermute | solution.py:57
  35.3 1.5 %collective-permute-start.8 = (bf16[256,1152]{1,0:T(8,128)(2,1)S(1)}, bf16[256,1152]{1,0:T(8,128)(2,1)S(1)}, u32[]{:S(2)}, u32[]{:S(2)}) collective-permute-start(bf16[256,1152]{1,0:T(8,128)(2,1)S(1)} %collective-permute-done.2.refs_2_), channel_id=1, source_target_pairs={{8,0},{9,1},{10,2},{11,3},{12,4},{13,5},{14,6},{15,7},{0,8},{1,9},... | collective-permute-start | bytes 1769480 | tf_op jit(solution)/shard_map/ppermute | solution.py:57
  38.1 2.4 %shard_map.41 = (bf16[768,1024]{1,0:T(8,128)(2,1)S(1)}, f32[768,128]{1,0:T(8,128)S(1)}) custom-call(s32[8,2048]{1,0:T(8,128)S(1)} %shard_map.37.flags, bf16[256,1152]{1,0:T(8,128)(2,1)S(1)} %shard_map.38.unit_ref.refs_0_, bf16[256,1152]{1,0:T(8,128)(2,1)S(1)} %collective-permute-done.1.refs_1_, bf16[256,1152]{1,0:T(8,128)(2,1)S(1)} %collective-permute-done.2.refs_2_, ...), custom_call_target="tpu_custom_call" | custom-call | flops 1811939328 | bytes 4128768 | tf_op jit(solution)/shard_map/pallas_call | solution.py:233
  40.5 7.1 %collective-permute-done.7.refs_3_.refs_7_ = bf16[256,1152]{1,0:T(8,128)(2,1)S(1)} collective-permute-done((bf16[256,1152]{1,0:T(8,128)(2,1)S(1)}, bf16[256,1152]{1,0:T(8,128)(2,1)S(1)}, u32[]{:S(2)}, u32[]{:S(2)}) %collective-permute-start.7) | collective-permute-done | bytes 589856 | tf_op jit(solution)/shard_map/ppermute | solution.py:57
  50.1 1.5 %shard_map.44 = (bf16[256,1792]{1,0:T(8,128)(2,1)S(1)}, f32[256,128]{1,0:T(8,128)S(1)}) custom-call(s32[8,2048]{1,0:T(8,128)S(1)} %shard_map.37.flags, bf16[256,1152]{1,0:T(8,128)(2,1)S(1)} %collective-permute-done.8.refs_0_.refs_3_, bf16[256,1408]{1,0:T(8,128)(2,1)S(1)} %shard_map.40.refs_3_.refs_1_.refs_10_, ...), custom_call_target="tpu_custom_call" | custom-call | flops 1056964608 | bytes 4718592 | tf_op jit(solution)/shard_map/pallas_call | solution.py:233
  53.5 2.5 %collective-permute-start.13 = (bf16[272,256]{1,0:T(8,128)(2,1)S(1)}, bf16[272,256]{1,0:T(8,128)(2,1)S(1)}, u32[]{:S(2)}, u32[]{:S(2)}) collective-permute-start(bf16[272,256]{1,0:T(8,128)(2,1)S(1)} %get-tuple-element.55), channel_id=1, source_target_pairs={{2,0},{3,1},{0,2},{1,3},{6,4},{7,5},{4,6},{5,7},{10,8},{11,9},{8,1... | collective-permute-start | bytes 417800 | tf_op jit(solution)/shard_map/ppermute | solution.py:57
  58.1 2.2 %collective-permute-done.13.refs_1_ = bf16[272,256]{1,0:T(8,128)(2,1)S(1)} collective-permute-done((bf16[272,256]{1,0:T(8,128)(2,1)S(1)}, bf16[272,256]{1,0:T(8,128)(2,1)S(1)}, u32[]{:S(2)}, u32[]{:S(2)}) %collective-permute-start.13) | collective-permute-done | bytes 139296 | tf_op jit(solution)/shard_map/ppermute | solution.py:57
  60.3 2.2 %collective-permute-done.14.refs_2_ = bf16[272,256]{1,0:T(8,128)(2,1)S(1)} collective-permute-done((bf16[272,256]{1,0:T(8,128)(2,1)S(1)}, bf16[272,256]{1,0:T(8,128)(2,1)S(1)}, u32[]{:S(2)}, u32[]{:S(2)}) %collective-permute-start.14) | collective-permute-done | bytes 139296 | tf_op jit(solution)/shard_map/ppermute | solution.py:57
  62.5 1.4 %collective-permute-done.12.refs_0_ = bf16[272,256]{1,0:T(8,128)(2,1)S(1)} collective-permute-done((bf16[272,256]{1,0:T(8,128)(2,1)S(1)}, bf16[272,256]{1,0:T(8,128)(2,1)S(1)}, u32[]{:S(2)}, u32[]{:S(2)}) %collective-permute-start.12) | collective-permute-done | bytes 139296 | tf_op jit(solution)/shard_map/ppermute | solution.py:57
  64.0 2.1 %collective-permute-start.18 = (bf16[256,256]{1,0:T(8,128)(2,1)S(1)}, bf16[256,256]{1,0:T(8,128)(2,1)S(1)}, u32[]{:S(2)}, u32[]{:S(2)}) collective-permute-start(bf16[256,256]{1,0:T(8,128)(2,1)S(1)} %get-tuple-element.57.refs_5_), channel_id=1, source_target_pairs={{4,0},{5,1},{6,2},{7,3},{0,4},{1,5},{2,6},{3,7},{12,8},{13,9},{14,... | collective-permute-start | bytes 393224 | tf_op jit(solution)/shard_map/ppermute | solution.py:57
  66.1 1.8 %collective-permute-start.16 = (bf16[256,256]{1,0:T(8,128)(2,1)S(1)}, bf16[256,256]{1,0:T(8,128)(2,1)S(1)}, u32[]{:S(2)}, u32[]{:S(2)}) collective-permute-start(bf16[256,256]{1,0:T(8,128)(2,1)S(1)} %get-tuple-element.57.refs_5_), channel_id=1, source_target_pairs={{16,0},{17,1},{18,2},{19,3},{20,4},{21,5},{22,6},{23,7},{24,8},{25... | collective-permute-start | bytes 393224 | tf_op jit(solution)/shard_map/ppermute | solution.py:57
  67.9 3.7 %collective-permute-done.18.refs_9_ = bf16[256,256]{1,0:T(8,128)(2,1)S(1)} collective-permute-done((bf16[256,256]{1,0:T(8,128)(2,1)S(1)}, bf16[256,256]{1,0:T(8,128)(2,1)S(1)}, u32[]{:S(2)}, u32[]{:S(2)}) %collective-permute-start.18) | collective-permute-done | bytes 131104 | tf_op jit(solution)/shard_map/ppermute | solution.py:57
  71.7 2.1 %collective-permute-start.20 = (bf16[256,256]{1,0:T(8,128)(2,1)S(1)}, bf16[256,256]{1,0:T(8,128)(2,1)S(1)}, u32[]{:S(2)}, u32[]{:S(2)}) collective-permute-start(bf16[256,256]{1,0:T(8,128)(2,1)S(1)} %collective-permute-done.18.refs_9_), channel_id=1, source_target_pairs={{16,0},{17,1},{18,2},{19,3},{20,4},{21,5},{22,6},{23,7},{24,8},{25... | collective-permute-start | bytes 393224 | tf_op jit(solution)/shard_map/ppermute | solution.py:57
  74.3 2.4 %collective-permute-done.20.refs_6_ = bf16[256,256]{1,0:T(8,128)(2,1)S(1)} collective-permute-done((bf16[256,256]{1,0:T(8,128)(2,1)S(1)}, bf16[256,256]{1,0:T(8,128)(2,1)S(1)}, u32[]{:S(2)}, u32[]{:S(2)}) %collective-permute-start.20) | collective-permute-done | bytes 131104 | tf_op jit(solution)/shard_map/ppermute | solution.py:57
  80.3 1.7 %collective-permute-start.24 = (bf16[256,256]{1,0:T(8,128)(2,1)S(1)}, bf16[256,256]{1,0:T(8,128)(2,1)S(1)}, u32[]{:S(2)}, u32[]{:S(2)}) collective-permute-start(bf16[256,256]{1,0:T(8,128)(2,1)S(1)} %get-tuple-element.62), channel_id=1, source_target_pairs={{10,0},{11,1},{8,2},{9,3},{14,4},{15,5},{12,6},{13,7},{2,8},{3,9},... | collective-permute-start | bytes 393224 | tf_op jit(solution)/shard_map/ppermute | solution.py:57
  82.0 2.1 %collective-permute-done.22.refs_0_ = bf16[256,256]{1,0:T(8,128)(2,1)S(1)} collective-permute-done((bf16[256,256]{1,0:T(8,128)(2,1)S(1)}, bf16[256,256]{1,0:T(8,128)(2,1)S(1)}, u32[]{:S(2)}, u32[]{:S(2)}) %collective-permute-start.22) | collective-permute-done | bytes 131104 | tf_op jit(solution)/shard_map/ppermute | solution.py:57
  84.1 1.6 %collective-permute-done.23.refs_1_ = bf16[256,256]{1,0:T(8,128)(2,1)S(1)} collective-permute-done((bf16[256,256]{1,0:T(8,128)(2,1)S(1)}, bf16[256,256]{1,0:T(8,128)(2,1)S(1)}, u32[]{:S(2)}, u32[]{:S(2)}) %collective-permute-start.23) | collective-permute-done | bytes 131104 | tf_op jit(solution)/shard_map/ppermute | solution.py:57
  85.7 2.4 %collective-permute-done.24.refs_2_ = bf16[256,256]{1,0:T(8,128)(2,1)S(1)} collective-permute-done((bf16[256,256]{1,0:T(8,128)(2,1)S(1)}, bf16[256,256]{1,0:T(8,128)(2,1)S(1)}, u32[]{:S(2)}, u32[]{:S(2)}) %collective-permute-start.24) | collective-permute-done | bytes 131104 | tf_op jit(solution)/shard_map/ppermute | solution.py:57
  (50 shorter events, 16.8 us)
Async XLA Ops:
  1.4 30.2 %collective-permute-start = (bf16[256,1152]{1,0:T(8,128)(2,1)S(1)}, bf16[256,1152]{1,0:T(8,128)(2,1)S(1)}, u32[]{:S(2)}, u32[]{:S(2)}) collective-permute-start(bf16[256,1152]{1,0:T(8,128)(2,1)S(1)} %shard_map.38.unit_ref.refs_0_), channel_id=1, source_target_pairs={{4,0},{5,1},{6,2},{7,3},{0,4},{1,5},{2,6},{3,7},{12,8},{13,9},{14,... | collective-permute-start | bytes 1769480 | tf_op jit(solution)/shard_map/ppermute | solution.py:57
  5.5 26.3 %collective-permute-start.2 = (bf16[256,1152]{1,0:T(8,128)(2,1)S(1)}, bf16[256,1152]{1,0:T(8,128)(2,1)S(1)}, u32[]{:S(2)}, u32[]{:S(2)}) collective-permute-start(bf16[256,1152]{1,0:T(8,128)(2,1)S(1)} %shard_map.38.unit_ref.refs_0_), channel_id=1, source_target_pairs={{2,0},{3,1},{0,2},{1,3},{6,4},{7,5},{4,6},{5,7},{10,8},{11,9},{8,1... | collective-permute-start | bytes 1769480 | tf_op jit(solution)/shard_map/ppermute | solution.py:57
  7.1 24.7 %collective-permute-start.1 = (bf16[256,1152]{1,0:T(8,128)(2,1)S(1)}, bf16[256,1152]{1,0:T(8,128)(2,1)S(1)}, u32[]{:S(2)}, u32[]{:S(2)}) collective-permute-start(bf16[256,1152]{1,0:T(8,128)(2,1)S(1)} %shard_map.38.unit_ref.refs_0_), channel_id=1, source_target_pairs={{8,0},{9,1},{10,2},{11,3},{12,4},{13,5},{14,6},{15,7},{0,8},{1,9},... | collective-permute-start | bytes 1769480 | tf_op jit(solution)/shard_map/ppermute | solution.py:57
  9.5 22.2 %collective-permute-start.4 = (bf16[256,1408]{1,0:T(8,128)(2,1)S(1)}, bf16[256,1408]{1,0:T(8,128)(2,1)S(1)}, u32[]{:S(2)}, u32[]{:S(2)}) collective-permute-start(bf16[256,1408]{1,0:T(8,128)(2,1)S(1)} %shard_map.40.refs_3_.refs_1_.refs_10_), channel_id=1, source_target_pairs={{16,0},{17,1},{18,2},{19,3},{20,4},{21,5},{22,6},{23,7},{24,8},{25... | collective-permute-start | bytes 2162696 | tf_op jit(solution)/shard_map/ppermute | solution.py:57
  11.1 20.7 %collective-permute-start.3 = (bf16[256,1408]{1,0:T(8,128)(2,1)S(1)}, bf16[256,1408]{1,0:T(8,128)(2,1)S(1)}, u32[]{:S(2)}, u32[]{:S(2)}) collective-permute-start(bf16[256,1408]{1,0:T(8,128)(2,1)S(1)} %shard_map.40.refs_3_.refs_1_.refs_10_), channel_id=1, source_target_pairs={{1,0},{0,1},{3,2},{2,3},{5,4},{4,5},{7,6},{6,7},{9,8},{8,9},{11,10... | collective-permute-start | bytes 2162696 | tf_op jit(solution)/shard_map/ppermute | solution.py:57
  31.8 6.3 %collective-permute-start.5 = (bf16[256,1408]{1,0:T(8,128)(2,1)S(1)}, bf16[256,1408]{1,0:T(8,128)(2,1)S(1)}, u32[]{:S(2)}, u32[]{:S(2)}) collective-permute-start(bf16[256,1408]{1,0:T(8,128)(2,1)S(1)} %collective-permute-done.4.refs_5_.refs_3_.refs_0_.refs_12_), channel_id=1, source_target_pairs={{1,0},{0,1},{3,2},{2,3},{5,4},{4,5},{7,6},{6,7},{9,8},{8,9},{11,10... | collective-permute-start | bytes 2162696 | tf_op jit(solution)/shard_map/ppermute | solution.py:57
  31.8 5.0 %collective-permute-start.6 = (bf16[256,1152]{1,0:T(8,128)(2,1)S(1)}, bf16[256,1152]{1,0:T(8,128)(2,1)S(1)}, u32[]{:S(2)}, u32[]{:S(2)}) collective-permute-start(bf16[256,1152]{1,0:T(8,128)(2,1)S(1)} %collective-permute-done.refs_3_.refs_5_), channel_id=1, source_target_pairs={{1,0},{0,1},{3,2},{2,3},{5,4},{4,5},{7,6},{6,7},{9,8},{8,9},{11,10... | collective-permute-start | bytes 1769480 | tf_op jit(solution)/shard_map/ppermute | solution.py:57
  32.3 15.3 %collective-permute-start.7 = (bf16[256,1152]{1,0:T(8,128)(2,1)S(1)}, bf16[256,1152]{1,0:T(8,128)(2,1)S(1)}, u32[]{:S(2)}, u32[]{:S(2)}) collective-permute-start(bf16[256,1152]{1,0:T(8,128)(2,1)S(1)} %collective-permute-done.refs_3_.refs_5_), channel_id=1, source_target_pairs={{16,0},{17,1},{18,2},{19,3},{20,4},{21,5},{22,6},{23,7},{24,8},{25... | collective-permute-start | bytes 1769480 | tf_op jit(solution)/shard_map/ppermute | solution.py:57
  33.9 14.6 %collective-permute-start.10 = (bf16[512,256]{1,0:T(8,128)(2,1)S(1)}, bf16[512,256]{1,0:T(8,128)(2,1)S(1)}, u32[]{:S(2)}, u32[]{:S(2)}) collective-permute-start(bf16[512,256]{1,0:T(8,128)(2,1)S(1)} %shard_map.46), channel_id=1, source_target_pairs={{4,0},{5,1},{6,2},{7,3},{0,4},{1,5},{2,6},{3,7},{12,8},{13,9},{14,... | collective-permute-start | bytes 786440 | tf_op jit(solution)/shard_map/ppermute | solution.py:57
  35.3 14.8 %collective-permute-start.8 = (bf16[256,1152]{1,0:T(8,128)(2,1)S(1)}, bf16[256,1152]{1,0:T(8,128)(2,1)S(1)}, u32[]{:S(2)}, u32[]{:S(2)}) collective-permute-start(bf16[256,1152]{1,0:T(8,128)(2,1)S(1)} %collective-permute-done.2.refs_2_), channel_id=1, source_target_pairs={{8,0},{9,1},{10,2},{11,3},{12,4},{13,5},{14,6},{15,7},{0,8},{1,9},... | collective-permute-start | bytes 1769480 | tf_op jit(solution)/shard_map/ppermute | solution.py:57
  47.6 3.9 %collective-permute-start.9 = (bf16[256,1152]{1,0:T(8,128)(2,1)S(1)}, bf16[256,1152]{1,0:T(8,128)(2,1)S(1)}, u32[]{:S(2)}, u32[]{:S(2)}) collective-permute-start(bf16[256,1152]{1,0:T(8,128)(2,1)S(1)} %collective-permute-done.7.refs_3_.refs_7_), channel_id=1, source_target_pairs={{1,0},{0,1},{3,2},{2,3},{5,4},{4,5},{7,6},{6,7},{9,8},{8,9},{11,10... | collective-permute-start | bytes 1769480 | tf_op jit(solution)/shard_map/ppermute | solution.py:57
  48.5 4.0 %collective-permute-start.11 = (bf16[512,256]{1,0:T(8,128)(2,1)S(1)}, bf16[512,256]{1,0:T(8,128)(2,1)S(1)}, u32[]{:S(2)}, u32[]{:S(2)}) collective-permute-start(bf16[512,256]{1,0:T(8,128)(2,1)S(1)} %shard_map.47.refs_14_), channel_id=1, source_target_pairs={{1,0},{0,1},{3,2},{2,3},{5,4},{4,5},{7,6},{6,7},{9,8},{8,9},{11,10... | collective-permute-start | bytes 786440 | tf_op jit(solution)/shard_map/ppermute | solution.py:57
  53.5 6.8 %collective-permute-start.13 = (bf16[272,256]{1,0:T(8,128)(2,1)S(1)}, bf16[272,256]{1,0:T(8,128)(2,1)S(1)}, u32[]{:S(2)}, u32[]{:S(2)}) collective-permute-start(bf16[272,256]{1,0:T(8,128)(2,1)S(1)} %get-tuple-element.55), channel_id=1, source_target_pairs={{2,0},{3,1},{0,2},{1,3},{6,4},{7,5},{4,6},{5,7},{10,8},{11,9},{8,1... | collective-permute-start | bytes 417800 | tf_op jit(solution)/shard_map/ppermute | solution.py:57
  56.1 6.5 %collective-permute-start.14 = (bf16[272,256]{1,0:T(8,128)(2,1)S(1)}, bf16[272,256]{1,0:T(8,128)(2,1)S(1)}, u32[]{:S(2)}, u32[]{:S(2)}) collective-permute-start(bf16[272,256]{1,0:T(8,128)(2,1)S(1)} %get-tuple-element.56), channel_id=1, source_target_pairs={{10,0},{11,1},{8,2},{9,3},{14,4},{15,5},{12,6},{13,7},{2,8},{3,9},... | collective-permute-start | bytes 417800 | tf_op jit(solution)/shard_map/ppermute | solution.py:57
  57.5 6.4 %collective-permute-start.12 = (bf16[272,256]{1,0:T(8,128)(2,1)S(1)}, bf16[272,256]{1,0:T(8,128)(2,1)S(1)}, u32[]{:S(2)}, u32[]{:S(2)}) collective-permute-start(bf16[272,256]{1,0:T(8,128)(2,1)S(1)} %shard_map.49), channel_id=1, source_target_pairs={{8,0},{9,1},{10,2},{11,3},{12,4},{13,5},{14,6},{15,7},{0,8},{1,9},... | collective-permute-start | bytes 417800 | tf_op jit(solution)/shard_map/ppermute | solution.py:57
  64.0 7.6 %collective-permute-start.18 = (bf16[256,256]{1,0:T(8,128)(2,1)S(1)}, bf16[256,256]{1,0:T(8,128)(2,1)S(1)}, u32[]{:S(2)}, u32[]{:S(2)}) collective-permute-start(bf16[256,256]{1,0:T(8,128)(2,1)S(1)} %get-tuple-element.57.refs_5_), channel_id=1, source_target_pairs={{4,0},{5,1},{6,2},{7,3},{0,4},{1,5},{2,6},{3,7},{12,8},{13,9},{14,... | collective-permute-start | bytes 393224 | tf_op jit(solution)/shard_map/ppermute | solution.py:57
  66.1 8.1 %collective-permute-start.16 = (bf16[256,256]{1,0:T(8,128)(2,1)S(1)}, bf16[256,256]{1,0:T(8,128)(2,1)S(1)}, u32[]{:S(2)}, u32[]{:S(2)}) collective-permute-start(bf16[256,256]{1,0:T(8,128)(2,1)S(1)} %get-tuple-element.57.refs_5_), channel_id=1, source_target_pairs={{16,0},{17,1},{18,2},{19,3},{20,4},{21,5},{22,6},{23,7},{24,8},{25... | collective-permute-start | bytes 393224 | tf_op jit(solution)/shard_map/ppermute | solution.py:57
  71.7 5.0 %collective-permute-start.20 = (bf16[256,256]{1,0:T(8,128)(2,1)S(1)}, bf16[256,256]{1,0:T(8,128)(2,1)S(1)}, u32[]{:S(2)}, u32[]{:S(2)}) collective-permute-start(bf16[256,256]{1,0:T(8,128)(2,1)S(1)} %collective-permute-done.18.refs_9_), channel_id=1, source_target_pairs={{16,0},{17,1},{18,2},{19,3},{20,4},{21,5},{22,6},{23,7},{24,8},{25... | collective-permute-start | bytes 393224 | tf_op jit(solution)/shard_map/ppermute | solution.py:57
  73.7 3.0 %collective-permute-start.15 = (bf16[256,256]{1,0:T(8,128)(2,1)S(1)}, bf16[256,256]{1,0:T(8,128)(2,1)S(1)}, u32[]{:S(2)}, u32[]{:S(2)}) collective-permute-start(bf16[256,256]{1,0:T(8,128)(2,1)S(1)} %get-tuple-element.57.refs_5_), channel_id=1, source_target_pairs={{1,0},{0,1},{3,2},{2,3},{5,4},{4,5},{7,6},{6,7},{9,8},{8,9},{11,10... | collective-permute-start | bytes 393224 | tf_op jit(solution)/shard_map/ppermute | solution.py:57
  73.7 3.0 %collective-permute-start.19 = (bf16[256,256]{1,0:T(8,128)(2,1)S(1)}, bf16[256,256]{1,0:T(8,128)(2,1)S(1)}, u32[]{:S(2)}, u32[]{:S(2)}) collective-permute-start(bf16[256,256]{1,0:T(8,128)(2,1)S(1)} %collective-permute-done.18.refs_9_), channel_id=1, source_target_pairs={{1,0},{0,1},{3,2},{2,3},{5,4},{4,5},{7,6},{6,7},{9,8},{8,9},{11,10... | collective-permute-start | bytes 393224 | tf_op jit(solution)/shard_map/ppermute | solution.py:57
  74.3 2.4 %collective-permute-start.17 = (bf16[256,256]{1,0:T(8,128)(2,1)S(1)}, bf16[256,256]{1,0:T(8,128)(2,1)S(1)}, u32[]{:S(2)}, u32[]{:S(2)}) collective-permute-start(bf16[256,256]{1,0:T(8,128)(2,1)S(1)} %collective-permute-done.16.refs_7_), channel_id=1, source_target_pairs={{1,0},{0,1},{3,2},{2,3},{5,4},{4,5},{7,6},{6,7},{9,8},{8,9},{11,10... | collective-permute-start | bytes 393224 | tf_op jit(solution)/shard_map/ppermute | solution.py:57
  78.5 5.6 %collective-permute-start.22 = (bf16[256,256]{1,0:T(8,128)(2,1)S(1)}, bf16[256,256]{1,0:T(8,128)(2,1)S(1)}, u32[]{:S(2)}, u32[]{:S(2)}) collective-permute-start(bf16[256,256]{1,0:T(8,128)(2,1)S(1)} %get-tuple-element.60), channel_id=1, source_target_pairs={{8,0},{9,1},{10,2},{11,3},{12,4},{13,5},{14,6},{15,7},{0,8},{1,9},... | collective-permute-start | bytes 393224 | tf_op jit(solution)/shard_map/ppermute | solution.py:57
  79.3 6.4 %collective-permute-start.23 = (bf16[256,256]{1,0:T(8,128)(2,1)S(1)}, bf16[256,256]{1,0:T(8,128)(2,1)S(1)}, u32[]{:S(2)}, u32[]{:S(2)}) collective-permute-start(bf16[256,256]{1,0:T(8,128)(2,1)S(1)} %get-tuple-element.61), channel_id=1, source_target_pairs={{2,0},{3,1},{0,2},{1,3},{6,4},{7,5},{4,6},{5,7},{10,8},{11,9},{8,1... | collective-permute-start | bytes 393224 | tf_op jit(solution)/shard_map/ppermute | solution.py:57
  80.3 7.8 %collective-permute-start.24 = (bf16[256,256]{1,0:T(8,128)(2,1)S(1)}, bf16[256,256]{1,0:T(8,128)(2,1)S(1)}, u32[]{:S(2)}, u32[]{:S(2)}) collective-permute-start(bf16[256,256]{1,0:T(8,128)(2,1)S(1)} %get-tuple-element.62), channel_id=1, source_target_pairs={{10,0},{11,1},{8,2},{9,3},{14,4},{15,5},{12,6},{13,7},{2,8},{3,9},... | collective-permute-start | bytes 393224 | tf_op jit(solution)/shard_map/ppermute | solution.py:57
  (4 other events, 14.4 us)

commit v16 on v15

--- a/solution.py
+++ b/solution.py
@@ -512,8 +512,8 @@
         return near + far + fetch(far, "core") + far_y + fetch(far_y, "core")
 
     seeds = s_pieces[0] + seeds_zh + seeds_core
-    over_x = tuple(i for i, o in enumerate(t_offsets) if o["x"] and not o["zl"])
-    along = tuple(i for i in range(len(t_offsets)) if i not in over_x)
+    over_x = tuple(i for i, o in enumerate(t_offsets) if i)
+    along = (0,)
     every = tuple(range(len(t_offsets)))
     sent = spread_call(kerns, accs, seeds, c, (*plan, seeds_map, 0, over_x))
     own, totals, *rest = spread_call(kerns, accs, seeds, c, (*plan, seeds_map, 0, along))

time: 89.1 us -> 88.4 us (level)
  starting transfers between devices: 28.4 us -> 25.6 us
  waiting for transfers between devices: 46.3 us -> 48.4 us
    ppermute x25, starting transfers between devices: 28.4 us -> 25.6 us  [fetch(): return lax.ppermute(value, AXES, pairs)]
    ppermute x25, waiting for transfers between devices: 46.3 us -> 48.4 us  [fetch(): return lax.ppermute(value, AXES, pairs)]
where the time goes in v16:
time: 88.4 us; the launch traced here: 88.3 us
  waiting for transfers between devices  48.4 us (55%)
  starting transfers between devices  25.6 us (29%)
  Pallas kernels  12.1 us (14%)
  local copies, waits for them, and re-layouts  1.97 us (2%)
    ppermute x25, waiting for transfers between devices, fetch(): return lax.ppermute(value, AXES, pairs)  48.4 us
    ppermute x25, starting transfers between devices, fetch(): return lax.ppermute(value, AXES, pairs)  25.6 us
    pallas_call x5, Pallas kernels, gram_call(): pl.pallas_call(functools.partial(gram_kernel, len(t_pieces), len(s_pieces...  6.95 us
    unnamed x6, local copies, waits for them, and re-layouts  1.97 us
    pallas_call x3, Pallas kernels, spread_call(): pl.pallas_call(functools.partial(spread_kernel, plan, len(kerns), len(acc...  1.95 us
  transfers between devices with their start and end apart: 25, of which 14 were waited for; matrix products, arithmetic and copies ran while one was open for 0% of the time, Pallas kernels for 11%

profile of v16, /device:TPU:0, one launch (start us, length us, event | category | flops | bytes accessed | tf_op | source)
XLA Modules:
  0.0 88.3 jit_solution(6397943107670074354)
XLA Ops:
  1.4 4.1 %collective-permute-start = (bf16[256,1152]{1,0:T(8,128)(2,1)S(1)}, bf16[256,1152]{1,0:T(8,128)(2,1)S(1)}, u32[]{:S(2)}, u32[]{:S(2)}) collective-permute-start(bf16[256,1152]{1,0:T(8,128)(2,1)S(1)} %shard_map.38.unit_ref.refs_0_), channel_id=1, source_target_pairs={{4,0},{5,1},{6,2},{7,3},{0,4},{1,5},{2,6},{3,7},{12,8},{13,9},{14,... | collective-permute-start | bytes 1769480 | tf_op jit(solution)/shard_map/ppermute | solution.py:57
  5.5 1.6 %collective-permute-start.2 = (bf16[256,1152]{1,0:T(8,128)(2,1)S(1)}, bf16[256,1152]{1,0:T(8,128)(2,1)S(1)}, u32[]{:S(2)}, u32[]{:S(2)}) collective-permute-start(bf16[256,1152]{1,0:T(8,128)(2,1)S(1)} %shard_map.38.unit_ref.refs_0_), channel_id=1, source_target_pairs={{2,0},{3,1},{0,2},{1,3},{6,4},{7,5},{4,6},{5,7},{10,8},{11,9},{8,1... | collective-permute-start | bytes 1769480 | tf_op jit(solution)/shard_map/ppermute | solution.py:57
  7.1 1.5 %collective-permute-start.1 = (bf16[256,1152]{1,0:T(8,128)(2,1)S(1)}, bf16[256,1152]{1,0:T(8,128)(2,1)S(1)}, u32[]{:S(2)}, u32[]{:S(2)}) collective-permute-start(bf16[256,1152]{1,0:T(8,128)(2,1)S(1)} %shard_map.38.unit_ref.refs_0_), channel_id=1, source_target_pairs={{8,0},{9,1},{10,2},{11,3},{12,4},{13,5},{14,6},{15,7},{0,8},{1,9},... | collective-permute-start | bytes 1769480 | tf_op jit(solution)/shard_map/ppermute | solution.py:57
  9.5 1.6 %collective-permute-start.4 = (bf16[256,1408]{1,0:T(8,128)(2,1)S(1)}, bf16[256,1408]{1,0:T(8,128)(2,1)S(1)}, u32[]{:S(2)}, u32[]{:S(2)}) collective-permute-start(bf16[256,1408]{1,0:T(8,128)(2,1)S(1)} %shard_map.40.refs_3_.refs_1_.refs_10_), channel_id=1, source_target_pairs={{16,0},{17,1},{18,2},{19,3},{20,4},{21,5},{22,6},{23,7},{24,8},{25... | collective-permute-start | bytes 2162696 | tf_op jit(solution)/shard_map/ppermute | solution.py:57
  12.0 19.5 %collective-permute-done.refs_3_.refs_5_ = bf16[256,1152]{1,0:T(8,128)(2,1)S(1)} collective-permute-done((bf16[256,1152]{1,0:T(8,128)(2,1)S(1)}, bf16[256,1152]{1,0:T(8,128)(2,1)S(1)}, u32[]{:S(2)}, u32[]{:S(2)}) %collective-permute-start) | collective-permute-done | bytes 589856 | tf_op jit(solution)/shard_map/ppermute | solution.py:57
  32.3 1.6 %collective-permute-start.7 = (bf16[256,1152]{1,0:T(8,128)(2,1)S(1)}, bf16[256,1152]{1,0:T(8,128)(2,1)S(1)}, u32[]{:S(2)}, u32[]{:S(2)}) collective-permute-start(bf16[256,1152]{1,0:T(8,128)(2,1)S(1)} %collective-permute-done.refs_3_.refs_5_), channel_id=1, source_target_pairs={{16,0},{17,1},{18,2},{19,3},{20,4},{21,5},{22,6},{23,7},{24,8},{25... | collective-permute-start | bytes 1769480 | tf_op jit(solution)/shard_map/ppermute | solution.py:57
  33.9 1.4 %collective-permute-start.10 = (bf16[512,256]{1,0:T(8,128)(2,1)S(1)}, bf16[512,256]{1,0:T(8,128)(2,1)S(1)}, u32[]{:S(2)}, u32[]{:S(2)}) collective-permute-start(bf16[512,256]{1,0:T(8,128)(2,1)S(1)} %shard_map.46), channel_id=1, source_target_pairs={{4,0},{5,1},{6,2},{7,3},{0,4},{1,5},{2,6},{3,7},{12,8},{13,9},{14,... | collective-permute-start | bytes 786440 | tf_op jit(solution)/shard_map/ppermute | solution.py:57
  35.3 1.5 %collective-permute-start.8 = (bf16[256,1152]{1,0:T(8,128)(2,1)S(1)}, bf16[256,1152]{1,0:T(8,128)(2,1)S(1)}, u32[]{:S(2)}, u32[]{:S(2)}) collective-permute-start(bf16[256,1152]{1,0:T(8,128)(2,1)S(1)} %collective-permute-done.2.refs_2_), channel_id=1, source_target_pairs={{8,0},{9,1},{10,2},{11,3},{12,4},{13,5},{14,6},{15,7},{0,8},{1,9},... | collective-permute-start | bytes 1769480 | tf_op jit(solution)/shard_map/ppermute | solution.py:57
  36.8 1.3 %shard_map.42 = (bf16[768,512]{1,0:T(8,128)(2,1)S(1)}, f32[768,128]{1,0:T(8,128)S(1)}) custom-call(s32[8,2048]{1,0:T(8,128)S(1)} %shard_map.37.flags, bf16[256,1152]{1,0:T(8,128)(2,1)S(1)} %shard_map.38.unit_ref.refs_0_, bf16[256,1152]{1,0:T(8,128)(2,1)S(1)} %collective-permute-done.1.refs_1_, bf16[256,1152]{1,0:T(8,128)(2,1)S(1)} %collective-permute-done.2.refs_2_, ...), custom_call_target="tpu_custom_call" | custom-call | flops 905969664 | bytes 2949120 | tf_op jit(solution)/shard_map/pallas_call | solution.py:233
  38.2 2.4 %shard_map.41 = (bf16[768,1024]{1,0:T(8,128)(2,1)S(1)}, f32[768,128]{1,0:T(8,128)S(1)}) custom-call(s32[8,2048]{1,0:T(8,128)S(1)} %shard_map.37.flags, bf16[256,1152]{1,0:T(8,128)(2,1)S(1)} %shard_map.38.unit_ref.refs_0_, bf16[256,1152]{1,0:T(8,128)(2,1)S(1)} %collective-permute-done.1.refs_1_, bf16[256,1152]{1,0:T(8,128)(2,1)S(1)} %collective-permute-done.2.refs_2_, ...), custom_call_target="tpu_custom_call" | custom-call | flops 1811939328 | bytes 4128768 | tf_op jit(solution)/shard_map/pallas_call | solution.py:233
  40.6 7.1 %collective-permute-done.7.refs_3_.refs_7_ = bf16[256,1152]{1,0:T(8,128)(2,1)S(1)} collective-permute-done((bf16[256,1152]{1,0:T(8,128)(2,1)S(1)}, bf16[256,1152]{1,0:T(8,128)(2,1)S(1)}, u32[]{:S(2)}, u32[]{:S(2)}) %collective-permute-start.7) | collective-permute-done | bytes 589856 | tf_op jit(solution)/shard_map/ppermute | solution.py:57
  50.1 1.5 %shard_map.44 = (bf16[256,1792]{1,0:T(8,128)(2,1)S(1)}, f32[256,128]{1,0:T(8,128)S(1)}) custom-call(s32[8,2048]{1,0:T(8,128)S(1)} %shard_map.37.flags, bf16[256,1152]{1,0:T(8,128)(2,1)S(1)} %collective-permute-done.8.refs_0_.refs_3_, bf16[256,1408]{1,0:T(8,128)(2,1)S(1)} %shard_map.40.refs_3_.refs_1_.refs_10_, ...), custom_call_target="tpu_custom_call" | custom-call | flops 1056964608 | bytes 4718592 | tf_op jit(solution)/shard_map/pallas_call | solution.py:233
  53.6 1.5 %collective-permute-start.12 = (bf16[272,256]{1,0:T(8,128)(2,1)S(1)}, bf16[272,256]{1,0:T(8,128)(2,1)S(1)}, u32[]{:S(2)}, u32[]{:S(2)}) collective-permute-start(bf16[272,256]{1,0:T(8,128)(2,1)S(1)} %get-tuple-element.56), channel_id=1, source_target_pairs={{8,0},{9,1},{10,2},{11,3},{12,4},{13,5},{14,6},{15,7},{0,8},{1,9},... | collective-permute-start | bytes 417800 | tf_op jit(solution)/shard_map/ppermute | solution.py:57
  55.1 2.5 %collective-permute-start.13 = (bf16[272,256]{1,0:T(8,128)(2,1)S(1)}, bf16[272,256]{1,0:T(8,128)(2,1)S(1)}, u32[]{:S(2)}, u32[]{:S(2)}) collective-permute-start(bf16[272,256]{1,0:T(8,128)(2,1)S(1)} %get-tuple-element.57), channel_id=1, source_target_pairs={{2,0},{3,1},{0,2},{1,3},{6,4},{7,5},{4,6},{5,7},{10,8},{11,9},{8,1... | collective-permute-start | bytes 417800 | tf_op jit(solution)/shard_map/ppermute | solution.py:57
  58.9 2.3 %collective-permute-done.13.refs_1_ = bf16[272,256]{1,0:T(8,128)(2,1)S(1)} collective-permute-done((bf16[272,256]{1,0:T(8,128)(2,1)S(1)}, bf16[272,256]{1,0:T(8,128)(2,1)S(1)}, u32[]{:S(2)}, u32[]{:S(2)}) %collective-permute-start.13) | collective-permute-done | bytes 139296 | tf_op jit(solution)/shard_map/ppermute | solution.py:57
  61.3 2.3 %collective-permute-done.14.refs_2_ = bf16[272,256]{1,0:T(8,128)(2,1)S(1)} collective-permute-done((bf16[272,256]{1,0:T(8,128)(2,1)S(1)}, bf16[272,256]{1,0:T(8,128)(2,1)S(1)}, u32[]{:S(2)}, u32[]{:S(2)}) %collective-permute-start.14) | collective-permute-done | bytes 139296 | tf_op jit(solution)/shard_map/ppermute | solution.py:57
  63.7 1.2 %collective-permute-start.18 = (bf16[256,256]{1,0:T(8,128)(2,1)S(1)}, bf16[256,256]{1,0:T(8,128)(2,1)S(1)}, u32[]{:S(2)}, u32[]{:S(2)}) collective-permute-start(bf16[256,256]{1,0:T(8,128)(2,1)S(1)} %get-tuple-element.59.refs_5_), channel_id=1, source_target_pairs={{4,0},{5,1},{6,2},{7,3},{0,4},{1,5},{2,6},{3,7},{12,8},{13,9},{14,... | collective-permute-start | bytes 393224 | tf_op jit(solution)/shard_map/ppermute | solution.py:57
  65.0 1.3 %collective-permute-start.16 = (bf16[256,256]{1,0:T(8,128)(2,1)S(1)}, bf16[256,256]{1,0:T(8,128)(2,1)S(1)}, u32[]{:S(2)}, u32[]{:S(2)}) collective-permute-start(bf16[256,256]{1,0:T(8,128)(2,1)S(1)} %get-tuple-element.59.refs_5_), channel_id=1, source_target_pairs={{16,0},{17,1},{18,2},{19,3},{20,4},{21,5},{22,6},{23,7},{24,8},{25... | collective-permute-start | bytes 393224 | tf_op jit(solution)/shard_map/ppermute | solution.py:57
  66.2 4.9 %collective-permute-done.18.refs_9_ = bf16[256,256]{1,0:T(8,128)(2,1)S(1)} collective-permute-done((bf16[256,256]{1,0:T(8,128)(2,1)S(1)}, bf16[256,256]{1,0:T(8,128)(2,1)S(1)}, u32[]{:S(2)}, u32[]{:S(2)}) %collective-permute-start.18) | collective-permute-done | bytes 131104 | tf_op jit(solution)/shard_map/ppermute | solution.py:57
  72.4 3.7 %collective-permute-done.20.refs_6_ = bf16[256,256]{1,0:T(8,128)(2,1)S(1)} collective-permute-done((bf16[256,256]{1,0:T(8,128)(2,1)S(1)}, bf16[256,256]{1,0:T(8,128)(2,1)S(1)}, u32[]{:S(2)}, u32[]{:S(2)}) %collective-permute-start.20) | collective-permute-done | bytes 131104 | tf_op jit(solution)/shard_map/ppermute | solution.py:57
  79.2 2.2 %collective-permute-start.24 = (bf16[256,256]{1,0:T(8,128)(2,1)S(1)}, bf16[256,256]{1,0:T(8,128)(2,1)S(1)}, u32[]{:S(2)}, u32[]{:S(2)}) collective-permute-start(bf16[256,256]{1,0:T(8,128)(2,1)S(1)} %get-tuple-element.64), channel_id=1, source_target_pairs={{10,0},{11,1},{8,2},{9,3},{14,4},{15,5},{12,6},{13,7},{2,8},{3,9},... | collective-permute-start | bytes 393224 | tf_op jit(solution)/shard_map/ppermute | solution.py:57
  81.4 2.1 %collective-permute-done.22.refs_0_ = bf16[256,256]{1,0:T(8,128)(2,1)S(1)} collective-permute-done((bf16[256,256]{1,0:T(8,128)(2,1)S(1)}, bf16[256,256]{1,0:T(8,128)(2,1)S(1)}, u32[]{:S(2)}, u32[]{:S(2)}) %collective-permute-start.22) | collective-permute-done | bytes 131104 | tf_op jit(solution)/shard_map/ppermute | solution.py:57
  83.5 1.4 %collective-permute-done.23.refs_1_ = bf16[256,256]{1,0:T(8,128)(2,1)S(1)} collective-permute-done((bf16[256,256]{1,0:T(8,128)(2,1)S(1)}, bf16[256,256]{1,0:T(8,128)(2,1)S(1)}, u32[]{:S(2)}, u32[]{:S(2)}) %collective-permute-start.23) | collective-permute-done | bytes 131104 | tf_op jit(solution)/shard_map/ppermute | solution.py:57
  84.9 2.6 %collective-permute-done.24.refs_2_ = bf16[256,256]{1,0:T(8,128)(2,1)S(1)} collective-permute-done((bf16[256,256]{1,0:T(8,128)(2,1)S(1)}, bf16[256,256]{1,0:T(8,128)(2,1)S(1)}, u32[]{:S(2)}, u32[]{:S(2)}) %collective-permute-start.24) | collective-permute-done | bytes 131104 | tf_op jit(solution)/shard_map/ppermute | solution.py:57
  (50 shorter events, 15.1 us)
Async XLA Ops:
  1.4 30.2 %collective-permute-start = (bf16[256,1152]{1,0:T(8,128)(2,1)S(1)}, bf16[256,1152]{1,0:T(8,128)(2,1)S(1)}, u32[]{:S(2)}, u32[]{:S(2)}) collective-permute-start(bf16[256,1152]{1,0:T(8,128)(2,1)S(1)} %shard_map.38.unit_ref.refs_0_), channel_id=1, source_target_pairs={{4,0},{5,1},{6,2},{7,3},{0,4},{1,5},{2,6},{3,7},{12,8},{13,9},{14,... | collective-permute-start | bytes 1769480 | tf_op jit(solution)/shard_map/ppermute | solution.py:57
  5.5 26.3 %collective-permute-start.2 = (bf16[256,1152]{1,0:T(8,128)(2,1)S(1)}, bf16[256,1152]{1,0:T(8,128)(2,1)S(1)}, u32[]{:S(2)}, u32[]{:S(2)}) collective-permute-start(bf16[256,1152]{1,0:T(8,128)(2,1)S(1)} %shard_map.38.unit_ref.refs_0_), channel_id=1, source_target_pairs={{2,0},{3,1},{0,2},{1,3},{6,4},{7,5},{4,6},{5,7},{10,8},{11,9},{8,1... | collective-permute-start | bytes 1769480 | tf_op jit(solution)/shard_map/ppermute | solution.py:57
  7.1 24.7 %collective-permute-start.1 = (bf16[256,1152]{1,0:T(8,128)(2,1)S(1)}, bf16[256,1152]{1,0:T(8,128)(2,1)S(1)}, u32[]{:S(2)}, u32[]{:S(2)}) collective-permute-start(bf16[256,1152]{1,0:T(8,128)(2,1)S(1)} %shard_map.38.unit_ref.refs_0_), channel_id=1, source_target_pairs={{8,0},{9,1},{10,2},{11,3},{12,4},{13,5},{14,6},{15,7},{0,8},{1,9},... | collective-permute-start | bytes 1769480 | tf_op jit(solution)/shard_map/ppermute | solution.py:57
  9.5 22.2 %collective-permute-start.4 = (bf16[256,1408]{1,0:T(8,128)(2,1)S(1)}, bf16[256,1408]{1,0:T(8,128)(2,1)S(1)}, u32[]{:S(2)}, u32[]{:S(2)}) collective-permute-start(bf16[256,1408]{1,0:T(8,128)(2,1)S(1)} %shard_map.40.refs_3_.refs_1_.refs_10_), channel_id=1, source_target_pairs={{16,0},{17,1},{18,2},{19,3},{20,4},{21,5},{22,6},{23,7},{24,8},{25... | collective-permute-start | bytes 2162696 | tf_op jit(solution)/shard_map/ppermute | solution.py:57
  11.1 20.7 %collective-permute-start.3 = (bf16[256,1408]{1,0:T(8,128)(2,1)S(1)}, bf16[256,1408]{1,0:T(8,128)(2,1)S(1)}, u32[]{:S(2)}, u32[]{:S(2)}) collective-permute-start(bf16[256,1408]{1,0:T(8,128)(2,1)S(1)} %shard_map.40.refs_3_.refs_1_.refs_10_), channel_id=1, source_target_pairs={{1,0},{0,1},{3,2},{2,3},{5,4},{4,5},{7,6},{6,7},{9,8},{8,9},{11,10... | collective-permute-start | bytes 2162696 | tf_op jit(solution)/shard_map/ppermute | solution.py:57
  31.8 6.4 %collective-permute-start.5 = (bf16[256,1408]{1,0:T(8,128)(2,1)S(1)}, bf16[256,1408]{1,0:T(8,128)(2,1)S(1)}, u32[]{:S(2)}, u32[]{:S(2)}) collective-permute-start(bf16[256,1408]{1,0:T(8,128)(2,1)S(1)} %collective-permute-done.4.refs_5_.refs_3_.refs_0_.refs_12_), channel_id=1, source_target_pairs={{1,0},{0,1},{3,2},{2,3},{5,4},{4,5},{7,6},{6,7},{9,8},{8,9},{11,10... | collective-permute-start | bytes 2162696 | tf_op jit(solution)/shard_map/ppermute | solution.py:57
  31.8 5.0 %collective-permute-start.6 = (bf16[256,1152]{1,0:T(8,128)(2,1)S(1)}, bf16[256,1152]{1,0:T(8,128)(2,1)S(1)}, u32[]{:S(2)}, u32[]{:S(2)}) collective-permute-start(bf16[256,1152]{1,0:T(8,128)(2,1)S(1)} %collective-permute-done.refs_3_.refs_5_), channel_id=1, source_target_pairs={{1,0},{0,1},{3,2},{2,3},{5,4},{4,5},{7,6},{6,7},{9,8},{8,9},{11,10... | collective-permute-start | bytes 1769480 | tf_op jit(solution)/shard_map/ppermute | solution.py:57
  32.3 15.3 %collective-permute-start.7 = (bf16[256,1152]{1,0:T(8,128)(2,1)S(1)}, bf16[256,1152]{1,0:T(8,128)(2,1)S(1)}, u32[]{:S(2)}, u32[]{:S(2)}) collective-permute-start(bf16[256,1152]{1,0:T(8,128)(2,1)S(1)} %collective-permute-done.refs_3_.refs_5_), channel_id=1, source_target_pairs={{16,0},{17,1},{18,2},{19,3},{20,4},{21,5},{22,6},{23,7},{24,8},{25... | collective-permute-start | bytes 1769480 | tf_op jit(solution)/shard_map/ppermute | solution.py:57
  33.9 14.6 %collective-permute-start.10 = (bf16[512,256]{1,0:T(8,128)(2,1)S(1)}, bf16[512,256]{1,0:T(8,128)(2,1)S(1)}, u32[]{:S(2)}, u32[]{:S(2)}) collective-permute-start(bf16[512,256]{1,0:T(8,128)(2,1)S(1)} %shard_map.46), channel_id=1, source_target_pairs={{4,0},{5,1},{6,2},{7,3},{0,4},{1,5},{2,6},{3,7},{12,8},{13,9},{14,... | collective-permute-start | bytes 786440 | tf_op jit(solution)/shard_map/ppermute | solution.py:57
  35.3 14.8 %collective-permute-start.8 = (bf16[256,1152]{1,0:T(8,128)(2,1)S(1)}, bf16[256,1152]{1,0:T(8,128)(2,1)S(1)}, u32[]{:S(2)}, u32[]{:S(2)}) collective-permute-start(bf16[256,1152]{1,0:T(8,128)(2,1)S(1)} %collective-permute-done.2.refs_2_), channel_id=1, source_target_pairs={{8,0},{9,1},{10,2},{11,3},{12,4},{13,5},{14,6},{15,7},{0,8},{1,9},... | collective-permute-start | bytes 1769480 | tf_op jit(solution)/shard_map/ppermute | solution.py:57
  47.6 3.9 %collective-permute-start.9 = (bf16[256,1152]{1,0:T(8,128)(2,1)S(1)}, bf16[256,1152]{1,0:T(8,128)(2,1)S(1)}, u32[]{:S(2)}, u32[]{:S(2)}) collective-permute-start(bf16[256,1152]{1,0:T(8,128)(2,1)S(1)} %collective-permute-done.7.refs_3_.refs_7_), channel_id=1, source_target_pairs={{1,0},{0,1},{3,2},{2,3},{5,4},{4,5},{7,6},{6,7},{9,8},{8,9},{11,10... | collective-permute-start | bytes 1769480 | tf_op jit(solution)/shard_map/ppermute | solution.py:57
  48.5 4.0 %collective-permute-start.11 = (bf16[512,256]{1,0:T(8,128)(2,1)S(1)}, bf16[512,256]{1,0:T(8,128)(2,1)S(1)}, u32[]{:S(2)}, u32[]{:S(2)}) collective-permute-start(bf16[512,256]{1,0:T(8,128)(2,1)S(1)} %shard_map.47.refs_14_), channel_id=1, source_target_pairs={{1,0},{0,1},{3,2},{2,3},{5,4},{4,5},{7,6},{6,7},{9,8},{8,9},{11,10... | collective-permute-start | bytes 786440 | tf_op jit(solution)/shard_map/ppermute | solution.py:57
  53.6 5.3 %collective-permute-start.12 = (bf16[272,256]{1,0:T(8,128)(2,1)S(1)}, bf16[272,256]{1,0:T(8,128)(2,1)S(1)}, u32[]{:S(2)}, u32[]{:S(2)}) collective-permute-start(bf16[272,256]{1,0:T(8,128)(2,1)S(1)} %get-tuple-element.56), channel_id=1, source_target_pairs={{8,0},{9,1},{10,2},{11,3},{12,4},{13,5},{14,6},{15,7},{0,8},{1,9},... | collective-permute-start | bytes 417800 | tf_op jit(solution)/shard_map/ppermute | solution.py:57
  55.1 6.1 %collective-permute-start.13 = (bf16[272,256]{1,0:T(8,128)(2,1)S(1)}, bf16[272,256]{1,0:T(8,128)(2,1)S(1)}, u32[]{:S(2)}, u32[]{:S(2)}) collective-permute-start(bf16[272,256]{1,0:T(8,128)(2,1)S(1)} %get-tuple-element.57), channel_id=1, source_target_pairs={{2,0},{3,1},{0,2},{1,3},{6,4},{7,5},{4,6},{5,7},{10,8},{11,9},{8,1... | collective-permute-start | bytes 417800 | tf_op jit(solution)/shard_map/ppermute | solution.py:57
  57.6 6.0 %collective-permute-start.14 = (bf16[272,256]{1,0:T(8,128)(2,1)S(1)}, bf16[272,256]{1,0:T(8,128)(2,1)S(1)}, u32[]{:S(2)}, u32[]{:S(2)}) collective-permute-start(bf16[272,256]{1,0:T(8,128)(2,1)S(1)} %get-tuple-element.58), channel_id=1, source_target_pairs={{10,0},{11,1},{8,2},{9,3},{14,4},{15,5},{12,6},{13,7},{2,8},{3,9},... | collective-permute-start | bytes 417800 | tf_op jit(solution)/shard_map/ppermute | solution.py:57
  63.7 7.3 %collective-permute-start.18 = (bf16[256,256]{1,0:T(8,128)(2,1)S(1)}, bf16[256,256]{1,0:T(8,128)(2,1)S(1)}, u32[]{:S(2)}, u32[]{:S(2)}) collective-permute-start(bf16[256,256]{1,0:T(8,128)(2,1)S(1)} %get-tuple-element.59.refs_5_), channel_id=1, source_target_pairs={{4,0},{5,1},{6,2},{7,3},{0,4},{1,5},{2,6},{3,7},{12,8},{13,9},{14,... | collective-permute-start | bytes 393224 | tf_op jit(solution)/shard_map/ppermute | solution.py:57
  65.0 7.4 %collective-permute-start.16 = (bf16[256,256]{1,0:T(8,128)(2,1)S(1)}, bf16[256,256]{1,0:T(8,128)(2,1)S(1)}, u32[]{:S(2)}, u32[]{:S(2)}) collective-permute-start(bf16[256,256]{1,0:T(8,128)(2,1)S(1)} %get-tuple-element.59.refs_5_), channel_id=1, source_target_pairs={{16,0},{17,1},{18,2},{19,3},{20,4},{21,5},{22,6},{23,7},{24,8},{25... | collective-permute-start | bytes 393224 | tf_op jit(solution)/shard_map/ppermute | solution.py:57
  71.1 5.0 %collective-permute-start.20 = (bf16[256,256]{1,0:T(8,128)(2,1)S(1)}, bf16[256,256]{1,0:T(8,128)(2,1)S(1)}, u32[]{:S(2)}, u32[]{:S(2)}) collective-permute-start(bf16[256,256]{1,0:T(8,128)(2,1)S(1)} %collective-permute-done.18.refs_9_), channel_id=1, source_target_pairs={{16,0},{17,1},{18,2},{19,3},{20,4},{21,5},{22,6},{23,7},{24,8},{25... | collective-permute-start | bytes 393224 | tf_op jit(solution)/shard_map/ppermute | solution.py:57
  71.8 4.2 %collective-permute-start.15 = (bf16[256,256]{1,0:T(8,128)(2,1)S(1)}, bf16[256,256]{1,0:T(8,128)(2,1)S(1)}, u32[]{:S(2)}, u32[]{:S(2)}) collective-permute-start(bf16[256,256]{1,0:T(8,128)(2,1)S(1)} %get-tuple-element.59.refs_5_), channel_id=1, source_target_pairs={{1,0},{0,1},{3,2},{2,3},{5,4},{4,5},{7,6},{6,7},{9,8},{8,9},{11,10... | collective-permute-start | bytes 393224 | tf_op jit(solution)/shard_map/ppermute | solution.py:57
  71.8 4.2 %collective-permute-start.19 = (bf16[256,256]{1,0:T(8,128)(2,1)S(1)}, bf16[256,256]{1,0:T(8,128)(2,1)S(1)}, u32[]{:S(2)}, u32[]{:S(2)}) collective-permute-start(bf16[256,256]{1,0:T(8,128)(2,1)S(1)} %collective-permute-done.18.refs_9_), channel_id=1, source_target_pairs={{1,0},{0,1},{3,2},{2,3},{5,4},{4,5},{7,6},{6,7},{9,8},{8,9},{11,10... | collective-permute-start | bytes 393224 | tf_op jit(solution)/shard_map/ppermute | solution.py:57
  72.4 3.7 %collective-permute-start.17 = (bf16[256,256]{1,0:T(8,128)(2,1)S(1)}, bf16[256,256]{1,0:T(8,128)(2,1)S(1)}, u32[]{:S(2)}, u32[]{:S(2)}) collective-permute-start(bf16[256,256]{1,0:T(8,128)(2,1)S(1)} %collective-permute-done.16.refs_7_), channel_id=1, source_target_pairs={{1,0},{0,1},{3,2},{2,3},{5,4},{4,5},{7,6},{6,7},{9,8},{8,9},{11,10... | collective-permute-start | bytes 393224 | tf_op jit(solution)/shard_map/ppermute | solution.py:57
  77.8 5.7 %collective-permute-start.22 = (bf16[256,256]{1,0:T(8,128)(2,1)S(1)}, bf16[256,256]{1,0:T(8,128)(2,1)S(1)}, u32[]{:S(2)}, u32[]{:S(2)}) collective-permute-start(bf16[256,256]{1,0:T(8,128)(2,1)S(1)} %get-tuple-element.62), channel_id=1, source_target_pairs={{8,0},{9,1},{10,2},{11,3},{12,4},{13,5},{14,6},{15,7},{0,8},{1,9},... | collective-permute-start | bytes 393224 | tf_op jit(solution)/shard_map/ppermute | solution.py:57
  78.6 6.4 %collective-permute-start.23 = (bf16[256,256]{1,0:T(8,128)(2,1)S(1)}, bf16[256,256]{1,0:T(8,128)(2,1)S(1)}, u32[]{:S(2)}, u32[]{:S(2)}) collective-permute-start(bf16[256,256]{1,0:T(8,128)(2,1)S(1)} %get-tuple-element.63), channel_id=1, source_target_pairs={{2,0},{3,1},{0,2},{1,3},{6,4},{7,5},{4,6},{5,7},{10,8},{11,9},{8,1... | collective-permute-start | bytes 393224 | tf_op jit(solution)/shard_map/ppermute | solution.py:57
  79.2 8.3 %collective-permute-start.24 = (bf16[256,256]{1,0:T(8,128)(2,1)S(1)}, bf16[256,256]{1,0:T(8,128)(2,1)S(1)}, u32[]{:S(2)}, u32[]{:S(2)}) collective-permute-start(bf16[256,256]{1,0:T(8,128)(2,1)S(1)} %get-tuple-element.64), channel_id=1, source_target_pairs={{10,0},{11,1},{8,2},{9,3},{14,4},{15,5},{12,6},{13,7},{2,8},{3,9},... | collective-permute-start | bytes 393224 | tf_op jit(solution)/shard_map/ppermute | solution.py:57
  (4 other events, 14.4 us)
